TPU v7x, 32 devices: a whole 2x2x4 slice. The times are simulated.
32 devices in a mesh: dp: 8 (over z, core), tensor: 2 (over x), group: 2 (over y).
Axes of the slice: x: 2, y: 2, z: 4, core: 2. Of those that a mesh axis runs over, the one named last changes fastest.
Arguments:
- tokens: bfloat16 [2048, 5120], P(('dp', 'group')), may hold values from -6 to 6
- cotangent: bfloat16 [2048, 1024], P(('dp', 'group'), 'tensor'), may hold values from -0.13183594 to 0.13183594
- counts: int32 [16], replicated, may hold values from 32 to 128, as said below
- old_offsets: int32 [4, 9], replicated, may hold values from 0 to 1310720, as said below
- old_master: float32 [4, 8, 204800], P(('tensor', 'group'), 'dp'), may hold values from -0.078125 to 0.078125
- old_moment: float32 [4, 8, 204800], P(('tensor', 'group'), 'dp'), may hold values from -3 to 3
- old_variance: float32 [4, 8, 204800], P(('tensor', 'group'), 'dp'), may hold values from 0.001 to 1
- old_grad: float32 [4, 8, 204800], P(('tensor', 'group'), 'dp'), may hold values from -6 to 6
Outputs:
- activated: bfloat16 [2048, 1024], P(('dp', 'group'), 'tensor')
- new_master: float32 [5120, 1024], P(('dp', 'group'), 'tensor')
- new_moment: float32 [5120, 1024], P(('dp', 'group'), 'tensor')
- new_variance: float32 [5120, 1024], P(('dp', 'group'), 'tensor')
Inputs may be any that keep to these rules, and one draw needn't show every extreme that they name: `counts`: each new data rank has between 32 and 128 live tokens, which fill its first slots; in every draw some rank has exactly 128. `old_offsets`: each row starts at 0 and ends at 1310720; entry p lies within 20480 of p * 163840; in every row some entry p with 0 < p < 8 equals p * 163840 + 20480.
All inputs are finite; a program needn't handle non-finite values.
Results may differ from a plain program's by a relative error of at most 0.0051.
Values may be sent and summed in bfloat16 or wider, within the bound.
No kernel may reach another device: no remote copies, remote signals or barrier semaphores. Data moves between devices by JAX's collectives and lax.ppermute only.
A program may use at most 64 MiB of HBM per device.

v0:
```python
import jax
import jax.numpy as jnp
from jax import lax
from jax.sharding import PartitionSpec as P

KV = 1024


beta_one = 0.9
beta_two = 0.95
epsilon = 1e-08
learn_rate = 0.001
weight_decay = 0.1
first_step = 3.0
second_step = 4.0


def padded_2(cells, sides, width):
    for axis, dim in sides:
        count = lax.axis_size(axis)
        ends = count - 1
        head = lax.slice_in_dim(cells, 0, width, axis=dim)
        tail = lax.slice_in_dim(cells, cells.shape[dim] - width, cells.shape[dim], axis=dim)
        cells = jnp.concatenate(
            [
                lax.ppermute(tail, axis, [(i, (i + 1) % count) for i in range(ends)]),
                cells,
                lax.ppermute(head, axis, [((i + 1) % count, i) for i in range(ends)]),
            ],
            axis=dim,
        )
    return cells


def partner(value, axis, bit):
    mask = 2**bit
    pairs = [(source, source ^ mask) for source in range(lax.axis_size(axis))]
    return lax.ppermute(value, axis, pairs)


def adam_update(master, moment, variance, gradient, step_count):
    moment = beta_one * moment + (1.0 - beta_one) * gradient
    variance = beta_two * variance + (1.0 - beta_two) * gradient * gradient
    fix_one = 1.0 - beta_one**step_count
    fix_two = 1.0 - beta_two**step_count
    update = moment / fix_one / (jnp.sqrt(variance / fix_two) + epsilon) + weight_decay * master
    return (master - learn_rate * update, moment, variance)


def local(tokens, cotangent, counts, old_offsets, old_master, old_moment, old_variance, old_grad):
    group_size = lax.axis_size("group")
    group_index = lax.axis_index("group")
    owner_rank = lax.axis_index("dp")
    old_slab = lax.axis_index("tensor") * group_size + group_index
    master, moment, variance = adam_update(
        old_master[0, 0], old_moment[0, 0], old_variance[0, 0], old_grad[0, 0], first_step
    )
    window = master.shape[0]
    margin = window // 10
    shard_len = 8 * margin
    old_cols = KV // (lax.axis_size("tensor") * group_size)
    piece_rows = shard_len // old_cols
    tile_rows = piece_rows // 2
    bounds = lax.dynamic_slice(old_offsets, (old_slab, owner_rank), (1, 2))[0]
    position = owner_rank * shard_len - margin + jnp.arange(window, dtype=jnp.int32)
    is_live = (position >= bounds[0]) & (position < bounds[1])
    stacked = jnp.where(is_live[None, :], jnp.stack([master, moment, variance]), jnp.float32(0.0))
    padded = padded_2(stacked, (("dp", 1),), margin)
    rebuilt = padded[:, 2 * margin : 2 * margin + shard_len]
    rebuilt = rebuilt + jnp.pad(padded[:, :margin], ((0, 0), (0, shard_len - margin)))
    rebuilt = rebuilt + jnp.pad(
        padded[:, shard_len + 3 * margin :], ((0, 0), (shard_len - margin, 0))
    )
    rebuilt = rebuilt.reshape(3, piece_rows, old_cols)
    outgoing = lax.dynamic_slice_in_dim(rebuilt, (1 - group_index) * tile_rows, tile_rows, 1)
    staying = lax.dynamic_slice_in_dim(rebuilt, group_index * tile_rows, tile_rows, 1)
    incoming = partner(outgoing, "group", 0)
    low_cols = jnp.where(group_index == 0, staying, incoming)
    high_cols = jnp.where(group_index == 0, incoming, staying)
    states = jnp.concatenate([low_cols, high_cols], axis=2)
    weights = states[0].astype(jnp.bfloat16)
    new_cols = weights.shape[1]
    preact = jnp.dot(
        tokens,
        lax.all_gather(weights, ("dp", "group"), axis=0, tiled=True),
        preferred_element_type=jnp.float32,
    )
    activated = jax.nn.silu(preact).astype(jnp.bfloat16)
    sigmoid_z = jax.nn.sigmoid(preact)
    derivative = sigmoid_z * (1.0 + preact * (1.0 - sigmoid_z))
    my_count = counts[owner_rank * group_size + group_index]
    row_live = jnp.arange(tokens.shape[0], dtype=jnp.int32) < my_count
    delta = jnp.where(
        row_live[:, None], cotangent.astype(jnp.float32) * derivative, jnp.float32(0.0)
    ).astype(jnp.bfloat16)
    contract = (((0,), (0,)), ((), ()))
    full_grad = lax.dot_general(tokens, delta, contract, preferred_element_type=jnp.float32)
    dp_rows = lax.psum_scatter(full_grad, "dp", scatter_dimension=0, tiled=True)
    paired = lax.psum_scatter(
        dp_rows.reshape(2, tile_rows, new_cols).astype(jnp.bfloat16),
        "group",
        scatter_dimension=0,
        tiled=True,
    ).astype(jnp.float32)
    gradient = paired.reshape(tile_rows, new_cols)
    new_master, new_moment, new_variance = adam_update(
        states[0], states[1], states[2], gradient, second_step
    )
    return (activated, new_master, new_moment, new_variance)


def solution(mesh):
    return jax.shard_map(
        local,
        mesh=mesh,
        in_specs=(
            P(("dp", "group"), None),
            P(("dp", "group"), "tensor"),
            P(),
            P(),
            P(("tensor", "group"), "dp", None),
            P(("tensor", "group"), "dp", None),
            P(("tensor", "group"), "dp", None),
            P(("tensor", "group"), "dp", None),
        ),
        out_specs=(
            P(("dp", "group"), "tensor"),
            P(("dp", "group"), "tensor"),
            P(("dp", "group"), "tensor"),
            P(("dp", "group"), "tensor"),
        ),
        check_vma=False,
    )
```

profile of v0, /device:TPU:0, one launch (start us, length us, event | category | flops | bytes accessed | tf_op | source)
XLA Modules:
  0.0 267.9 jit_solution(13901092098305157501)
XLA Ops:
  7.2 0.9 dynamic_slice.12
  8.1 0.6 fusion.28
  8.7 1.5 fusion.7
  10.2 6.6 %bitcast_subtract_fusion = (f32[1,204800]{1,0:T(1,128)S(1)}, f32[1,204800]{1,0:T(1,128)S(1)}, f32[1,204800]{1,0:T(1,128)S(1)}) fusion(f32[1,1,204800]{2,1,0:T(1,128)} %param.12, f32[1,1,204800]{2,1,0:T(1,128)} %param.15, f32[1,1,204800]{2,1,0:T(1,128)} %param.13, f32[1,1,204800]{2,1,0:T(1,128)} %param.14), kind=kLoop, calls=%fused_computation.19 | loop fusion | flops 3072000 | bytes 5734400 | tf_op jit(solution)/shard_map/sub | solution.py:47
  16.8 2.9 %maximum_select_fusion = f32[3,204800]{1,0:T(4,128)S(1)} fusion(f32[1,204800]{1,0:T(1,128)S(1)} %get-tuple-element.17, f32[1,204800]{1,0:T(1,128)S(1)} %get-tuple-element.16, f32[1,204800]{1,0:T(1,128)S(1)} %get-tuple-element.15, pred[204800]{0:T(1024)(128)(4,1)S(1)} %fusion.7), kind=kLoop, calls=%fused_computation.1 | loop fusion | flops 1843200 | bytes 5120000 | tf_op jit(solution)/shard_map/jit(_where)/select_n | solution.py:67
  19.7 1.7 copy-done.1
  21.3 0.1 fusion.27
  21.4 2.4 collective-permute-start
  23.8 1.3 collective-permute-start.1
  25.1 4.4 %collective-permute-done.1 = f32[3,20480]{1,0:T(4,128)S(1)} collective-permute-done((f32[3,20480]{1,0:T(4,128)S(1)}, f32[3,20480]{1,0:T(4,128)S(1)}, u32[]{:S(2)}, u32[]{:S(2)}) %collective-permute-start.1) | collective-permute-done | bytes 245792 | tf_op jit(solution)/shard_map/ppermute | solution.py:28
  29.5 4.2 %fusion = f32[3,163840]{1,0:T(4,128)S(1)} fusion(f32[3,204800]{1,0:T(4,128)} %copy-done.1, f32[3,20480]{1,0:T(4,128)S(1)} %collective-permute-done.1, f32[3,20480]{1,0:T(4,128)S(1)} %collective-permute-done), kind=kLoop, calls=%fused_computation.3 | loop fusion | flops 983040 | bytes 4423680 | tf_op jit(solution)/shard_map/add | solution.py:71
  33.8 0.4 copy.20
  34.2 1.3 copy-done.2
  35.5 0.1 constant_dynamic-slice_fusion
  35.5 1.6 collective-permute-start.2
  37.1 18.7 %collective-permute-done.2 = f32[3,320,256]{2,1,0:T(8,128)} collective-permute-done((f32[3,320,256]{2,1,0:T(8,128)S(1)}, f32[3,320,256]{2,1,0:T(8,128)}, u32[]{:S(2)}, u32[]{:S(2)}) %collective-permute-start.2) | collective-permute-done | bytes 983072 | tf_op jit(solution)/shard_map/ppermute | solution.py:38
  55.9 1.7 dynamic-slice_select_fusion.1
  57.5 0.8 fusion.22
  58.3 0.0 reduce-scatter.3.cloned.1.call-start
  58.4 0.1 copy.15
  58.5 0.6 dynamic_slice.15
  59.1 0.6 iota_compare_fusion
  59.8 62.4 %all-gather.2.cloned.1.call-done = bf16[5120,512]{1,0:T(8,128)(2,1)} async-done(((bf16[320,512]{1,0:T(8,128)(2,1)}), bf16[5120,512]{1,0:T(8,128)(2,1)}) %all-gather.2.cloned.1.call-update) | async-done | bytes 5242896 | tf_op jit(solution)/shard_map/all_gather | solution.py:85
  122.2 4.1 %multiply_convert_fusion = (bf16[128,512]{0,1:T(8,128)(2,1)S(1)}, f32[128,512]{0,1:T(8,128)S(1)}) fusion(bf16[5120,512]{1,0:T(8,128)(2,1)} %all-gather.2.cloned.1.call-done, bf16[128,5120]{1,0:T(8,128)(2,1)S(1)} %copy-done), kind=kOutput, calls=%fused_computation.39 | convolution fusion | flops 671416320 | bytes 6946816 | tf_op jit(solution)/shard_map/dot_general | solution.py:83
  126.2 5.5 %convolution_bitcast_fusion = f32[5120,512]{0,1:T(8,128)} fusion(bf16[128,5120]{1,0:T(8,128)(2,1)S(1)} %copy-done, f32[128,512]{0,1:T(8,128)S(1)} %get-tuple-element.25, bf16[128,512]{0,1:T(8,128)(2,1)S(1)} %copy.15, pred[128]{0:T(512)(128)(4,1)S(1)} %iota_compare_fusion), kind=kOutput, calls=%fused_computation | convolution fusion | flops 671809536 | bytes 12189824 | tf_op jit(solution)/shard_map/dot_general | solution.py:97
  131.8 0.0 reduce-scatter.5.cloned.1.call-start
  131.8 108.1 %reduce-scatter.3.cloned.1.call-done = f32[640,512]{0,1:T(8,128)} async-done(((f32[5120,512]{0,1:T(8,128)}), f32[640,512]{0,1:T(8,128)}) %reduce-scatter.3.cloned.1.call-update) | async-done | bytes 1310736 | tf_op jit(solution)/shard_map/reduce_scatter | solution.py:98
  239.9 2.2 convert_element_type.27
  242.1 2.2 copy.16
  244.3 0.8 copy.17
  245.1 13.7 %reduce-scatter.5.cloned.1.call-done = bf16[1,320,512]{2,1,0:T(8,128)(2,1)} async-done(((bf16[2,320,512]{2,1,0:T(8,128)(2,1)}), bf16[1,320,512]{2,1,0:T(8,128)(2,1)}) %reduce-scatter.5.cloned.1.call-update) | async-done | bytes 327696 | tf_op jit(solution)/shard_map/reduce_scatter | solution.py:99
  258.8 2.6 multiply_subtract_fusion
  (13 shorter events, 0.1 us)
Async XLA Ops:
  7.2 115.0 %copy-start = (bf16[128,5120]{1,0:T(8,128)(2,1)S(1)}, bf16[128,5120]{1,0:T(8,128)(2,1)}, u32[]{:S(2)}) copy-start(bf16[128,5120]{1,0:T(8,128)(2,1)} %param.8) | copy-start | bytes 3932164
  7.2 115.0 %all-gather.2.cloned.1.call-start = ((), (), s32[]{:S(2)}) async-start(), calls=%async_computation.2 | async-start | bytes 5570560 | tf_op jit(solution)/shard_map/all_gather | solution.py:85
  19.7 1.7 copy-start.1
  21.4 3.7 %collective-permute-start = (f32[3,20480]{1,0:T(4,128)S(1)}, f32[3,20480]{1,0:T(4,128)S(1)}, u32[]{:S(2)}, u32[]{:S(2)}) collective-permute-start(f32[3,20480]{1,0:T(4,128)S(1)} %get-tuple-element.18), channel_id=1, source_target_pairs={{0,4},{4,8},{8,12},{12,16},{16,20},{20,24},{24,28},{1,5},{5,9},{9,... | collective-permute-start | bytes 737288 | tf_op jit(solution)/shard_map/ppermute | solution.py:26
  23.8 5.7 %collective-permute-start.1 = (f32[3,20480]{1,0:T(4,128)S(1)}, f32[3,20480]{1,0:T(4,128)S(1)}, u32[]{:S(2)}, u32[]{:S(2)}) collective-permute-start(f32[3,20480]{1,0:T(4,128)S(1)} %get-tuple-element.19), channel_id=1, source_target_pairs={{4,0},{8,4},{12,8},{16,12},{20,16},{24,20},{28,24},{5,1},{9,5},{13... | collective-permute-start | bytes 737288 | tf_op jit(solution)/shard_map/ppermute | solution.py:28
  34.2 1.3 copy-start.2
  35.5 20.3 %collective-permute-start.2 = (f32[3,320,256]{2,1,0:T(8,128)S(1)}, f32[3,320,256]{2,1,0:T(8,128)}, u32[]{:S(2)}, u32[]{:S(2)}) collective-permute-start(f32[3,320,256]{2,1,0:T(8,128)S(1)} %constant_dynamic-slice_fusion), channel_id=1, source_target_pairs={{0,1},{1,0},{2,3},{3,2},{4,5},{5,4},{6,7},{7,6},{8,9},{9,8},{10,11... | collective-permute-start | bytes 2949128 | tf_op jit(solution)/shard_map/ppermute | solution.py:38
  37.1 21.3 %copy-start.3 = (bf16[128,512]{1,0:T(8,128)(2,1)S(1)}, bf16[128,512]{1,0:T(8,128)(2,1)}, u32[]{:S(2)}) copy-start(bf16[128,512]{1,0:T(8,128)(2,1)} %param.9) | copy-start | bytes 393220
  37.1 21.4 %copy-start.4 = (s32[16]{0:T(128)S(1)}, s32[16]{0:T(128)}, u32[]{:S(2)}) copy-start(s32[16]{0:T(128)} %param.10) | copy-start | bytes 196
  58.3 181.6 %reduce-scatter.3.cloned.1.call-start = ((), (), s32[]{:S(2)}) async-start(), calls=%async_computation.3 | async-start | bytes 11796480 | tf_op jit(solution)/shard_map/reduce_scatter | solution.py:98
  131.8 127.0 %reduce-scatter.5.cloned.1.call-start = ((), (), s32[]{:S(2)}) async-start(), calls=%async_computation.4 | async-start | bytes 983040 | tf_op jit(solution)/shard_map/reduce_scatter | solution.py:99
Sparse Core Ops, SparseCore 0:
  58.4 63.6 all-gather.1
  131.9 107.9 reduce-scatter.2
  244.4 14.3 reduce-scatter.4
where the time goes:
time: 268 us
  waiting for transfers between devices  207 us (77%)
  other arithmetic  23.1 us (9%)
  between operations  13.9 us (5%)
  matrix products  9.58 us (4%)
  local copies, waits for them, and re-layouts  8.61 us (3%)
  starting transfers between devices  5.38 us (2%)
    reduce_scatter x1, waiting for transfers between devices, local(): dp_rows = lax.psum_scatter(full_grad, 'dp', scatter_dimension=0, tiled=True)  108 us
    all_gather x1, waiting for transfers between devices, local(): lax.all_gather(weights, ('dp', 'group'), axis=0, tiled=True)  62.4 us
    ppermute x1, waiting for transfers between devices, partner(): return lax.ppermute(value, axis, pairs)  18.7 us
    reduce_scatter x1, waiting for transfers between devices, local(): lax.psum_scatter(dp_rows.reshape(2, tile_rows, new_cols).astype(jnp.bfloa...  13.7 us
    sub x2, other arithmetic, adam_update(): return (master - learn_rate * update, moment, variance)  9.13 us
    dot_general x1, matrix products, local(): lax.dot_general(tokens, delta, contract, preferred_element_type=jnp.float32)  5.53 us
  transfers between devices with their start and end apart: 6, of which 5 were waited for; matrix products, arithmetic and copies ran while one was open for 1% of the time, Pallas kernels for 0%

commit v1 on v0

v1 whole, which is shorter than its diff:
```python
import jax
import jax.numpy as jnp
from jax import lax
from jax.sharding import PartitionSpec as P

beta_one = 0.9
beta_two = 0.95
epsilon = 1e-08
learn_rate = 0.001
weight_decay = 0.1
first_step = 3.0
second_step = 4.0

LANES = 128
CORES = 2


def swap(value, axis, bits):
    pairs = [(source, source ^ bits) for source in range(lax.axis_size(axis))]
    return lax.ppermute(value, axis, pairs)


def swap_border(value):
    pairs = []
    for right in range(CORES, lax.axis_size("dp"), CORES):
        pairs += [(right - 1, right), (right, right - 1)]
    return lax.ppermute(value, "dp", pairs)


def adam_update(master, moment, variance, gradient, step_count):
    moment = beta_one * moment + (1.0 - beta_one) * gradient
    variance = beta_two * variance + (1.0 - beta_two) * gradient * gradient
    fix_one = 1.0 - beta_one**step_count
    fix_two = 1.0 - beta_two**step_count
    update = moment / fix_one / (jnp.sqrt(variance / fix_two) + epsilon) + weight_decay * master
    return (master - learn_rate * update, moment, variance)


def local(tokens, cotangent, counts, old_offsets, old_master, old_moment, old_variance, old_grad):
    f32, bf16 = jnp.float32, jnp.bfloat16
    ranks = lax.axis_size("dp")
    chips = ranks // CORES
    groups = lax.axis_size("group")
    rank = lax.axis_index("dp")
    chip, core = rank // CORES, rank % CORES
    group = lax.axis_index("group")
    slab = lax.axis_index("tensor") * groups + group
    slots, width = tokens.shape
    cols = cotangent.shape[1]
    old_cols = cols // groups
    depth = width // chips

    def token_block(of_chip):
        return lax.dynamic_slice(tokens, (0, of_chip * depth), (slots, depth))

    blocks = [token_block(chip)]
    for step in range(1, chips):
        blocks.append(swap(token_block(chip ^ step), "dp", step * CORES))

    windows = jnp.stack([old_master[0, 0], old_moment[0, 0], old_variance[0, 0], old_grad[0, 0]])
    length = windows.shape[1]
    margin = length // 10
    shard = length - 2 * margin
    windows = windows.reshape(4, 10, margin // LANES, LANES)
    head, tail = windows[:, 0], windows[:, 9]
    first = core == 0
    inner = swap(jnp.where(first, tail, head), "dp", 1)
    outer = swap_border(jnp.where(first, head, tail))
    from_left = jnp.where(first, outer, inner)
    from_right = jnp.where(first, inner, outer)
    bounds = lax.dynamic_slice(old_offsets, (slab, rank), (1, 2))[0] - rank * shard
    place = lax.broadcasted_iota(jnp.int32, head.shape[1:], 0) * LANES
    place = place + lax.broadcasted_iota(jnp.int32, head.shape[1:], 1)
    left = jnp.where(place < bounds[0], from_left, windows[:, 1])
    right = jnp.where(place + (shard - margin) >= bounds[1], from_right, windows[:, 8])
    nominal = jnp.concatenate([left[:, None], windows[:, 2:8], right[:, None]], axis=1)
    states = jnp.stack(adam_update(*nominal, first_step))
    piece = shard // old_cols
    states = states.reshape(3, piece, old_cols)
    tile = piece // groups

    own = states[0].astype(bf16)
    other = swap(own, "group", 1)
    low = group == 0
    wide = jnp.concatenate([jnp.where(low, own, other), jnp.where(low, other, own)], axis=1)
    mate = swap(wide, "dp", 1)
    weights = jnp.concatenate(
        [jnp.where(first, wide, mate), jnp.where(first, mate, wide)], axis=0
    )

    outgoing = lax.dynamic_slice_in_dim(states, (1 - group) * tile, tile, 1)
    staying = lax.dynamic_slice_in_dim(states, group * tile, tile, 1)
    incoming = swap(outgoing, "group", 1)
    states = jnp.concatenate(
        [jnp.where(low, staying, incoming), jnp.where(low, incoming, staying)], axis=2
    )

    total = jnp.dot(blocks[0], weights, preferred_element_type=f32)
    for step in range(1, chips):
        part = jnp.dot(blocks[step], weights, preferred_element_type=f32).astype(bf16)
        total = total + swap(part, "dp", step * CORES).astype(f32)
    preact = total
    activated = jax.nn.silu(preact).astype(bf16)
    sigmoid = jax.nn.sigmoid(preact)
    derivative = sigmoid * (1.0 + preact * (1.0 - sigmoid))
    live = jnp.arange(slots, dtype=jnp.int32) < counts[rank * groups + group]
    delta = jnp.where(live[:, None], cotangent.astype(f32) * derivative, 0.0).astype(bf16)

    contract = (((0,), (0,)), ((), ()))
    deltas = [delta] + [swap(delta, "dp", step * CORES) for step in range(1, chips)]
    gradient = lax.dot_general(
        jnp.concatenate(blocks), jnp.concatenate(deltas), contract, preferred_element_type=f32
    )
    gradient = gradient.reshape(CORES, groups, tile, cols)
    keep = lax.dynamic_index_in_dim(gradient, core, 0, keepdims=False)
    send = lax.dynamic_index_in_dim(gradient, 1 - core, 0, keepdims=False)
    gradient = keep + swap(send.astype(bf16), "dp", 1).astype(f32)
    keep = lax.dynamic_index_in_dim(gradient, group, 0, keepdims=False)
    send = lax.dynamic_index_in_dim(gradient, 1 - group, 0, keepdims=False)
    gradient = keep + swap(send.astype(bf16), "group", 1).astype(f32)

    new_master, new_moment, new_variance = adam_update(*states, gradient, second_step)
    return (activated, new_master, new_moment, new_variance)


def solution(mesh):
    rows = P(("dp", "group"), "tensor")
    window = P(("tensor", "group"), "dp", None)
    return jax.shard_map(
        local,
        mesh=mesh,
        in_specs=(P(("dp", "group"), None), rows, P(), P(), window, window, window, window),
        out_specs=(rows, rows, rows, rows),
        check_vma=False,
    )
```

time: 268 us -> 128 us (0.48)
  waiting for transfers between devices: 207 us -> 62.7 us
  starting transfers between devices: 5.38 us -> 26.8 us
  between operations: 13.9 us -> 0.88 us
  other arithmetic: 23.1 us -> 17 us
    reduce_scatter x2 -> x0, waiting for transfers between devices: 122 us -> none  [the longest x1 108 us: local(): dp_rows = lax.psum_scatter(full_grad, 'dp', scatter_dimension=0, tiled=True)]
    all_gather x1 -> x0, waiting for transfers between devices: 62.4 us -> none  [local(): lax.all_gather(weights, ('dp', 'group'), axis=0, tiled=True)]
    ppermute x3 -> x16, waiting for transfers between devices: 23.1 us -> 62.7 us  [the longest x15 62.7 us: swap(): return lax.ppermute(value, axis, pairs)]
    ppermute x3 -> x16, starting transfers between devices: 5.25 us -> 26.8 us  [the longest x15 25.4 us: swap(): return lax.ppermute(value, axis, pairs)]
    sub x2 -> x1, other arithmetic: 9.13 us -> 2.64 us  [adam_update(): return (master - learn_rate * update, moment, variance)]
    dot_general x2 -> x5, matrix products: 9.58 us -> 10.7 us  [the longest x3 5.9 us: local(): jnp.dot(blocks[step], weights, preferred_element_type=f32).astype(bf16)]
    select_n x2 -> x5, other arithmetic: 4.56 us -> 5.5 us  [the longest x1 1.98 us: local(): outer = swap_border(jnp.where(first, head, tail))]
  transfers between devices with their start and end apart: 6 -> 16, of which waited for: 5 -> 8; matrix products, arithmetic and copies ran while one was open for 1% -> 18% of each run, Pallas kernels for 0% -> 0%
where the time goes in v1:
time: 128 us
  waiting for transfers between devices  62.7 us (49%)
  starting transfers between devices  26.8 us (21%)
  other arithmetic  17 us (13%)
  matrix products  10.7 us (8%)
  local copies, waits for them, and re-layouts  9.62 us (8%)
    ppermute x15, waiting for transfers between devices, swap(): return lax.ppermute(value, axis, pairs)  62.7 us
    ppermute x15, starting transfers between devices, swap(): return lax.ppermute(value, axis, pairs)  25.4 us
    dot_general x3, matrix products, local(): jnp.dot(blocks[step], weights, preferred_element_type=f32).astype(bf16)  5.9 us
    unnamed x12, local copies, waits for them, and re-layouts  2.71 us
    sub x1, other arithmetic, adam_update(): return (master - learn_rate * update, moment, variance)  2.64 us
    dot_general x1, matrix products, local(): total = jnp.dot(blocks[0], weights, preferred_element_type=f32)  2.6 us
  transfers between devices with their start and end apart: 16, of which 8 were waited for; matrix products, arithmetic and copies ran while one was open for 18% of the time, Pallas kernels for 0%

profile of v1, /device:TPU:0, one launch (start us, length us, event | category | flops | bytes accessed | tf_op | source)
XLA Modules:
  0.0 127.7 jit_solution(12644781276393228423)
XLA Ops:
  0.6 2.0 %select_bitcast_fusion.1 = (f32[4,160,128]{2,1,0:T(8,128)}, f32[4,1,160,128]{3,2,0,1:T(8,128)S(1)}, f32[4,1,160,128]{3,2,0,1:T(8,128)S(1)}) fusion(pred[]{:T(512)S(6)} %eq.8, f32[1,10,160,128]{3,2,0,1:T(8,128)} %bitcast.78, f32[1,10,160,128]{3,2,0,1:T(8,128)} %bitcast.81, f32[1,10,160,128]{3,2,0,1:T(8,128)} %bitcast.84, f32[1,10,160,128]{3,2,0,1:T(8,128)} %bitcast.87), kind=kLoop, calls=%fused_computation.66 | loop fusion | flops 573440 | bytes 4259841 | tf_op jit(solution)/shard_map/jit(_where)/select_n | solution.py:68
  3.8 1.4 %collective-permute-start = (f32[4,160,128]{2,1,0:T(8,128)}, f32[4,160,128]{2,1,0:T(8,128)}, u32[]{:S(2)}, u32[]{:S(2)}) collective-permute-start(f32[4,160,128]{2,1,0:T(8,128)} %get-tuple-element.11), channel_id=1, source_target_pairs={{4,8},{8,4},{12,16},{16,12},{20,24},{24,20},{5,9},{9,5},{13,17},{1... | collective-permute-start | bytes 983048 | tf_op jit(solution)/shard_map/ppermute | solution.py:27
  5.2 2.2 %pad_maximum_fusion = f32[4,10,160,128]{3,2,0,1:T(8,128)S(1)} fusion(f32[1,10,160,128]{3,2,0,1:T(8,128)} %bitcast.79, f32[1,10,160,128]{3,2,0,1:T(8,128)} %bitcast.82, f32[1,10,160,128]{3,2,0,1:T(8,128)} %bitcast.85, f32[1,10,160,128]{3,2,0,1:T(8,128)} %bitcast.88), kind=kLoop, calls=%fused_computation | loop fusion | flops 2457600 | bytes 6553600 | tf_op jit(solution)/shard_map/stack | solution.py:60
  8.8 1.4 %fusion.34 = (pred[160,128]{1,0:T(8,128)(4,1)S(1)}, pred[160,128]{1,0:T(8,128)(4,1)S(1)}) fusion(s32[]{:T(128)} %bitcast, s32[160]{0:T(256)S(1)} %iota_multiply_fusion, s32[]{:T(128)} %bitcast.14), kind=kLoop, calls=%fused_computation.74 | loop fusion | flops 81920 | bytes 41608 | tf_op jit(solution)/shard_map/lt | solution.py:74
  10.2 1.5 %fusion.33 = (f32[4,1,160,128]{3,2,1,0:T(8,128)S(1)}, f32[4,1,160,128]{3,2,1,0:T(8,128)S(1)}) fusion(f32[1,10,160,128]{3,2,0,1:T(8,128)} %bitcast.80, f32[1,10,160,128]{3,2,0,1:T(8,128)} %bitcast.83, f32[1,10,160,128]{3,2,0,1:T(8,128)} %bitcast.86, f32[1,10,160,128]{3,2,0,1:T(8,128)} %bitcast.89, f32[4,160,128]{2,1,0:T(8,128)} %collective-permute-done, ...), kind=kLoop, calls=%fused_computation.62 | loop fusion | flops 819200 | bytes 4628481 | tf_op jit(solution)/shard_map/broadcast_in_dim | solution.py:76
  12.5 2.6 %collective-permute-start.2 = (bf16[640,256]{1,0:T(8,128)(2,1)S(1)}, bf16[640,256]{1,0:T(8,128)(2,1)S(1)}, u32[]{:S(2)}, u32[]{:S(2)}) collective-permute-start(bf16[640,256]{1,0:T(8,128)(2,1)S(1)} %convert_element_type.52), channel_id=1, source_target_pairs={{0,1},{1,0},{2,3},{3,2},{4,5},{5,4},{6,7},{7,6},{8,9},{9,8},{10,11... | collective-permute-start | bytes 983048 | tf_op jit(solution)/shard_map/ppermute | solution.py:20
  15.1 6.3 %collective-permute-done.2 = bf16[640,256]{1,0:T(8,128)(2,1)S(1)} collective-permute-done((bf16[640,256]{1,0:T(8,128)(2,1)S(1)}, bf16[640,256]{1,0:T(8,128)(2,1)S(1)}, u32[]{:S(2)}, u32[]{:S(2)}) %collective-permute-start.2) | collective-permute-done | bytes 327712 | tf_op jit(solution)/shard_map/ppermute | solution.py:20
  21.5 2.1 %collective-permute-start.3 = (bf16[640,512]{1,0:T(8,128)(2,1)S(1)}, bf16[640,512]{1,0:T(8,128)(2,1)}, u32[]{:S(2)}, u32[]{:S(2)}) collective-permute-start(bf16[640,512]{1,0:T(8,128)(2,1)S(1)} %pad_maximum_fusion.4), channel_id=1, source_target_pairs={{0,4},{4,0},{8,12},{12,8},{16,20},{20,16},{24,28},{28,24},{1,5},{5... | collective-permute-start | bytes 1966088 | tf_op jit(solution)/shard_map/ppermute | solution.py:20
  23.6 2.4 %constant_dynamic-slice_fusion.3 = (bf16[128,1280]{1,0:T(8,128)(2,1)}, bf16[128,1280]{1,0:T(8,128)(2,1)}, bf16[128,1280]{1,0:T(8,128)(2,1)}, bf16[128,1280]{1,0:T(8,128)(2,1)}) fusion(bf16[128,5120]{1,0:T(8,128)(2,1)} %param.8, s32[]{:T(128)S(6)} %select_n.148, s32[]{:T(128)S(6)} %select_n.128, s32[]{:T(128)S(6)} %select_n.150, s32[]{:T(128)S(6)} %select_n.149), kind=kLoop, calls=%fused_computation.81 | loop fusion | bytes 2621456 | tf_op jit(solution)/shard_map/dynamic_slice | solution.py:54
  26.0 4.2 %collective-permute-start.4 = (bf16[128,1280]{1,0:T(8,128)(2,1)}, bf16[128,1280]{1,0:T(8,128)(2,1)}, u32[]{:S(2)}, u32[]{:S(2)}) collective-permute-start(bf16[128,1280]{1,0:T(8,128)(2,1)} %get-tuple-element.18), channel_id=1, source_target_pairs={{0,8},{4,12},{8,0},{12,4},{16,24},{20,28},{24,16},{28,20},{1,9},{5... | collective-permute-start | bytes 983048 | tf_op jit(solution)/shard_map/ppermute | solution.py:20
  31.2 1.5 %collective-permute-start.8 = (bf16[128,1280]{1,0:T(8,128)(2,1)}, bf16[128,1280]{1,0:T(8,128)(2,1)}, u32[]{:S(2)}, u32[]{:S(2)}) collective-permute-start(bf16[128,1280]{1,0:T(8,128)(2,1)} %get-tuple-element.20), channel_id=1, source_target_pairs={{0,24},{4,28},{8,16},{12,20},{16,8},{20,12},{24,0},{28,4},{1,25},{... | collective-permute-start | bytes 983048 | tf_op jit(solution)/shard_map/ppermute | solution.py:20
  33.2 1.3 %broadcast_select_fusion.1 = (bf16[640,512]{1,0:T(8,128)(2,1)S(1)}, bf16[640,512]{1,0:T(8,128)(2,1)S(1)}) fusion(bf16[640,512]{1,0:T(8,128)(2,1)} %collective-permute-done.3, pred[]{:T(512)S(6)} %eq.8, bf16[640,256]{1,0:T(8,128)(2,1)S(1)} %get-tuple-element.25, bf16[640,256]{1,0:T(8,128)(2,1)S(1)} %get-tuple-element.24), kind=kLoop, calls=%fused_computation.48 | loop fusion | flops 1966080 | bytes 2621441 | tf_op jit(solution)/shard_map/jit(_where)/select_n | solution.py:88
  34.6 10.8 %collective-permute-done.4 = bf16[128,1280]{1,0:T(8,128)(2,1)} collective-permute-done((bf16[128,1280]{1,0:T(8,128)(2,1)}, bf16[128,1280]{1,0:T(8,128)(2,1)}, u32[]{:S(2)}, u32[]{:S(2)}) %collective-permute-start.4) | collective-permute-done | bytes 327712 | tf_op jit(solution)/shard_map/ppermute | solution.py:20
  45.4 2.0 %convolution_convert_fusion.2 = bf16[128,512]{1,0:T(8,128)(2,1)} fusion(bf16[128,1280]{1,0:T(8,128)(2,1)} %collective-permute-done.4, bf16[640,512]{1,0:T(8,128)(2,1)S(1)} %get-tuple-element.23, bf16[640,512]{1,0:T(8,128)(2,1)S(1)} %get-tuple-element.22), kind=kOutput, calls=%fused_computation.22 | convolution fusion | flops 170459136 | bytes 1769472 | tf_op jit(solution)/shard_map/dot_general | solution.py:100
  47.4 8.7 %collective-permute-done.6 = bf16[128,1280]{1,0:T(8,128)(2,1)} collective-permute-done((bf16[128,1280]{1,0:T(8,128)(2,1)}, bf16[128,1280]{1,0:T(8,128)(2,1)}, u32[]{:S(2)}, u32[]{:S(2)}) %collective-permute-start.6) | collective-permute-done | bytes 327712 | tf_op jit(solution)/shard_map/ppermute | solution.py:20
  56.1 2.0 %convolution_convert_fusion.1 = bf16[128,512]{1,0:T(8,128)(2,1)} fusion(bf16[128,1280]{1,0:T(8,128)(2,1)} %collective-permute-done.6, bf16[640,512]{1,0:T(8,128)(2,1)S(1)} %get-tuple-element.23, bf16[640,512]{1,0:T(8,128)(2,1)S(1)} %get-tuple-element.22), kind=kOutput, calls=%fused_computation.21 | convolution fusion | flops 170459136 | bytes 1769472 | tf_op jit(solution)/shard_map/dot_general | solution.py:100
  58.1 2.0 %convolution_convert_fusion = bf16[128,512]{1,0:T(8,128)(2,1)} fusion(bf16[128,1280]{1,0:T(8,128)(2,1)} %collective-permute-done.8, bf16[640,512]{1,0:T(8,128)(2,1)S(1)} %get-tuple-element.23, bf16[640,512]{1,0:T(8,128)(2,1)S(1)} %get-tuple-element.22), kind=kOutput, calls=%fused_computation.20 | convolution fusion | flops 170459136 | bytes 1769472 | tf_op jit(solution)/shard_map/dot_general | solution.py:100
  60.1 2.5 %collective-permute-start.9 = (bf16[128,512]{1,0:T(8,128)(2,1)}, bf16[128,512]{1,0:T(8,128)(2,1)}, u32[]{:S(2)}, u32[]{:S(2)}) collective-permute-start(bf16[128,512]{1,0:T(8,128)(2,1)} %convolution_convert_fusion), channel_id=1, source_target_pairs={{0,24},{4,28},{8,16},{12,20},{16,8},{20,12},{24,0},{28,4},{1,25},{... | collective-permute-start | bytes 393224 | tf_op jit(solution)/shard_map/ppermute | solution.py:20
  65.5 5.3 %collective-permute-done.7 = bf16[128,512]{1,0:T(8,128)(2,1)} collective-permute-done((bf16[128,512]{1,0:T(8,128)(2,1)}, bf16[128,512]{1,0:T(8,128)(2,1)}, u32[]{:S(2)}, u32[]{:S(2)}) %collective-permute-start.7) | collective-permute-done | bytes 131104 | tf_op jit(solution)/shard_map/ppermute | solution.py:20
  70.8 2.6 %select_convert_fusion = (bf16[128,512]{1,0:T(8,128)(2,1)}, bf16[128,512]{1,0:T(8,128)(2,1)}) fusion(bf16[128,512]{1,0:T(8,128)(2,1)S(1)} %copy-done.3, pred[128]{0:T(512)(128)(4,1)S(1)} %iota_compare_fusion, bf16[128,512]{1,0:T(8,128)(2,1)} %collective-permute-done.9, bf16[128,512]{1,0:T(8,128)(2,1)} %collective-permute-done.7, ...), kind=kOutput, calls=%fused_computation.69 | convolution fusion | flops 171638784 | bytes 2424960 | tf_op jit(solution)/shard_map/dot_general | solution.py:98
  73.4 5.8 %collective-permute-start.11 = (bf16[128,512]{1,0:T(8,128)(2,1)}, bf16[128,512]{1,0:T(8,128)(2,1)S(1)}, u32[]{:S(2)}, u32[]{:S(2)}) collective-permute-start(bf16[128,512]{1,0:T(8,128)(2,1)} %get-tuple-element.26), channel_id=1, source_target_pairs={{0,8},{4,12},{8,0},{12,4},{16,24},{20,28},{24,16},{28,20},{1,9},{5... | collective-permute-start | bytes 393224 | tf_op jit(solution)/shard_map/ppermute | solution.py:20
  80.2 1.5 %collective-permute-start.13 = (bf16[128,512]{1,0:T(8,128)(2,1)}, bf16[128,512]{1,0:T(8,128)(2,1)}, u32[]{:S(2)}, u32[]{:S(2)}) collective-permute-start(bf16[128,512]{1,0:T(8,128)(2,1)} %get-tuple-element.26), channel_id=1, source_target_pairs={{0,24},{4,28},{8,16},{12,20},{16,8},{20,12},{24,0},{28,4},{1,25},{... | collective-permute-start | bytes 393224 | tf_op jit(solution)/shard_map/ppermute | solution.py:20
  81.9 2.0 %collective-permute-done.11 = bf16[128,512]{1,0:T(8,128)(2,1)S(1)} collective-permute-done((bf16[128,512]{1,0:T(8,128)(2,1)}, bf16[128,512]{1,0:T(8,128)(2,1)S(1)}, u32[]{:S(2)}, u32[]{:S(2)}) %collective-permute-start.11) | collective-permute-done | bytes 131104 | tf_op jit(solution)/shard_map/ppermute | solution.py:20
  83.9 4.7 %collective-permute-done.12 = bf16[128,512]{1,0:T(8,128)(2,1)S(1)} collective-permute-done((bf16[128,512]{1,0:T(8,128)(2,1)}, bf16[128,512]{1,0:T(8,128)(2,1)S(1)}, u32[]{:S(2)}, u32[]{:S(2)}) %collective-permute-start.12) | collective-permute-done | bytes 131104 | tf_op jit(solution)/shard_map/ppermute | solution.py:20
  88.6 2.2 %fusion = f32[1280,512]{1,0:T(8,128)S(1)} fusion(bf16[128,1280]{1,0:T(8,128)(2,1)} %collective-permute-done.8, bf16[128,1280]{1,0:T(8,128)(2,1)} %collective-permute-done.6, bf16[128,1280]{1,0:T(8,128)(2,1)} %collective-permute-done.4, bf16[128,1280]{1,0:T(8,128)(2,1)} %get-tuple-element.19, bf16[128,512]{1,0:T(8,128)(2,1)} %collective-permute-done.13, ...), kind=kOutput, calls=%fused_computation.7 | convolution fusion | flops 678428672 | bytes 4456448 | tf_op jit(solution)/shard_map/dot_general | solution.py:111
  90.8 1.5 %copy-done = f32[1280,512]{1,0:T(8,128)} copy-done((f32[1280,512]{1,0:T(8,128)}, f32[1280,512]{1,0:T(8,128)S(1)}, u32[]{:S(2)}) %copy-start) | copy-done | bytes 2621464
  93.5 1.5 %collective-permute-start.10 = (f32[3,320,256]{2,1,0:T(8,128)}, f32[3,320,256]{2,1,0:T(8,128)}, u32[]{:S(2)}, u32[]{:S(2)}) collective-permute-start(f32[3,320,256]{2,1,0:T(8,128)} %constant_dynamic-slice_fusion), channel_id=1, source_target_pairs={{0,1},{1,0},{2,3},{3,2},{4,5},{5,4},{6,7},{7,6},{8,9},{9,8},{10,11... | collective-permute-start | bytes 2949128 | tf_op jit(solution)/shard_map/ppermute | solution.py:20
  95.1 1.7 %bitcast_add_fusion = f32[2,320,512]{2,1,0:T(8,128)S(1)} fusion(bf16[2,320,512]{2,1,0:T(8,128)(2,1)} %collective-permute-done.14, f32[2,2,320,512]{3,2,1,0:T(8,128)} %bitcast.91, s32[]{:T(128)S(6)} %select_n.158), kind=kLoop, calls=%fused_computation.15 | loop fusion | flops 655360 | bytes 3276804 | tf_op jit(solution)/shard_map/add | solution.py:117
  98.8 19.6 %collective-permute-done.10 = f32[3,320,256]{2,1,0:T(8,128)} collective-permute-done((f32[3,320,256]{2,1,0:T(8,128)}, f32[3,320,256]{2,1,0:T(8,128)}, u32[]{:S(2)}, u32[]{:S(2)}) %collective-permute-start.10) | collective-permute-done | bytes 983072 | tf_op jit(solution)/shard_map/ppermute | solution.py:20
  118.4 1.4 %dynamic-slice_select_fusion.1 = (f32[3,320,256]{2,1,0:T(8,128)S(1)}, f32[3,320,256]{2,1,0:T(8,128)S(1)}) fusion(f32[3,320,256]{2,1,0:T(8,128)} %collective-permute-done.10, f32[3,640,256]{2,1,0:T(8,128)S(1)} %constant_dynamic-update-slice_fusion, s32[]{:T(128)S(6)} %select_n.152, pred[]{:T(512)S(6)} %eq.9), kind=kLoop, calls=%fused_computation.26 | loop fusion | flops 491520 | bytes 3932165 | tf_op jit(solution)/shard_map/jit(_where)/select_n | solution.py:95
  119.8 5.2 %collective-permute-done.15 = bf16[320,512]{1,0:T(8,128)(2,1)} collective-permute-done((bf16[320,512]{1,0:T(8,128)(2,1)}, bf16[320,512]{1,0:T(8,128)(2,1)}, u32[]{:S(2)}, u32[]{:S(2)}) %collective-permute-start.15) | collective-permute-done | bytes 327712 | tf_op jit(solution)/shard_map/ppermute | solution.py:20
  125.0 2.6 %multiply_subtract_fusion = (f32[320,512]{1,0:T(8,128)}, f32[320,512]{1,0:T(8,128)}, f32[320,512]{1,0:T(8,128)}) fusion(f32[3,320,256]{2,1,0:T(8,128)S(1)} %get-tuple-element.17, f32[3,320,256]{2,1,0:T(8,128)S(1)} %get-tuple-element.16, bf16[320,512]{1,0:T(8,128)(2,1)} %collective-permute-done.15, f32[2,320,512]{2,1,0:T(8,128)S(1)} %bitcast_add_fusion, ...), kind=kLoop, calls=%fused_computation.44 | loop fusion | flops 3276800 | bytes 4915204 | tf_op jit(solution)/shard_map/sub | solution.py:36
  (44 shorter events, 12.4 us)
Async XLA Ops:
  3.4 6.8 %collective-permute-start.1 = (f32[4,160,128]{2,1,0:T(8,128)}, f32[4,160,128]{2,1,0:T(8,128)}, u32[]{:S(2)}, u32[]{:S(2)}) collective-permute-start(f32[4,160,128]{2,1,0:T(8,128)} %select_bitcast_fusion), channel_id=1, source_target_pairs={{0,4},{4,0},{8,12},{12,8},{16,20},{20,16},{24,28},{28,24},{1,5},{5... | collective-permute-start | bytes 983048 | tf_op jit(solution)/shard_map/ppermute | solution.py:20
  3.8 6.3 %collective-permute-start = (f32[4,160,128]{2,1,0:T(8,128)}, f32[4,160,128]{2,1,0:T(8,128)}, u32[]{:S(2)}, u32[]{:S(2)}) collective-permute-start(f32[4,160,128]{2,1,0:T(8,128)} %get-tuple-element.11), channel_id=1, source_target_pairs={{4,8},{8,4},{12,16},{16,12},{20,24},{24,20},{5,9},{9,5},{13,17},{1... | collective-permute-start | bytes 983048 | tf_op jit(solution)/shard_map/ppermute | solution.py:27
  12.5 8.9 %collective-permute-start.2 = (bf16[640,256]{1,0:T(8,128)(2,1)S(1)}, bf16[640,256]{1,0:T(8,128)(2,1)S(1)}, u32[]{:S(2)}, u32[]{:S(2)}) collective-permute-start(bf16[640,256]{1,0:T(8,128)(2,1)S(1)} %convert_element_type.52), channel_id=1, source_target_pairs={{0,1},{1,0},{2,3},{3,2},{4,5},{5,4},{6,7},{7,6},{8,9},{9,8},{10,11... | collective-permute-start | bytes 983048 | tf_op jit(solution)/shard_map/ppermute | solution.py:20
  21.4 11.2 %copy-start.4 = (s32[16]{0:T(128)S(1)}, s32[16]{0:T(128)}, u32[]{:S(2)}) copy-start(s32[16]{0:T(128)} %param.10) | copy-start | bytes 196
  21.5 11.7 %collective-permute-start.3 = (bf16[640,512]{1,0:T(8,128)(2,1)S(1)}, bf16[640,512]{1,0:T(8,128)(2,1)}, u32[]{:S(2)}, u32[]{:S(2)}) collective-permute-start(bf16[640,512]{1,0:T(8,128)(2,1)S(1)} %pad_maximum_fusion.4), channel_id=1, source_target_pairs={{0,4},{4,0},{8,12},{12,8},{16,20},{20,16},{24,28},{28,24},{1,5},{5... | collective-permute-start | bytes 1966088 | tf_op jit(solution)/shard_map/ppermute | solution.py:20
  26.0 19.4 %collective-permute-start.4 = (bf16[128,1280]{1,0:T(8,128)(2,1)}, bf16[128,1280]{1,0:T(8,128)(2,1)}, u32[]{:S(2)}, u32[]{:S(2)}) collective-permute-start(bf16[128,1280]{1,0:T(8,128)(2,1)} %get-tuple-element.18), channel_id=1, source_target_pairs={{0,8},{4,12},{8,0},{12,4},{16,24},{20,28},{24,16},{28,20},{1,9},{5... | collective-permute-start | bytes 983048 | tf_op jit(solution)/shard_map/ppermute | solution.py:20
  30.2 25.9 %collective-permute-start.6 = (bf16[128,1280]{1,0:T(8,128)(2,1)}, bf16[128,1280]{1,0:T(8,128)(2,1)}, u32[]{:S(2)}, u32[]{:S(2)}) collective-permute-start(bf16[128,1280]{1,0:T(8,128)(2,1)} %get-tuple-element.21), channel_id=1, source_target_pairs={{0,16},{4,20},{8,24},{12,28},{16,0},{20,4},{24,8},{28,12},{1,17},{... | collective-permute-start | bytes 983048 | tf_op jit(solution)/shard_map/ppermute | solution.py:20
  31.2 26.8 %collective-permute-start.8 = (bf16[128,1280]{1,0:T(8,128)(2,1)}, bf16[128,1280]{1,0:T(8,128)(2,1)}, u32[]{:S(2)}, u32[]{:S(2)}) collective-permute-start(bf16[128,1280]{1,0:T(8,128)(2,1)} %get-tuple-element.20), channel_id=1, source_target_pairs={{0,24},{4,28},{8,16},{12,20},{16,8},{20,12},{24,0},{28,4},{1,25},{... | collective-permute-start | bytes 983048 | tf_op jit(solution)/shard_map/ppermute | solution.py:20
  34.6 23.5 %copy-start.1 = (bf16[640,512]{1,0:T(8,128)(2,1)}, bf16[640,512]{1,0:T(8,128)(2,1)S(1)}, u32[]{:S(2)}) copy-start(bf16[640,512]{1,0:T(8,128)(2,1)S(1)} %get-tuple-element.22) | copy-start | bytes 1966084
  34.6 23.5 %copy-start.2 = (bf16[640,512]{1,0:T(8,128)(2,1)}, bf16[640,512]{1,0:T(8,128)(2,1)S(1)}, u32[]{:S(2)}) copy-start(bf16[640,512]{1,0:T(8,128)(2,1)S(1)} %get-tuple-element.23) | copy-start | bytes 1966084
  47.4 18.1 %collective-permute-start.5 = (bf16[128,512]{1,0:T(8,128)(2,1)}, bf16[128,512]{1,0:T(8,128)(2,1)S(1)}, u32[]{:S(2)}, u32[]{:S(2)}) collective-permute-start(bf16[128,512]{1,0:T(8,128)(2,1)} %convolution_convert_fusion.2), channel_id=1, source_target_pairs={{0,8},{4,12},{8,0},{12,4},{16,24},{20,28},{24,16},{28,20},{1,9},{5... | collective-permute-start | bytes 393224 | tf_op jit(solution)/shard_map/ppermute | solution.py:20
  58.1 12.7 %collective-permute-start.7 = (bf16[128,512]{1,0:T(8,128)(2,1)}, bf16[128,512]{1,0:T(8,128)(2,1)}, u32[]{:S(2)}, u32[]{:S(2)}) collective-permute-start(bf16[128,512]{1,0:T(8,128)(2,1)} %convolution_convert_fusion.1), channel_id=1, source_target_pairs={{0,16},{4,20},{8,24},{12,28},{16,0},{20,4},{24,8},{28,12},{1,17},{... | collective-permute-start | bytes 393224 | tf_op jit(solution)/shard_map/ppermute | solution.py:20
  60.1 10.7 %collective-permute-start.9 = (bf16[128,512]{1,0:T(8,128)(2,1)}, bf16[128,512]{1,0:T(8,128)(2,1)}, u32[]{:S(2)}, u32[]{:S(2)}) collective-permute-start(bf16[128,512]{1,0:T(8,128)(2,1)} %convolution_convert_fusion), channel_id=1, source_target_pairs={{0,24},{4,28},{8,16},{12,20},{16,8},{20,12},{24,0},{28,4},{1,25},{... | collective-permute-start | bytes 393224 | tf_op jit(solution)/shard_map/ppermute | solution.py:20
  63.1 7.7 %copy-start.3 = (bf16[128,512]{1,0:T(8,128)(2,1)S(1)}, bf16[128,512]{1,0:T(8,128)(2,1)}, u32[]{:S(2)}) copy-start(bf16[128,512]{1,0:T(8,128)(2,1)} %param.9) | copy-start | bytes 393220
  73.4 10.5 %collective-permute-start.11 = (bf16[128,512]{1,0:T(8,128)(2,1)}, bf16[128,512]{1,0:T(8,128)(2,1)S(1)}, u32[]{:S(2)}, u32[]{:S(2)}) collective-permute-start(bf16[128,512]{1,0:T(8,128)(2,1)} %get-tuple-element.26), channel_id=1, source_target_pairs={{0,8},{4,12},{8,0},{12,4},{16,24},{20,28},{24,16},{28,20},{1,9},{5... | collective-permute-start | bytes 393224 | tf_op jit(solution)/shard_map/ppermute | solution.py:20
  79.2 9.4 %collective-permute-start.12 = (bf16[128,512]{1,0:T(8,128)(2,1)}, bf16[128,512]{1,0:T(8,128)(2,1)S(1)}, u32[]{:S(2)}, u32[]{:S(2)}) collective-permute-start(bf16[128,512]{1,0:T(8,128)(2,1)} %get-tuple-element.26), channel_id=1, source_target_pairs={{0,16},{4,20},{8,24},{12,28},{16,0},{20,4},{24,8},{28,12},{1,17},{... | collective-permute-start | bytes 393224 | tf_op jit(solution)/shard_map/ppermute | solution.py:20
  80.2 8.4 %collective-permute-start.13 = (bf16[128,512]{1,0:T(8,128)(2,1)}, bf16[128,512]{1,0:T(8,128)(2,1)}, u32[]{:S(2)}, u32[]{:S(2)}) collective-permute-start(bf16[128,512]{1,0:T(8,128)(2,1)} %get-tuple-element.26), channel_id=1, source_target_pairs={{0,24},{4,28},{8,16},{12,20},{16,8},{20,12},{24,0},{28,4},{1,25},{... | collective-permute-start | bytes 393224 | tf_op jit(solution)/shard_map/ppermute | solution.py:20
  90.8 1.5 %copy-start = (f32[1280,512]{1,0:T(8,128)}, f32[1280,512]{1,0:T(8,128)S(1)}, u32[]{:S(2)}) copy-start(f32[1280,512]{1,0:T(8,128)S(1)} %fusion) | copy-start | bytes 7864324
  92.4 2.6 %collective-permute-start.14 = (bf16[2,320,512]{2,1,0:T(8,128)(2,1)S(1)}, bf16[2,320,512]{2,1,0:T(8,128)(2,1)}, u32[]{:S(2)}, u32[]{:S(2)}) collective-permute-start(bf16[2,320,512]{2,1,0:T(8,128)(2,1)S(1)} %fusion.12), channel_id=1, source_target_pairs={{0,4},{4,0},{8,12},{12,8},{16,20},{20,16},{24,28},{28,24},{1,5},{5... | collective-permute-start | bytes 1966088 | tf_op jit(solution)/shard_map/ppermute | solution.py:20
  93.5 24.9 %collective-permute-start.10 = (f32[3,320,256]{2,1,0:T(8,128)}, f32[3,320,256]{2,1,0:T(8,128)}, u32[]{:S(2)}, u32[]{:S(2)}) collective-permute-start(f32[3,320,256]{2,1,0:T(8,128)} %constant_dynamic-slice_fusion), channel_id=1, source_target_pairs={{0,1},{1,0},{2,3},{3,2},{4,5},{5,4},{6,7},{7,6},{8,9},{9,8},{10,11... | collective-permute-start | bytes 2949128 | tf_op jit(solution)/shard_map/ppermute | solution.py:20
  97.6 27.4 %collective-permute-start.15 = (bf16[320,512]{1,0:T(8,128)(2,1)}, bf16[320,512]{1,0:T(8,128)(2,1)}, u32[]{:S(2)}, u32[]{:S(2)}) collective-permute-start(bf16[320,512]{1,0:T(8,128)(2,1)} %fusion.29), channel_id=1, source_target_pairs={{0,1},{1,0},{2,3},{3,2},{4,5},{5,4},{6,7},{7,6},{8,9},{9,8},{10,11... | collective-permute-start | bytes 983048 | tf_op jit(solution)/shard_map/ppermute | solution.py:20

commit v2 on v1

v2 whole, which is shorter than its diff:
```python
import functools

import jax
import jax.numpy as jnp
from jax import lax
from jax.experimental import pallas as pl
from jax.experimental.pallas import tpu as pltpu
from jax.sharding import PartitionSpec as P

beta_one = 0.9
beta_two = 0.95
epsilon = 1e-08
learn_rate = 0.001
weight_decay = 0.1
first_step = 3.0
second_step = 4.0

LANES = 128
CORES = 2
f32, bf16 = jnp.float32, jnp.bfloat16
VMEM = 16 * 2**20
LONG = 10**11


def swap(value, axis, bits):
    pairs = [(source, source ^ bits) for source in range(lax.axis_size(axis))]
    return lax.ppermute(value, axis, pairs)


def swap_border(value):
    pairs = []
    for right in range(CORES, lax.axis_size("dp"), CORES):
        pairs += [(right - 1, right), (right, right - 1)]
    return lax.ppermute(value, "dp", pairs)


def adam_update(master, moment, variance, gradient, step_count):
    moment = beta_one * moment + (1.0 - beta_one) * gradient
    variance = beta_two * variance + (1.0 - beta_two) * gradient * gradient
    fix_one = 1.0 / (1.0 - beta_one**step_count)
    fix_two = 1.0 / (1.0 - beta_two**step_count)
    update = moment * fix_one / (jnp.sqrt(variance * fix_two) + epsilon) + weight_decay * master
    return (master - learn_rate * update, moment, variance)


def call(kernel, shapes, *args, scalars=0, flops=0):
    whole = pl.BlockSpec(memory_space=pltpu.VMEM)
    small = pl.BlockSpec(memory_space=pltpu.SMEM)
    touched = sum(a.size * a.dtype.itemsize for a in args)
    return pl.pallas_call(
        kernel,
        out_shape=shapes,
        in_specs=[small] * scalars + [whole] * (len(args) - scalars),
        out_specs=jax.tree.map(lambda _: whole, shapes),
        compiler_params=pltpu.CompilerParams(vmem_limit_bytes=VMEM),
        cost_estimate=pl.CostEstimate(flops=flops, bytes_accessed=touched, transcendentals=0),
    )(*args)


def shape(dims, dtype):
    return jax.ShapeDtypeStruct(dims, dtype)


def first_kernel(moves, *refs):
    windows, refs = refs[:4], refs[4:]
    tokens, refs = (refs[0], refs[1:]) if moves else (None, refs)
    weights, leaving, staying, end_states = refs[:4]
    blocks, (held, sems, *block_sems) = refs[4 : 4 + moves], refs[4 + moves :]
    group, tensor, rank = (lax.axis_index(a) for a in ("group", "tensor", "dp"))
    tensors = lax.axis_size("tensor")
    chip, core = rank // CORES, rank % CORES
    rows, cols = weights.shape[1:]
    count = weights.shape[0] - 2
    half, per = count // 2, cols // LANES
    runs = [(0, 1), (count + 1, 1), ((1 - group) * half + 1, half), (group * half + 1, half)]
    copies = [
        [
            pltpu.make_async_copy(
                windows[i].at[pl.ds(start, size)], held.at[i, pl.ds(start, size)], sems.at[j, i]
            )
            for i in range(4)
        ]
        for j, (start, size) in enumerate(runs)
    ]
    moved = []
    for step, out in enumerate(blocks):
        share, depth = out.shape[0] // (tensors if step == 0 else 1), out.shape[1] // CORES
        for j in range(out.shape[0] // share):
            row = pl.multiple_of((tensor ^ j) * share, share)
            for i in range(CORES):
                col = pl.multiple_of(((chip ^ step) * CORES + (core ^ i)) * depth, depth)
                moved.append(
                    pltpu.make_async_copy(
                        tokens.at[pl.ds(row, share), pl.ds(col, depth)],
                        out.at[pl.ds(j * share, share), pl.ds(i * depth, depth)],
                        block_sems[0].at[step, j, i],
                    )
                )
    for copy in [c for run in copies for c in run] + moved:
        copy.start()

    def update(block, h):
        picks = pl.ds(h, rows, stride=per) if per > 1 else pl.ds(0, rows)
        return adam_update(*[held[i, block, picks, :] for i in range(4)], first_step)

    for j, (start, size) in enumerate(runs):
        for copy in copies[j]:
            copy.wait()
        for k in range(size):
            for h in range(per):
                at = slice(h * LANES, (h + 1) * LANES)
                values = update(start + k, h)
                weights[start + k, :, at] = values[0].astype(bf16)
                if j < 2:
                    for i in range(3):
                        end_states[j, i, :, at] = values[i]
                else:
                    for i in range(3):
                        (leaving, staying)[j - 2][i, k, :, at] = values[i]
    for copy in moved:
        copy.wait()


def first(windows, tokens, old_cols, chips, tensors):
    count, rows = windows[0].shape[0] - 2, windows[0].shape[1]
    short = rows * LANES // old_cols
    slots, depth = tokens.shape[0], tokens.shape[1] // chips
    share = slots // tensors
    aligned = depth % (CORES * LANES) == 0 and share % 16 == 0
    moves = chips if aligned else 0
    blocks = [shape((slots if i == 0 else share, depth), bf16) for i in range(moves)]
    tile = shape((3, count // 2, short, old_cols), f32)
    outs = [
        shape((count + 2, short, old_cols), bf16),
        tile,
        tile,
        shape((2, 3, short, old_cols), f32),
        *blocks,
    ]
    operands = [*windows, tokens] if moves else windows
    scratch = [pltpu.VMEM((4, count + 2, rows, LANES), f32), pltpu.SemaphoreType.DMA((4, 4))]
    if moves:
        scratch.append(pltpu.SemaphoreType.DMA((chips, tensors, CORES)))
    out = pl.pallas_call(
        functools.partial(first_kernel, moves),
        out_shape=outs,
        in_specs=[pl.BlockSpec(memory_space=pl.ANY)] * len(operands),
        out_specs=[pl.BlockSpec(memory_space=pltpu.VMEM)] * len(outs),
        scratch_shapes=scratch,
        cost_estimate=pl.CostEstimate(flops=0, bytes_accessed=10**7, transcendentals=0),
    )(*operands)
    return out[:4], out[4:]


def live_bounds(offsets, span, rank, other):
    slab = lax.axis_index("tensor") * lax.axis_size("group") + (lax.axis_index("group") ^ other)
    start = rank * span
    return offsets[slab, rank] - start, offsets[slab, rank + 1] - start


def place_of(rows, cols, first):
    place = lax.broadcasted_iota(jnp.int32, (rows, cols), 0) * cols
    return first + place + lax.broadcasted_iota(jnp.int32, (rows, cols), 1)


def patch_weights_kernel(offsets, mine, other, inner, outer, out):
    rows, cols = mine.shape[1:]
    count = mine.shape[0] - 2
    span = count * rows * cols
    is_first = lax.axis_index("dp") % CORES == 0
    for i, piece in enumerate((mine, other)):
        at = slice(i * cols, (i + 1) * cols)
        low, high = live_bounds(offsets, span, lax.axis_index("dp"), i)
        near, far = inner[:, at].astype(f32), outer[:, at].astype(f32)
        before = place_of(rows, cols, 0) < low
        after = place_of(rows, cols, span - rows * cols) >= high
        begin, end = piece[1].astype(f32), piece[count].astype(f32)
        out[0, :, at] = jnp.where(before, jnp.where(is_first, far, near), begin).astype(bf16)
        out[1 : count - 1, :, at] = piece[2:count]
        out[count - 1, :, at] = jnp.where(after, jnp.where(is_first, near, far), end).astype(bf16)


def patch_states_kernel(offsets, leaving, staying, inner, outer, out_leaving, out_staying):
    _, half, rows, cols = leaving.shape
    span = 2 * half * rows * cols
    low, high = live_bounds(offsets, span, lax.axis_index("dp"), 0)
    first = lax.axis_index("dp") % CORES == 0
    group = lax.axis_index("group")
    for tile, states, out in ((1 - group, leaving, out_leaving), (group, staying, out_staying)):
        before = place_of(rows, cols, tile * (span // 2)) < low
        after = place_of(rows, cols, tile * (span // 2) + (half - 1) * rows * cols) >= high
        for i in range(3):
            left = jnp.where(first, outer[i], inner[i])
            right = jnp.where(first, inner[i], outer[i])
            out[i, 0] = jnp.where(before, left, states[i, 0])
            out[i, 1 : half - 1] = states[i, 1 : half - 1]
            out[i, half - 1] = jnp.where(after, right, states[i, half - 1])


def part_kernel(pieces, *refs):
    mine, mate, out = refs[pieces:]
    rows = jnp.concatenate([r[...] for r in refs[:pieces]], axis=0)
    depth = mine.shape[0]
    value = jnp.dot(rows[:, :depth], mine[...], preferred_element_type=f32)
    value = value + jnp.dot(rows[:, depth:], mate[...], preferred_element_type=f32)
    out[...] = value.astype(out.dtype)


def part(pieces, weights, dtype):
    rows = sum(p.shape[0] for p in pieces)
    cols = weights[0].shape[1]
    return call(
        functools.partial(part_kernel, len(pieces)),
        shape((rows, cols), dtype),
        *pieces,
        *weights,
        flops=2 * rows * pieces[0].shape[1] * cols,
    )


def own_order(rows, cols):
    tensors, groups = lax.axis_size("tensor"), lax.axis_size("group")
    share, wide = rows // tensors, cols // groups
    for j in range(tensors):
        row = pl.multiple_of((lax.axis_index("tensor") ^ j) * share, share)
        for i in range(groups):
            col = pl.multiple_of((lax.axis_index("group") ^ i) * wide, wide)
            here = (slice(j * share, (j + 1) * share), slice(i * wide, (i + 1) * wide))
            yield here, (pl.ds(row, share), pl.ds(col, wide)), row


def live_kernel(counts, _, cotangent, out):
    live = counts[lax.axis_index("dp") * lax.axis_size("group") + lax.axis_index("group")]
    for here, there, first_row in own_order(*cotangent.shape):
        value = cotangent[there].astype(f32)
        row = first_row + lax.broadcasted_iota(jnp.int32, value.shape, 0)
        out[here] = jnp.where(row < live, value, 0.0).astype(bf16)


def delta_kernel(*refs):
    own, (cotangent, activated, delta) = refs[0], refs[-3:]
    preact = own[...]
    for r in refs[1:-3]:
        preact = preact + r[...].astype(f32)
    sigmoid = 1.0 / (1.0 + jnp.exp(-preact))
    activated[...] = (preact * sigmoid).astype(bf16)
    derivative = sigmoid * (1.0 + preact * (1.0 - sigmoid))
    delta[...] = (cotangent[...].astype(f32) * derivative).astype(bf16)


def natural_kernel(value, out):
    for here, there, _ in own_order(*value.shape):
        out[there] = value[here]


def gradient_kernel(tokens, *refs):
    deltas, out = refs[:-1], refs[-1]
    delta = jnp.concatenate([r[...] for r in deltas], axis=0)
    value = lax.dot_general(
        tokens[...], delta, (((0,), (0,)), ((), ())), preferred_element_type=f32
    ).astype(out.dtype)
    tile = out.shape[1]
    for i in range(out.shape[0]):
        out[i] = value[i * tile : (i + 1) * tile]


def core_sum_kernel(mine, received, keep, send):
    group = lax.axis_index("group")
    cols = keep.shape[1] // 2
    keep[...] = mine[group] + received[group].astype(f32)
    value = (mine[1 - group] + received[1 - group].astype(f32)).astype(bf16)
    send[:, :cols] = value[:, cols:]
    send[:, cols:] = value[:, :cols]


def second_adam_kernel(staying, incoming, keep, back, master, moment, variance):
    cols = staying.shape[2]
    group = lax.axis_index("group")
    for i, states in enumerate((staying, incoming)):
        here = slice(i * cols, (i + 1) * cols)
        there = pl.ds(pl.multiple_of((group ^ i) * cols, cols), cols)
        gradient = keep[:, here] + back[:, here].astype(f32)
        result = adam_update(states[0], states[1], states[2], gradient, second_step)
        for ref, value in zip((master, moment, variance), result, strict=True):
            ref[:, there] = value


def local(tokens, cotangent, counts, old_offsets, old_master, old_moment, old_variance, old_grad):
    ranks = lax.axis_size("dp")
    chips = ranks // CORES
    groups = lax.axis_size("group")
    tensors = lax.axis_size("tensor")
    rank = lax.axis_index("dp")
    chip, core = rank // CORES, rank % CORES
    tensor = lax.axis_index("tensor")
    slots, width = tokens.shape
    cols = cotangent.shape[1]
    old_cols = cols // groups
    depth = width // chips
    half = depth // CORES
    share = slots // tensors

    length = old_master.shape[2]
    margin = length // 10
    windows = [
        w.reshape(10, margin // LANES, LANES)
        for w in (old_master, old_moment, old_variance, old_grad)
    ]
    (window, leaving, staying, end_states), blocks = first(
        windows, tokens, old_cols, chips, tensors
    )

    def token_block(of_chip, of_tensor):
        return jnp.concatenate(
            [
                lax.dynamic_slice(
                    tokens, (of_tensor * share, of_chip * depth + (core ^ i) * half), (share, half)
                )
                for i in range(CORES)
            ],
            axis=1,
        )

    blocks = blocks or [
        jnp.concatenate([token_block(chip, tensor ^ j) for j in range(tensors)]),
        *[token_block(chip ^ step, tensor) for step in range(1, chips)],
    ]
    turned = call(
        live_kernel, shape((slots, cols), bf16), counts, window, cotangent, scalars=1, flops=LONG
    )
    arrived = [swap(b, "dp", step * CORES) for step, b in enumerate(blocks) if step]
    arrived = [lax.optimization_barrier((a, turned))[0] for a in arrived]
    blocks = [[blocks[0]]] + [
        [a] + [swap(a, "tensor", j) for j in range(1, tensors)] for a in arrived
    ]

    other = swap(window, "group", 1)
    ends = [jnp.concatenate([window[i], other[i]], axis=1) for i in (0, -1)]
    inner = swap(jnp.where(core == 0, ends[1], ends[0]), "dp", 1)
    outer = swap_border(jnp.where(core == 0, ends[0], ends[1]))
    count, rows = window.shape[0] - 2, window.shape[1]
    mine = call(
        patch_weights_kernel,
        shape((count, rows, cols), bf16),
        old_offsets,
        window,
        other,
        inner,
        outer,
        scalars=1,
    )
    mine = mine.reshape(half, cols)
    weights = [mine, swap(mine, "dp", 1)]

    parts = [part(blocks[step], weights, bf16) for step in range(1, chips)]
    back = [swap(p, "dp", step * CORES) for step, p in enumerate(parts, 1)]

    total = part(blocks[0], weights, f32)

    end_states, arrived[-1] = lax.optimization_barrier((end_states, arrived[-1]))
    mate_end = swap(jnp.where(core == 0, end_states[1], end_states[0]), "dp", 1)
    next_end = swap_border(jnp.where(core == 0, end_states[0], end_states[1]))
    leaving, *parts = lax.optimization_barrier((leaving, *parts))
    leaving, staying = call(
        patch_states_kernel,
        [shape(leaving.shape, f32)] * 2,
        old_offsets,
        leaving,
        staying,
        mate_end,
        next_end,
        scalars=1,
    )
    tile = half // groups
    staying = staying.reshape(3, tile, old_cols)
    incoming = swap(leaving.reshape(3, tile, old_cols), "group", 1)
    activated, delta = call(
        delta_kernel, [shape((slots, cols), bf16)] * 2, total, *back, turned
    )
    activated = call(natural_kernel, shape((slots, cols), bf16), activated)
    deltas = [delta] + [swap(delta, "dp", step * CORES) for step in range(1, chips)]

    deltas[-1], incoming = lax.optimization_barrier((deltas[-1], incoming))

    gathered = jnp.concatenate([p for b in blocks for p in b])
    flops = 2 * half * cols * chips * slots
    rows = (groups, tile, cols)
    to_mate = call(gradient_kernel, shape(rows, bf16), gathered[:, half:], *deltas, flops=flops)
    mine = call(gradient_kernel, shape(rows, f32), gathered[:, :half], *deltas, flops=flops)
    keep, send = call(
        core_sum_kernel,
        [shape((tile, cols), f32), shape((tile, cols), bf16)],
        mine,
        swap(to_mate, "dp", 1),
    )
    new = call(
        second_adam_kernel,
        [shape((tile, cols), f32)] * 3,
        staying,
        incoming,
        keep,
        swap(send, "group", 1),
    )
    return (activated, *new)


def solution(mesh):
    rows = P(("dp", "group"), "tensor")
    window = P(("tensor", "group"), "dp", None)
    return jax.shard_map(
        local,
        mesh=mesh,
        in_specs=(P(("dp", "group"), None), rows, P(), P(), window, window, window, window),
        out_specs=(rows, rows, rows, rows),
        check_vma=False,
    )
```

time: 128 us -> 81.2 us (0.63)
  waiting for transfers between devices: 62.7 us -> 39 us
  other arithmetic: 17 us -> 0.07 us
  Pallas kernels: 0 us -> 11.9 us
  matrix products: 10.7 us -> 0 us
  local copies, waits for them, and re-layouts: 9.62 us -> 1.64 us
    ppermute x15 -> x19, waiting for transfers between devices: 62.7 us -> 39 us  [swap(): return lax.ppermute(value, axis, pairs)]
    pallas_call x0 -> x14, Pallas kernels: none -> 11.9 us  [the longest x13 7.29 us: call(): pl.pallas_call(kernel, out_shape=shapes, in_specs=[small] * scalars + [wh...]
    dot_general x5 -> x0, matrix products: 10.7 us -> none  [the longest x3 5.9 us: local(): jnp.dot(blocks[step], weights, preferred_element_type=f32).astype(bf16)]
    select_n x5 -> x2, other arithmetic: 5.5 us -> 0.07 us  [the longest x1 0.04 us: local(): next_end = swap_border(jnp.where(core == 0, end_states[0], end_states[1]))]
    dynamic_slice x3 -> x0, local copies, waits for them, and re-layouts: 3.93 us -> none  [the longest x1 2.35 us: token_block(): return lax.dynamic_slice(tokens, (0, of_chip * depth), (slots, depth))]
    sub x2 -> x0, other arithmetic: 3.4 us -> none  [the longest x1 2.64 us: adam_update(): return (master - learn_rate * update, moment, variance)]
    another operation x1 -> x0, other arithmetic: 2.17 us -> none  [local(): jnp.stack([old_master[0, 0], old_moment[0, 0], old_variance[0, 0], old_gr...]
    lt x2 -> x0, other arithmetic: 1.93 us -> none  [the longest x1 1.38 us: local(): left = jnp.where(place < bounds[0], from_left, windows[:, 1])]
  transfers between devices with their start and end apart: 16 -> 21, of which waited for: 8 -> 12; matrix products, arithmetic and copies ran while one was open for 18% -> 0% of each run, Pallas kernels for 0% -> 5%
where the time goes in v2:
time: 81.2 us; the launch traced here: 81 us
  waiting for transfers between devices  39 us (48%)
  starting transfers between devices  27.4 us (34%)
  Pallas kernels  11.9 us (15%)
  local copies, waits for them, and re-layouts  1.64 us (2%)
  between operations  0.95 us (1%)
    ppermute x19, waiting for transfers between devices, swap(): return lax.ppermute(value, axis, pairs)  39 us
    ppermute x19, starting transfers between devices, swap(): return lax.ppermute(value, axis, pairs)  26 us
    pallas_call x13, Pallas kernels, call(): pl.pallas_call(kernel, out_shape=shapes, in_specs=[small] * scalars + [wh...  7.29 us
    pallas_call x1, Pallas kernels, first(): pl.pallas_call(functools.partial(first_kernel, moves), out_shape=outs, in...  4.66 us
  transfers between devices with their start and end apart: 21, of which 12 were waited for; matrix products, arithmetic and copies ran while one was open for 0% of the time, Pallas kernels for 5%

profile of v2, /device:TPU:0, one launch (start us, length us, event | category | flops | bytes accessed | tf_op | source)
XLA Modules:
  0.0 81.0 jit_solution(2381477725401798587)
XLA Ops:
  0.7 4.7 %shard_map.111 = (bf16[10,80,256]{2,1,0:T(8,128)(2,1)}, f32[3,4,80,256]{3,2,1,0:T(8,128)}, f32[3,4,80,256]{3,2,1,0:T(8,128)}, f32[2,3,80,256]{3,2,1,0:T(8,128)},...) custom-call(f32[10,160,128]{2,1,0:T(8,128)} %bitcast.26, ...), custom_call_target="tpu_custom_call" | custom-call | bytes 10000000 | tf_op jit(solution)/shard_map/pallas_call | solution.py:144
  5.3 3.0 %collective-permute-start = (bf16[10,80,256]{2,1,0:T(8,128)(2,1)}, bf16[10,80,256]{2,1,0:T(8,128)(2,1)S(1)}, u32[]{:S(2)}, u32[]{:S(2)}) collective-permute-start(bf16[10,80,256]{2,1,0:T(8,128)(2,1)} %get-tuple-element.29.mine._), channel_id=1, source_target_pairs={{0,1},{1,0},{2,3},{3,2},{4,5},{5,4},{6,7},{7,6},{8,9},{9,8},{10,11... | collective-permute-start | bytes 1228808 | tf_op jit(solution)/shard_map/ppermute | solution.py:27
  8.3 1.6 %collective-permute-start.4 = (bf16[64,1280]{1,0:T(8,128)(2,1)}, bf16[64,1280]{1,0:T(8,128)(2,1)S(1)}, u32[]{:S(2)}, u32[]{:S(2)}) collective-permute-start(bf16[64,1280]{1,0:T(8,128)(2,1)} %get-tuple-element.30), channel_id=1, source_target_pairs={{0,8},{4,12},{8,0},{12,4},{16,24},{20,28},{24,16},{28,20},{1,9},{5... | collective-permute-start | bytes 491528 | tf_op jit(solution)/shard_map/ppermute | solution.py:27
  9.9 2.6 %collective-permute-start.7 = (bf16[64,1280]{1,0:T(8,128)(2,1)}, bf16[64,1280]{1,0:T(8,128)(2,1)S(1)}, u32[]{:S(2)}, u32[]{:S(2)}) collective-permute-start(bf16[64,1280]{1,0:T(8,128)(2,1)} %get-tuple-element.32), channel_id=1, source_target_pairs={{0,16},{4,20},{8,24},{12,28},{16,0},{20,4},{24,8},{28,12},{1,17},{... | collective-permute-start | bytes 491528 | tf_op jit(solution)/shard_map/ppermute | solution.py:27
  12.7 1.0 %copy-done.3 = bf16[10,80,256]{2,1,0:T(8,128)(2,1)S(1)} copy-done((bf16[10,80,256]{2,1,0:T(8,128)(2,1)S(1)}, bf16[10,80,256]{2,1,0:T(8,128)(2,1)}, u32[]{:S(2)}) %copy-start.3) | copy-done | bytes 409624
  13.8 0.6 shard_map.114.refs_4_
  14.8 3.3 %collective-permute-done.other = bf16[10,80,256]{2,1,0:T(8,128)(2,1)S(1)} collective-permute-done((bf16[10,80,256]{2,1,0:T(8,128)(2,1)}, bf16[10,80,256]{2,1,0:T(8,128)(2,1)S(1)}, u32[]{:S(2)}, u32[]{:S(2)}) %collective-permute-start) | collective-permute-done | bytes 409632 | tf_op jit(solution)/shard_map/ppermute | solution.py:27
  18.2 0.8 collective-permute-start.2
  19.0 1.8 %collective-permute-start.5 = (bf16[64,1280]{1,0:T(8,128)(2,1)S(1)}, bf16[64,1280]{1,0:T(8,128)(2,1)S(1)}, u32[]{:S(2)}, u32[]{:S(2)}) collective-permute-start(bf16[64,1280]{1,0:T(8,128)(2,1)S(1)} %collective-permute-done.4.refs_0_), channel_id=1, source_target_pairs={{0,2},{2,0},{1,3},{3,1},{4,6},{6,4},{5,7},{7,5},{8,10},{10,8},{9,1... | collective-permute-start | bytes 491528 | tf_op jit(solution)/shard_map/ppermute | solution.py:27
  20.8 4.4 %collective-permute-done.7.refs_0_ = bf16[64,1280]{1,0:T(8,128)(2,1)S(1)} collective-permute-done((bf16[64,1280]{1,0:T(8,128)(2,1)}, bf16[64,1280]{1,0:T(8,128)(2,1)S(1)}, u32[]{:S(2)}, u32[]{:S(2)}) %collective-permute-start.7) | collective-permute-done | bytes 163872 | tf_op jit(solution)/shard_map/ppermute | solution.py:27
  25.2 1.5 %collective-permute-start.8 = (bf16[64,1280]{1,0:T(8,128)(2,1)S(1)}, bf16[64,1280]{1,0:T(8,128)(2,1)S(1)}, u32[]{:S(2)}, u32[]{:S(2)}) collective-permute-start(bf16[64,1280]{1,0:T(8,128)(2,1)S(1)} %collective-permute-done.7.refs_0_), channel_id=1, source_target_pairs={{0,2},{2,0},{1,3},{3,1},{4,6},{6,4},{5,7},{7,5},{8,10},{10,8},{9,1... | collective-permute-start | bytes 491528 | tf_op jit(solution)/shard_map/ppermute | solution.py:27
  27.2 0.7 shard_map.112
  28.6 0.7 collective-permute-start.14
  29.3 0.7 collective-permute-done.3.refs_2_.refs_3_
  30.4 1.4 %collective-permute-done.8.refs_1_ = bf16[64,1280]{1,0:T(8,128)(2,1)S(1)} collective-permute-done((bf16[64,1280]{1,0:T(8,128)(2,1)S(1)}, bf16[64,1280]{1,0:T(8,128)(2,1)S(1)}, u32[]{:S(2)}, u32[]{:S(2)}) %collective-permute-start.8) | collective-permute-done | bytes 163872 | tf_op jit(solution)/shard_map/ppermute | solution.py:27
  32.2 1.4 %collective-permute-done.11.refs_1_ = bf16[64,1280]{1,0:T(8,128)(2,1)S(1)} collective-permute-done((bf16[64,1280]{1,0:T(8,128)(2,1)S(1)}, bf16[64,1280]{1,0:T(8,128)(2,1)S(1)}, u32[]{:S(2)}, u32[]{:S(2)}) %collective-permute-start.11) | collective-permute-done | bytes 163872 | tf_op jit(solution)/shard_map/ppermute | solution.py:27
  34.0 0.8 shard_map.120
  34.8 1.6 %collective-permute-start.16 = (f32[3,320,256]{2,1,0:T(8,128)S(1)}, f32[3,320,256]{2,1,0:T(8,128)S(1)}, u32[]{:S(2)}, u32[]{:S(2)}) collective-permute-start(f32[3,320,256]{2,1,0:T(8,128)S(1)} %bitcast.25), channel_id=1, source_target_pairs={{0,1},{1,0},{2,3},{3,2},{4,5},{5,4},{6,7},{7,6},{8,9},{9,8},{10,11... | collective-permute-start | bytes 2949128 | tf_op jit(solution)/shard_map/ppermute | solution.py:27
  36.4 3.1 %collective-permute-start.6 = (bf16[128,512]{1,0:T(8,128)(2,1)S(1)}, bf16[128,512]{1,0:T(8,128)(2,1)S(1)}, u32[]{:S(2)}, u32[]{:S(2)}) collective-permute-start(bf16[128,512]{1,0:T(8,128)(2,1)S(1)} %shard_map.115), channel_id=1, source_target_pairs={{0,8},{4,12},{8,0},{12,4},{16,24},{20,28},{24,16},{28,20},{1,9},{5... | collective-permute-start | bytes 393224 | tf_op jit(solution)/shard_map/ppermute | solution.py:27
  39.5 2.7 %collective-permute-start.9 = (bf16[128,512]{1,0:T(8,128)(2,1)S(1)}, bf16[128,512]{1,0:T(8,128)(2,1)S(1)}, u32[]{:S(2)}, u32[]{:S(2)}) collective-permute-start(bf16[128,512]{1,0:T(8,128)(2,1)S(1)} %shard_map.116), channel_id=1, source_target_pairs={{0,16},{4,20},{8,24},{12,28},{16,0},{20,4},{24,8},{28,12},{1,17},{... | collective-permute-start | bytes 393224 | tf_op jit(solution)/shard_map/ppermute | solution.py:27
  43.2 2.5 %collective-permute-done.6.refs_1_ = bf16[128,512]{1,0:T(8,128)(2,1)S(1)} collective-permute-done((bf16[128,512]{1,0:T(8,128)(2,1)S(1)}, bf16[128,512]{1,0:T(8,128)(2,1)S(1)}, u32[]{:S(2)}, u32[]{:S(2)}) %collective-permute-start.6) | collective-permute-done | bytes 131104 | tf_op jit(solution)/shard_map/ppermute | solution.py:27
  45.7 6.8 %collective-permute-done.9.refs_2_ = bf16[128,512]{1,0:T(8,128)(2,1)S(1)} collective-permute-done((bf16[128,512]{1,0:T(8,128)(2,1)S(1)}, bf16[128,512]{1,0:T(8,128)(2,1)S(1)}, u32[]{:S(2)}, u32[]{:S(2)}) %collective-permute-start.9) | collective-permute-done | bytes 131104 | tf_op jit(solution)/shard_map/ppermute | solution.py:27
  52.6 3.1 %collective-permute-start.15 = (bf16[128,512]{1,0:T(8,128)(2,1)S(1)}, bf16[128,512]{1,0:T(8,128)(2,1)S(1)}, u32[]{:S(2)}, u32[]{:S(2)}) collective-permute-start(bf16[128,512]{1,0:T(8,128)(2,1)S(1)} %get-tuple-element.43.refs_0_), channel_id=1, source_target_pairs={{0,24},{4,28},{8,16},{12,20},{16,8},{20,12},{24,0},{28,4},{1,25},{... | collective-permute-start | bytes 393224 | tf_op jit(solution)/shard_map/ppermute | solution.py:27
  55.7 1.3 %collective-permute-start.17 = (bf16[128,512]{1,0:T(8,128)(2,1)S(1)}, bf16[128,512]{1,0:T(8,128)(2,1)S(1)}, u32[]{:S(2)}, u32[]{:S(2)}) collective-permute-start(bf16[128,512]{1,0:T(8,128)(2,1)S(1)} %get-tuple-element.43.refs_0_), channel_id=1, source_target_pairs={{0,8},{4,12},{8,0},{12,4},{16,24},{20,28},{24,16},{28,20},{1,9},{5... | collective-permute-start | bytes 393224 | tf_op jit(solution)/shard_map/ppermute | solution.py:27
  57.2 3.8 %collective-permute-done.15.refs_3_ = bf16[128,512]{1,0:T(8,128)(2,1)S(1)} collective-permute-done((bf16[128,512]{1,0:T(8,128)(2,1)S(1)}, bf16[128,512]{1,0:T(8,128)(2,1)S(1)}, u32[]{:S(2)}, u32[]{:S(2)}) %collective-permute-start.15) | collective-permute-done | bytes 131104 | tf_op jit(solution)/shard_map/ppermute | solution.py:27
  60.9 1.2 %collective-permute-done.17.refs_1_ = bf16[128,512]{1,0:T(8,128)(2,1)S(1)} collective-permute-done((bf16[128,512]{1,0:T(8,128)(2,1)S(1)}, bf16[128,512]{1,0:T(8,128)(2,1)S(1)}, u32[]{:S(2)}, u32[]{:S(2)}) %collective-permute-start.17) | collective-permute-done | bytes 131104 | tf_op jit(solution)/shard_map/ppermute | solution.py:27
  62.1 4.5 %collective-permute-done.18.refs_2_ = bf16[128,512]{1,0:T(8,128)(2,1)S(1)} collective-permute-done((bf16[128,512]{1,0:T(8,128)(2,1)S(1)}, bf16[128,512]{1,0:T(8,128)(2,1)S(1)}, u32[]{:S(2)}, u32[]{:S(2)}) %collective-permute-start.18) | collective-permute-done | bytes 131104 | tf_op jit(solution)/shard_map/ppermute | solution.py:27
  67.8 1.5 %collective-permute-done.19.received = bf16[2,320,512]{2,1,0:T(8,128)(2,1)S(1)} collective-permute-done((bf16[2,320,512]{2,1,0:T(8,128)(2,1)S(1)}, bf16[2,320,512]{2,1,0:T(8,128)(2,1)S(1)}, u32[]{:S(2)}, u32[]{:S(2)}) %collective-permute-start.19) | collective-permute-done | bytes 655392 | tf_op jit(solution)/shard_map/ppermute | solution.py:27
  69.4 1.6 %collective-permute-start.20 = (bf16[320,512]{1,0:T(8,128)(2,1)S(1)}, bf16[320,512]{1,0:T(8,128)(2,1)S(1)}, u32[]{:S(2)}, u32[]{:S(2)}) collective-permute-start(bf16[320,512]{1,0:T(8,128)(2,1)S(1)} %get-tuple-element.48), channel_id=1, source_target_pairs={{0,1},{1,0},{2,3},{3,2},{4,5},{5,4},{6,7},{7,6},{8,9},{9,8},{10,11... | collective-permute-start | bytes 983048 | tf_op jit(solution)/shard_map/ppermute | solution.py:27
  71.0 0.7 shard_map.119
  71.7 7.6 %collective-permute-done.20.back = bf16[320,512]{1,0:T(8,128)(2,1)S(1)} collective-permute-done((bf16[320,512]{1,0:T(8,128)(2,1)S(1)}, bf16[320,512]{1,0:T(8,128)(2,1)S(1)}, u32[]{:S(2)}, u32[]{:S(2)}) %collective-permute-start.20) | collective-permute-done | bytes 327712 | tf_op jit(solution)/shard_map/ppermute | solution.py:27
  79.2 1.8 %shard_map.124 = (f32[320,512]{1,0:T(8,128)}, f32[320,512]{1,0:T(8,128)}, f32[320,512]{1,0:T(8,128)}) custom-call(f32[3,320,256]{2,1,0:T(8,128)S(1)} %bitcast.24, f32[3,320,256]{2,1,0:T(8,128)S(1)} %collective-permute-done.16.incoming, f32[320,512]{1,0:T(8,128)S(1)} %get-tuple-element.47.keep, bf16[320,512]{1,0:T(8,128)(2,1)S(1)} %collective-permute-done.20.back), custom_call_target="tpu_custom_call" | custom-call | bytes 2949120 | tf_op jit(solution)/shard_map/pallas_call | solution.py:50
  (54 shorter events, 5.7 us)
Async XLA Ops:
  0.6 12.1 %copy-start.6 = (bf16[128,512]{1,0:T(8,128)(2,1)S(1)}, bf16[128,512]{1,0:T(8,128)(2,1)}, u32[]{:S(2)}) copy-start(bf16[128,512]{1,0:T(8,128)(2,1)} %cotangent.1) | copy-start | bytes 393220
  0.6 12.1 %copy-start.7 = (s32[16]{0:T(128)S(1)}, s32[16]{0:T(128)}, u32[]{:S(2)}) copy-start(s32[16]{0:T(128)} %counts.1) | copy-start | bytes 196
  5.3 12.7 %collective-permute-start = (bf16[10,80,256]{2,1,0:T(8,128)(2,1)}, bf16[10,80,256]{2,1,0:T(8,128)(2,1)S(1)}, u32[]{:S(2)}, u32[]{:S(2)}) collective-permute-start(bf16[10,80,256]{2,1,0:T(8,128)(2,1)} %get-tuple-element.29.mine._), channel_id=1, source_target_pairs={{0,1},{1,0},{2,3},{3,2},{4,5},{5,4},{6,7},{7,6},{8,9},{9,8},{10,11... | collective-permute-start | bytes 1228808 | tf_op jit(solution)/shard_map/ppermute | solution.py:27
  8.3 10.7 %collective-permute-start.4 = (bf16[64,1280]{1,0:T(8,128)(2,1)}, bf16[64,1280]{1,0:T(8,128)(2,1)S(1)}, u32[]{:S(2)}, u32[]{:S(2)}) collective-permute-start(bf16[64,1280]{1,0:T(8,128)(2,1)} %get-tuple-element.30), channel_id=1, source_target_pairs={{0,8},{4,12},{8,0},{12,4},{16,24},{20,28},{24,16},{28,20},{1,9},{5... | collective-permute-start | bytes 491528 | tf_op jit(solution)/shard_map/ppermute | solution.py:27
  9.9 15.3 %collective-permute-start.7 = (bf16[64,1280]{1,0:T(8,128)(2,1)}, bf16[64,1280]{1,0:T(8,128)(2,1)S(1)}, u32[]{:S(2)}, u32[]{:S(2)}) collective-permute-start(bf16[64,1280]{1,0:T(8,128)(2,1)} %get-tuple-element.32), channel_id=1, source_target_pairs={{0,16},{4,20},{8,24},{12,28},{16,0},{20,4},{24,8},{28,12},{1,17},{... | collective-permute-start | bytes 491528 | tf_op jit(solution)/shard_map/ppermute | solution.py:27
  12.5 6.5 %copy-start = (bf16[128,1280]{1,0:T(8,128)(2,1)S(1)}, bf16[128,1280]{1,0:T(8,128)(2,1)}, u32[]{:S(2)}) copy-start(bf16[128,1280]{1,0:T(8,128)(2,1)} %get-tuple-element.28.refs_0_) | copy-start | bytes 983044
  12.5 14.2 %collective-permute-start.10 = (bf16[64,1280]{1,0:T(8,128)(2,1)}, bf16[64,1280]{1,0:T(8,128)(2,1)S(1)}, u32[]{:S(2)}, u32[]{:S(2)}) collective-permute-start(bf16[64,1280]{1,0:T(8,128)(2,1)} %get-tuple-element.34), channel_id=1, source_target_pairs={{0,24},{4,28},{8,16},{12,20},{16,8},{20,12},{24,0},{28,4},{1,25},{... | collective-permute-start | bytes 491528 | tf_op jit(solution)/shard_map/ppermute | solution.py:27
  12.7 1.0 %copy-start.3 = (bf16[10,80,256]{2,1,0:T(8,128)(2,1)S(1)}, bf16[10,80,256]{2,1,0:T(8,128)(2,1)}, u32[]{:S(2)}) copy-start(bf16[10,80,256]{2,1,0:T(8,128)(2,1)} %get-tuple-element.29.mine._) | copy-start | bytes 1228804
  13.7 1.0 %copy-start.4 = (bf16[10,80,256]{2,1,0:T(8,128)(2,1)S(1)}, bf16[10,80,256]{2,1,0:T(8,128)(2,1)}, u32[]{:S(2)}) copy-start(bf16[10,80,256]{2,1,0:T(8,128)(2,1)} %get-tuple-element.29.mine._) | copy-start | bytes 1228804
  14.3 12.9 %copy-start.5 = (s32[4,9]{1,0:T(4,128)S(1)}, s32[4,9]{1,0:T(4,128)}, u32[]{:S(2)}) copy-start(s32[4,9]{1,0:T(4,128)} %offsets.3) | copy-start | bytes 436
  18.0 10.0 %copy-start.8 = (f32[2,3,80,256]{3,2,1,0:T(8,128)S(1)}, f32[2,3,80,256]{3,2,1,0:T(8,128)}, u32[]{:S(2)}) copy-start(f32[2,3,80,256]{3,2,1,0:T(8,128)} %get-tuple-element.41) | copy-start | bytes 1474564
  18.1 9.2 %collective-permute-start.1 = (bf16[80,512]{1,0:T(8,128)(2,1)S(1)}, bf16[80,512]{1,0:T(8,128)(2,1)S(1)}, u32[]{:S(2)}, u32[]{:S(2)}) collective-permute-start(bf16[80,512]{1,0:T(8,128)(2,1)S(1)} %get-tuple-element.61), channel_id=1, source_target_pairs={{0,4},{4,0},{8,12},{12,8},{16,20},{20,16},{24,28},{28,24},{1,5},{5... | collective-permute-start | bytes 245768 | tf_op jit(solution)/shard_map/ppermute | solution.py:27
  18.2 9.1 %collective-permute-start.2 = (bf16[80,512]{1,0:T(8,128)(2,1)S(1)}, bf16[80,512]{1,0:T(8,128)(2,1)S(1)}, u32[]{:S(2)}, u32[]{:S(2)}) collective-permute-start(bf16[80,512]{1,0:T(8,128)(2,1)S(1)} %get-tuple-element.60), channel_id=1, source_target_pairs={{4,8},{8,4},{12,16},{16,12},{20,24},{24,20},{5,9},{9,5},{13,17},{1... | collective-permute-start | bytes 245768 | tf_op jit(solution)/shard_map/ppermute | solution.py:34
  19.0 9.6 %collective-permute-start.5 = (bf16[64,1280]{1,0:T(8,128)(2,1)S(1)}, bf16[64,1280]{1,0:T(8,128)(2,1)S(1)}, u32[]{:S(2)}, u32[]{:S(2)}) collective-permute-start(bf16[64,1280]{1,0:T(8,128)(2,1)S(1)} %collective-permute-done.4.refs_0_), channel_id=1, source_target_pairs={{0,2},{2,0},{1,3},{3,1},{4,6},{6,4},{5,7},{7,5},{8,10},{10,8},{9,1... | collective-permute-start | bytes 491528 | tf_op jit(solution)/shard_map/ppermute | solution.py:27
  25.2 6.7 %collective-permute-start.8 = (bf16[64,1280]{1,0:T(8,128)(2,1)S(1)}, bf16[64,1280]{1,0:T(8,128)(2,1)S(1)}, u32[]{:S(2)}, u32[]{:S(2)}) collective-permute-start(bf16[64,1280]{1,0:T(8,128)(2,1)S(1)} %collective-permute-done.7.refs_0_), channel_id=1, source_target_pairs={{0,2},{2,0},{1,3},{3,1},{4,6},{6,4},{5,7},{7,5},{8,10},{10,8},{9,1... | collective-permute-start | bytes 491528 | tf_op jit(solution)/shard_map/ppermute | solution.py:27
  26.7 6.9 %collective-permute-start.11 = (bf16[64,1280]{1,0:T(8,128)(2,1)S(1)}, bf16[64,1280]{1,0:T(8,128)(2,1)S(1)}, u32[]{:S(2)}, u32[]{:S(2)}) collective-permute-start(bf16[64,1280]{1,0:T(8,128)(2,1)S(1)} %collective-permute-done.10.refs_0_), channel_id=1, source_target_pairs={{0,2},{2,0},{1,3},{3,1},{4,6},{6,4},{5,7},{7,5},{8,10},{10,8},{9,1... | collective-permute-start | bytes 491528 | tf_op jit(solution)/shard_map/ppermute | solution.py:27
  27.9 2.2 %collective-permute-start.3 = (bf16[640,512]{1,0:T(8,128)(2,1)S(1)}, bf16[640,512]{1,0:T(8,128)(2,1)S(1)}, u32[]{:S(2)}, u32[]{:S(2)}) collective-permute-start(bf16[640,512]{1,0:T(8,128)(2,1)S(1)} %bitcast.19), channel_id=1, source_target_pairs={{0,4},{4,0},{8,12},{12,8},{16,20},{20,16},{24,28},{28,24},{1,5},{5... | collective-permute-start | bytes 1966088 | tf_op jit(solution)/shard_map/ppermute | solution.py:27
  28.1 5.9 %collective-permute-start.13 = (f32[3,80,256]{2,1,0:T(8,128)S(1)}, f32[3,80,256]{2,1,0:T(8,128)S(1)}, u32[]{:S(2)}, u32[]{:S(2)}) collective-permute-start(f32[3,80,256]{2,1,0:T(8,128)S(1)} %get-tuple-element.55), channel_id=1, source_target_pairs={{0,4},{4,0},{8,12},{12,8},{16,20},{20,16},{24,28},{28,24},{1,5},{5... | collective-permute-start | bytes 737288 | tf_op jit(solution)/shard_map/ppermute | solution.py:27
  28.6 5.4 %collective-permute-start.14 = (f32[3,80,256]{2,1,0:T(8,128)S(1)}, f32[3,80,256]{2,1,0:T(8,128)S(1)}, u32[]{:S(2)}, u32[]{:S(2)}) collective-permute-start(f32[3,80,256]{2,1,0:T(8,128)S(1)} %get-tuple-element.54), channel_id=1, source_target_pairs={{4,8},{8,4},{12,16},{16,12},{20,24},{24,20},{5,9},{9,5},{13,17},{1... | collective-permute-start | bytes 737288 | tf_op jit(solution)/shard_map/ppermute | solution.py:34
  31.9 2.1 %copy-start.2 = (f32[3,4,80,256]{3,2,1,0:T(8,128)S(1)}, f32[3,4,80,256]{3,2,1,0:T(8,128)}, u32[]{:S(2)}) copy-start(f32[3,4,80,256]{3,2,1,0:T(8,128)} %get-tuple-element.39.staying) | copy-start | bytes 2949124
  32.2 1.8 %copy-start.1 = (f32[3,4,80,256]{3,2,1,0:T(8,128)S(1)}, f32[3,4,80,256]{3,2,1,0:T(8,128)}, u32[]{:S(2)}) copy-start(f32[3,4,80,256]{3,2,1,0:T(8,128)} %get-tuple-element.38.leaving) | copy-start | bytes 2949124
  34.8 26.1 %collective-permute-start.16 = (f32[3,320,256]{2,1,0:T(8,128)S(1)}, f32[3,320,256]{2,1,0:T(8,128)S(1)}, u32[]{:S(2)}, u32[]{:S(2)}) collective-permute-start(f32[3,320,256]{2,1,0:T(8,128)S(1)} %bitcast.25), channel_id=1, source_target_pairs={{0,1},{1,0},{2,3},{3,2},{4,5},{5,4},{6,7},{7,6},{8,9},{9,8},{10,11... | collective-permute-start | bytes 2949128 | tf_op jit(solution)/shard_map/ppermute | solution.py:27
  36.4 9.2 %collective-permute-start.6 = (bf16[128,512]{1,0:T(8,128)(2,1)S(1)}, bf16[128,512]{1,0:T(8,128)(2,1)S(1)}, u32[]{:S(2)}, u32[]{:S(2)}) collective-permute-start(bf16[128,512]{1,0:T(8,128)(2,1)S(1)} %shard_map.115), channel_id=1, source_target_pairs={{0,8},{4,12},{8,0},{12,4},{16,24},{20,28},{24,16},{28,20},{1,9},{5... | collective-permute-start | bytes 393224 | tf_op jit(solution)/shard_map/ppermute | solution.py:27
  39.5 12.9 %collective-permute-start.9 = (bf16[128,512]{1,0:T(8,128)(2,1)S(1)}, bf16[128,512]{1,0:T(8,128)(2,1)S(1)}, u32[]{:S(2)}, u32[]{:S(2)}) collective-permute-start(bf16[128,512]{1,0:T(8,128)(2,1)S(1)} %shard_map.116), channel_id=1, source_target_pairs={{0,16},{4,20},{8,24},{12,28},{16,0},{20,4},{24,8},{28,12},{1,17},{... | collective-permute-start | bytes 393224 | tf_op jit(solution)/shard_map/ppermute | solution.py:27
  42.3 10.2 %collective-permute-start.12 = (bf16[128,512]{1,0:T(8,128)(2,1)S(1)}, bf16[128,512]{1,0:T(8,128)(2,1)S(1)}, u32[]{:S(2)}, u32[]{:S(2)}) collective-permute-start(bf16[128,512]{1,0:T(8,128)(2,1)S(1)} %shard_map.117), channel_id=1, source_target_pairs={{0,24},{4,28},{8,16},{12,20},{16,8},{20,12},{24,0},{28,4},{1,25},{... | collective-permute-start | bytes 393224 | tf_op jit(solution)/shard_map/ppermute | solution.py:27
  52.6 8.3 %collective-permute-start.15 = (bf16[128,512]{1,0:T(8,128)(2,1)S(1)}, bf16[128,512]{1,0:T(8,128)(2,1)S(1)}, u32[]{:S(2)}, u32[]{:S(2)}) collective-permute-start(bf16[128,512]{1,0:T(8,128)(2,1)S(1)} %get-tuple-element.43.refs_0_), channel_id=1, source_target_pairs={{0,24},{4,28},{8,16},{12,20},{16,8},{20,12},{24,0},{28,4},{1,25},{... | collective-permute-start | bytes 393224 | tf_op jit(solution)/shard_map/ppermute | solution.py:27
  55.7 6.4 %collective-permute-start.17 = (bf16[128,512]{1,0:T(8,128)(2,1)S(1)}, bf16[128,512]{1,0:T(8,128)(2,1)S(1)}, u32[]{:S(2)}, u32[]{:S(2)}) collective-permute-start(bf16[128,512]{1,0:T(8,128)(2,1)S(1)} %get-tuple-element.43.refs_0_), channel_id=1, source_target_pairs={{0,8},{4,12},{8,0},{12,4},{16,24},{20,28},{24,16},{28,20},{1,9},{5... | collective-permute-start | bytes 393224 | tf_op jit(solution)/shard_map/ppermute | solution.py:27
  57.0 9.6 %collective-permute-start.18 = (bf16[128,512]{1,0:T(8,128)(2,1)S(1)}, bf16[128,512]{1,0:T(8,128)(2,1)S(1)}, u32[]{:S(2)}, u32[]{:S(2)}) collective-permute-start(bf16[128,512]{1,0:T(8,128)(2,1)S(1)} %get-tuple-element.43.refs_0_), channel_id=1, source_target_pairs={{0,16},{4,20},{8,24},{12,28},{16,0},{20,4},{24,8},{28,12},{1,17},{... | collective-permute-start | bytes 393224 | tf_op jit(solution)/shard_map/ppermute | solution.py:27
  67.1 2.2 %collective-permute-start.19 = (bf16[2,320,512]{2,1,0:T(8,128)(2,1)S(1)}, bf16[2,320,512]{2,1,0:T(8,128)(2,1)S(1)}, u32[]{:S(2)}, u32[]{:S(2)}) collective-permute-start(bf16[2,320,512]{2,1,0:T(8,128)(2,1)S(1)} %shard_map.122), channel_id=1, source_target_pairs={{0,4},{4,0},{8,12},{12,8},{16,20},{20,16},{24,28},{28,24},{1,5},{5... | collective-permute-start | bytes 1966088 | tf_op jit(solution)/shard_map/ppermute | solution.py:27
  69.4 9.8 %collective-permute-start.20 = (bf16[320,512]{1,0:T(8,128)(2,1)S(1)}, bf16[320,512]{1,0:T(8,128)(2,1)S(1)}, u32[]{:S(2)}, u32[]{:S(2)}) collective-permute-start(bf16[320,512]{1,0:T(8,128)(2,1)S(1)} %get-tuple-element.48), channel_id=1, source_target_pairs={{0,1},{1,0},{2,3},{3,2},{4,5},{5,4},{6,7},{7,6},{8,9},{9,8},{10,11... | collective-permute-start | bytes 983048 | tf_op jit(solution)/shard_map/ppermute | solution.py:27

commit v3 on v2

v3 whole, which is shorter than its diff:
```python
import functools

import jax
import jax.numpy as jnp
from jax import lax
from jax.experimental import pallas as pl
from jax.experimental.pallas import tpu as pltpu
from jax.sharding import PartitionSpec as P

beta_one = 0.9
beta_two = 0.95
epsilon = 1e-08
learn_rate = 0.001
weight_decay = 0.1
first_step = 3.0
second_step = 4.0

LANES = 128
CORES = 2
f32, bf16 = jnp.float32, jnp.bfloat16
VMEM = 16 * 2**20
DIRECT = 2
LONG = 10**11


def swap(value, axis, bits):
    pairs = [(source, source ^ bits) for source in range(lax.axis_size(axis))]
    return lax.ppermute(value, axis, pairs)


def swap_border(value):
    pairs = []
    for right in range(CORES, lax.axis_size("dp"), CORES):
        pairs += [(right - 1, right), (right, right - 1)]
    return lax.ppermute(value, "dp", pairs)


def adam_update(master, moment, variance, gradient, step_count):
    moment = beta_one * moment + (1.0 - beta_one) * gradient
    variance = beta_two * variance + (1.0 - beta_two) * gradient * gradient
    fix_one = 1.0 / (1.0 - beta_one**step_count)
    fix_two = 1.0 / (1.0 - beta_two**step_count)
    update = moment * fix_one / (jnp.sqrt(variance * fix_two) + epsilon) + weight_decay * master
    return (master - learn_rate * update, moment, variance)


def call(kernel, shapes, *args, scalars=0, flops=0, after=()):
    whole = pl.BlockSpec(memory_space=pltpu.VMEM)
    small = pl.BlockSpec(memory_space=pltpu.SMEM)
    touched = sum(a.size * a.dtype.itemsize for a in args)
    end = len(args)

    def body(*refs):
        kernel(*refs[:end], *refs[end + len(after) :])

    return pl.pallas_call(
        body,
        out_shape=shapes,
        in_specs=[small] * scalars
        + [whole] * (end - scalars)
        + [pl.BlockSpec(memory_space=pl.ANY)] * len(after),
        out_specs=jax.tree.map(lambda _: whole, shapes),
        compiler_params=pltpu.CompilerParams(vmem_limit_bytes=VMEM),
        cost_estimate=pl.CostEstimate(flops=flops, bytes_accessed=touched, transcendentals=0),
    )(*args, *after)


def shape(dims, dtype):
    return jax.ShapeDtypeStruct(dims, dtype)


def blocks_kernel(steps, skip, tokens, *refs):
    outs, sems = refs[skip:-1], refs[-1]
    rank, tensor = lax.axis_index("dp"), lax.axis_index("tensor")
    chip, core = rank // CORES, rank % CORES
    share = tokens.shape[0] // lax.axis_size("tensor")
    copies = []
    for step, out in zip(steps, outs, strict=True):
        depth = out.shape[1] // CORES
        for j in range(out.shape[0] // share):
            row = pl.multiple_of((tensor ^ j) * share, share)
            for i in range(CORES):
                col = pl.multiple_of(((chip ^ step) * CORES + (core ^ i)) * depth, depth)
                copies.append(
                    pltpu.make_async_copy(
                        tokens.at[pl.ds(row, share), pl.ds(col, depth)],
                        out.at[pl.ds(j * share, share), pl.ds(i * depth, depth)],
                        sems.at[len(copies)],
                    )
                )
    for copy in copies:
        copy.start()
    for copy in copies:
        copy.wait()


def token_blocks(tokens, steps, share, depth, after):
    slots = tokens.shape[0]
    outs = [shape((slots if step < DIRECT else share, depth), bf16) for step in steps]
    copies = sum(CORES * (out.shape[0] // share) for out in outs)
    return pl.pallas_call(
        functools.partial(blocks_kernel, steps, len(after)),
        out_shape=outs,
        in_specs=[pl.BlockSpec(memory_space=pl.ANY)] * (1 + len(after)),
        out_specs=[pl.BlockSpec(memory_space=pltpu.VMEM)] * len(outs),
        scratch_shapes=[pltpu.SemaphoreType.DMA((copies,))],
        compiler_params=pltpu.CompilerParams(vmem_limit_bytes=VMEM),
        cost_estimate=pl.CostEstimate(flops=0, bytes_accessed=10**6, transcendentals=0),
    )(tokens, *after)


def first_adam_kernel(*refs):
    windows, (weights, leaving, staying, ends) = refs[:4], refs[4:]
    group = lax.axis_index("group")
    _, half, rows, cols = staying.shape
    per = cols // LANES
    runs = [(ends.at[0], 0, 1), (ends.at[1], 2 * half + 1, 1)]
    runs += [(leaving, (1 - group) * half + 1, half), (staying, group * half + 1, half)]
    for out, start, size in runs:
        for k in range(size):
            for h in range(per):
                at = slice(h * LANES, (h + 1) * LANES)
                picks = pl.ds(h, rows, stride=per) if per > 1 else pl.ds(0, rows)
                values = adam_update(*[w[start + k, picks, :] for w in windows], first_step)
                weights[start + k, :, at] = values[0].astype(bf16)
                for i in range(3):
                    out[i, k, :, at] = values[i].astype(out.dtype)


def first_adam(windows, old_cols, after):
    count, rows = windows[0].shape[0] - 2, windows[0].shape[1]
    short = rows * LANES // old_cols
    tile = shape((3, count // 2, short, old_cols), f32)
    ends = shape((2, 3, 1, short, old_cols), bf16)
    weights = shape((count + 2, short, old_cols), bf16)
    return call(first_adam_kernel, [weights, tile, tile, ends], *windows, after=after)


def live_bounds(offsets, span, rank, other):
    slab = lax.axis_index("tensor") * lax.axis_size("group") + (lax.axis_index("group") ^ other)
    start = rank * span
    return offsets[slab, rank] - start, offsets[slab, rank + 1] - start


def place_of(rows, cols, first):
    place = lax.broadcasted_iota(jnp.int32, (rows, cols), 0) * cols
    return first + place + lax.broadcasted_iota(jnp.int32, (rows, cols), 1)


def patch_weights_kernel(offsets, own, other, mate_own, mate_other, outer, mate_outer, mine, mate):
    rows, cols = own.shape[1:]
    count = own.shape[0] - 2
    span = count * rows * cols
    rank = lax.axis_index("dp")
    first = rank % CORES == 0
    for i, (here, there) in enumerate(((own, mate_own), (other, mate_other))):
        at = slice(i * cols, (i + 1) * cols)
        for out, window, near, far, swapped in (
            (mine, here, there, outer, 0),
            (mate, there, here, mate_outer, 1),
        ):
            low, high = live_bounds(offsets, span, rank ^ swapped, i)
            left_far = first if swapped == 0 else jnp.logical_not(first)
            before = place_of(rows, cols, 0) < low
            after = place_of(rows, cols, span - rows * cols) >= high
            far_end = far[i].astype(f32)
            left = jnp.where(left_far, far_end, near[count + 1].astype(f32))
            right = jnp.where(left_far, near[0].astype(f32), far_end)
            out[0, :, at] = jnp.where(before, left, window[1].astype(f32)).astype(bf16)
            out[1 : count - 1, :, at] = window[2:count]
            out[count - 1, :, at] = jnp.where(after, right, window[count].astype(f32)).astype(bf16)


def patch_states_kernel(offsets, leaving, staying, inner, outer, out_leaving, out_staying):
    _, half, rows, cols = leaving.shape
    span = 2 * half * rows * cols
    low, high = live_bounds(offsets, span, lax.axis_index("dp"), 0)
    first = lax.axis_index("dp") % CORES == 0
    group = lax.axis_index("group")
    for tile, states, out in ((1 - group, leaving, out_leaving), (group, staying, out_staying)):
        before = place_of(rows, cols, tile * (span // 2)) < low
        after = place_of(rows, cols, tile * (span // 2) + (half - 1) * rows * cols) >= high
        for i in range(3):
            near, far = inner[i].astype(f32), outer[i].astype(f32)
            left, right = jnp.where(first, far, near), jnp.where(first, near, far)
            out[i, 0] = jnp.where(before, left, states[i, 0]).astype(out.dtype)
            out[i, 1 : half - 1] = states[i, 1 : half - 1].astype(out.dtype)
            out[i, half - 1] = jnp.where(after, right, states[i, half - 1]).astype(out.dtype)


def part_kernel(pieces, *refs):
    mine, mate, out = refs[pieces:]
    rows = jnp.concatenate([r[...] for r in refs[:pieces]], axis=0)
    depth = mine.shape[0]
    value = jnp.dot(rows[:, :depth], mine[...], preferred_element_type=f32)
    value = value + jnp.dot(rows[:, depth:], mate[...], preferred_element_type=f32)
    out[...] = value.astype(out.dtype)


def part(pieces, weights, dtype, flops=0, after=()):
    rows = sum(p.shape[0] for p in pieces)
    cols = weights[0].shape[1]
    return call(
        functools.partial(part_kernel, len(pieces)),
        shape((rows, cols), dtype),
        *pieces,
        *weights,
        flops=flops or 2 * rows * pieces[0].shape[1] * cols,
        after=after,
    )


def own_order(rows, cols):
    tensors, groups = lax.axis_size("tensor"), lax.axis_size("group")
    share, wide = rows // tensors, cols // groups
    for j in range(tensors):
        row = pl.multiple_of((lax.axis_index("tensor") ^ j) * share, share)
        for i in range(groups):
            col = pl.multiple_of((lax.axis_index("group") ^ i) * wide, wide)
            here = (slice(j * share, (j + 1) * share), slice(i * wide, (i + 1) * wide))
            yield here, (pl.ds(row, share), pl.ds(col, wide)), row


def live_kernel(counts, cotangent, out):
    live = counts[lax.axis_index("dp") * lax.axis_size("group") + lax.axis_index("group")]
    for here, there, first_row in own_order(*cotangent.shape):
        value = cotangent[there].astype(f32)
        row = first_row + lax.broadcasted_iota(jnp.int32, value.shape, 0)
        out[here] = jnp.where(row < live, value, 0.0).astype(bf16)


def delta_kernel(*refs):
    own, (cotangent, activated, delta) = refs[0], refs[-3:]
    preact = own[...]
    for r in refs[1:-3]:
        preact = preact + r[...].astype(f32)
    sigmoid = 1.0 / (1.0 + jnp.exp(-preact))
    activated[...] = (preact * sigmoid).astype(bf16)
    derivative = sigmoid * (1.0 + preact * (1.0 - sigmoid))
    delta[...] = (cotangent[...].astype(f32) * derivative).astype(bf16)


def natural_kernel(value, out):
    for here, there, _ in own_order(*value.shape):
        out[there] = value[here]


def place_kernel(value, out):
    out[...] = value[...]


def zero_kernel(out):
    out[...] = jnp.zeros(out.shape, out.dtype)


def gather_kernel(*refs):
    start = 0
    for r in refs[:-1]:
        refs[-1][start : start + r.shape[0]] = r[...]
        start += r.shape[0]


def gradient_kernel(second, tokens, *refs):
    deltas, out = refs[:-1], refs[-1]
    depth = tokens.shape[1] // CORES
    value = lax.dot_general(
        tokens[:, depth * second : depth * (second + 1)],
        jnp.concatenate([r[...] for r in deltas], axis=0),
        (((0,), (0,)), ((), ())),
        preferred_element_type=f32,
    ).astype(out.dtype)
    tile = out.shape[1]
    for i in range(out.shape[0]):
        out[i] = value[i * tile : (i + 1) * tile]


def core_sum_kernel(mine, received, keep, send):
    group = lax.axis_index("group")
    cols = keep.shape[1] // 2
    keep[...] = mine[group] + received[group].astype(f32)
    value = (mine[1 - group] + received[1 - group].astype(f32)).astype(bf16)
    send[:, :cols] = value[:, cols:]
    send[:, cols:] = value[:, :cols]


def second_adam_kernel(staying, incoming, keep, back, master, moment, variance):
    _, half, rows, cols = staying.shape
    group = lax.axis_index("group")
    for k in range(half):
        for i, states in enumerate((staying, incoming)):
            here = (slice(k * rows, (k + 1) * rows), slice(i * cols, (i + 1) * cols))
            there = pl.ds(pl.multiple_of((group ^ i) * cols, cols), cols)
            gradient = keep[here] + back[here].astype(f32)
            values = [states[j, k].astype(f32) for j in range(3)]
            result = adam_update(*values, gradient, second_step)
            for ref, value in zip((master, moment, variance), result, strict=True):
                ref[k * rows : (k + 1) * rows, there] = value


def local(tokens, cotangent, counts, old_offsets, old_master, old_moment, old_variance, old_grad):
    ranks = lax.axis_size("dp")
    chips = ranks // CORES
    groups = lax.axis_size("group")
    tensors = lax.axis_size("tensor")
    rank = lax.axis_index("dp")
    chip, core = rank // CORES, rank % CORES
    tensor = lax.axis_index("tensor")
    slots, width = tokens.shape
    cols = cotangent.shape[1]
    old_cols = cols // groups
    depth = width // chips
    half = depth // CORES
    share = slots // tensors

    length = old_master.shape[2]
    margin = length // 10
    windows = [
        w.reshape(10, margin // LANES, LANES)
        for w in (old_master, old_moment, old_variance, old_grad)
    ]
    ahead = call(zero_kernel, shape((8, LANES), f32), flops=LONG)
    window, leaving, staying, ends = first_adam(windows, old_cols, [ahead])

    def token_block(of_chip, of_tensor):
        return jnp.concatenate(
            [
                lax.dynamic_slice(
                    tokens, (of_tensor * share, of_chip * depth + (core ^ i) * half), (share, half)
                )
                for i in range(CORES)
            ],
            axis=1,
        )

    def blocks_of(steps, after):
        if half % LANES == 0 and share % 16 == 0:
            return token_blocks(tokens, steps, share, depth, after)
        return [
            jnp.concatenate(
                [
                    token_block(chip ^ step, tensor ^ j)
                    for j in range(tensors if step < DIRECT else 1)
                ]
            )
            for step in steps
        ]

    leaving_blocks = blocks_of(range(1, chips), [])

    cleared = call(place_kernel, shape(window.shape[1:], bf16), window[0], flops=LONG)
    other = swap(window, "group", 1)
    arrived = [swap(b, "dp", step * CORES) for step, b in enumerate(leaving_blocks, 1)]
    arrived = [lax.optimization_barrier((a, cleared))[0] for a in arrived]

    ends = jnp.concatenate([ends[:, :, 0], jnp.stack([other[0], other[-1]])[:, None]], axis=1)
    inner = swap(jnp.where(core == 0, ends[1], ends[0]), "dp", 1)
    outer = swap_border(jnp.where(core == 0, ends[0], ends[1]))

    turned = call(
        live_kernel, shape((slots, cols), bf16), counts, cotangent, scalars=1, after=[other]
    )
    blocks = [[b] for b in [*blocks_of(range(1), [other]), *arrived]]
    for block in blocks[DIRECT:]:
        block += [swap(block[0], "tensor", j) for j in range(1, tensors)]

    far, _ = lax.optimization_barrier((jnp.stack([outer[0], outer[3]]), blocks[DIRECT]))
    leaving, far = lax.optimization_barrier((leaving, far))
    leaving, staying = call(
        patch_states_kernel,
        [shape(leaving.shape, bf16), shape(leaving.shape, f32)],
        old_offsets,
        leaving,
        staying,
        inner,
        outer,
        scalars=1,
    )
    incoming = swap(leaving, "group", 1)

    count, rows = window.shape[0] - 2, window.shape[1]
    mates = [swap(w, "dp", 1) for w in (window, other, far)]
    window, *_ = lax.optimization_barrier((window, leaving, *blocks[-1]))
    weights = call(
        patch_weights_kernel,
        [shape((count, rows, cols), bf16)] * 2,
        old_offsets,
        window,
        other,
        *mates[:2],
        far,
        mates[2],
        scalars=1,
    )
    weights = [w.reshape(half, cols) for w in weights]

    steps = range(chips - 1, 0, -1)
    parts = []
    for step in steps:
        parts.append(part(blocks[step], weights, bf16, after=parts[-1:]))
    back = [swap(p, "dp", step * CORES) for step, p in zip(steps, parts, strict=True)]

    own_block, *_ = lax.optimization_barrier((blocks[0][0], *parts))
    total = part([own_block], weights, f32, LONG)
    total, incoming = lax.optimization_barrier((total, incoming))
    activated, delta = call(
        delta_kernel, [shape((slots, cols), bf16)] * 2, total, *back, turned
    )

    deltas = [delta] + [swap(delta, "dp", step * CORES) for step in steps]

    flat = [p for step in (0, *steps) for p in blocks[step]]
    flat[0], _ = lax.optimization_barrier((flat[0], delta))
    gathered = call(gather_kernel, shape((chips * slots, depth), bf16), *flat, flops=LONG)
    flops = 2 * half * cols * chips * slots
    tile = half // groups
    to_mate, mine = (
        call(
            functools.partial(gradient_kernel, second),
            shape((groups, tile, cols), dtype),
            gathered,
            *deltas,
            flops=flops,
        )
        for second, dtype in ((1, bf16), (0, f32))
    )
    keep, send = call(
        core_sum_kernel,
        [shape((tile, cols), f32), shape((tile, cols), bf16)],
        mine,
        swap(to_mate, "dp", 1),
    )
    new = call(
        second_adam_kernel,
        [shape((tile, cols), f32)] * 3,
        staying,
        incoming,
        keep,
        swap(send, "group", 1),
    )
    activated = call(natural_kernel, shape((slots, cols), bf16), activated)
    return (activated, *new)


def solution(mesh):
    rows = P(("dp", "group"), "tensor")
    window = P(("tensor", "group"), "dp", None)
    return jax.shard_map(
        local,
        mesh=mesh,
        in_specs=(P(("dp", "group"), None), rows, P(), P(), window, window, window, window),
        out_specs=(rows, rows, rows, rows),
        check_vma=False,
    )
```

time: 81.2 us -> 78.6 us (0.968)
  waiting for transfers between devices: 39 us -> 33.7 us
  local copies, waits for them, and re-layouts: 1.64 us -> 3.54 us
  starting transfers between devices: 27.4 us -> 25.8 us
  Pallas kernels: 11.9 us -> 13.4 us
  other arithmetic: 0.07 us -> 1.08 us
    ppermute x19, waiting for transfers between devices: 39 us -> 33.7 us  [swap(): return lax.ppermute(value, axis, pairs)]
    unnamed x24 -> x22, local copies, waits for them, and re-layouts: 1.51 us -> 3.53 us
    pallas_call x14 -> x18, Pallas kernels: 11.9 us -> 13.4 us  [the longest x16 12.2 us: call(): pl.pallas_call(body, out_shape=shapes, in_specs=[small] * scalars + [whol...]
    ppermute x19, starting transfers between devices: 26 us -> 25 us  [swap(): return lax.ppermute(value, axis, pairs)]
    select_n x2 -> x1, other arithmetic: 0.07 us -> 1.06 us  [local(): inner = swap(jnp.where(core == 0, ends[1], ends[0]), 'dp', 1)]
  transfers between devices with their start and end apart: 21 -> 20, of which waited for: 12 -> 10; matrix products, arithmetic and copies ran while one was open for 0% -> 1% of each run, Pallas kernels for 5% -> 13%
where the time goes in v3:
time: 78.6 us; the launch traced here: 78.3 us
  waiting for transfers between devices  33.7 us (43%)
  starting transfers between devices  25.8 us (33%)
  Pallas kernels  13.4 us (17%)
  local copies, waits for them, and re-layouts  3.54 us (5%)
  other arithmetic  1.08 us (1%)
  between operations  0.9 us (1%)
    ppermute x19, waiting for transfers between devices, swap(): return lax.ppermute(value, axis, pairs)  33.7 us
    ppermute x19, starting transfers between devices, swap(): return lax.ppermute(value, axis, pairs)  25 us
    pallas_call x16, Pallas kernels, call(): pl.pallas_call(body, out_shape=shapes, in_specs=[small] * scalars + [whol...  12.2 us
    unnamed x22, local copies, waits for them, and re-layouts  3.53 us
  transfers between devices with their start and end apart: 20, of which 10 were waited for; matrix products, arithmetic and copies ran while one was open for 1% of the time, Pallas kernels for 13%

profile of v3, /device:TPU:0, one launch (start us, length us, event | category | flops | bytes accessed | tf_op | source)
XLA Modules:
  0.0 78.3 jit_solution(11990422833633775812)
XLA Ops:
  0.7 1.1 %copy-done.3 = f32[1,1,204800]{2,1,0:T(1,128)S(1)} copy-done((f32[1,1,204800]{2,1,0:T(1,128)S(1)}, f32[1,1,204800]{2,1,0:T(1,128)}, u32[]{:S(2)}) %copy-start.3) | copy-done | bytes 819224
  2.5 0.8 %shard_map.112 = (bf16[10,80,256]{2,1,0:T(8,128)(2,1)S(1)}, f32[3,4,80,256]{3,2,1,0:T(8,128)S(1)}, f32[3,4,80,256]{3,2,1,0:T(8,128)S(1)}, bf16[2,3,1,80,256]{4,3,2,1,0:T(8,128)(2,1)S(1)}) custom-call(f32[10,160,128]{2,1,0:T(8,128)S(1)} %bitcast.25, f32[10,160,128]{2,1,0:T(8,128)S(1)} %bitcast.26, f32[10,160,128]{2,1,0:T(8,128)S(1)} %bitcast.27, ...), custom_call_target="tpu_custom_call" | custom-call | bytes 3276800 | tf_op jit(solution)/shard_map/pallas_call | solution.py:56
  3.3 1.0 %copy-done.1 = f32[3,4,80,256]{3,2,1,0:T(8,128)} copy-done((f32[3,4,80,256]{3,2,1,0:T(8,128)}, f32[3,4,80,256]{3,2,1,0:T(8,128)S(1)}, u32[]{:S(2)}) %copy-start.1) | copy-done | bytes 983064
  5.0 3.0 %collective-permute-start = (bf16[10,80,256]{2,1,0:T(8,128)(2,1)S(1)}, bf16[10,80,256]{2,1,0:T(8,128)(2,1)S(1)}, u32[]{:S(2)}, u32[]{:S(2)}) collective-permute-start(bf16[10,80,256]{2,1,0:T(8,128)(2,1)S(1)} %get-tuple-element.44.refs_1_), channel_id=1, source_target_pairs={{0,1},{1,0},{2,3},{3,2},{4,5},{5,4},{6,7},{7,6},{8,9},{9,8},{10,11... | collective-permute-start | bytes 1228808 | tf_op jit(solution)/shard_map/ppermute | solution.py:28
  8.0 1.0 %shard_map.114 = (bf16[128,1280]{1,0:T(8,128)(2,1)}, bf16[64,1280]{1,0:T(8,128)(2,1)}, bf16[64,1280]{1,0:T(8,128)(2,1)}) custom-call(bf16[128,5120]{1,0:T(8,128)(2,1)S(1)} %copy-done), custom_call_target="tpu_custom_call" | custom-call | bytes 1000000 | tf_op jit(solution)/shard_map/pallas_call | solution.py:101
  9.0 2.7 %collective-permute-start.4 = (bf16[64,1280]{1,0:T(8,128)(2,1)}, bf16[64,1280]{1,0:T(8,128)(2,1)}, u32[]{:S(2)}, u32[]{:S(2)}) collective-permute-start(bf16[64,1280]{1,0:T(8,128)(2,1)} %get-tuple-element.38), channel_id=1, source_target_pairs={{0,16},{4,20},{8,24},{12,28},{16,0},{20,4},{24,8},{28,12},{1,17},{... | collective-permute-start | bytes 491528 | tf_op jit(solution)/shard_map/ppermute | solution.py:28
  11.7 1.3 %collective-permute-start.1 = (bf16[64,1280]{1,0:T(8,128)(2,1)}, bf16[64,1280]{1,0:T(8,128)(2,1)}, u32[]{:S(2)}, u32[]{:S(2)}) collective-permute-start(bf16[64,1280]{1,0:T(8,128)(2,1)} %get-tuple-element.34), channel_id=1, source_target_pairs={{0,24},{4,28},{8,16},{12,20},{16,8},{20,12},{24,0},{28,4},{1,25},{... | collective-permute-start | bytes 491528 | tf_op jit(solution)/shard_map/ppermute | solution.py:28
  13.2 4.2 %collective-permute-done.refs_0_.refs_2_ = bf16[10,80,256]{2,1,0:T(8,128)(2,1)S(1)} collective-permute-done((bf16[10,80,256]{2,1,0:T(8,128)(2,1)S(1)}, bf16[10,80,256]{2,1,0:T(8,128)(2,1)S(1)}, u32[]{:S(2)}, u32[]{:S(2)}) %collective-permute-start) | collective-permute-done | bytes 409632 | tf_op jit(solution)/shard_map/ppermute | solution.py:28
  17.4 1.1 %select_bitcast_fusion = (bf16[4,80,256]{2,1,0:T(8,128)(2,1)S(1)}, bf16[4,80,256]{2,1,0:T(8,128)(2,1)S(1)}) fusion(pred[]{:T(512)S(6)} %eq.6, bf16[2,1,80,256]{3,2,1,0:T(8,128)(2,1)S(1)} %maximum_bitcast_fusion, bf16[2,3,80,256]{3,2,1,0:T(8,128)(2,1)} %bitcast.29), kind=kLoop, calls=%fused_computation.4 | loop fusion | flops 409600 | bytes 655361 | tf_op jit(solution)/shard_map/jit(_where)/select_n | solution.py:356
  18.5 0.8 %collective-permute-start.3 = (bf16[4,80,256]{2,1,0:T(8,128)(2,1)S(1)}, bf16[4,80,256]{2,1,0:T(8,128)(2,1)S(1)}, u32[]{:S(2)}, u32[]{:S(2)}) collective-permute-start(bf16[4,80,256]{2,1,0:T(8,128)(2,1)S(1)} %get-tuple-element.65), channel_id=1, source_target_pairs={{4,8},{8,4},{12,16},{16,12},{20,24},{24,20},{5,9},{9,5},{13,17},{1... | collective-permute-start | bytes 491528 | tf_op jit(solution)/shard_map/ppermute | solution.py:35
  19.3 5.0 %collective-permute-done.4.refs_0_.refs_3_ = bf16[64,1280]{1,0:T(8,128)(2,1)} collective-permute-done((bf16[64,1280]{1,0:T(8,128)(2,1)}, bf16[64,1280]{1,0:T(8,128)(2,1)}, u32[]{:S(2)}, u32[]{:S(2)}) %collective-permute-start.4) | collective-permute-done | bytes 163872 | tf_op jit(solution)/shard_map/ppermute | solution.py:28
  24.3 1.5 %collective-permute-start.5 = (bf16[64,1280]{1,0:T(8,128)(2,1)}, bf16[64,1280]{1,0:T(8,128)(2,1)S(1)}, u32[]{:S(2)}, u32[]{:S(2)}) collective-permute-start(bf16[64,1280]{1,0:T(8,128)(2,1)} %collective-permute-done.4.refs_0_.refs_3_), channel_id=1, source_target_pairs={{0,2},{2,0},{1,3},{3,1},{4,6},{6,4},{5,7},{7,5},{8,10},{10,8},{9,1... | collective-permute-start | bytes 491528 | tf_op jit(solution)/shard_map/ppermute | solution.py:28
  26.4 4.2 %collective-permute-start.8 = (bf16[10,80,256]{2,1,0:T(8,128)(2,1)S(1)}, bf16[10,80,256]{2,1,0:T(8,128)(2,1)S(1)}, u32[]{:S(2)}, u32[]{:S(2)}) collective-permute-start(bf16[10,80,256]{2,1,0:T(8,128)(2,1)S(1)} %collective-permute-done.refs_0_.refs_2_), channel_id=1, source_target_pairs={{0,4},{4,0},{8,12},{12,8},{16,20},{20,16},{24,28},{28,24},{1,5},{5... | collective-permute-start | bytes 1228808 | tf_op jit(solution)/shard_map/ppermute | solution.py:28
  30.6 1.1 %collective-permute-done.5.refs_1_.refs_4_ = bf16[64,1280]{1,0:T(8,128)(2,1)S(1)} collective-permute-done((bf16[64,1280]{1,0:T(8,128)(2,1)}, bf16[64,1280]{1,0:T(8,128)(2,1)S(1)}, u32[]{:S(2)}, u32[]{:S(2)}) %collective-permute-start.5) | collective-permute-done | bytes 163872 | tf_op jit(solution)/shard_map/ppermute | solution.py:28
  33.1 0.8 %shard_map.115 = (bf16[3,4,80,256]{3,2,1,0:T(8,128)(2,1)S(1)}, f32[3,4,80,256]{3,2,1,0:T(8,128)S(1)}) custom-call(s32[4,9]{1,0:T(4,128)S(1)} %copy-done.9, f32[3,4,80,256]{3,2,1,0:T(8,128)S(1)} %get-tuple-element.41.refs_1_, f32[3,4,80,256]{3,2,1,0:T(8,128)S(1)} %copy-done.2, bf16[4,80,256]{2,1,0:T(8,128)(2,1)S(1)} %collective-permute-done.6.refs_3_, ...), custom_call_target="tpu_custom_call" | custom-call | bytes 2293904 | tf_op jit(solution)/shard_map/pallas_call | solution.py:56
  34.2 0.8 shard_map.116
  35.0 1.3 %shard_map.117.refs_4_ = bf16[128,512]{1,0:T(8,128)(2,1)S(1)} custom-call(bf16[64,1280]{1,0:T(8,128)(2,1)} %collective-permute-done.1.refs_0_.refs_1_, bf16[64,1280]{1,0:T(8,128)(2,1)S(1)} %collective-permute-done.2.refs_1_.refs_2_, bf16[640,512]{1,0:T(8,128)(2,1)S(1)} %bitcast.17, bf16[640,512]{1,0:T(8,128)(2,1)S(1)} %bitcast.21), custom_call_target="tpu_custom_call" | custom-call | flops 167772160 | bytes 1638400 | tf_op jit(solution)/shard_map/pallas_call | solution.py:56
  36.2 3.5 %collective-permute-start.12 = (bf16[128,512]{1,0:T(8,128)(2,1)S(1)}, bf16[128,512]{1,0:T(8,128)(2,1)S(1)}, u32[]{:S(2)}, u32[]{:S(2)}) collective-permute-start(bf16[128,512]{1,0:T(8,128)(2,1)S(1)} %shard_map.117.refs_4_), channel_id=1, source_target_pairs={{0,24},{4,28},{8,16},{12,20},{16,8},{20,12},{24,0},{28,4},{1,25},{... | collective-permute-start | bytes 393224 | tf_op jit(solution)/shard_map/ppermute | solution.py:28
  39.7 1.3 %shard_map.118.refs_3_ = bf16[128,512]{1,0:T(8,128)(2,1)S(1)} custom-call(bf16[64,1280]{1,0:T(8,128)(2,1)} %collective-permute-done.4.refs_0_.refs_3_, bf16[64,1280]{1,0:T(8,128)(2,1)S(1)} %collective-permute-done.5.refs_1_.refs_4_, bf16[640,512]{1,0:T(8,128)(2,1)S(1)} %bitcast.18, bf16[640,512]{1,0:T(8,128)(2,1)S(1)} %bitcast.22, ...), custom_call_target="tpu_custom_call" | custom-call | flops 167772160 | bytes 1638400 | tf_op jit(solution)/shard_map/pallas_call | solution.py:56
  41.1 1.3 %shard_map.119 = bf16[128,512]{1,0:T(8,128)(2,1)S(1)} custom-call(bf16[128,1280]{1,0:T(8,128)(2,1)} %collective-permute-done.10.refs_0_.refs_5_, bf16[640,512]{1,0:T(8,128)(2,1)S(1)} %bitcast.19, bf16[640,512]{1,0:T(8,128)(2,1)S(1)} %bitcast.23, bf16[128,512]{1,0:T(8,128)(2,1)S(1)} %shard_map.118.refs_3_), custom_call_target="tpu_custom_call" | custom-call | flops 167772160 | bytes 1638400 | tf_op jit(solution)/shard_map/pallas_call | solution.py:56
  42.4 1.1 %collective-permute-start.14 = (bf16[128,512]{1,0:T(8,128)(2,1)S(1)}, bf16[128,512]{1,0:T(8,128)(2,1)S(1)}, u32[]{:S(2)}, u32[]{:S(2)}) collective-permute-start(bf16[128,512]{1,0:T(8,128)(2,1)S(1)} %shard_map.119), channel_id=1, source_target_pairs={{0,8},{4,12},{8,0},{12,4},{16,24},{20,28},{24,16},{28,20},{1,9},{5... | collective-permute-start | bytes 393224 | tf_op jit(solution)/shard_map/ppermute | solution.py:28
  43.8 3.6 %collective-permute-done.11.refs_1_ = bf16[3,4,80,256]{3,2,1,0:T(8,128)(2,1)S(1)} collective-permute-done((bf16[3,4,80,256]{3,2,1,0:T(8,128)(2,1)S(1)}, bf16[3,4,80,256]{3,2,1,0:T(8,128)(2,1)S(1)}, u32[]{:S(2)}, u32[]{:S(2)}) %collective-permute-start.11) | collective-permute-done | bytes 491552 | tf_op jit(solution)/shard_map/ppermute | solution.py:28
  47.4 3.0 %collective-permute-done.14.refs_3_ = bf16[128,512]{1,0:T(8,128)(2,1)S(1)} collective-permute-done((bf16[128,512]{1,0:T(8,128)(2,1)S(1)}, bf16[128,512]{1,0:T(8,128)(2,1)S(1)}, u32[]{:S(2)}, u32[]{:S(2)}) %collective-permute-start.14) | collective-permute-done | bytes 131104 | tf_op jit(solution)/shard_map/ppermute | solution.py:28
  50.6 2.8 %collective-permute-start.15 = (bf16[128,512]{1,0:T(8,128)(2,1)S(1)}, bf16[128,512]{1,0:T(8,128)(2,1)S(1)}, u32[]{:S(2)}, u32[]{:S(2)}) collective-permute-start(bf16[128,512]{1,0:T(8,128)(2,1)S(1)} %get-tuple-element.55.refs_1_), channel_id=1, source_target_pairs={{0,24},{4,28},{8,16},{12,20},{16,8},{20,12},{24,0},{28,4},{1,25},{... | collective-permute-start | bytes 393224 | tf_op jit(solution)/shard_map/ppermute | solution.py:28
  53.4 1.6 %collective-permute-start.17 = (bf16[128,512]{1,0:T(8,128)(2,1)S(1)}, bf16[128,512]{1,0:T(8,128)(2,1)S(1)}, u32[]{:S(2)}, u32[]{:S(2)}) collective-permute-start(bf16[128,512]{1,0:T(8,128)(2,1)S(1)} %get-tuple-element.55.refs_1_), channel_id=1, source_target_pairs={{0,8},{4,12},{8,0},{12,4},{16,24},{20,28},{24,16},{28,20},{1,9},{5... | collective-permute-start | bytes 393224 | tf_op jit(solution)/shard_map/ppermute | solution.py:28
  55.1 1.2 %shard_map.124.refs_0_ = bf16[512,1280]{1,0:T(8,128)(2,1)S(1)} custom-call(bf16[128,1280]{1,0:T(8,128)(2,1)S(1)} %shard_map.113.refs_0_, bf16[64,1280]{1,0:T(8,128)(2,1)} %collective-permute-done.1.refs_0_.refs_1_, bf16[64,1280]{1,0:T(8,128)(2,1)S(1)} %collective-permute-done.2.refs_1_.refs_2_, bf16[64,1280]{1,0:T(8,128)(2,1)} %collective-permute-done.4.refs_0_.refs_3_, ...), custom_call_target="tpu_custom_call" | custom-call | flops 99999997952 | bytes 1310720 | tf_op jit(solution)/shard_map/pallas_call | solution.py:56
  56.3 2.6 %collective-permute-done.15.refs_2_ = bf16[128,512]{1,0:T(8,128)(2,1)S(1)} collective-permute-done((bf16[128,512]{1,0:T(8,128)(2,1)S(1)}, bf16[128,512]{1,0:T(8,128)(2,1)S(1)}, u32[]{:S(2)}, u32[]{:S(2)}) %collective-permute-start.15) | collective-permute-done | bytes 131104 | tf_op jit(solution)/shard_map/ppermute | solution.py:28
  58.9 5.0 %collective-permute-done.16.refs_3_ = bf16[128,512]{1,0:T(8,128)(2,1)S(1)} collective-permute-done((bf16[128,512]{1,0:T(8,128)(2,1)S(1)}, bf16[128,512]{1,0:T(8,128)(2,1)S(1)}, u32[]{:S(2)}, u32[]{:S(2)}) %collective-permute-start.16) | collective-permute-done | bytes 131104 | tf_op jit(solution)/shard_map/ppermute | solution.py:28
  65.0 1.5 %collective-permute-done.18.refs_1_ = bf16[2,320,512]{2,1,0:T(8,128)(2,1)S(1)} collective-permute-done((bf16[2,320,512]{2,1,0:T(8,128)(2,1)S(1)}, bf16[2,320,512]{2,1,0:T(8,128)(2,1)S(1)}, u32[]{:S(2)}, u32[]{:S(2)}) %collective-permute-start.18) | collective-permute-done | bytes 655392 | tf_op jit(solution)/shard_map/ppermute | solution.py:28
  66.7 1.6 %collective-permute-start.19 = (bf16[320,512]{1,0:T(8,128)(2,1)S(1)}, bf16[320,512]{1,0:T(8,128)(2,1)S(1)}, u32[]{:S(2)}, u32[]{:S(2)}) collective-permute-start(bf16[320,512]{1,0:T(8,128)(2,1)S(1)} %get-tuple-element.58), channel_id=1, source_target_pairs={{0,1},{1,0},{2,3},{3,2},{4,5},{5,4},{6,7},{7,6},{8,9},{9,8},{10,11... | collective-permute-start | bytes 983048 | tf_op jit(solution)/shard_map/ppermute | solution.py:28
  69.0 7.6 %collective-permute-done.19.refs_3_ = bf16[320,512]{1,0:T(8,128)(2,1)S(1)} collective-permute-done((bf16[320,512]{1,0:T(8,128)(2,1)S(1)}, bf16[320,512]{1,0:T(8,128)(2,1)S(1)}, u32[]{:S(2)}, u32[]{:S(2)}) %collective-permute-start.19) | collective-permute-done | bytes 327712 | tf_op jit(solution)/shard_map/ppermute | solution.py:28
  76.5 1.8 %shard_map.128 = (f32[320,512]{1,0:T(8,128)}, f32[320,512]{1,0:T(8,128)}, f32[320,512]{1,0:T(8,128)}) custom-call(f32[3,4,80,256]{3,2,1,0:T(8,128)S(1)} %get-tuple-element.53.refs_0_, bf16[3,4,80,256]{3,2,1,0:T(8,128)(2,1)S(1)} %collective-permute-done.11.refs_1_, f32[320,512]{1,0:T(8,128)S(1)} %get-tuple-element.57.refs_2_, ...), custom_call_target="tpu_custom_call" | custom-call | bytes 2457600 | tf_op jit(solution)/shard_map/pallas_call | solution.py:56
  (53 shorter events, 6.4 us)
Async XLA Ops:
  0.6 1.1 %copy-start.3 = (f32[1,1,204800]{2,1,0:T(1,128)S(1)}, f32[1,1,204800]{2,1,0:T(1,128)}, u32[]{:S(2)}) copy-start(f32[1,1,204800]{2,1,0:T(1,128)} %param.12) | copy-start | bytes 2457604
  0.6 1.4 %copy-start.4 = (f32[1,1,204800]{2,1,0:T(1,128)S(1)}, f32[1,1,204800]{2,1,0:T(1,128)}, u32[]{:S(2)}) copy-start(f32[1,1,204800]{2,1,0:T(1,128)} %param.13) | copy-start | bytes 2457604
  0.7 1.6 %copy-start.5 = (f32[1,1,204800]{2,1,0:T(1,128)S(1)}, f32[1,1,204800]{2,1,0:T(1,128)}, u32[]{:S(2)}) copy-start(f32[1,1,204800]{2,1,0:T(1,128)} %param.14) | copy-start | bytes 2457604
  0.7 1.9 %copy-start.6 = (f32[1,1,204800]{2,1,0:T(1,128)S(1)}, f32[1,1,204800]{2,1,0:T(1,128)}, u32[]{:S(2)}) copy-start(f32[1,1,204800]{2,1,0:T(1,128)} %param.15) | copy-start | bytes 2457604
  2.5 5.4 %copy-start = (bf16[128,5120]{1,0:T(8,128)(2,1)S(1)}, bf16[128,5120]{1,0:T(8,128)(2,1)}, u32[]{:S(2)}) copy-start(bf16[128,5120]{1,0:T(8,128)(2,1)} %tokens.3) | copy-start | bytes 3932164
  3.3 1.0 %copy-start.1 = (f32[3,4,80,256]{3,2,1,0:T(8,128)}, f32[3,4,80,256]{3,2,1,0:T(8,128)S(1)}, u32[]{:S(2)}) copy-start(f32[3,4,80,256]{3,2,1,0:T(8,128)S(1)} %get-tuple-element.42.refs_2_) | copy-start | bytes 2949124
  4.3 0.7 copy-start.7
  5.0 12.4 %collective-permute-start = (bf16[10,80,256]{2,1,0:T(8,128)(2,1)S(1)}, bf16[10,80,256]{2,1,0:T(8,128)(2,1)S(1)}, u32[]{:S(2)}, u32[]{:S(2)}) collective-permute-start(bf16[10,80,256]{2,1,0:T(8,128)(2,1)S(1)} %get-tuple-element.44.refs_1_), channel_id=1, source_target_pairs={{0,1},{1,0},{2,3},{3,2},{4,5},{5,4},{6,7},{7,6},{8,9},{9,8},{10,11... | collective-permute-start | bytes 1228808 | tf_op jit(solution)/shard_map/ppermute | solution.py:28
  8.0 26.2 %collective-permute-start.7 = (bf16[10,80,256]{2,1,0:T(8,128)(2,1)S(1)}, bf16[10,80,256]{2,1,0:T(8,128)(2,1)S(1)}, u32[]{:S(2)}, u32[]{:S(2)}) collective-permute-start(bf16[10,80,256]{2,1,0:T(8,128)(2,1)S(1)} %get-tuple-element.44.refs_1_), channel_id=1, source_target_pairs={{0,4},{4,0},{8,12},{12,8},{16,20},{20,16},{24,28},{28,24},{1,5},{5... | collective-permute-start | bytes 1228808 | tf_op jit(solution)/shard_map/ppermute | solution.py:28
  9.0 15.3 %collective-permute-start.4 = (bf16[64,1280]{1,0:T(8,128)(2,1)}, bf16[64,1280]{1,0:T(8,128)(2,1)}, u32[]{:S(2)}, u32[]{:S(2)}) collective-permute-start(bf16[64,1280]{1,0:T(8,128)(2,1)} %get-tuple-element.38), channel_id=1, source_target_pairs={{0,16},{4,20},{8,24},{12,28},{16,0},{20,4},{24,8},{28,12},{1,17},{... | collective-permute-start | bytes 491528 | tf_op jit(solution)/shard_map/ppermute | solution.py:28
  11.7 14.2 %collective-permute-start.1 = (bf16[64,1280]{1,0:T(8,128)(2,1)}, bf16[64,1280]{1,0:T(8,128)(2,1)}, u32[]{:S(2)}, u32[]{:S(2)}) collective-permute-start(bf16[64,1280]{1,0:T(8,128)(2,1)} %get-tuple-element.34), channel_id=1, source_target_pairs={{0,24},{4,28},{8,16},{12,20},{16,8},{20,12},{24,0},{28,4},{1,25},{... | collective-permute-start | bytes 491528 | tf_op jit(solution)/shard_map/ppermute | solution.py:28
  13.0 18.7 %collective-permute-start.10 = (bf16[128,1280]{1,0:T(8,128)(2,1)}, bf16[128,1280]{1,0:T(8,128)(2,1)}, u32[]{:S(2)}, u32[]{:S(2)}) collective-permute-start(bf16[128,1280]{1,0:T(8,128)(2,1)} %get-tuple-element.48), channel_id=1, source_target_pairs={{0,8},{4,12},{8,0},{12,4},{16,24},{20,28},{24,16},{28,20},{1,9},{5... | collective-permute-start | bytes 983048 | tf_op jit(solution)/shard_map/ppermute | solution.py:28
  18.5 13.9 %copy-start.8 = (bf16[128,512]{1,0:T(8,128)(2,1)S(1)}, bf16[128,512]{1,0:T(8,128)(2,1)}, u32[]{:S(2)}) copy-start(bf16[128,512]{1,0:T(8,128)(2,1)} %refs_1_.1) | copy-start | bytes 393220
  18.5 13.9 %copy-start.10 = (s32[16]{0:T(128)S(1)}, s32[16]{0:T(128)}, u32[]{:S(2)}) copy-start(s32[16]{0:T(128)} %refs_0_.5) | copy-start | bytes 196
  18.5 7.8 %collective-permute-start.3 = (bf16[4,80,256]{2,1,0:T(8,128)(2,1)S(1)}, bf16[4,80,256]{2,1,0:T(8,128)(2,1)S(1)}, u32[]{:S(2)}, u32[]{:S(2)}) collective-permute-start(bf16[4,80,256]{2,1,0:T(8,128)(2,1)S(1)} %get-tuple-element.65), channel_id=1, source_target_pairs={{4,8},{8,4},{12,16},{16,12},{20,24},{24,20},{5,9},{9,5},{13,17},{1... | collective-permute-start | bytes 491528 | tf_op jit(solution)/shard_map/ppermute | solution.py:35
  24.3 7.3 %collective-permute-start.5 = (bf16[64,1280]{1,0:T(8,128)(2,1)}, bf16[64,1280]{1,0:T(8,128)(2,1)S(1)}, u32[]{:S(2)}, u32[]{:S(2)}) collective-permute-start(bf16[64,1280]{1,0:T(8,128)(2,1)} %collective-permute-done.4.refs_0_.refs_3_), channel_id=1, source_target_pairs={{0,2},{2,0},{1,3},{3,1},{4,6},{6,4},{5,7},{7,5},{8,10},{10,8},{9,1... | collective-permute-start | bytes 491528 | tf_op jit(solution)/shard_map/ppermute | solution.py:28
  25.8 8.3 %collective-permute-start.2 = (bf16[64,1280]{1,0:T(8,128)(2,1)}, bf16[64,1280]{1,0:T(8,128)(2,1)S(1)}, u32[]{:S(2)}, u32[]{:S(2)}) collective-permute-start(bf16[64,1280]{1,0:T(8,128)(2,1)} %collective-permute-done.1.refs_0_.refs_1_), channel_id=1, source_target_pairs={{0,2},{2,0},{1,3},{3,1},{4,6},{6,4},{5,7},{7,5},{8,10},{10,8},{9,1... | collective-permute-start | bytes 491528 | tf_op jit(solution)/shard_map/ppermute | solution.py:28
  26.4 7.8 %collective-permute-start.8 = (bf16[10,80,256]{2,1,0:T(8,128)(2,1)S(1)}, bf16[10,80,256]{2,1,0:T(8,128)(2,1)S(1)}, u32[]{:S(2)}, u32[]{:S(2)}) collective-permute-start(bf16[10,80,256]{2,1,0:T(8,128)(2,1)S(1)} %collective-permute-done.refs_0_.refs_2_), channel_id=1, source_target_pairs={{0,4},{4,0},{8,12},{12,8},{16,20},{20,16},{24,28},{28,24},{1,5},{5... | collective-permute-start | bytes 1228808 | tf_op jit(solution)/shard_map/ppermute | solution.py:28
  31.7 1.4 %collective-permute-start.6 = (bf16[4,80,256]{2,1,0:T(8,128)(2,1)S(1)}, bf16[4,80,256]{2,1,0:T(8,128)(2,1)S(1)}, u32[]{:S(2)}, u32[]{:S(2)}) collective-permute-start(bf16[4,80,256]{2,1,0:T(8,128)(2,1)S(1)} %get-tuple-element.64), channel_id=1, source_target_pairs={{0,4},{4,0},{8,12},{12,8},{16,20},{20,16},{24,28},{28,24},{1,5},{5... | collective-permute-start | bytes 491528 | tf_op jit(solution)/shard_map/ppermute | solution.py:28
  31.7 1.4 %copy-start.2 = (f32[3,4,80,256]{3,2,1,0:T(8,128)S(1)}, f32[3,4,80,256]{3,2,1,0:T(8,128)}, u32[]{:S(2)}) copy-start(f32[3,4,80,256]{3,2,1,0:T(8,128)} %copy-done.1) | copy-start | bytes 2949124
  31.7 1.4 %copy-start.9 = (s32[4,9]{1,0:T(4,128)S(1)}, s32[4,9]{1,0:T(4,128)}, u32[]{:S(2)}) copy-start(s32[4,9]{1,0:T(4,128)} %refs_0_.4) | copy-start | bytes 436
  31.7 2.4 %collective-permute-start.9 = (bf16[2,80,256]{2,1,0:T(8,128)(2,1)S(1)}, bf16[2,80,256]{2,1,0:T(8,128)(2,1)S(1)}, u32[]{:S(2)}, u32[]{:S(2)}) collective-permute-start(bf16[2,80,256]{2,1,0:T(8,128)(2,1)S(1)} %pad_maximum_fusion.1.refs_5_), channel_id=1, source_target_pairs={{0,4},{4,0},{8,12},{12,8},{16,20},{20,16},{24,28},{28,24},{1,5},{5... | collective-permute-start | bytes 245768 | tf_op jit(solution)/shard_map/ppermute | solution.py:28
  33.9 13.5 %collective-permute-start.11 = (bf16[3,4,80,256]{3,2,1,0:T(8,128)(2,1)S(1)}, bf16[3,4,80,256]{3,2,1,0:T(8,128)(2,1)S(1)}, u32[]{:S(2)}, u32[]{:S(2)}) collective-permute-start(bf16[3,4,80,256]{3,2,1,0:T(8,128)(2,1)S(1)} %get-tuple-element.43), channel_id=1, source_target_pairs={{0,1},{1,0},{2,3},{3,2},{4,5},{5,4},{6,7},{7,6},{8,9},{9,8},{10,11... | collective-permute-start | bytes 1474568 | tf_op jit(solution)/shard_map/ppermute | solution.py:28
  36.2 14.2 %collective-permute-start.12 = (bf16[128,512]{1,0:T(8,128)(2,1)S(1)}, bf16[128,512]{1,0:T(8,128)(2,1)S(1)}, u32[]{:S(2)}, u32[]{:S(2)}) collective-permute-start(bf16[128,512]{1,0:T(8,128)(2,1)S(1)} %shard_map.117.refs_4_), channel_id=1, source_target_pairs={{0,24},{4,28},{8,16},{12,20},{16,8},{20,12},{24,0},{28,4},{1,25},{... | collective-permute-start | bytes 393224 | tf_op jit(solution)/shard_map/ppermute | solution.py:28
  41.0 9.5 %collective-permute-start.13 = (bf16[128,512]{1,0:T(8,128)(2,1)S(1)}, bf16[128,512]{1,0:T(8,128)(2,1)S(1)}, u32[]{:S(2)}, u32[]{:S(2)}) collective-permute-start(bf16[128,512]{1,0:T(8,128)(2,1)S(1)} %shard_map.118.refs_3_), channel_id=1, source_target_pairs={{0,16},{4,20},{8,24},{12,28},{16,0},{20,4},{24,8},{28,12},{1,17},{... | collective-permute-start | bytes 393224 | tf_op jit(solution)/shard_map/ppermute | solution.py:28
  42.4 8.0 %collective-permute-start.14 = (bf16[128,512]{1,0:T(8,128)(2,1)S(1)}, bf16[128,512]{1,0:T(8,128)(2,1)S(1)}, u32[]{:S(2)}, u32[]{:S(2)}) collective-permute-start(bf16[128,512]{1,0:T(8,128)(2,1)S(1)} %shard_map.119), channel_id=1, source_target_pairs={{0,8},{4,12},{8,0},{12,4},{16,24},{20,28},{24,16},{28,20},{1,9},{5... | collective-permute-start | bytes 393224 | tf_op jit(solution)/shard_map/ppermute | solution.py:28
  50.6 8.3 %collective-permute-start.15 = (bf16[128,512]{1,0:T(8,128)(2,1)S(1)}, bf16[128,512]{1,0:T(8,128)(2,1)S(1)}, u32[]{:S(2)}, u32[]{:S(2)}) collective-permute-start(bf16[128,512]{1,0:T(8,128)(2,1)S(1)} %get-tuple-element.55.refs_1_), channel_id=1, source_target_pairs={{0,24},{4,28},{8,16},{12,20},{16,8},{20,12},{24,0},{28,4},{1,25},{... | collective-permute-start | bytes 393224 | tf_op jit(solution)/shard_map/ppermute | solution.py:28
  53.4 10.4 %collective-permute-start.16 = (bf16[128,512]{1,0:T(8,128)(2,1)S(1)}, bf16[128,512]{1,0:T(8,128)(2,1)S(1)}, u32[]{:S(2)}, u32[]{:S(2)}) collective-permute-start(bf16[128,512]{1,0:T(8,128)(2,1)S(1)} %get-tuple-element.55.refs_1_), channel_id=1, source_target_pairs={{0,16},{4,20},{8,24},{12,28},{16,0},{20,4},{24,8},{28,12},{1,17},{... | collective-permute-start | bytes 393224 | tf_op jit(solution)/shard_map/ppermute | solution.py:28
  53.4 10.4 %collective-permute-start.17 = (bf16[128,512]{1,0:T(8,128)(2,1)S(1)}, bf16[128,512]{1,0:T(8,128)(2,1)S(1)}, u32[]{:S(2)}, u32[]{:S(2)}) collective-permute-start(bf16[128,512]{1,0:T(8,128)(2,1)S(1)} %get-tuple-element.55.refs_1_), channel_id=1, source_target_pairs={{0,8},{4,12},{8,0},{12,4},{16,24},{20,28},{24,16},{28,20},{1,9},{5... | collective-permute-start | bytes 393224 | tf_op jit(solution)/shard_map/ppermute | solution.py:28
  64.4 2.2 %collective-permute-start.18 = (bf16[2,320,512]{2,1,0:T(8,128)(2,1)S(1)}, bf16[2,320,512]{2,1,0:T(8,128)(2,1)S(1)}, u32[]{:S(2)}, u32[]{:S(2)}) collective-permute-start(bf16[2,320,512]{2,1,0:T(8,128)(2,1)S(1)} %shard_map.126), channel_id=1, source_target_pairs={{0,4},{4,0},{8,12},{12,8},{16,20},{20,16},{24,28},{28,24},{1,5},{5... | collective-permute-start | bytes 1966088 | tf_op jit(solution)/shard_map/ppermute | solution.py:28
  66.7 9.8 %collective-permute-start.19 = (bf16[320,512]{1,0:T(8,128)(2,1)S(1)}, bf16[320,512]{1,0:T(8,128)(2,1)S(1)}, u32[]{:S(2)}, u32[]{:S(2)}) collective-permute-start(bf16[320,512]{1,0:T(8,128)(2,1)S(1)} %get-tuple-element.58), channel_id=1, source_target_pairs={{0,1},{1,0},{2,3},{3,2},{4,5},{5,4},{6,7},{7,6},{8,9},{9,8},{10,11... | collective-permute-start | bytes 983048 | tf_op jit(solution)/shard_map/ppermute | solution.py:28

commit v4 on v3

--- a/solution.py
+++ b/solution.py
@@ -109,8 +109,23 @@
     )(tokens, *after)
 
 
-def first_adam_kernel(*refs):
-    windows, (weights, leaving, staying, ends) = refs[:4], refs[4:]
+def updated(windows, block, h, rows, per):
+    picks = pl.ds(h, rows, stride=per) if per > 1 else pl.ds(0, rows)
+    return adam_update(*[w[block, picks, :] for w in windows], first_step)
+
+
+def first_weights_kernel(*refs):
+    windows, out = refs[:4], refs[4]
+    blocks, rows, cols = out.shape
+    per = cols // LANES
+    for k in range(blocks):
+        for h in range(per):
+            value = updated(windows, k, h, rows, per)[0]
+            out[k, :, h * LANES : (h + 1) * LANES] = value.astype(bf16)
+
+
+def first_states_kernel(*refs):
+    windows, (leaving, staying, ends) = refs[:4], refs[4:]
     group = lax.axis_index("group")
     _, half, rows, cols = staying.shape
     per = cols // LANES
@@ -119,21 +134,9 @@
     for out, start, size in runs:
         for k in range(size):
             for h in range(per):
-                at = slice(h * LANES, (h + 1) * LANES)
-                picks = pl.ds(h, rows, stride=per) if per > 1 else pl.ds(0, rows)
-                values = adam_update(*[w[start + k, picks, :] for w in windows], first_step)
-                weights[start + k, :, at] = values[0].astype(bf16)
+                values = updated(windows, start + k, h, rows, per)
                 for i in range(3):
-                    out[i, k, :, at] = values[i].astype(out.dtype)
-
-
-def first_adam(windows, old_cols, after):
-    count, rows = windows[0].shape[0] - 2, windows[0].shape[1]
-    short = rows * LANES // old_cols
-    tile = shape((3, count // 2, short, old_cols), f32)
-    ends = shape((2, 3, 1, short, old_cols), bf16)
-    weights = shape((count + 2, short, old_cols), bf16)
-    return call(first_adam_kernel, [weights, tile, tile, ends], *windows, after=after)
+                    out[i, k, :, h * LANES : (h + 1) * LANES] = values[i].astype(out.dtype)
 
 
 def live_bounds(offsets, span, rank, other):
@@ -319,7 +322,10 @@
         for w in (old_master, old_moment, old_variance, old_grad)
     ]
     ahead = call(zero_kernel, shape((8, LANES), f32), flops=LONG)
-    window, leaving, staying, ends = first_adam(windows, old_cols, [ahead])
+    count, rows = windows[0].shape[0] - 2, windows[0].shape[1] * LANES // old_cols
+    window = call(
+        first_weights_kernel, shape((count + 2, rows, old_cols), bf16), *windows, after=[ahead]
+    )
 
     def token_block(of_chip, of_tensor):
         return jnp.concatenate(
@@ -352,6 +358,15 @@
     arrived = [swap(b, "dp", step * CORES) for step, b in enumerate(leaving_blocks, 1)]
     arrived = [lax.optimization_barrier((a, cleared))[0] for a in arrived]
 
+    mate_window = swap(window, "dp", 1)
+    tile = shape((3, count // 2, rows, old_cols), f32)
+    leaving, staying, ends = call(
+        first_states_kernel,
+        [tile, tile, shape((2, 3, 1, rows, old_cols), bf16)],
+        *windows,
+        after=[mate_window],
+    )
+
     ends = jnp.concatenate([ends[:, :, 0], jnp.stack([other[0], other[-1]])[:, None]], axis=1)
     inner = swap(jnp.where(core == 0, ends[1], ends[0]), "dp", 1)
     outer = swap_border(jnp.where(core == 0, ends[0], ends[1]))
@@ -364,22 +379,8 @@
         block += [swap(block[0], "tensor", j) for j in range(1, tensors)]
 
     far, _ = lax.optimization_barrier((jnp.stack([outer[0], outer[3]]), blocks[DIRECT]))
-    leaving, far = lax.optimization_barrier((leaving, far))
-    leaving, staying = call(
-        patch_states_kernel,
-        [shape(leaving.shape, bf16), shape(leaving.shape, f32)],
-        old_offsets,
-        leaving,
-        staying,
-        inner,
-        outer,
-        scalars=1,
-    )
-    incoming = swap(leaving, "group", 1)
-
-    count, rows = window.shape[0] - 2, window.shape[1]
-    mates = [swap(w, "dp", 1) for w in (window, other, far)]
-    window, *_ = lax.optimization_barrier((window, leaving, *blocks[-1]))
+
+    mates = [mate_window] + [swap(w, "dp", 1) for w in (other, far)]
     weights = call(
         patch_weights_kernel,
         [shape((count, rows, cols), bf16)] * 2,
@@ -399,9 +400,20 @@
         parts.append(part(blocks[step], weights, bf16, after=parts[-1:]))
     back = [swap(p, "dp", step * CORES) for step, p in zip(steps, parts, strict=True)]
 
-    own_block, *_ = lax.optimization_barrier((blocks[0][0], *parts))
+    leaving, staying = call(
+        patch_states_kernel,
+        [shape(leaving.shape, bf16), shape(leaving.shape, f32)],
+        old_offsets,
+        leaving,
+        staying,
+        inner,
+        outer,
+        scalars=1,
+        after=parts[-1:],
+    )
+    incoming = swap(leaving, "group", 1)
+    own_block = blocks[0][0]
     total = part([own_block], weights, f32, LONG)
-    total, incoming = lax.optimization_barrier((total, incoming))
     activated, delta = call(
         delta_kernel, [shape((slots, cols), bf16)] * 2, total, *back, turned
     )
@@ -409,8 +421,13 @@
     deltas = [delta] + [swap(delta, "dp", step * CORES) for step in steps]
 
     flat = [p for step in (0, *steps) for p in blocks[step]]
-    flat[0], _ = lax.optimization_barrier((flat[0], delta))
-    gathered = call(gather_kernel, shape((chips * slots, depth), bf16), *flat, flops=LONG)
+    gathered = call(
+        gather_kernel,
+        shape((chips * slots, depth), bf16),
+        *flat,
+        flops=LONG,
+        after=[incoming, delta],
+    )
     flops = 2 * half * cols * chips * slots
     tile = half // groups
     to_mate, mine = (

time: 78.6 us -> 75.9 us (0.966)
  waiting for transfers between devices: 33.7 us -> 31.3 us
  other arithmetic: 1.08 us -> 0.05 us
  starting transfers between devices: 25.8 us -> 24.9 us
  Pallas kernels: 13.4 us -> 14.2 us
    ppermute x19, waiting for transfers between devices: 33.7 us -> 31.3 us  [swap(): return lax.ppermute(value, axis, pairs)]
    select_n x1, other arithmetic: 1.06 us -> 0.03 us  [local(): inner = swap(jnp.where(core == 0, ends[1], ends[0]), 'dp', 1)]
    ppermute x19, starting transfers between devices: 25 us -> 24.1 us  [swap(): return lax.ppermute(value, axis, pairs)]
    pallas_call x16 -> x17, Pallas kernels: 12.2 us -> 13.1 us  [call(): pl.pallas_call(body, out_shape=shapes, in_specs=[small] * scalars + [whol...]
    unnamed x22 -> x20, local copies, waits for them, and re-layouts: 3.53 us -> 4.16 us
  transfers between devices with their start and end apart: 20 -> 20, of which waited for: 10 -> 11; matrix products, arithmetic and copies ran while one was open for 1% -> 0% of each run, Pallas kernels for 13% -> 14%
where the time goes in v4:
time: 75.9 us; the launch traced here: 75.6 us
  waiting for transfers between devices  31.3 us (41%)
  starting transfers between devices  24.9 us (33%)
  Pallas kernels  14.2 us (19%)
  local copies, waits for them, and re-layouts  4.17 us (5%)
  between operations  0.88 us (1%)
    ppermute x19, waiting for transfers between devices, swap(): return lax.ppermute(value, axis, pairs)  31.3 us
    ppermute x19, starting transfers between devices, swap(): return lax.ppermute(value, axis, pairs)  24.1 us
    pallas_call x17, Pallas kernels, call(): pl.pallas_call(body, out_shape=shapes, in_specs=[small] * scalars + [whol...  13.1 us
    unnamed x20, local copies, waits for them, and re-layouts  4.16 us
  transfers between devices with their start and end apart: 20, of which 11 were waited for; matrix products, arithmetic and copies ran while one was open for 0% of the time, Pallas kernels for 14%

profile of v4, /device:TPU:0, one launch (start us, length us, event | category | flops | bytes accessed | tf_op | source)
XLA Modules:
  0.0 75.6 jit_solution(14959182001445089114)
XLA Ops:
  0.7 1.1 %copy-done.1 = f32[1,1,204800]{2,1,0:T(1,128)S(1)} copy-done((f32[1,1,204800]{2,1,0:T(1,128)S(1)}, f32[1,1,204800]{2,1,0:T(1,128)}, u32[]{:S(2)}) %copy-start.1) | copy-done | bytes 819224
  2.5 1.4 %shard_map.112.refs_1_ = bf16[10,80,256]{2,1,0:T(8,128)(2,1)} custom-call(f32[10,160,128]{2,1,0:T(8,128)S(1)} %bitcast.23, f32[10,160,128]{2,1,0:T(8,128)S(1)} %bitcast.25, f32[10,160,128]{2,1,0:T(8,128)S(1)} %bitcast.27, f32[10,160,128]{2,1,0:T(8,128)S(1)} %bitcast.29, f32[8,128]{1,0:T(8,128)S(1)} %shard_map.111.refs_4_), custom_call_target="tpu_custom_call" | custom-call | bytes 3276800 | tf_op jit(solution)/shard_map/pallas_call | solution.py:56
  4.0 3.0 %collective-permute-start = (bf16[10,80,256]{2,1,0:T(8,128)(2,1)}, bf16[10,80,256]{2,1,0:T(8,128)(2,1)S(1)}, u32[]{:S(2)}, u32[]{:S(2)}) collective-permute-start(bf16[10,80,256]{2,1,0:T(8,128)(2,1)} %shard_map.112.refs_1_), channel_id=1, source_target_pairs={{0,1},{1,0},{2,3},{3,2},{4,5},{5,4},{6,7},{7,6},{8,9},{9,8},{10,11... | collective-permute-start | bytes 1228808 | tf_op jit(solution)/shard_map/ppermute | solution.py:28
  6.9 1.0 %shard_map.115 = (bf16[128,1280]{1,0:T(8,128)(2,1)}, bf16[64,1280]{1,0:T(8,128)(2,1)}, bf16[64,1280]{1,0:T(8,128)(2,1)}) custom-call(bf16[128,5120]{1,0:T(8,128)(2,1)S(1)} %copy-done), custom_call_target="tpu_custom_call" | custom-call | bytes 1000000 | tf_op jit(solution)/shard_map/pallas_call | solution.py:101
  8.0 2.7 %collective-permute-start.4 = (bf16[64,1280]{1,0:T(8,128)(2,1)}, bf16[64,1280]{1,0:T(8,128)(2,1)}, u32[]{:S(2)}, u32[]{:S(2)}) collective-permute-start(bf16[64,1280]{1,0:T(8,128)(2,1)} %get-tuple-element.26), channel_id=1, source_target_pairs={{0,16},{4,20},{8,24},{12,28},{16,0},{20,4},{24,8},{28,12},{1,17},{... | collective-permute-start | bytes 491528 | tf_op jit(solution)/shard_map/ppermute | solution.py:28
  10.6 1.3 %collective-permute-start.7 = (bf16[64,1280]{1,0:T(8,128)(2,1)}, bf16[64,1280]{1,0:T(8,128)(2,1)S(1)}, u32[]{:S(2)}, u32[]{:S(2)}) collective-permute-start(bf16[64,1280]{1,0:T(8,128)(2,1)} %get-tuple-element.31), channel_id=1, source_target_pairs={{0,24},{4,28},{8,16},{12,20},{16,8},{20,12},{24,0},{28,4},{1,25},{... | collective-permute-start | bytes 491528 | tf_op jit(solution)/shard_map/ppermute | solution.py:28
  12.2 4.4 %collective-permute-done.refs_0_.refs_2_ = bf16[10,80,256]{2,1,0:T(8,128)(2,1)S(1)} collective-permute-done((bf16[10,80,256]{2,1,0:T(8,128)(2,1)}, bf16[10,80,256]{2,1,0:T(8,128)(2,1)S(1)}, u32[]{:S(2)}, u32[]{:S(2)}) %collective-permute-start) | collective-permute-done | bytes 409632 | tf_op jit(solution)/shard_map/ppermute | solution.py:28
  16.6 1.1 %copy-done.4 = f32[1,1,204800]{2,1,0:T(1,128)S(1)} copy-done((f32[1,1,204800]{2,1,0:T(1,128)S(1)}, f32[1,1,204800]{2,1,0:T(1,128)}, u32[]{:S(2)}) %copy-start.4) | copy-done | bytes 819224
  17.8 1.1 %copy-done.6 = f32[1,1,204800]{2,1,0:T(1,128)S(1)} copy-done((f32[1,1,204800]{2,1,0:T(1,128)S(1)}, f32[1,1,204800]{2,1,0:T(1,128)}, u32[]{:S(2)}) %copy-start.6) | copy-done | bytes 819224
  19.6 0.8 %collective-permute-start.3 = (bf16[4,80,256]{2,1,0:T(8,128)(2,1)S(1)}, bf16[4,80,256]{2,1,0:T(8,128)(2,1)S(1)}, u32[]{:S(2)}, u32[]{:S(2)}) collective-permute-start(bf16[4,80,256]{2,1,0:T(8,128)(2,1)S(1)} %get-tuple-element.49), channel_id=1, source_target_pairs={{4,8},{8,4},{12,16},{16,12},{20,24},{24,20},{5,9},{9,5},{13,17},{1... | collective-permute-start | bytes 491528 | tf_op jit(solution)/shard_map/ppermute | solution.py:35
  20.5 2.8 %collective-permute-done.4.refs_0_.refs_3_ = bf16[64,1280]{1,0:T(8,128)(2,1)} collective-permute-done((bf16[64,1280]{1,0:T(8,128)(2,1)}, bf16[64,1280]{1,0:T(8,128)(2,1)}, u32[]{:S(2)}, u32[]{:S(2)}) %collective-permute-start.4) | collective-permute-done | bytes 163872 | tf_op jit(solution)/shard_map/ppermute | solution.py:28
  23.3 1.5 %collective-permute-start.5 = (bf16[64,1280]{1,0:T(8,128)(2,1)}, bf16[64,1280]{1,0:T(8,128)(2,1)S(1)}, u32[]{:S(2)}, u32[]{:S(2)}) collective-permute-start(bf16[64,1280]{1,0:T(8,128)(2,1)} %collective-permute-done.4.refs_0_.refs_3_), channel_id=1, source_target_pairs={{0,2},{2,0},{1,3},{3,1},{4,6},{6,4},{5,7},{7,5},{8,10},{10,8},{9,1... | collective-permute-start | bytes 491528 | tf_op jit(solution)/shard_map/ppermute | solution.py:28
  25.4 4.2 %collective-permute-start.2 = (bf16[10,80,256]{2,1,0:T(8,128)(2,1)S(1)}, bf16[10,80,256]{2,1,0:T(8,128)(2,1)S(1)}, u32[]{:S(2)}, u32[]{:S(2)}) collective-permute-start(bf16[10,80,256]{2,1,0:T(8,128)(2,1)S(1)} %collective-permute-done.refs_0_.refs_2_), channel_id=1, source_target_pairs={{0,4},{4,0},{8,12},{12,8},{16,20},{20,16},{24,28},{28,24},{1,5},{5... | collective-permute-start | bytes 1228808 | tf_op jit(solution)/shard_map/ppermute | solution.py:28
  29.6 1.0 %collective-permute-done.5.refs_1_.refs_4_ = bf16[64,1280]{1,0:T(8,128)(2,1)S(1)} collective-permute-done((bf16[64,1280]{1,0:T(8,128)(2,1)}, bf16[64,1280]{1,0:T(8,128)(2,1)S(1)}, u32[]{:S(2)}, u32[]{:S(2)}) %collective-permute-start.5) | collective-permute-done | bytes 163872 | tf_op jit(solution)/shard_map/ppermute | solution.py:28
  31.8 1.3 %shard_map.116 = (bf16[8,80,512]{2,1,0:T(8,128)(2,1)S(1)}, bf16[8,80,512]{2,1,0:T(8,128)(2,1)S(1)}) custom-call(s32[4,9]{1,0:T(4,128)S(1)} %copy-done.8, bf16[10,80,256]{2,1,0:T(8,128)(2,1)} %shard_map.112.refs_1_, bf16[10,80,256]{2,1,0:T(8,128)(2,1)S(1)} %collective-permute-done.refs_0_.refs_2_, ...), custom_call_target="tpu_custom_call" | custom-call | bytes 1802384 | tf_op jit(solution)/shard_map/pallas_call | solution.py:56
  33.9 2.9 %collective-permute-start.9 = (bf16[128,512]{1,0:T(8,128)(2,1)S(1)}, bf16[128,512]{1,0:T(8,128)(2,1)S(1)}, u32[]{:S(2)}, u32[]{:S(2)}) collective-permute-start(bf16[128,512]{1,0:T(8,128)(2,1)S(1)} %shard_map.118.refs_4_), channel_id=1, source_target_pairs={{0,24},{4,28},{8,16},{12,20},{16,8},{20,12},{24,0},{28,4},{1,25},{... | collective-permute-start | bytes 393224 | tf_op jit(solution)/shard_map/ppermute | solution.py:28
  36.8 1.3 %shard_map.119.refs_3_ = bf16[128,512]{1,0:T(8,128)(2,1)S(1)} custom-call(bf16[64,1280]{1,0:T(8,128)(2,1)} %collective-permute-done.4.refs_0_.refs_3_, bf16[64,1280]{1,0:T(8,128)(2,1)S(1)} %collective-permute-done.5.refs_1_.refs_4_, bf16[640,512]{1,0:T(8,128)(2,1)S(1)} %bitcast.16, bf16[640,512]{1,0:T(8,128)(2,1)S(1)} %bitcast.20, ...), custom_call_target="tpu_custom_call" | custom-call | flops 167772160 | bytes 1638400 | tf_op jit(solution)/shard_map/pallas_call | solution.py:56
  38.2 1.3 %shard_map.120.refs_5_ = bf16[128,512]{1,0:T(8,128)(2,1)S(1)} custom-call(bf16[128,1280]{1,0:T(8,128)(2,1)} %collective-permute-done.11.refs_0_.refs_5_, bf16[640,512]{1,0:T(8,128)(2,1)S(1)} %bitcast.17, bf16[640,512]{1,0:T(8,128)(2,1)S(1)} %bitcast.21, bf16[128,512]{1,0:T(8,128)(2,1)S(1)} %shard_map.119.refs_3_), custom_call_target="tpu_custom_call" | custom-call | flops 167772160 | bytes 1638400 | tf_op jit(solution)/shard_map/pallas_call | solution.py:56
  39.5 1.6 %collective-permute-start.12 = (bf16[128,512]{1,0:T(8,128)(2,1)S(1)}, bf16[128,512]{1,0:T(8,128)(2,1)S(1)}, u32[]{:S(2)}, u32[]{:S(2)}) collective-permute-start(bf16[128,512]{1,0:T(8,128)(2,1)S(1)} %shard_map.120.refs_5_), channel_id=1, source_target_pairs={{0,8},{4,12},{8,0},{12,4},{16,24},{20,28},{24,16},{28,20},{1,9},{5... | collective-permute-start | bytes 393224 | tf_op jit(solution)/shard_map/ppermute | solution.py:28
  41.1 0.8 %shard_map.124 = (bf16[3,4,80,256]{3,2,1,0:T(8,128)(2,1)S(1)}, f32[3,4,80,256]{3,2,1,0:T(8,128)S(1)}) custom-call(s32[4,9]{1,0:T(4,128)S(1)} %copy-done.8, f32[3,4,80,256]{3,2,1,0:T(8,128)S(1)} %get-tuple-element.36.refs_1_, f32[3,4,80,256]{3,2,1,0:T(8,128)S(1)} %get-tuple-element.37.refs_2_, bf16[4,80,256]{2,1,0:T(8,128)(2,1)S(1)} %collective-permute-done.13.refs_3_, ...), custom_call_target="tpu_custom_call" | custom-call | bytes 2293904 | tf_op jit(solution)/shard_map/pallas_call | solution.py:56
  42.7 5.4 %collective-permute-done.10.refs_2_ = bf16[128,512]{1,0:T(8,128)(2,1)S(1)} collective-permute-done((bf16[128,512]{1,0:T(8,128)(2,1)S(1)}, bf16[128,512]{1,0:T(8,128)(2,1)S(1)}, u32[]{:S(2)}, u32[]{:S(2)}) %collective-permute-start.10) | collective-permute-done | bytes 131104 | tf_op jit(solution)/shard_map/ppermute | solution.py:28
  48.3 2.3 %collective-permute-start.15 = (bf16[128,512]{1,0:T(8,128)(2,1)S(1)}, bf16[128,512]{1,0:T(8,128)(2,1)S(1)}, u32[]{:S(2)}, u32[]{:S(2)}) collective-permute-start(bf16[128,512]{1,0:T(8,128)(2,1)S(1)} %get-tuple-element.40.refs_7_.refs_1_), channel_id=1, source_target_pairs={{0,24},{4,28},{8,16},{12,20},{16,8},{20,12},{24,0},{28,4},{1,25},{... | collective-permute-start | bytes 393224 | tf_op jit(solution)/shard_map/ppermute | solution.py:28
  50.6 2.1 %collective-permute-start.17 = (bf16[128,512]{1,0:T(8,128)(2,1)S(1)}, bf16[128,512]{1,0:T(8,128)(2,1)S(1)}, u32[]{:S(2)}, u32[]{:S(2)}) collective-permute-start(bf16[128,512]{1,0:T(8,128)(2,1)S(1)} %get-tuple-element.40.refs_7_.refs_1_), channel_id=1, source_target_pairs={{0,8},{4,12},{8,0},{12,4},{16,24},{20,28},{24,16},{28,20},{1,9},{5... | collective-permute-start | bytes 393224 | tf_op jit(solution)/shard_map/ppermute | solution.py:28
  52.7 1.4 %collective-permute-done.14.refs_6_.refs_1_ = bf16[3,4,80,256]{3,2,1,0:T(8,128)(2,1)S(1)} collective-permute-done((bf16[3,4,80,256]{3,2,1,0:T(8,128)(2,1)S(1)}, bf16[3,4,80,256]{3,2,1,0:T(8,128)(2,1)S(1)}, u32[]{:S(2)}, u32[]{:S(2)}) %collective-permute-start.14) | collective-permute-done | bytes 491552 | tf_op jit(solution)/shard_map/ppermute | solution.py:28
  54.1 1.1 %shard_map.125.refs_0_ = bf16[512,1280]{1,0:T(8,128)(2,1)S(1)} custom-call(bf16[128,1280]{1,0:T(8,128)(2,1)S(1)} %shard_map.113.refs_0_, bf16[64,1280]{1,0:T(8,128)(2,1)S(1)} %collective-permute-done.7.refs_0_.refs_1_, bf16[64,1280]{1,0:T(8,128)(2,1)S(1)} %collective-permute-done.8.refs_1_.refs_2_, bf16[64,1280]{1,0:T(8,128)(2,1)} %collective-permute-done.4.refs_0_.refs_3_, ...), custom_call_target="tpu_custom_call" | custom-call | flops 99999997952 | bytes 1310720 | tf_op jit(solution)/shard_map/pallas_call | solution.py:56
  55.2 1.3 %collective-permute-done.15.refs_2_ = bf16[128,512]{1,0:T(8,128)(2,1)S(1)} collective-permute-done((bf16[128,512]{1,0:T(8,128)(2,1)S(1)}, bf16[128,512]{1,0:T(8,128)(2,1)S(1)}, u32[]{:S(2)}, u32[]{:S(2)}) %collective-permute-start.15) | collective-permute-done | bytes 131104 | tf_op jit(solution)/shard_map/ppermute | solution.py:28
  56.6 4.5 %collective-permute-done.16.refs_3_ = bf16[128,512]{1,0:T(8,128)(2,1)S(1)} collective-permute-done((bf16[128,512]{1,0:T(8,128)(2,1)S(1)}, bf16[128,512]{1,0:T(8,128)(2,1)S(1)}, u32[]{:S(2)}, u32[]{:S(2)}) %collective-permute-start.16) | collective-permute-done | bytes 131104 | tf_op jit(solution)/shard_map/ppermute | solution.py:28
  62.3 1.5 %collective-permute-done.18.refs_1_ = bf16[2,320,512]{2,1,0:T(8,128)(2,1)S(1)} collective-permute-done((bf16[2,320,512]{2,1,0:T(8,128)(2,1)S(1)}, bf16[2,320,512]{2,1,0:T(8,128)(2,1)S(1)}, u32[]{:S(2)}, u32[]{:S(2)}) %collective-permute-start.18) | collective-permute-done | bytes 655392 | tf_op jit(solution)/shard_map/ppermute | solution.py:28
  63.9 1.1 %collective-permute-start.19 = (bf16[320,512]{1,0:T(8,128)(2,1)S(1)}, bf16[320,512]{1,0:T(8,128)(2,1)S(1)}, u32[]{:S(2)}, u32[]{:S(2)}) collective-permute-start(bf16[320,512]{1,0:T(8,128)(2,1)S(1)} %get-tuple-element.42), channel_id=1, source_target_pairs={{0,1},{1,0},{2,3},{3,2},{4,5},{5,4},{6,7},{7,6},{8,9},{9,8},{10,11... | collective-permute-start | bytes 983048 | tf_op jit(solution)/shard_map/ppermute | solution.py:28
  65.0 0.7 shard_map.123
  65.7 8.0 %collective-permute-done.19.refs_3_ = bf16[320,512]{1,0:T(8,128)(2,1)S(1)} collective-permute-done((bf16[320,512]{1,0:T(8,128)(2,1)S(1)}, bf16[320,512]{1,0:T(8,128)(2,1)S(1)}, u32[]{:S(2)}, u32[]{:S(2)}) %collective-permute-start.19) | collective-permute-done | bytes 327712 | tf_op jit(solution)/shard_map/ppermute | solution.py:28
  73.7 1.8 %shard_map.129 = (f32[320,512]{1,0:T(8,128)}, f32[320,512]{1,0:T(8,128)}, f32[320,512]{1,0:T(8,128)}) custom-call(f32[3,4,80,256]{3,2,1,0:T(8,128)S(1)} %get-tuple-element.38.refs_0_, bf16[3,4,80,256]{3,2,1,0:T(8,128)(2,1)S(1)} %collective-permute-done.14.refs_6_.refs_1_, f32[320,512]{1,0:T(8,128)S(1)} %get-tuple-element.41.refs_2_, ...), custom_call_target="tpu_custom_call" | custom-call | bytes 2457600 | tf_op jit(solution)/shard_map/pallas_call | solution.py:56
  (52 shorter events, 6.5 us)
Async XLA Ops:
  0.6 1.1 %copy-start.1 = (f32[1,1,204800]{2,1,0:T(1,128)S(1)}, f32[1,1,204800]{2,1,0:T(1,128)}, u32[]{:S(2)}) copy-start(f32[1,1,204800]{2,1,0:T(1,128)} %param.12) | copy-start | bytes 2457604
  0.6 1.4 %copy-start.2 = (f32[1,1,204800]{2,1,0:T(1,128)S(1)}, f32[1,1,204800]{2,1,0:T(1,128)}, u32[]{:S(2)}) copy-start(f32[1,1,204800]{2,1,0:T(1,128)} %param.13) | copy-start | bytes 2457604
  0.7 1.6 %copy-start.3 = (f32[1,1,204800]{2,1,0:T(1,128)S(1)}, f32[1,1,204800]{2,1,0:T(1,128)}, u32[]{:S(2)}) copy-start(f32[1,1,204800]{2,1,0:T(1,128)} %param.14) | copy-start | bytes 2457604
  0.7 1.9 %copy-start.5 = (f32[1,1,204800]{2,1,0:T(1,128)S(1)}, f32[1,1,204800]{2,1,0:T(1,128)}, u32[]{:S(2)}) copy-start(f32[1,1,204800]{2,1,0:T(1,128)} %param.15) | copy-start | bytes 2457604
  2.5 4.4 %copy-start = (bf16[128,5120]{1,0:T(8,128)(2,1)S(1)}, bf16[128,5120]{1,0:T(8,128)(2,1)}, u32[]{:S(2)}) copy-start(bf16[128,5120]{1,0:T(8,128)(2,1)} %tokens.3) | copy-start | bytes 3932164
  4.0 12.6 %collective-permute-start = (bf16[10,80,256]{2,1,0:T(8,128)(2,1)}, bf16[10,80,256]{2,1,0:T(8,128)(2,1)S(1)}, u32[]{:S(2)}, u32[]{:S(2)}) collective-permute-start(bf16[10,80,256]{2,1,0:T(8,128)(2,1)} %shard_map.112.refs_1_), channel_id=1, source_target_pairs={{0,1},{1,0},{2,3},{3,2},{4,5},{5,4},{6,7},{7,6},{8,9},{9,8},{10,11... | collective-permute-start | bytes 1228808 | tf_op jit(solution)/shard_map/ppermute | solution.py:28
  6.9 9.7 %collective-permute-start.1 = (bf16[10,80,256]{2,1,0:T(8,128)(2,1)}, bf16[10,80,256]{2,1,0:T(8,128)(2,1)}, u32[]{:S(2)}, u32[]{:S(2)}) collective-permute-start(bf16[10,80,256]{2,1,0:T(8,128)(2,1)} %shard_map.112.refs_1_), channel_id=1, source_target_pairs={{0,4},{4,0},{8,12},{12,8},{16,20},{20,16},{24,28},{28,24},{1,5},{5... | collective-permute-start | bytes 1228808 | tf_op jit(solution)/shard_map/ppermute | solution.py:28
  8.0 15.3 %collective-permute-start.4 = (bf16[64,1280]{1,0:T(8,128)(2,1)}, bf16[64,1280]{1,0:T(8,128)(2,1)}, u32[]{:S(2)}, u32[]{:S(2)}) collective-permute-start(bf16[64,1280]{1,0:T(8,128)(2,1)} %get-tuple-element.26), channel_id=1, source_target_pairs={{0,16},{4,20},{8,24},{12,28},{16,0},{20,4},{24,8},{28,12},{1,17},{... | collective-permute-start | bytes 491528 | tf_op jit(solution)/shard_map/ppermute | solution.py:28
  10.6 14.2 %collective-permute-start.7 = (bf16[64,1280]{1,0:T(8,128)(2,1)}, bf16[64,1280]{1,0:T(8,128)(2,1)S(1)}, u32[]{:S(2)}, u32[]{:S(2)}) collective-permute-start(bf16[64,1280]{1,0:T(8,128)(2,1)} %get-tuple-element.31), channel_id=1, source_target_pairs={{0,24},{4,28},{8,16},{12,20},{16,8},{20,12},{24,0},{28,4},{1,25},{... | collective-permute-start | bytes 491528 | tf_op jit(solution)/shard_map/ppermute | solution.py:28
  12.0 18.6 %collective-permute-start.11 = (bf16[128,1280]{1,0:T(8,128)(2,1)}, bf16[128,1280]{1,0:T(8,128)(2,1)}, u32[]{:S(2)}, u32[]{:S(2)}) collective-permute-start(bf16[128,1280]{1,0:T(8,128)(2,1)} %get-tuple-element.33), channel_id=1, source_target_pairs={{0,8},{4,12},{8,0},{12,4},{16,24},{20,28},{24,16},{28,20},{1,9},{5... | collective-permute-start | bytes 983048 | tf_op jit(solution)/shard_map/ppermute | solution.py:28
  16.6 1.1 %copy-start.4 = (f32[1,1,204800]{2,1,0:T(1,128)S(1)}, f32[1,1,204800]{2,1,0:T(1,128)}, u32[]{:S(2)}) copy-start(f32[1,1,204800]{2,1,0:T(1,128)} %param.14) | copy-start | bytes 2457604
  17.8 1.1 %copy-start.6 = (f32[1,1,204800]{2,1,0:T(1,128)S(1)}, f32[1,1,204800]{2,1,0:T(1,128)}, u32[]{:S(2)}) copy-start(f32[1,1,204800]{2,1,0:T(1,128)} %param.15) | copy-start | bytes 2457604
  19.6 11.0 %copy-start.7 = (bf16[128,512]{1,0:T(8,128)(2,1)S(1)}, bf16[128,512]{1,0:T(8,128)(2,1)}, u32[]{:S(2)}) copy-start(bf16[128,512]{1,0:T(8,128)(2,1)} %refs_1_.1) | copy-start | bytes 393220
  19.6 11.0 %copy-start.9 = (s32[16]{0:T(128)S(1)}, s32[16]{0:T(128)}, u32[]{:S(2)}) copy-start(s32[16]{0:T(128)} %refs_0_.4) | copy-start | bytes 196
  19.6 5.7 %collective-permute-start.3 = (bf16[4,80,256]{2,1,0:T(8,128)(2,1)S(1)}, bf16[4,80,256]{2,1,0:T(8,128)(2,1)S(1)}, u32[]{:S(2)}, u32[]{:S(2)}) collective-permute-start(bf16[4,80,256]{2,1,0:T(8,128)(2,1)S(1)} %get-tuple-element.49), channel_id=1, source_target_pairs={{4,8},{8,4},{12,16},{16,12},{20,24},{24,20},{5,9},{9,5},{13,17},{1... | collective-permute-start | bytes 491528 | tf_op jit(solution)/shard_map/ppermute | solution.py:35
  23.3 7.2 %collective-permute-start.5 = (bf16[64,1280]{1,0:T(8,128)(2,1)}, bf16[64,1280]{1,0:T(8,128)(2,1)S(1)}, u32[]{:S(2)}, u32[]{:S(2)}) collective-permute-start(bf16[64,1280]{1,0:T(8,128)(2,1)} %collective-permute-done.4.refs_0_.refs_3_), channel_id=1, source_target_pairs={{0,2},{2,0},{1,3},{3,1},{4,6},{6,4},{5,7},{7,5},{8,10},{10,8},{9,1... | collective-permute-start | bytes 491528 | tf_op jit(solution)/shard_map/ppermute | solution.py:28
  24.8 8.7 %collective-permute-start.8 = (bf16[64,1280]{1,0:T(8,128)(2,1)S(1)}, bf16[64,1280]{1,0:T(8,128)(2,1)S(1)}, u32[]{:S(2)}, u32[]{:S(2)}) collective-permute-start(bf16[64,1280]{1,0:T(8,128)(2,1)S(1)} %collective-permute-done.7.refs_0_.refs_1_), channel_id=1, source_target_pairs={{0,2},{2,0},{1,3},{3,1},{4,6},{6,4},{5,7},{7,5},{8,10},{10,8},{9,1... | collective-permute-start | bytes 491528 | tf_op jit(solution)/shard_map/ppermute | solution.py:28
  25.4 15.7 %collective-permute-start.13 = (bf16[4,80,256]{2,1,0:T(8,128)(2,1)S(1)}, bf16[4,80,256]{2,1,0:T(8,128)(2,1)S(1)}, u32[]{:S(2)}, u32[]{:S(2)}) collective-permute-start(bf16[4,80,256]{2,1,0:T(8,128)(2,1)S(1)} %get-tuple-element.48), channel_id=1, source_target_pairs={{0,4},{4,0},{8,12},{12,8},{16,20},{20,16},{24,28},{28,24},{1,5},{5... | collective-permute-start | bytes 491528 | tf_op jit(solution)/shard_map/ppermute | solution.py:28
  25.4 6.5 %collective-permute-start.2 = (bf16[10,80,256]{2,1,0:T(8,128)(2,1)S(1)}, bf16[10,80,256]{2,1,0:T(8,128)(2,1)S(1)}, u32[]{:S(2)}, u32[]{:S(2)}) collective-permute-start(bf16[10,80,256]{2,1,0:T(8,128)(2,1)S(1)} %collective-permute-done.refs_0_.refs_2_), channel_id=1, source_target_pairs={{0,4},{4,0},{8,12},{12,8},{16,20},{20,16},{24,28},{28,24},{1,5},{5... | collective-permute-start | bytes 1228808 | tf_op jit(solution)/shard_map/ppermute | solution.py:28
  29.6 2.3 %copy-start.8 = (s32[4,9]{1,0:T(4,128)S(1)}, s32[4,9]{1,0:T(4,128)}, u32[]{:S(2)}) copy-start(s32[4,9]{1,0:T(4,128)} %refs_0_.5) | copy-start | bytes 436
  30.5 1.3 %collective-permute-start.6 = (bf16[2,80,256]{2,1,0:T(8,128)(2,1)S(1)}, bf16[2,80,256]{2,1,0:T(8,128)(2,1)S(1)}, u32[]{:S(2)}, u32[]{:S(2)}) collective-permute-start(bf16[2,80,256]{2,1,0:T(8,128)(2,1)S(1)} %pad_maximum_fusion.1.refs_5_), channel_id=1, source_target_pairs={{0,4},{4,0},{8,12},{12,8},{16,20},{20,16},{24,28},{28,24},{1,5},{5... | collective-permute-start | bytes 245768 | tf_op jit(solution)/shard_map/ppermute | solution.py:28
  33.9 8.8 %collective-permute-start.9 = (bf16[128,512]{1,0:T(8,128)(2,1)S(1)}, bf16[128,512]{1,0:T(8,128)(2,1)S(1)}, u32[]{:S(2)}, u32[]{:S(2)}) collective-permute-start(bf16[128,512]{1,0:T(8,128)(2,1)S(1)} %shard_map.118.refs_4_), channel_id=1, source_target_pairs={{0,24},{4,28},{8,16},{12,20},{16,8},{20,12},{24,0},{28,4},{1,25},{... | collective-permute-start | bytes 393224 | tf_op jit(solution)/shard_map/ppermute | solution.py:28
  38.1 10.0 %collective-permute-start.10 = (bf16[128,512]{1,0:T(8,128)(2,1)S(1)}, bf16[128,512]{1,0:T(8,128)(2,1)S(1)}, u32[]{:S(2)}, u32[]{:S(2)}) collective-permute-start(bf16[128,512]{1,0:T(8,128)(2,1)S(1)} %shard_map.119.refs_3_), channel_id=1, source_target_pairs={{0,16},{4,20},{8,24},{12,28},{16,0},{20,4},{24,8},{28,12},{1,17},{... | collective-permute-start | bytes 393224 | tf_op jit(solution)/shard_map/ppermute | solution.py:28
  39.5 8.6 %collective-permute-start.12 = (bf16[128,512]{1,0:T(8,128)(2,1)S(1)}, bf16[128,512]{1,0:T(8,128)(2,1)S(1)}, u32[]{:S(2)}, u32[]{:S(2)}) collective-permute-start(bf16[128,512]{1,0:T(8,128)(2,1)S(1)} %shard_map.120.refs_5_), channel_id=1, source_target_pairs={{0,8},{4,12},{8,0},{12,4},{16,24},{20,28},{24,16},{28,20},{1,9},{5... | collective-permute-start | bytes 393224 | tf_op jit(solution)/shard_map/ppermute | solution.py:28
  41.9 12.2 %collective-permute-start.14 = (bf16[3,4,80,256]{3,2,1,0:T(8,128)(2,1)S(1)}, bf16[3,4,80,256]{3,2,1,0:T(8,128)(2,1)S(1)}, u32[]{:S(2)}, u32[]{:S(2)}) collective-permute-start(bf16[3,4,80,256]{3,2,1,0:T(8,128)(2,1)S(1)} %get-tuple-element.39), channel_id=1, source_target_pairs={{0,1},{1,0},{2,3},{3,2},{4,5},{5,4},{6,7},{7,6},{8,9},{9,8},{10,11... | collective-permute-start | bytes 1474568 | tf_op jit(solution)/shard_map/ppermute | solution.py:28
  48.3 8.3 %collective-permute-start.15 = (bf16[128,512]{1,0:T(8,128)(2,1)S(1)}, bf16[128,512]{1,0:T(8,128)(2,1)S(1)}, u32[]{:S(2)}, u32[]{:S(2)}) collective-permute-start(bf16[128,512]{1,0:T(8,128)(2,1)S(1)} %get-tuple-element.40.refs_7_.refs_1_), channel_id=1, source_target_pairs={{0,24},{4,28},{8,16},{12,20},{16,8},{20,12},{24,0},{28,4},{1,25},{... | collective-permute-start | bytes 393224 | tf_op jit(solution)/shard_map/ppermute | solution.py:28
  50.6 10.5 %collective-permute-start.16 = (bf16[128,512]{1,0:T(8,128)(2,1)S(1)}, bf16[128,512]{1,0:T(8,128)(2,1)S(1)}, u32[]{:S(2)}, u32[]{:S(2)}) collective-permute-start(bf16[128,512]{1,0:T(8,128)(2,1)S(1)} %get-tuple-element.40.refs_7_.refs_1_), channel_id=1, source_target_pairs={{0,16},{4,20},{8,24},{12,28},{16,0},{20,4},{24,8},{28,12},{1,17},{... | collective-permute-start | bytes 393224 | tf_op jit(solution)/shard_map/ppermute | solution.py:28
  50.6 10.5 %collective-permute-start.17 = (bf16[128,512]{1,0:T(8,128)(2,1)S(1)}, bf16[128,512]{1,0:T(8,128)(2,1)S(1)}, u32[]{:S(2)}, u32[]{:S(2)}) collective-permute-start(bf16[128,512]{1,0:T(8,128)(2,1)S(1)} %get-tuple-element.40.refs_7_.refs_1_), channel_id=1, source_target_pairs={{0,8},{4,12},{8,0},{12,4},{16,24},{20,28},{24,16},{28,20},{1,9},{5... | collective-permute-start | bytes 393224 | tf_op jit(solution)/shard_map/ppermute | solution.py:28
  61.6 2.2 %collective-permute-start.18 = (bf16[2,320,512]{2,1,0:T(8,128)(2,1)S(1)}, bf16[2,320,512]{2,1,0:T(8,128)(2,1)S(1)}, u32[]{:S(2)}, u32[]{:S(2)}) collective-permute-start(bf16[2,320,512]{2,1,0:T(8,128)(2,1)S(1)} %shard_map.127), channel_id=1, source_target_pairs={{0,4},{4,0},{8,12},{12,8},{16,20},{20,16},{24,28},{28,24},{1,5},{5... | collective-permute-start | bytes 1966088 | tf_op jit(solution)/shard_map/ppermute | solution.py:28
  63.9 9.8 %collective-permute-start.19 = (bf16[320,512]{1,0:T(8,128)(2,1)S(1)}, bf16[320,512]{1,0:T(8,128)(2,1)S(1)}, u32[]{:S(2)}, u32[]{:S(2)}) collective-permute-start(bf16[320,512]{1,0:T(8,128)(2,1)S(1)} %get-tuple-element.42), channel_id=1, source_target_pairs={{0,1},{1,0},{2,3},{3,2},{4,5},{5,4},{6,7},{7,6},{8,9},{9,8},{10,11... | collective-permute-start | bytes 983048 | tf_op jit(solution)/shard_map/ppermute | solution.py:28

commit v5 on v4

--- a/solution.py
+++ b/solution.py
@@ -19,6 +19,8 @@
 CORES = 2
 f32, bf16 = jnp.float32, jnp.bfloat16
 VMEM = 16 * 2**20
+CUTS = 2
+LAST = 1
 DIRECT = 2
 LONG = 10**11
 
@@ -69,22 +71,23 @@
     return jax.ShapeDtypeStruct(dims, dtype)
 
 
-def blocks_kernel(steps, skip, tokens, *refs):
+def blocks_kernel(plan, skip, tokens, *refs):
     outs, sems = refs[skip:-1], refs[-1]
     rank, tensor = lax.axis_index("dp"), lax.axis_index("tensor")
     chip, core = rank // CORES, rank % CORES
     share = tokens.shape[0] // lax.axis_size("tensor")
     copies = []
-    for step, out in zip(steps, outs, strict=True):
+    for (step, start), out in zip(plan, outs, strict=True):
         depth = out.shape[1] // CORES
-        for j in range(out.shape[0] // share):
-            row = pl.multiple_of((tensor ^ j) * share, share)
+        size = min(out.shape[0], share)
+        for j in range(out.shape[0] // size):
+            row = pl.multiple_of((tensor ^ j) * share + start, size)
             for i in range(CORES):
                 col = pl.multiple_of(((chip ^ step) * CORES + (core ^ i)) * depth, depth)
                 copies.append(
                     pltpu.make_async_copy(
-                        tokens.at[pl.ds(row, share), pl.ds(col, depth)],
-                        out.at[pl.ds(j * share, share), pl.ds(i * depth, depth)],
+                        tokens.at[pl.ds(row, size), pl.ds(col, depth)],
+                        out.at[pl.ds(j * size, size), pl.ds(i * depth, depth)],
                         sems.at[len(copies)],
                     )
                 )
@@ -94,12 +97,12 @@
         copy.wait()
 
 
-def token_blocks(tokens, steps, share, depth, after):
-    slots = tokens.shape[0]
-    outs = [shape((slots if step < DIRECT else share, depth), bf16) for step in steps]
-    copies = sum(CORES * (out.shape[0] // share) for out in outs)
+def token_blocks(tokens, plan, sizes, depth, after):
+    outs = [shape((size, depth), bf16) for size in sizes]
+    share = tokens.shape[0] // lax.axis_size("tensor")
+    copies = sum(CORES * max(1, size // share) for size in sizes)
     return pl.pallas_call(
-        functools.partial(blocks_kernel, steps, len(after)),
+        functools.partial(blocks_kernel, plan, len(after)),
         out_shape=outs,
         in_specs=[pl.BlockSpec(memory_space=pl.ANY)] * (1 + len(after)),
         out_specs=[pl.BlockSpec(memory_space=pltpu.VMEM)] * len(outs),
@@ -263,41 +266,89 @@
         start += r.shape[0]
 
 
-def gradient_kernel(second, tokens, *refs):
+def mate_gradient_kernel(tokens, *refs):
+    deltas, (first, second) = refs[:-2], refs[-2:]
+    depth = tokens.shape[1] // CORES
+    value = lax.dot_general(
+        tokens[:, depth:],
+        jnp.concatenate([r[...] for r in deltas], axis=0),
+        (((0,), (0,)), ((), ())),
+        preferred_element_type=f32,
+    )
+    tile = first.shape[0]
+    low = lax.axis_index("group") == 0
+    first[...] = jnp.where(low, value[tile:], value[:tile]).astype(bf16)
+    second[...] = jnp.where(low, value[:tile], value[tile:]).astype(bf16)
+
+
+def own_gradient_kernel(tokens, *refs):
     deltas, out = refs[:-1], refs[-1]
     depth = tokens.shape[1] // CORES
     value = lax.dot_general(
-        tokens[:, depth * second : depth * (second + 1)],
+        tokens[:, :depth],
         jnp.concatenate([r[...] for r in deltas], axis=0),
         (((0,), (0,)), ((), ())),
         preferred_element_type=f32,
-    ).astype(out.dtype)
+    )
     tile = out.shape[1]
     for i in range(out.shape[0]):
         out[i] = value[i * tile : (i + 1) * tile]
 
 
-def core_sum_kernel(mine, received, keep, send):
-    group = lax.axis_index("group")
-    cols = keep.shape[1] // 2
-    keep[...] = mine[group] + received[group].astype(f32)
-    value = (mine[1 - group] + received[1 - group].astype(f32)).astype(bf16)
-    send[:, :cols] = value[:, cols:]
-    send[:, cols:] = value[:, :cols]
-
-
-def second_adam_kernel(staying, incoming, keep, back, master, moment, variance):
+def send_kernel(mine, received, *outs):
+    other = 1 - lax.axis_index("group")
+    cols = received.shape[1] // 2
+    rows = outs[0].shape[0]
+    for i, out in enumerate(outs):
+        at = slice(i * rows, (i + 1) * rows)
+        value = (mine[other, at] + received[at].astype(f32)).astype(bf16)
+        out[:, :cols] = value[:, cols:]
+        out[:, cols:] = value[:, :cols]
+
+
+def second_adam_kernel(cut, staying, incoming, mine, received, back, *refs):
+    outs, results, sems = refs[-7:-4], refs[-4:-1], refs[-1]
     _, half, rows, cols = staying.shape
     group = lax.axis_index("group")
-    for k in range(half):
+    size = back.shape[0] // rows
+    for k in range(size):
+        block = cut * size + k
         for i, states in enumerate((staying, incoming)):
-            here = (slice(k * rows, (k + 1) * rows), slice(i * cols, (i + 1) * cols))
+            at = slice(i * cols, (i + 1) * cols)
             there = pl.ds(pl.multiple_of((group ^ i) * cols, cols), cols)
-            gradient = keep[here] + back[here].astype(f32)
-            values = [states[j, k].astype(f32) for j in range(3)]
+            tile_rows = slice(block * rows, (block + 1) * rows)
+            here = slice(k * rows, (k + 1) * rows)
+            gradient = mine[group, tile_rows, at] + received[tile_rows, at].astype(f32)
+            gradient = gradient + back[here, at].astype(f32)
+            values = [states[j, block].astype(f32) for j in range(3)]
             result = adam_update(*values, gradient, second_step)
-            for ref, value in zip((master, moment, variance), result, strict=True):
-                ref[k * rows : (k + 1) * rows, there] = value
+            for ref, value in zip(results, result, strict=True):
+                ref[here, there] = value
+    total = back.shape[0]
+    copies = [
+        pltpu.make_async_copy(ref, out.at[pl.ds(cut * total, total)], sems.at[i])
+        for i, (ref, out) in enumerate(zip(results, outs, strict=True))
+    ]
+    for copy in copies:
+        copy.start()
+    for copy in copies:
+        copy.wait()
+
+
+def second_adam(cut, staying, incoming, mine, received, back, done):
+    rows, cols = received.shape
+    whole = pl.BlockSpec(memory_space=pltpu.VMEM)
+    anywhere = pl.BlockSpec(memory_space=pl.ANY)
+    return pl.pallas_call(
+        functools.partial(second_adam_kernel, cut),
+        out_shape=[shape((rows, cols), f32)] * 3,
+        in_specs=[whole] * 5 + [anywhere] * len(done),
+        out_specs=[anywhere] * 3,
+        scratch_shapes=[pltpu.VMEM(back.shape, f32)] * 3 + [pltpu.SemaphoreType.DMA((3,))],
+        input_output_aliases={5 + i: i for i in range(len(done))},
+        compiler_params=pltpu.CompilerParams(vmem_limit_bytes=VMEM),
+        cost_estimate=pl.CostEstimate(flops=0, bytes_accessed=10**6, transcendentals=0),
+    )(staying, incoming, mine, received, back, *done)
 
 
 def local(tokens, cotangent, counts, old_offsets, old_master, old_moment, old_variance, old_grad):
@@ -327,36 +378,45 @@
         first_weights_kernel, shape((count + 2, rows, old_cols), bf16), *windows, after=[ahead]
     )
 
-    def token_block(of_chip, of_tensor):
-        return jnp.concatenate(
-            [
-                lax.dynamic_slice(
-                    tokens, (of_tensor * share, of_chip * depth + (core ^ i) * half), (share, half)
-                )
-                for i in range(CORES)
-            ],
-            axis=1,
-        )
-
-    def blocks_of(steps, after):
-        if half % LANES == 0 and share % 16 == 0:
-            return token_blocks(tokens, steps, share, depth, after)
+    aligned = half % LANES == 0 and share % 16 == 0
+    last = share // LAST if aligned and share % (16 * LAST) == 0 else share
+    plan = [(step, 0) for step in range(1, chips - 1)]
+    plan += [(chips - 1, start) for start in range(0, share, last)]
+    sizes = [slots if step < DIRECT else share for step in range(1, chips - 1)]
+    sizes += [last] * (share // last)
+
+    def blocks_of(plan, sizes, after):
+        if aligned:
+            return token_blocks(tokens, plan, sizes, depth, after)
         return [
             jnp.concatenate(
                 [
-                    token_block(chip ^ step, tensor ^ j)
-                    for j in range(tensors if step < DIRECT else 1)
+                    jnp.concatenate(
+                        [
+                            lax.dynamic_slice(
+                                tokens,
+                                (
+                                    (tensor ^ j) * share + start,
+                                    (chip ^ step) * depth + (core ^ i) * half,
+                                ),
+                                (min(size, share), half),
+                            )
+                            for i in range(CORES)
+                        ],
+                        axis=1,
+                    )
+                    for j in range(max(1, size // share))
                 ]
             )
-            for step in steps
+            for (step, start), size in zip(plan, sizes, strict=True)
         ]
 
-    leaving_blocks = blocks_of(range(1, chips), [])
-
-    cleared = call(place_kernel, shape(window.shape[1:], bf16), window[0], flops=LONG)
     other = swap(window, "group", 1)
-    arrived = [swap(b, "dp", step * CORES) for step, b in enumerate(leaving_blocks, 1)]
-    arrived = [lax.optimization_barrier((a, cleared))[0] for a in arrived]
+    leaving_blocks = blocks_of(plan, sizes, [])
+    arrived = [
+        (step, swap(b, "dp", step * CORES))
+        for (step, _), b in zip(plan, leaving_blocks, strict=True)
+    ]
 
     mate_window = swap(window, "dp", 1)
     tile = shape((3, count // 2, rows, old_cols), f32)
@@ -364,7 +424,7 @@
         first_states_kernel,
         [tile, tile, shape((2, 3, 1, rows, old_cols), bf16)],
         *windows,
-        after=[mate_window],
+        after=leaving_blocks[:1],
     )
 
     ends = jnp.concatenate([ends[:, :, 0], jnp.stack([other[0], other[-1]])[:, None]], axis=1)
@@ -374,9 +434,12 @@
     turned = call(
         live_kernel, shape((slots, cols), bf16), counts, cotangent, scalars=1, after=[other]
     )
-    blocks = [[b] for b in [*blocks_of(range(1), [other]), *arrived]]
-    for block in blocks[DIRECT:]:
-        block += [swap(block[0], "tensor", j) for j in range(1, tensors)]
+    blocks = [blocks_of([(0, 0)], [slots], [other])]
+    for step in range(1, chips):
+        block = [b for at, b in arrived if at == step]
+        if step >= DIRECT:
+            block += [swap(b, "tensor", j) for j in range(1, tensors) for b in list(block)]
+        blocks.append(block)
 
     far, _ = lax.optimization_barrier((jnp.stack([outer[0], outer[3]]), blocks[DIRECT]))
 
@@ -418,9 +481,9 @@
         delta_kernel, [shape((slots, cols), bf16)] * 2, total, *back, turned
     )
 
-    deltas = [delta] + [swap(delta, "dp", step * CORES) for step in steps]
-
-    flat = [p for step in (0, *steps) for p in blocks[step]]
+    deltas = [delta] + [swap(delta, "dp", step * CORES) for step in range(1, chips)]
+
+    flat = [p for step in range(chips) for p in blocks[step]]
     gathered = call(
         gather_kernel,
         shape((chips * slots, depth), bf16),
@@ -430,30 +493,17 @@
     )
     flops = 2 * half * cols * chips * slots
     tile = half // groups
-    to_mate, mine = (
-        call(
-            functools.partial(gradient_kernel, second),
-            shape((groups, tile, cols), dtype),
-            gathered,
-            *deltas,
-            flops=flops,
-        )
-        for second, dtype in ((1, bf16), (0, f32))
-    )
-    keep, send = call(
-        core_sum_kernel,
-        [shape((tile, cols), f32), shape((tile, cols), bf16)],
-        mine,
-        swap(to_mate, "dp", 1),
-    )
-    new = call(
-        second_adam_kernel,
-        [shape((tile, cols), f32)] * 3,
-        staying,
-        incoming,
-        keep,
-        swap(send, "group", 1),
-    )
+    cuts = CUTS if tile % (CUTS * 16) == 0 and leaving.shape[1] % CUTS == 0 else 1
+    first, second = call(
+        mate_gradient_kernel, [shape((tile, cols), bf16)] * 2, gathered, *deltas, flops=flops
+    )
+    first = swap(first, "dp", 1)
+    mine = call(own_gradient_kernel, shape((groups, tile, cols), f32), gathered, *deltas, flops=flops)
+    second = swap(second, "dp", 1)
+    sends = call(send_kernel, [shape((tile // cuts, cols), bf16)] * cuts, mine, first)
+    new = []
+    for cut, send in enumerate(sends):
+        new = second_adam(cut, staying, incoming, mine, second, swap(send, "group", 1), new)
     activated = call(natural_kernel, shape((slots, cols), bf16), activated)
     return (activated, *new)
 

time: 75.9 us -> 74.8 us (0.986)
  waiting for transfers between devices: 31.3 us -> 25.9 us
  starting transfers between devices: 24.9 us -> 28.1 us
  local copies, waits for them, and re-layouts: 4.17 us -> 5.87 us
    ppermute x19 -> x21, waiting for transfers between devices: 31.3 us -> 25.9 us  [swap(): return lax.ppermute(value, axis, pairs)]
    ppermute x19 -> x21, starting transfers between devices: 24.1 us -> 27.3 us  [swap(): return lax.ppermute(value, axis, pairs)]
    pallas_call x17 -> x16, Pallas kernels: 13.1 us -> 10 us  [call(): pl.pallas_call(body, out_shape=shapes, in_specs=[small] * scalars + [whol...]
    pallas_call x2 -> x4, Pallas kernels: 1.11 us -> 3.57 us  [the longest x2 2.56 us: second_adam(): pl.pallas_call(functools.partial(second_adam_kernel, cut), out_shape=[sha...]
    unnamed x20 -> x24, local copies, waits for them, and re-layouts: 4.16 us -> 5.85 us
  transfers between devices with their start and end apart: 20 -> 22, of which waited for: 11 -> 11; matrix products, arithmetic and copies ran while one was open for 0% -> 0% of each run, Pallas kernels for 14% -> 14%
where the time goes in v5:
time: 74.8 us; the launch traced here: 74.5 us
  starting transfers between devices  28.1 us (38%)
  waiting for transfers between devices  25.9 us (35%)
  Pallas kernels  13.6 us (18%)
  local copies, waits for them, and re-layouts  5.87 us (8%)
  between operations  0.91 us (1%)
    ppermute x21, starting transfers between devices, swap(): return lax.ppermute(value, axis, pairs)  27.3 us
    ppermute x21, waiting for transfers between devices, swap(): return lax.ppermute(value, axis, pairs)  25.9 us
    pallas_call x16, Pallas kernels, call(): pl.pallas_call(body, out_shape=shapes, in_specs=[small] * scalars + [whol...  10 us
    unnamed x24, local copies, waits for them, and re-layouts  5.85 us
    pallas_call x2, Pallas kernels, second_adam(): pl.pallas_call(functools.partial(second_adam_kernel, cut), out_shape=[sha...  2.56 us
  transfers between devices with their start and end apart: 22, of which 11 were waited for; matrix products, arithmetic and copies ran while one was open for 0% of the time, Pallas kernels for 14%

profile of v5, /device:TPU:0, one launch (start us, length us, event | category | flops | bytes accessed | tf_op | source)
XLA Modules:
  0.0 74.5 jit_solution(14751200942533719684)
XLA Ops:
  0.7 1.1 %copy-done.5 = f32[1,1,204800]{2,1,0:T(1,128)S(1)} copy-done((f32[1,1,204800]{2,1,0:T(1,128)S(1)}, f32[1,1,204800]{2,1,0:T(1,128)}, u32[]{:S(2)}) %copy-start.5) | copy-done | bytes 819224
  2.5 1.4 %shard_map.112.refs_1_ = bf16[10,80,256]{2,1,0:T(8,128)(2,1)} custom-call(f32[10,160,128]{2,1,0:T(8,128)S(1)} %bitcast.21, f32[10,160,128]{2,1,0:T(8,128)S(1)} %bitcast.23, f32[10,160,128]{2,1,0:T(8,128)S(1)} %bitcast.25, f32[10,160,128]{2,1,0:T(8,128)S(1)} %bitcast.27, f32[8,128]{1,0:T(8,128)S(1)} %shard_map.111.refs_4_), custom_call_target="tpu_custom_call" | custom-call | bytes 3276800 | tf_op jit(solution)/shard_map/pallas_call | solution.py:58
  4.0 3.0 %collective-permute-start = (bf16[10,80,256]{2,1,0:T(8,128)(2,1)}, bf16[10,80,256]{2,1,0:T(8,128)(2,1)S(1)}, u32[]{:S(2)}, u32[]{:S(2)}) collective-permute-start(bf16[10,80,256]{2,1,0:T(8,128)(2,1)} %shard_map.112.refs_1_), channel_id=1, source_target_pairs={{0,1},{1,0},{2,3},{3,2},{4,5},{5,4},{6,7},{7,6},{8,9},{9,8},{10,11... | collective-permute-start | bytes 1228808 | tf_op jit(solution)/shard_map/ppermute | solution.py:30
  6.9 0.9 %shard_map.114 = (bf16[128,1280]{1,0:T(8,128)(2,1)S(1)}, bf16[64,1280]{1,0:T(8,128)(2,1)}, bf16[64,1280]{1,0:T(8,128)(2,1)}) custom-call(bf16[128,5120]{1,0:T(8,128)(2,1)S(1)} %copy-done), custom_call_target="tpu_custom_call" | custom-call | bytes 1000000 | tf_op jit(solution)/shard_map/pallas_call | solution.py:104
  8.6 2.6 %collective-permute-start.4 = (bf16[64,1280]{1,0:T(8,128)(2,1)}, bf16[64,1280]{1,0:T(8,128)(2,1)}, u32[]{:S(2)}, u32[]{:S(2)}) collective-permute-start(bf16[64,1280]{1,0:T(8,128)(2,1)} %get-tuple-element.29), channel_id=1, source_target_pairs={{0,16},{4,20},{8,24},{12,28},{16,0},{20,4},{24,8},{28,12},{1,17},{... | collective-permute-start | bytes 491528 | tf_op jit(solution)/shard_map/ppermute | solution.py:30
  11.2 1.3 %collective-permute-start.7 = (bf16[64,1280]{1,0:T(8,128)(2,1)}, bf16[64,1280]{1,0:T(8,128)(2,1)S(1)}, u32[]{:S(2)}, u32[]{:S(2)}) collective-permute-start(bf16[64,1280]{1,0:T(8,128)(2,1)} %get-tuple-element.33), channel_id=1, source_target_pairs={{0,24},{4,28},{8,16},{12,20},{16,8},{20,12},{24,0},{28,4},{1,25},{... | collective-permute-start | bytes 491528 | tf_op jit(solution)/shard_map/ppermute | solution.py:30
  12.5 1.1 %copy-done.4 = f32[1,1,204800]{2,1,0:T(1,128)S(1)} copy-done((f32[1,1,204800]{2,1,0:T(1,128)S(1)}, f32[1,1,204800]{2,1,0:T(1,128)}, u32[]{:S(2)}) %copy-start.4) | copy-done | bytes 819224
  13.7 1.1 %copy-done.6 = f32[1,1,204800]{2,1,0:T(1,128)S(1)} copy-done((f32[1,1,204800]{2,1,0:T(1,128)S(1)}, f32[1,1,204800]{2,1,0:T(1,128)}, u32[]{:S(2)}) %copy-start.6) | copy-done | bytes 819224
  14.8 1.0 %copy-done.8 = bf16[128,1280]{1,0:T(8,128)(2,1)S(1)} copy-done((bf16[128,1280]{1,0:T(8,128)(2,1)S(1)}, bf16[128,1280]{1,0:T(8,128)(2,1)}, u32[]{:S(2)}) %copy-start.8) | copy-done | bytes 327704
  17.5 3.2 %collective-permute-start.1 = (bf16[10,80,256]{2,1,0:T(8,128)(2,1)}, bf16[10,80,256]{2,1,0:T(8,128)(2,1)S(1)}, u32[]{:S(2)}, u32[]{:S(2)}) collective-permute-start(bf16[10,80,256]{2,1,0:T(8,128)(2,1)} %shard_map.112.refs_1_), channel_id=1, source_target_pairs={{0,4},{4,0},{8,12},{12,8},{16,20},{20,16},{24,28},{28,24},{1,5},{5... | collective-permute-start | bytes 1228808 | tf_op jit(solution)/shard_map/ppermute | solution.py:30
  20.7 1.6 %collective-permute-start.11 = (bf16[128,1280]{1,0:T(8,128)(2,1)S(1)}, bf16[128,1280]{1,0:T(8,128)(2,1)S(1)}, u32[]{:S(2)}, u32[]{:S(2)}) collective-permute-start(bf16[128,1280]{1,0:T(8,128)(2,1)S(1)} %copy-done.8), channel_id=1, source_target_pairs={{0,8},{4,12},{8,0},{12,4},{16,24},{20,28},{24,16},{28,20},{1,9},{5... | collective-permute-start | bytes 983048 | tf_op jit(solution)/shard_map/ppermute | solution.py:30
  22.3 1.3 %collective-permute-done.4.refs_0_.refs_2_ = bf16[64,1280]{1,0:T(8,128)(2,1)} collective-permute-done((bf16[64,1280]{1,0:T(8,128)(2,1)}, bf16[64,1280]{1,0:T(8,128)(2,1)}, u32[]{:S(2)}, u32[]{:S(2)}) %collective-permute-start.4) | collective-permute-done | bytes 163872 | tf_op jit(solution)/shard_map/ppermute | solution.py:30
  23.6 1.5 %collective-permute-start.5 = (bf16[64,1280]{1,0:T(8,128)(2,1)}, bf16[64,1280]{1,0:T(8,128)(2,1)S(1)}, u32[]{:S(2)}, u32[]{:S(2)}) collective-permute-start(bf16[64,1280]{1,0:T(8,128)(2,1)} %collective-permute-done.4.refs_0_.refs_2_), channel_id=1, source_target_pairs={{0,2},{2,0},{1,3},{3,1},{4,6},{6,4},{5,7},{7,5},{8,10},{10,8},{9,1... | collective-permute-start | bytes 491528 | tf_op jit(solution)/shard_map/ppermute | solution.py:30
  25.7 4.5 %collective-permute-done.5.refs_1_.refs_3_ = bf16[64,1280]{1,0:T(8,128)(2,1)S(1)} collective-permute-done((bf16[64,1280]{1,0:T(8,128)(2,1)}, bf16[64,1280]{1,0:T(8,128)(2,1)S(1)}, u32[]{:S(2)}, u32[]{:S(2)}) %collective-permute-start.5) | collective-permute-done | bytes 163872 | tf_op jit(solution)/shard_map/ppermute | solution.py:30
  31.7 1.2 %shard_map.116 = (bf16[8,80,512]{2,1,0:T(8,128)(2,1)S(1)}, bf16[8,80,512]{2,1,0:T(8,128)(2,1)S(1)}) custom-call(s32[4,9]{1,0:T(4,128)S(1)} %copy-done.10, bf16[10,80,256]{2,1,0:T(8,128)(2,1)} %shard_map.112.refs_1_, bf16[10,80,256]{2,1,0:T(8,128)(2,1)S(1)} %collective-permute-done.refs_0_.refs_2_, bf16[10,80,256]{2,1,0:T(8,128)(2,1)S(1)} %collective-permute-done.1.refs_3_, ...), custom_call_target="tpu_custom_call" | custom-call | bytes 1802384 | tf_op jit(solution)/shard_map/pallas_call | solution.py:58
  33.3 3.2 %collective-permute-start.9 = (bf16[128,512]{1,0:T(8,128)(2,1)S(1)}, bf16[128,512]{1,0:T(8,128)(2,1)S(1)}, u32[]{:S(2)}, u32[]{:S(2)}) collective-permute-start(bf16[128,512]{1,0:T(8,128)(2,1)S(1)} %shard_map.118.refs_4_), channel_id=1, source_target_pairs={{0,24},{4,28},{8,16},{12,20},{16,8},{20,12},{24,0},{28,4},{1,25},{... | collective-permute-start | bytes 393224 | tf_op jit(solution)/shard_map/ppermute | solution.py:30
  36.5 1.3 %shard_map.119.refs_3_ = bf16[128,512]{1,0:T(8,128)(2,1)S(1)} custom-call(bf16[64,1280]{1,0:T(8,128)(2,1)} %collective-permute-done.4.refs_0_.refs_2_, bf16[64,1280]{1,0:T(8,128)(2,1)S(1)} %collective-permute-done.5.refs_1_.refs_3_, bf16[640,512]{1,0:T(8,128)(2,1)S(1)} %bitcast.14, bf16[640,512]{1,0:T(8,128)(2,1)S(1)} %bitcast.18, ...), custom_call_target="tpu_custom_call" | custom-call | flops 167772160 | bytes 1638400 | tf_op jit(solution)/shard_map/pallas_call | solution.py:58
  38.3 1.3 %collective-permute-start.12 = (bf16[128,512]{1,0:T(8,128)(2,1)S(1)}, bf16[128,512]{1,0:T(8,128)(2,1)S(1)}, u32[]{:S(2)}, u32[]{:S(2)}) collective-permute-start(bf16[128,512]{1,0:T(8,128)(2,1)S(1)} %shard_map.120.refs_5_), channel_id=1, source_target_pairs={{0,8},{4,12},{8,0},{12,4},{16,24},{20,28},{24,16},{28,20},{1,9},{5... | collective-permute-start | bytes 393224 | tf_op jit(solution)/shard_map/ppermute | solution.py:30
  39.5 0.8 %shard_map.124 = (bf16[3,4,80,256]{3,2,1,0:T(8,128)(2,1)S(1)}, f32[3,4,80,256]{3,2,1,0:T(8,128)S(1)}) custom-call(s32[4,9]{1,0:T(4,128)S(1)} %copy-done.10, f32[3,4,80,256]{3,2,1,0:T(8,128)S(1)} %get-tuple-element.35.refs_1_, f32[3,4,80,256]{3,2,1,0:T(8,128)S(1)} %get-tuple-element.36.refs_2_, bf16[4,80,256]{2,1,0:T(8,128)(2,1)S(1)} %collective-permute-done.13.refs_3_, ...), custom_call_target="tpu_custom_call" | custom-call | bytes 2293904 | tf_op jit(solution)/shard_map/pallas_call | solution.py:58
  40.4 1.3 %collective-permute-start.14 = (bf16[3,4,80,256]{3,2,1,0:T(8,128)(2,1)S(1)}, bf16[3,4,80,256]{3,2,1,0:T(8,128)(2,1)S(1)}, u32[]{:S(2)}, u32[]{:S(2)}) collective-permute-start(bf16[3,4,80,256]{3,2,1,0:T(8,128)(2,1)S(1)} %get-tuple-element.38), channel_id=1, source_target_pairs={{0,1},{1,0},{2,3},{3,2},{4,5},{5,4},{6,7},{7,6},{8,9},{9,8},{10,11... | collective-permute-start | bytes 1474568 | tf_op jit(solution)/shard_map/ppermute | solution.py:30
  42.0 4.8 %collective-permute-done.12.refs_3_ = bf16[128,512]{1,0:T(8,128)(2,1)S(1)} collective-permute-done((bf16[128,512]{1,0:T(8,128)(2,1)S(1)}, bf16[128,512]{1,0:T(8,128)(2,1)S(1)}, u32[]{:S(2)}, u32[]{:S(2)}) %collective-permute-start.12) | collective-permute-done | bytes 131104 | tf_op jit(solution)/shard_map/ppermute | solution.py:30
  47.1 2.9 %collective-permute-start.17 = (bf16[128,512]{1,0:T(8,128)(2,1)S(1)}, bf16[128,512]{1,0:T(8,128)(2,1)S(1)}, u32[]{:S(2)}, u32[]{:S(2)}) collective-permute-start(bf16[128,512]{1,0:T(8,128)(2,1)S(1)} %get-tuple-element.39.refs_7_.refs_1_), channel_id=1, source_target_pairs={{0,24},{4,28},{8,16},{12,20},{16,8},{20,12},{24,0},{28,4},{1,25},{... | collective-permute-start | bytes 393224 | tf_op jit(solution)/shard_map/ppermute | solution.py:30
  50.0 1.5 %collective-permute-start.15 = (bf16[128,512]{1,0:T(8,128)(2,1)S(1)}, bf16[128,512]{1,0:T(8,128)(2,1)S(1)}, u32[]{:S(2)}, u32[]{:S(2)}) collective-permute-start(bf16[128,512]{1,0:T(8,128)(2,1)S(1)} %get-tuple-element.39.refs_7_.refs_1_), channel_id=1, source_target_pairs={{0,8},{4,12},{8,0},{12,4},{16,24},{20,28},{24,16},{28,20},{1,9},{5... | collective-permute-start | bytes 393224 | tf_op jit(solution)/shard_map/ppermute | solution.py:30
  51.5 1.6 %collective-permute-done.14.refs_6_.incoming = bf16[3,4,80,256]{3,2,1,0:T(8,128)(2,1)S(1)} collective-permute-done((bf16[3,4,80,256]{3,2,1,0:T(8,128)(2,1)S(1)}, bf16[3,4,80,256]{3,2,1,0:T(8,128)(2,1)S(1)}, u32[]{:S(2)}, u32[]{:S(2)}) %collective-permute-start.14) | collective-permute-done | bytes 491552 | tf_op jit(solution)/shard_map/ppermute | solution.py:30
  53.1 1.0 %shard_map.125.refs_0_ = bf16[512,1280]{1,0:T(8,128)(2,1)S(1)} custom-call(bf16[128,1280]{1,0:T(8,128)(2,1)S(1)} %shard_map.113.refs_0_, bf16[128,1280]{1,0:T(8,128)(2,1)S(1)} %collective-permute-done.11.refs_0_.refs_1_, bf16[64,1280]{1,0:T(8,128)(2,1)} %collective-permute-done.4.refs_0_.refs_2_, ...), custom_call_target="tpu_custom_call" | custom-call | flops 99999997952 | bytes 1310720 | tf_op jit(solution)/shard_map/pallas_call | solution.py:58
  54.1 1.3 %collective-permute-done.17.refs_4_ = bf16[128,512]{1,0:T(8,128)(2,1)S(1)} collective-permute-done((bf16[128,512]{1,0:T(8,128)(2,1)S(1)}, bf16[128,512]{1,0:T(8,128)(2,1)S(1)}, u32[]{:S(2)}, u32[]{:S(2)}) %collective-permute-start.17) | collective-permute-done | bytes 131104 | tf_op jit(solution)/shard_map/ppermute | solution.py:30
  55.4 5.7 %collective-permute-done.16.refs_3_ = bf16[128,512]{1,0:T(8,128)(2,1)S(1)} collective-permute-done((bf16[128,512]{1,0:T(8,128)(2,1)S(1)}, bf16[128,512]{1,0:T(8,128)(2,1)S(1)}, u32[]{:S(2)}, u32[]{:S(2)}) %collective-permute-start.16) | collective-permute-done | bytes 131104 | tf_op jit(solution)/shard_map/ppermute | solution.py:30
  63.9 1.5 %collective-permute-start.20 = (bf16[160,512]{1,0:T(8,128)(2,1)S(1)}, bf16[160,512]{1,0:T(8,128)(2,1)S(1)}, u32[]{:S(2)}, u32[]{:S(2)}) collective-permute-start(bf16[160,512]{1,0:T(8,128)(2,1)S(1)} %get-tuple-element.42), channel_id=1, source_target_pairs={{0,1},{1,0},{2,3},{3,2},{4,5},{5,4},{6,7},{7,6},{8,9},{9,8},{10,11... | collective-permute-start | bytes 491528 | tf_op jit(solution)/shard_map/ppermute | solution.py:30
  66.1 4.3 %collective-permute-done.21.back = bf16[160,512]{1,0:T(8,128)(2,1)S(1)} collective-permute-done((bf16[160,512]{1,0:T(8,128)(2,1)S(1)}, bf16[160,512]{1,0:T(8,128)(2,1)S(1)}, u32[]{:S(2)}, u32[]{:S(2)}) %collective-permute-start.21) | collective-permute-done | bytes 163872 | tf_op jit(solution)/shard_map/ppermute | solution.py:30
  70.5 1.3 %shard_map.129 = (f32[320,512]{1,0:T(8,128)}, f32[320,512]{1,0:T(8,128)}, f32[320,512]{1,0:T(8,128)}) custom-call(f32[3,4,80,256]{3,2,1,0:T(8,128)S(1)} %get-tuple-element.37.staying, bf16[3,4,80,256]{3,2,1,0:T(8,128)(2,1)S(1)} %collective-permute-done.14.refs_6_.incoming, f32[2,320,512]{2,1,0:T(8,128)S(1)} %shard_map.126.refs_0_.mine, ...), custom_call_target="tpu_custom_call" | custom-call | bytes 1000000 | tf_op jit(solution)/shard_map/pallas_call | solution.py:342
  71.8 1.4 %collective-permute-done.20.back = bf16[160,512]{1,0:T(8,128)(2,1)S(1)} collective-permute-done((bf16[160,512]{1,0:T(8,128)(2,1)S(1)}, bf16[160,512]{1,0:T(8,128)(2,1)S(1)}, u32[]{:S(2)}, u32[]{:S(2)}) %collective-permute-start.20) | collective-permute-done | bytes 163872 | tf_op jit(solution)/shard_map/ppermute | solution.py:30
  73.2 1.3 %shard_map.130 = (f32[320,512]{1,0:T(8,128)}, f32[320,512]{1,0:T(8,128)}, f32[320,512]{1,0:T(8,128)}) custom-call(f32[3,4,80,256]{3,2,1,0:T(8,128)S(1)} %get-tuple-element.37.staying, bf16[3,4,80,256]{3,2,1,0:T(8,128)(2,1)S(1)} %collective-permute-done.14.refs_6_.incoming, ...), custom_call_target="tpu_custom_call", output_to_operand_aliasing={{0}: (5, {}), {1}: (6, {}), {2}: (7, {})} | custom-call | bytes 1000000 | tf_op jit(solution)/shard_map/pallas_call | solution.py:342
  (61 shorter events, 10.1 us)
Async XLA Ops:
  0.6 1.1 %copy-start.5 = (f32[1,1,204800]{2,1,0:T(1,128)S(1)}, f32[1,1,204800]{2,1,0:T(1,128)}, u32[]{:S(2)}) copy-start(f32[1,1,204800]{2,1,0:T(1,128)} %param.15) | copy-start | bytes 2457604
  0.6 1.4 %copy-start.3 = (f32[1,1,204800]{2,1,0:T(1,128)S(1)}, f32[1,1,204800]{2,1,0:T(1,128)}, u32[]{:S(2)}) copy-start(f32[1,1,204800]{2,1,0:T(1,128)} %param.14) | copy-start | bytes 2457604
  0.7 1.6 %copy-start.2 = (f32[1,1,204800]{2,1,0:T(1,128)S(1)}, f32[1,1,204800]{2,1,0:T(1,128)}, u32[]{:S(2)}) copy-start(f32[1,1,204800]{2,1,0:T(1,128)} %param.13) | copy-start | bytes 2457604
  0.7 1.9 %copy-start.1 = (f32[1,1,204800]{2,1,0:T(1,128)S(1)}, f32[1,1,204800]{2,1,0:T(1,128)}, u32[]{:S(2)}) copy-start(f32[1,1,204800]{2,1,0:T(1,128)} %param.12) | copy-start | bytes 2457604
  2.5 4.4 %copy-start = (bf16[128,5120]{1,0:T(8,128)(2,1)S(1)}, bf16[128,5120]{1,0:T(8,128)(2,1)}, u32[]{:S(2)}) copy-start(bf16[128,5120]{1,0:T(8,128)(2,1)} %tokens.3) | copy-start | bytes 3932164
  4.0 12.6 %collective-permute-start = (bf16[10,80,256]{2,1,0:T(8,128)(2,1)}, bf16[10,80,256]{2,1,0:T(8,128)(2,1)S(1)}, u32[]{:S(2)}, u32[]{:S(2)}) collective-permute-start(bf16[10,80,256]{2,1,0:T(8,128)(2,1)} %shard_map.112.refs_1_), channel_id=1, source_target_pairs={{0,1},{1,0},{2,3},{3,2},{4,5},{5,4},{6,7},{7,6},{8,9},{9,8},{10,11... | collective-permute-start | bytes 1228808 | tf_op jit(solution)/shard_map/ppermute | solution.py:30
  8.6 15.1 %collective-permute-start.4 = (bf16[64,1280]{1,0:T(8,128)(2,1)}, bf16[64,1280]{1,0:T(8,128)(2,1)}, u32[]{:S(2)}, u32[]{:S(2)}) collective-permute-start(bf16[64,1280]{1,0:T(8,128)(2,1)} %get-tuple-element.29), channel_id=1, source_target_pairs={{0,16},{4,20},{8,24},{12,28},{16,0},{20,4},{24,8},{28,12},{1,17},{... | collective-permute-start | bytes 491528 | tf_op jit(solution)/shard_map/ppermute | solution.py:30
  11.2 14.0 %collective-permute-start.7 = (bf16[64,1280]{1,0:T(8,128)(2,1)}, bf16[64,1280]{1,0:T(8,128)(2,1)S(1)}, u32[]{:S(2)}, u32[]{:S(2)}) collective-permute-start(bf16[64,1280]{1,0:T(8,128)(2,1)} %get-tuple-element.33), channel_id=1, source_target_pairs={{0,24},{4,28},{8,16},{12,20},{16,8},{20,12},{24,0},{28,4},{1,25},{... | collective-permute-start | bytes 491528 | tf_op jit(solution)/shard_map/ppermute | solution.py:30
  12.5 1.1 %copy-start.4 = (f32[1,1,204800]{2,1,0:T(1,128)S(1)}, f32[1,1,204800]{2,1,0:T(1,128)}, u32[]{:S(2)}) copy-start(f32[1,1,204800]{2,1,0:T(1,128)} %param.14) | copy-start | bytes 2457604
  13.7 1.1 %copy-start.6 = (f32[1,1,204800]{2,1,0:T(1,128)S(1)}, f32[1,1,204800]{2,1,0:T(1,128)}, u32[]{:S(2)}) copy-start(f32[1,1,204800]{2,1,0:T(1,128)} %param.15) | copy-start | bytes 2457604
  16.7 14.2 %copy-start.9 = (bf16[128,512]{1,0:T(8,128)(2,1)S(1)}, bf16[128,512]{1,0:T(8,128)(2,1)}, u32[]{:S(2)}) copy-start(bf16[128,512]{1,0:T(8,128)(2,1)} %refs_1_.1) | copy-start | bytes 393220
  16.7 14.2 %copy-start.11 = (s32[16]{0:T(128)S(1)}, s32[16]{0:T(128)}, u32[]{:S(2)}) copy-start(s32[16]{0:T(128)} %refs_0_.4) | copy-start | bytes 196
  16.7 9.0 %collective-permute-start.3 = (bf16[4,80,256]{2,1,0:T(8,128)(2,1)S(1)}, bf16[4,80,256]{2,1,0:T(8,128)(2,1)S(1)}, u32[]{:S(2)}, u32[]{:S(2)}) collective-permute-start(bf16[4,80,256]{2,1,0:T(8,128)(2,1)S(1)} %get-tuple-element.53), channel_id=1, source_target_pairs={{4,8},{8,4},{12,16},{16,12},{20,24},{24,20},{5,9},{9,5},{13,17},{1... | collective-permute-start | bytes 491528 | tf_op jit(solution)/shard_map/ppermute | solution.py:37
  17.5 12.7 %collective-permute-start.1 = (bf16[10,80,256]{2,1,0:T(8,128)(2,1)}, bf16[10,80,256]{2,1,0:T(8,128)(2,1)S(1)}, u32[]{:S(2)}, u32[]{:S(2)}) collective-permute-start(bf16[10,80,256]{2,1,0:T(8,128)(2,1)} %shard_map.112.refs_1_), channel_id=1, source_target_pairs={{0,4},{4,0},{8,12},{12,8},{16,20},{20,16},{24,28},{28,24},{1,5},{5... | collective-permute-start | bytes 1228808 | tf_op jit(solution)/shard_map/ppermute | solution.py:30
  20.7 17.2 %collective-permute-start.11 = (bf16[128,1280]{1,0:T(8,128)(2,1)S(1)}, bf16[128,1280]{1,0:T(8,128)(2,1)S(1)}, u32[]{:S(2)}, u32[]{:S(2)}) collective-permute-start(bf16[128,1280]{1,0:T(8,128)(2,1)S(1)} %copy-done.8), channel_id=1, source_target_pairs={{0,8},{4,12},{8,0},{12,4},{16,24},{20,28},{24,16},{28,20},{1,9},{5... | collective-permute-start | bytes 983048 | tf_op jit(solution)/shard_map/ppermute | solution.py:30
  23.6 6.5 %collective-permute-start.5 = (bf16[64,1280]{1,0:T(8,128)(2,1)}, bf16[64,1280]{1,0:T(8,128)(2,1)S(1)}, u32[]{:S(2)}, u32[]{:S(2)}) collective-permute-start(bf16[64,1280]{1,0:T(8,128)(2,1)} %collective-permute-done.4.refs_0_.refs_2_), channel_id=1, source_target_pairs={{0,2},{2,0},{1,3},{3,1},{4,6},{6,4},{5,7},{7,5},{8,10},{10,8},{9,1... | collective-permute-start | bytes 491528 | tf_op jit(solution)/shard_map/ppermute | solution.py:30
  25.1 7.8 %collective-permute-start.8 = (bf16[64,1280]{1,0:T(8,128)(2,1)S(1)}, bf16[64,1280]{1,0:T(8,128)(2,1)S(1)}, u32[]{:S(2)}, u32[]{:S(2)}) collective-permute-start(bf16[64,1280]{1,0:T(8,128)(2,1)S(1)} %collective-permute-done.7.refs_0_.refs_4_), channel_id=1, source_target_pairs={{0,2},{2,0},{1,3},{3,1},{4,6},{6,4},{5,7},{7,5},{8,10},{10,8},{9,1... | collective-permute-start | bytes 491528 | tf_op jit(solution)/shard_map/ppermute | solution.py:30
  25.7 6.0 %collective-permute-start.2 = (bf16[10,80,256]{2,1,0:T(8,128)(2,1)S(1)}, bf16[10,80,256]{2,1,0:T(8,128)(2,1)S(1)}, u32[]{:S(2)}, u32[]{:S(2)}) collective-permute-start(bf16[10,80,256]{2,1,0:T(8,128)(2,1)S(1)} %collective-permute-done.refs_0_.refs_2_), channel_id=1, source_target_pairs={{0,4},{4,0},{8,12},{12,8},{16,20},{20,16},{24,28},{28,24},{1,5},{5... | collective-permute-start | bytes 1228808 | tf_op jit(solution)/shard_map/ppermute | solution.py:30
  30.2 9.4 %collective-permute-start.13 = (bf16[4,80,256]{2,1,0:T(8,128)(2,1)S(1)}, bf16[4,80,256]{2,1,0:T(8,128)(2,1)S(1)}, u32[]{:S(2)}, u32[]{:S(2)}) collective-permute-start(bf16[4,80,256]{2,1,0:T(8,128)(2,1)S(1)} %get-tuple-element.52), channel_id=1, source_target_pairs={{0,4},{4,0},{8,12},{12,8},{16,20},{20,16},{24,28},{28,24},{1,5},{5... | collective-permute-start | bytes 491528 | tf_op jit(solution)/shard_map/ppermute | solution.py:30
  30.2 1.5 %copy-start.10 = (s32[4,9]{1,0:T(4,128)S(1)}, s32[4,9]{1,0:T(4,128)}, u32[]{:S(2)}) copy-start(s32[4,9]{1,0:T(4,128)} %refs_0_.5) | copy-start | bytes 436
  30.2 1.5 %collective-permute-start.6 = (bf16[2,80,256]{2,1,0:T(8,128)(2,1)S(1)}, bf16[2,80,256]{2,1,0:T(8,128)(2,1)S(1)}, u32[]{:S(2)}, u32[]{:S(2)}) collective-permute-start(bf16[2,80,256]{2,1,0:T(8,128)(2,1)S(1)} %pad_maximum_fusion.1.refs_5_), channel_id=1, source_target_pairs={{0,4},{4,0},{8,12},{12,8},{16,20},{20,16},{24,28},{28,24},{1,5},{5... | collective-permute-start | bytes 245768 | tf_op jit(solution)/shard_map/ppermute | solution.py:30
  33.3 13.6 %collective-permute-start.9 = (bf16[128,512]{1,0:T(8,128)(2,1)S(1)}, bf16[128,512]{1,0:T(8,128)(2,1)S(1)}, u32[]{:S(2)}, u32[]{:S(2)}) collective-permute-start(bf16[128,512]{1,0:T(8,128)(2,1)S(1)} %shard_map.118.refs_4_), channel_id=1, source_target_pairs={{0,24},{4,28},{8,16},{12,20},{16,8},{20,12},{24,0},{28,4},{1,25},{... | collective-permute-start | bytes 393224 | tf_op jit(solution)/shard_map/ppermute | solution.py:30
  37.8 9.0 %collective-permute-start.10 = (bf16[128,512]{1,0:T(8,128)(2,1)S(1)}, bf16[128,512]{1,0:T(8,128)(2,1)S(1)}, u32[]{:S(2)}, u32[]{:S(2)}) collective-permute-start(bf16[128,512]{1,0:T(8,128)(2,1)S(1)} %shard_map.119.refs_3_), channel_id=1, source_target_pairs={{0,16},{4,20},{8,24},{12,28},{16,0},{20,4},{24,8},{28,12},{1,17},{... | collective-permute-start | bytes 393224 | tf_op jit(solution)/shard_map/ppermute | solution.py:30
  38.3 8.6 %collective-permute-start.12 = (bf16[128,512]{1,0:T(8,128)(2,1)S(1)}, bf16[128,512]{1,0:T(8,128)(2,1)S(1)}, u32[]{:S(2)}, u32[]{:S(2)}) collective-permute-start(bf16[128,512]{1,0:T(8,128)(2,1)S(1)} %shard_map.120.refs_5_), channel_id=1, source_target_pairs={{0,8},{4,12},{8,0},{12,4},{16,24},{20,28},{24,16},{28,20},{1,9},{5... | collective-permute-start | bytes 393224 | tf_op jit(solution)/shard_map/ppermute | solution.py:30
  40.4 12.7 %collective-permute-start.14 = (bf16[3,4,80,256]{3,2,1,0:T(8,128)(2,1)S(1)}, bf16[3,4,80,256]{3,2,1,0:T(8,128)(2,1)S(1)}, u32[]{:S(2)}, u32[]{:S(2)}) collective-permute-start(bf16[3,4,80,256]{3,2,1,0:T(8,128)(2,1)S(1)} %get-tuple-element.38), channel_id=1, source_target_pairs={{0,1},{1,0},{2,3},{3,2},{4,5},{5,4},{6,7},{7,6},{8,9},{9,8},{10,11... | collective-permute-start | bytes 1474568 | tf_op jit(solution)/shard_map/ppermute | solution.py:30
  47.1 8.3 %collective-permute-start.17 = (bf16[128,512]{1,0:T(8,128)(2,1)S(1)}, bf16[128,512]{1,0:T(8,128)(2,1)S(1)}, u32[]{:S(2)}, u32[]{:S(2)}) collective-permute-start(bf16[128,512]{1,0:T(8,128)(2,1)S(1)} %get-tuple-element.39.refs_7_.refs_1_), channel_id=1, source_target_pairs={{0,24},{4,28},{8,16},{12,20},{16,8},{20,12},{24,0},{28,4},{1,25},{... | collective-permute-start | bytes 393224 | tf_op jit(solution)/shard_map/ppermute | solution.py:30
  50.0 11.1 %collective-permute-start.16 = (bf16[128,512]{1,0:T(8,128)(2,1)S(1)}, bf16[128,512]{1,0:T(8,128)(2,1)S(1)}, u32[]{:S(2)}, u32[]{:S(2)}) collective-permute-start(bf16[128,512]{1,0:T(8,128)(2,1)S(1)} %get-tuple-element.39.refs_7_.refs_1_), channel_id=1, source_target_pairs={{0,16},{4,20},{8,24},{12,28},{16,0},{20,4},{24,8},{28,12},{1,17},{... | collective-permute-start | bytes 393224 | tf_op jit(solution)/shard_map/ppermute | solution.py:30
  50.0 11.1 %collective-permute-start.15 = (bf16[128,512]{1,0:T(8,128)(2,1)S(1)}, bf16[128,512]{1,0:T(8,128)(2,1)S(1)}, u32[]{:S(2)}, u32[]{:S(2)}) collective-permute-start(bf16[128,512]{1,0:T(8,128)(2,1)S(1)} %get-tuple-element.39.refs_7_.refs_1_), channel_id=1, source_target_pairs={{0,8},{4,12},{8,0},{12,4},{16,24},{20,28},{24,16},{28,20},{1,9},{5... | collective-permute-start | bytes 393224 | tf_op jit(solution)/shard_map/ppermute | solution.py:30
  61.6 1.7 %collective-permute-start.19 = (bf16[320,512]{1,0:T(8,128)(2,1)S(1)}, bf16[320,512]{1,0:T(8,128)(2,1)S(1)}, u32[]{:S(2)}, u32[]{:S(2)}) collective-permute-start(bf16[320,512]{1,0:T(8,128)(2,1)S(1)} %get-tuple-element.41), channel_id=1, source_target_pairs={{0,4},{4,0},{8,12},{12,8},{16,20},{20,16},{24,28},{28,24},{1,5},{5... | collective-permute-start | bytes 983048 | tf_op jit(solution)/shard_map/ppermute | solution.py:30
  61.7 4.5 %collective-permute-start.18 = (bf16[320,512]{1,0:T(8,128)(2,1)S(1)}, bf16[320,512]{1,0:T(8,128)(2,1)S(1)}, u32[]{:S(2)}, u32[]{:S(2)}) collective-permute-start(bf16[320,512]{1,0:T(8,128)(2,1)S(1)} %get-tuple-element.40), channel_id=1, source_target_pairs={{0,4},{4,0},{8,12},{12,8},{16,20},{20,16},{24,28},{28,24},{1,5},{5... | collective-permute-start | bytes 983048 | tf_op jit(solution)/shard_map/ppermute | solution.py:30
  63.4 7.1 %collective-permute-start.21 = (bf16[160,512]{1,0:T(8,128)(2,1)S(1)}, bf16[160,512]{1,0:T(8,128)(2,1)S(1)}, u32[]{:S(2)}, u32[]{:S(2)}) collective-permute-start(bf16[160,512]{1,0:T(8,128)(2,1)S(1)} %get-tuple-element.43), channel_id=1, source_target_pairs={{0,1},{1,0},{2,3},{3,2},{4,5},{5,4},{6,7},{7,6},{8,9},{9,8},{10,11... | collective-permute-start | bytes 491528 | tf_op jit(solution)/shard_map/ppermute | solution.py:30
  63.9 9.2 %collective-permute-start.20 = (bf16[160,512]{1,0:T(8,128)(2,1)S(1)}, bf16[160,512]{1,0:T(8,128)(2,1)S(1)}, u32[]{:S(2)}, u32[]{:S(2)}) collective-permute-start(bf16[160,512]{1,0:T(8,128)(2,1)S(1)} %get-tuple-element.42), channel_id=1, source_target_pairs={{0,1},{1,0},{2,3},{3,2},{4,5},{5,4},{6,7},{7,6},{8,9},{9,8},{10,11... | collective-permute-start | bytes 491528 | tf_op jit(solution)/shard_map/ppermute | solution.py:30
  (2 other events, 1.7 us)

commit v6 on v5

--- a/solution.py
+++ b/solution.py
@@ -21,7 +21,7 @@
 VMEM = 16 * 2**20
 CUTS = 2
 LAST = 1
-DIRECT = 2
+DIRECT = 1
 LONG = 10**11
 
 
@@ -118,28 +118,28 @@
 
 
 def first_weights_kernel(*refs):
-    windows, out = refs[:4], refs[4]
+    windows, out, ends = refs[:4], refs[4], refs[5]
     blocks, rows, cols = out.shape
     per = cols // LANES
     for k in range(blocks):
         for h in range(per):
-            value = updated(windows, k, h, rows, per)[0]
-            out[k, :, h * LANES : (h + 1) * LANES] = value.astype(bf16)
-
-
-def first_states_kernel(*refs):
-    windows, (leaving, staying, ends) = refs[:4], refs[4:]
-    group = lax.axis_index("group")
-    _, half, rows, cols = staying.shape
-    per = cols // LANES
-    runs = [(ends.at[0], 0, 1), (ends.at[1], 2 * half + 1, 1)]
-    runs += [(leaving, (1 - group) * half + 1, half), (staying, group * half + 1, half)]
-    for out, start, size in runs:
-        for k in range(size):
-            for h in range(per):
-                values = updated(windows, start + k, h, rows, per)
-                for i in range(3):
-                    out[i, k, :, h * LANES : (h + 1) * LANES] = values[i].astype(out.dtype)
+            at = slice(h * LANES, (h + 1) * LANES)
+            values = updated(windows, k, h, rows, per)
+            out[k, :, at] = values[0].astype(bf16)
+            if k in (0, blocks - 1):
+                for i in range(2):
+                    ends[min(k, 1), i, :, at] = values[i + 1].astype(bf16)
+
+
+def border_kernel(window, other, ends, to_mate, to_next):
+    first = lax.axis_index("dp") % CORES == 0
+    last = window.shape[0] - 1
+    pairs = [(window[0], window[last]), (other[0], other[last])]
+    pairs += [(ends[0, i], ends[1, i]) for i in range(2)]
+    for i, (head, tail) in enumerate(pairs):
+        head, tail = head.astype(f32), tail.astype(f32)
+        to_mate[i] = jnp.where(first, tail, head).astype(bf16)
+        to_next[i] = jnp.where(first, head, tail).astype(bf16)
 
 
 def live_bounds(offsets, span, rank, other):
@@ -177,21 +177,33 @@
             out[count - 1, :, at] = jnp.where(after, right, window[count].astype(f32)).astype(bf16)
 
 
-def patch_states_kernel(offsets, leaving, staying, inner, outer, out_leaving, out_staying):
-    _, half, rows, cols = leaving.shape
+def states_kernel(offsets, *refs):
+    windows, (inner, outer), outs = refs[:4], refs[4:6], refs[6:]
+    _, half, rows, cols = outs[0].shape
+    per = cols // LANES
     span = 2 * half * rows * cols
     low, high = live_bounds(offsets, span, lax.axis_index("dp"), 0)
     first = lax.axis_index("dp") % CORES == 0
     group = lax.axis_index("group")
-    for tile, states, out in ((1 - group, leaving, out_leaving), (group, staying, out_staying)):
-        before = place_of(rows, cols, tile * (span // 2)) < low
-        after = place_of(rows, cols, tile * (span // 2) + (half - 1) * rows * cols) >= high
-        for i in range(3):
-            near, far = inner[i].astype(f32), outer[i].astype(f32)
-            left, right = jnp.where(first, far, near), jnp.where(first, near, far)
-            out[i, 0] = jnp.where(before, left, states[i, 0]).astype(out.dtype)
-            out[i, 1 : half - 1] = states[i, 1 : half - 1].astype(out.dtype)
-            out[i, half - 1] = jnp.where(after, right, states[i, half - 1]).astype(out.dtype)
+    for tile, out in zip((1 - group, group), outs, strict=True):
+        for k in range(half):
+            block = tile * half + k
+            for h in range(per):
+                at = slice(h * LANES, (h + 1) * LANES)
+                values = updated(windows, block + 1, h, rows, per)
+                place = lax.broadcasted_iota(jnp.int32, (rows, LANES), 0) * cols
+                place = place + lax.broadcasted_iota(jnp.int32, (rows, LANES), 1)
+                place = place + (block * rows * cols + h * LANES)
+                for i in range(3):
+                    value = values[i]
+                    at_end = (0, 2, 3)[i]
+                    near = inner[at_end, :, at].astype(f32)
+                    far = outer[at_end, :, at].astype(f32)
+                    if k == 0:
+                        value = jnp.where(place < low, jnp.where(first, far, near), value)
+                    if k == half - 1:
+                        value = jnp.where(place >= high, jnp.where(first, near, far), value)
+                    out[i, k, :, at] = value.astype(out.dtype)
 
 
 def part_kernel(pieces, *refs):
@@ -372,12 +384,6 @@
         w.reshape(10, margin // LANES, LANES)
         for w in (old_master, old_moment, old_variance, old_grad)
     ]
-    ahead = call(zero_kernel, shape((8, LANES), f32), flops=LONG)
-    count, rows = windows[0].shape[0] - 2, windows[0].shape[1] * LANES // old_cols
-    window = call(
-        first_weights_kernel, shape((count + 2, rows, old_cols), bf16), *windows, after=[ahead]
-    )
-
     aligned = half % LANES == 0 and share % 16 == 0
     last = share // LAST if aligned and share % (16 * LAST) == 0 else share
     plan = [(step, 0) for step in range(1, chips - 1)]
@@ -411,25 +417,33 @@
             for (step, start), size in zip(plan, sizes, strict=True)
         ]
 
+    ahead = call(zero_kernel, shape((8, LANES), f32), flops=LONG)
+    leaving_blocks = blocks_of(plan, sizes, [ahead])
+    count, rows = windows[0].shape[0] - 2, windows[0].shape[1] * LANES // old_cols
+    window, ends = call(
+        first_weights_kernel,
+        [shape((count + 2, rows, old_cols), bf16), shape((2, 2, rows, old_cols), bf16)],
+        *windows,
+        after=leaving_blocks[:1],
+    )
+
     other = swap(window, "group", 1)
-    leaving_blocks = blocks_of(plan, sizes, [])
     arrived = [
         (step, swap(b, "dp", step * CORES))
         for (step, _), b in zip(plan, leaving_blocks, strict=True)
     ]
 
     mate_window = swap(window, "dp", 1)
-    tile = shape((3, count // 2, rows, old_cols), f32)
-    leaving, staying, ends = call(
-        first_states_kernel,
-        [tile, tile, shape((2, 3, 1, rows, old_cols), bf16)],
-        *windows,
-        after=leaving_blocks[:1],
-    )
-
-    ends = jnp.concatenate([ends[:, :, 0], jnp.stack([other[0], other[-1]])[:, None]], axis=1)
-    inner = swap(jnp.where(core == 0, ends[1], ends[0]), "dp", 1)
-    outer = swap_border(jnp.where(core == 0, ends[0], ends[1]))
+    to_mate, to_next = call(
+        border_kernel,
+        [shape((4, rows, old_cols), bf16)] * 2,
+        window,
+        other,
+        ends,
+        after=[mate_window],
+        flops=3 * 10**9,
+    )
+    inner, outer = swap(to_mate, "dp", 1), swap_border(to_next)
 
     turned = call(
         live_kernel, shape((slots, cols), bf16), counts, cotangent, scalars=1, after=[other]
@@ -441,7 +455,7 @@
             block += [swap(b, "tensor", j) for j in range(1, tensors) for b in list(block)]
         blocks.append(block)
 
-    far, _ = lax.optimization_barrier((jnp.stack([outer[0], outer[3]]), blocks[DIRECT]))
+    far, _ = lax.optimization_barrier((outer[:2], blocks[DIRECT]))
 
     mates = [mate_window] + [swap(w, "dp", 1) for w in (other, far)]
     weights = call(
@@ -457,18 +471,17 @@
     )
     weights = [w.reshape(half, cols) for w in weights]
 
-    steps = range(chips - 1, 0, -1)
+    steps = [chips - 1, *range(1, chips - 1)]
     parts = []
     for step in steps:
         parts.append(part(blocks[step], weights, bf16, after=parts[-1:]))
     back = [swap(p, "dp", step * CORES) for step, p in zip(steps, parts, strict=True)]
 
     leaving, staying = call(
-        patch_states_kernel,
-        [shape(leaving.shape, bf16), shape(leaving.shape, f32)],
+        states_kernel,
+        [shape((3, count // groups, rows, old_cols), dtype) for dtype in (bf16, f32)],
         old_offsets,
-        leaving,
-        staying,
+        *windows,
         inner,
         outer,
         scalars=1,

time: 74.8 us -> 72.1 us (0.964)
  waiting for transfers between devices: 25.9 us -> 31.7 us
  Pallas kernels: 13.6 us -> 9.73 us
  local copies, waits for them, and re-layouts: 5.87 us -> 2.47 us
  starting transfers between devices: 28.1 us -> 27.2 us
    ppermute x21 -> x22, waiting for transfers between devices: 25.9 us -> 31.7 us  [swap(): return lax.ppermute(value, axis, pairs)]
    unnamed x24 -> x16, local copies, waits for them, and re-layouts: 5.85 us -> 2.46 us
    pallas_call x16, Pallas kernels: 10 us -> 6.9 us  [call(): pl.pallas_call(body, out_shape=shapes, in_specs=[small] * scalars + [whol...]
    ppermute x21 -> x22, starting transfers between devices: 27.3 us -> 26.4 us  [swap(): return lax.ppermute(value, axis, pairs)]
    pallas_call x2, Pallas kernels: 1.01 us -> 0.24 us  [token_blocks(): pl.pallas_call(functools.partial(blocks_kernel, plan, len(after)), out_sh...]
  transfers between devices with their start and end apart: 22 -> 23, of which waited for: 11 -> 11; matrix products, arithmetic and copies ran while one was open for 0% -> 0% of each run, Pallas kernels for 14% -> 10%
where the time goes in v6:
time: 72.1 us; the launch traced here: 71.9 us
  waiting for transfers between devices  31.7 us (44%)
  starting transfers between devices  27.2 us (38%)
  Pallas kernels  9.73 us (13%)
  local copies, waits for them, and re-layouts  2.47 us (3%)
  between operations  0.89 us (1%)
    ppermute x22, waiting for transfers between devices, swap(): return lax.ppermute(value, axis, pairs)  31.7 us
    ppermute x22, starting transfers between devices, swap(): return lax.ppermute(value, axis, pairs)  26.4 us
    pallas_call x16, Pallas kernels, call(): pl.pallas_call(body, out_shape=shapes, in_specs=[small] * scalars + [whol...  6.9 us
    pallas_call x2, Pallas kernels, second_adam(): pl.pallas_call(functools.partial(second_adam_kernel, cut), out_shape=[sha...  2.58 us
    unnamed x16, local copies, waits for them, and re-layouts  2.46 us
  transfers between devices with their start and end apart: 23, of which 11 were waited for; matrix products, arithmetic and copies ran while one was open for 0% of the time, Pallas kernels for 10%

profile of v6, /device:TPU:0, one launch (start us, length us, event | category | flops | bytes accessed | tf_op | source)
XLA Modules:
  0.0 71.9 jit_solution(7676178769718860709)
XLA Ops:
  0.7 1.3 %copy-done = bf16[128,5120]{1,0:T(8,128)(2,1)S(1)} copy-done((bf16[128,5120]{1,0:T(8,128)(2,1)S(1)}, bf16[128,5120]{1,0:T(8,128)(2,1)}, u32[]{:S(2)}) %copy-start) | copy-done | bytes 1310744
  2.7 0.6 copy-done.1
  3.3 0.7 shard_map.113
  3.9 3.0 %collective-permute-start = (bf16[10,80,256]{2,1,0:T(8,128)(2,1)S(1)}, bf16[10,80,256]{2,1,0:T(8,128)(2,1)S(1)}, u32[]{:S(2)}, u32[]{:S(2)}) collective-permute-start(bf16[10,80,256]{2,1,0:T(8,128)(2,1)S(1)} %get-tuple-element.29.refs_0_.refs_1_), channel_id=1, source_target_pairs={{0,1},{1,0},{2,3},{3,2},{4,5},{5,4},{6,7},{7,6},{8,9},{9,8},{10,11... | collective-permute-start | bytes 1228808 | tf_op jit(solution)/shard_map/ppermute | solution.py:30
  7.0 1.6 %collective-permute-start.4 = (bf16[64,1280]{1,0:T(8,128)(2,1)S(1)}, bf16[64,1280]{1,0:T(8,128)(2,1)S(1)}, u32[]{:S(2)}, u32[]{:S(2)}) collective-permute-start(bf16[64,1280]{1,0:T(8,128)(2,1)S(1)} %get-tuple-element.28.refs_4_), channel_id=1, source_target_pairs={{0,8},{4,12},{8,0},{12,4},{16,24},{20,28},{24,16},{28,20},{1,9},{5... | collective-permute-start | bytes 491528 | tf_op jit(solution)/shard_map/ppermute | solution.py:30
  8.6 2.5 %collective-permute-start.7 = (bf16[64,1280]{1,0:T(8,128)(2,1)S(1)}, bf16[64,1280]{1,0:T(8,128)(2,1)S(1)}, u32[]{:S(2)}, u32[]{:S(2)}) collective-permute-start(bf16[64,1280]{1,0:T(8,128)(2,1)S(1)} %get-tuple-element.35), channel_id=1, source_target_pairs={{0,24},{4,28},{8,16},{12,20},{16,8},{20,12},{24,0},{28,4},{1,25},{... | collective-permute-start | bytes 491528 | tf_op jit(solution)/shard_map/ppermute | solution.py:30
  11.1 5.3 %collective-permute-done.refs_0_.refs_1_.refs_2_ = bf16[10,80,256]{2,1,0:T(8,128)(2,1)S(1)} collective-permute-done((bf16[10,80,256]{2,1,0:T(8,128)(2,1)S(1)}, bf16[10,80,256]{2,1,0:T(8,128)(2,1)S(1)}, u32[]{:S(2)}, u32[]{:S(2)}) %collective-permute-start) | collective-permute-done | bytes 409632 | tf_op jit(solution)/shard_map/ppermute | solution.py:30
  16.6 0.8 %collective-permute-start.3 = (bf16[4,80,256]{2,1,0:T(8,128)(2,1)S(1)}, bf16[4,80,256]{2,1,0:T(8,128)(2,1)S(1)}, u32[]{:S(2)}, u32[]{:S(2)}) collective-permute-start(bf16[4,80,256]{2,1,0:T(8,128)(2,1)S(1)} %get-tuple-element.31), channel_id=1, source_target_pairs={{4,8},{8,4},{12,16},{16,12},{20,24},{24,20},{5,9},{9,5},{13,17},{1... | collective-permute-start | bytes 491528 | tf_op jit(solution)/shard_map/ppermute | solution.py:37
  17.4 1.8 %collective-permute-start.5 = (bf16[64,1280]{1,0:T(8,128)(2,1)S(1)}, bf16[64,1280]{1,0:T(8,128)(2,1)S(1)}, u32[]{:S(2)}, u32[]{:S(2)}) collective-permute-start(bf16[64,1280]{1,0:T(8,128)(2,1)S(1)} %collective-permute-done.4.refs_0_.refs_1_), channel_id=1, source_target_pairs={{0,2},{2,0},{1,3},{3,1},{4,6},{6,4},{5,7},{7,5},{8,10},{10,8},{9,1... | collective-permute-start | bytes 491528 | tf_op jit(solution)/shard_map/ppermute | solution.py:30
  19.6 1.5 %collective-permute-start.8 = (bf16[64,1280]{1,0:T(8,128)(2,1)S(1)}, bf16[64,1280]{1,0:T(8,128)(2,1)S(1)}, u32[]{:S(2)}, u32[]{:S(2)}) collective-permute-start(bf16[64,1280]{1,0:T(8,128)(2,1)S(1)} %collective-permute-done.7.refs_0_.refs_5_), channel_id=1, source_target_pairs={{0,2},{2,0},{1,3},{3,1},{4,6},{6,4},{5,7},{7,5},{8,10},{10,8},{9,1... | collective-permute-start | bytes 491528 | tf_op jit(solution)/shard_map/ppermute | solution.py:30
  21.1 5.3 %collective-permute-done.11.refs_0_.refs_3_ = bf16[64,1280]{1,0:T(8,128)(2,1)S(1)} collective-permute-done((bf16[64,1280]{1,0:T(8,128)(2,1)S(1)}, bf16[64,1280]{1,0:T(8,128)(2,1)S(1)}, u32[]{:S(2)}, u32[]{:S(2)}) %collective-permute-start.11) | collective-permute-done | bytes 163872 | tf_op jit(solution)/shard_map/ppermute | solution.py:30
  26.4 1.5 %collective-permute-start.12 = (bf16[64,1280]{1,0:T(8,128)(2,1)S(1)}, bf16[64,1280]{1,0:T(8,128)(2,1)S(1)}, u32[]{:S(2)}, u32[]{:S(2)}) collective-permute-start(bf16[64,1280]{1,0:T(8,128)(2,1)S(1)} %collective-permute-done.11.refs_0_.refs_3_), channel_id=1, source_target_pairs={{0,2},{2,0},{1,3},{3,1},{4,6},{6,4},{5,7},{7,5},{8,10},{10,8},{9,1... | collective-permute-start | bytes 491528 | tf_op jit(solution)/shard_map/ppermute | solution.py:30
  27.9 0.6 collective-permute-start.6
  28.6 0.6 shard_map.121.refs_4_
  29.4 0.8 %shard_map.116 = (bf16[8,80,512]{2,1,0:T(8,128)(2,1)S(1)}, bf16[8,80,512]{2,1,0:T(8,128)(2,1)S(1)}) custom-call(s32[4,9]{1,0:T(4,128)S(1)} %copy-done.6, bf16[10,80,256]{2,1,0:T(8,128)(2,1)S(1)} %get-tuple-element.29.refs_0_.refs_1_, bf16[10,80,256]{2,1,0:T(8,128)(2,1)S(1)} %collective-permute-done.refs_0_.refs_1_.refs_2_, ...), custom_call_target="tpu_custom_call" | custom-call | bytes 1802384 | tf_op jit(solution)/shard_map/pallas_call | solution.py:58
  30.5 3.3 %collective-permute-start.9 = (bf16[128,512]{1,0:T(8,128)(2,1)S(1)}, bf16[128,512]{1,0:T(8,128)(2,1)S(1)}, u32[]{:S(2)}, u32[]{:S(2)}) collective-permute-start(bf16[128,512]{1,0:T(8,128)(2,1)S(1)} %shard_map.118.refs_4_), channel_id=1, source_target_pairs={{0,24},{4,28},{8,16},{12,20},{16,8},{20,12},{24,0},{28,4},{1,25},{... | collective-permute-start | bytes 393224 | tf_op jit(solution)/shard_map/ppermute | solution.py:30
  34.7 1.7 %collective-permute-start.13 = (bf16[128,512]{1,0:T(8,128)(2,1)S(1)}, bf16[128,512]{1,0:T(8,128)(2,1)S(1)}, u32[]{:S(2)}, u32[]{:S(2)}) collective-permute-start(bf16[128,512]{1,0:T(8,128)(2,1)S(1)} %shard_map.120.refs_7_), channel_id=1, source_target_pairs={{0,16},{4,20},{8,24},{12,28},{16,0},{20,4},{24,8},{28,12},{1,17},{... | collective-permute-start | bytes 393224 | tf_op jit(solution)/shard_map/ppermute | solution.py:30
  36.4 1.3 %shard_map.124 = (bf16[3,4,80,256]{3,2,1,0:T(8,128)(2,1)S(1)}, f32[3,4,80,256]{3,2,1,0:T(8,128)S(1)}) custom-call(s32[4,9]{1,0:T(4,128)S(1)} %copy-done.6, f32[10,160,128]{2,1,0:T(8,128)S(1)} %bitcast.15, f32[10,160,128]{2,1,0:T(8,128)S(1)} %bitcast.17, f32[10,160,128]{2,1,0:T(8,128)S(1)} %bitcast.19, f32[10,160,128]{2,1,0:T(8,128)S(1)} %bitcast.21, ...), custom_call_target="tpu_custom_call" | custom-call | bytes 3604624 | tf_op jit(solution)/shard_map/pallas_call | solution.py:58
  37.7 1.6 %collective-permute-start.15 = (bf16[3,4,80,256]{3,2,1,0:T(8,128)(2,1)S(1)}, bf16[3,4,80,256]{3,2,1,0:T(8,128)(2,1)S(1)}, u32[]{:S(2)}, u32[]{:S(2)}) collective-permute-start(bf16[3,4,80,256]{3,2,1,0:T(8,128)(2,1)S(1)} %get-tuple-element.40), channel_id=1, source_target_pairs={{0,1},{1,0},{2,3},{3,2},{4,5},{5,4},{6,7},{7,6},{8,9},{9,8},{10,11... | collective-permute-start | bytes 1474568 | tf_op jit(solution)/shard_map/ppermute | solution.py:30
  39.7 5.8 %collective-permute-done.13.refs_3_ = bf16[128,512]{1,0:T(8,128)(2,1)S(1)} collective-permute-done((bf16[128,512]{1,0:T(8,128)(2,1)S(1)}, bf16[128,512]{1,0:T(8,128)(2,1)S(1)}, u32[]{:S(2)}, u32[]{:S(2)}) %collective-permute-start.13) | collective-permute-done | bytes 131104 | tf_op jit(solution)/shard_map/ppermute | solution.py:30
  45.7 2.6 %collective-permute-start.18 = (bf16[128,512]{1,0:T(8,128)(2,1)S(1)}, bf16[128,512]{1,0:T(8,128)(2,1)S(1)}, u32[]{:S(2)}, u32[]{:S(2)}) collective-permute-start(bf16[128,512]{1,0:T(8,128)(2,1)S(1)} %get-tuple-element.41.refs_8_.refs_1_), channel_id=1, source_target_pairs={{0,24},{4,28},{8,16},{12,20},{16,8},{20,12},{24,0},{28,4},{1,25},{... | collective-permute-start | bytes 393224 | tf_op jit(solution)/shard_map/ppermute | solution.py:30
  48.3 1.8 %collective-permute-start.16 = (bf16[128,512]{1,0:T(8,128)(2,1)S(1)}, bf16[128,512]{1,0:T(8,128)(2,1)S(1)}, u32[]{:S(2)}, u32[]{:S(2)}) collective-permute-start(bf16[128,512]{1,0:T(8,128)(2,1)S(1)} %get-tuple-element.41.refs_8_.refs_1_), channel_id=1, source_target_pairs={{0,8},{4,12},{8,0},{12,4},{16,24},{20,28},{24,16},{28,20},{1,9},{5... | collective-permute-start | bytes 393224 | tf_op jit(solution)/shard_map/ppermute | solution.py:30
  50.1 0.6 collective-permute-done.15.refs_7_.incoming
  50.8 3.2 %collective-permute-done.18.refs_4_ = bf16[128,512]{1,0:T(8,128)(2,1)S(1)} collective-permute-done((bf16[128,512]{1,0:T(8,128)(2,1)S(1)}, bf16[128,512]{1,0:T(8,128)(2,1)S(1)}, u32[]{:S(2)}, u32[]{:S(2)}) %collective-permute-start.18) | collective-permute-done | bytes 131104 | tf_op jit(solution)/shard_map/ppermute | solution.py:30
  54.0 4.4 %collective-permute-done.17.refs_3_ = bf16[128,512]{1,0:T(8,128)(2,1)S(1)} collective-permute-done((bf16[128,512]{1,0:T(8,128)(2,1)S(1)}, bf16[128,512]{1,0:T(8,128)(2,1)S(1)}, u32[]{:S(2)}, u32[]{:S(2)}) %collective-permute-start.17) | collective-permute-done | bytes 131104 | tf_op jit(solution)/shard_map/ppermute | solution.py:30
  60.1 0.6 collective-permute-done.20.refs_1_
  60.7 1.9 %collective-permute-start.22 = (bf16[160,512]{1,0:T(8,128)(2,1)S(1)}, bf16[160,512]{1,0:T(8,128)(2,1)S(1)}, u32[]{:S(2)}, u32[]{:S(2)}) collective-permute-start(bf16[160,512]{1,0:T(8,128)(2,1)S(1)} %get-tuple-element.45), channel_id=1, source_target_pairs={{0,1},{1,0},{2,3},{3,2},{4,5},{5,4},{6,7},{7,6},{8,9},{9,8},{10,11... | collective-permute-start | bytes 491528 | tf_op jit(solution)/shard_map/ppermute | solution.py:30
  62.8 0.7 shard_map.123
  63.5 4.3 %collective-permute-done.22.back = bf16[160,512]{1,0:T(8,128)(2,1)S(1)} collective-permute-done((bf16[160,512]{1,0:T(8,128)(2,1)S(1)}, bf16[160,512]{1,0:T(8,128)(2,1)S(1)}, u32[]{:S(2)}, u32[]{:S(2)}) %collective-permute-start.22) | collective-permute-done | bytes 163872 | tf_op jit(solution)/shard_map/ppermute | solution.py:30
  67.8 1.3 %shard_map.129 = (f32[320,512]{1,0:T(8,128)}, f32[320,512]{1,0:T(8,128)}, f32[320,512]{1,0:T(8,128)}) custom-call(f32[3,4,80,256]{3,2,1,0:T(8,128)S(1)} %get-tuple-element.39.staying, bf16[3,4,80,256]{3,2,1,0:T(8,128)(2,1)S(1)} %collective-permute-done.15.refs_7_.incoming, f32[2,320,512]{2,1,0:T(8,128)S(1)} %shard_map.126.refs_0_.mine, ...), custom_call_target="tpu_custom_call" | custom-call | bytes 1000000 | tf_op jit(solution)/shard_map/pallas_call | solution.py:354
  69.1 1.5 %collective-permute-done.21.back = bf16[160,512]{1,0:T(8,128)(2,1)S(1)} collective-permute-done((bf16[160,512]{1,0:T(8,128)(2,1)S(1)}, bf16[160,512]{1,0:T(8,128)(2,1)S(1)}, u32[]{:S(2)}, u32[]{:S(2)}) %collective-permute-start.21) | collective-permute-done | bytes 163872 | tf_op jit(solution)/shard_map/ppermute | solution.py:30
  70.6 1.3 %shard_map.130 = (f32[320,512]{1,0:T(8,128)}, f32[320,512]{1,0:T(8,128)}, f32[320,512]{1,0:T(8,128)}) custom-call(f32[3,4,80,256]{3,2,1,0:T(8,128)S(1)} %get-tuple-element.39.staying, bf16[3,4,80,256]{3,2,1,0:T(8,128)(2,1)S(1)} %collective-permute-done.15.refs_7_.incoming, ...), custom_call_target="tpu_custom_call", output_to_operand_aliasing={{0}: (5, {}), {1}: (6, {}), {2}: (7, {})} | custom-call | bytes 1000000 | tf_op jit(solution)/shard_map/pallas_call | solution.py:354
  (51 shorter events, 5.4 us)
Async XLA Ops:
  0.6 1.3 %copy-start = (bf16[128,5120]{1,0:T(8,128)(2,1)S(1)}, bf16[128,5120]{1,0:T(8,128)(2,1)}, u32[]{:S(2)}) copy-start(bf16[128,5120]{1,0:T(8,128)(2,1)} %tokens.3) | copy-start | bytes 3932164
  0.6 1.5 %copy-start.2 = (f32[1,1,204800]{2,1,0:T(1,128)S(1)}, f32[1,1,204800]{2,1,0:T(1,128)}, u32[]{:S(2)}) copy-start(f32[1,1,204800]{2,1,0:T(1,128)} %param.13) | copy-start | bytes 2457604
  0.7 1.8 %copy-start.3 = (f32[1,1,204800]{2,1,0:T(1,128)S(1)}, f32[1,1,204800]{2,1,0:T(1,128)}, u32[]{:S(2)}) copy-start(f32[1,1,204800]{2,1,0:T(1,128)} %param.14) | copy-start | bytes 2457604
  0.7 2.0 %copy-start.4 = (f32[1,1,204800]{2,1,0:T(1,128)S(1)}, f32[1,1,204800]{2,1,0:T(1,128)}, u32[]{:S(2)}) copy-start(f32[1,1,204800]{2,1,0:T(1,128)} %param.15) | copy-start | bytes 2457604
  1.9 1.3 %copy-start.1 = (f32[1,1,204800]{2,1,0:T(1,128)S(1)}, f32[1,1,204800]{2,1,0:T(1,128)}, u32[]{:S(2)}) copy-start(f32[1,1,204800]{2,1,0:T(1,128)} %param.12) | copy-start | bytes 2457604
  3.9 12.5 %collective-permute-start = (bf16[10,80,256]{2,1,0:T(8,128)(2,1)S(1)}, bf16[10,80,256]{2,1,0:T(8,128)(2,1)S(1)}, u32[]{:S(2)}, u32[]{:S(2)}) collective-permute-start(bf16[10,80,256]{2,1,0:T(8,128)(2,1)S(1)} %get-tuple-element.29.refs_0_.refs_1_), channel_id=1, source_target_pairs={{0,1},{1,0},{2,3},{3,2},{4,5},{5,4},{6,7},{7,6},{8,9},{9,8},{10,11... | collective-permute-start | bytes 1228808 | tf_op jit(solution)/shard_map/ppermute | solution.py:30
  7.0 9.5 %collective-permute-start.1 = (bf16[10,80,256]{2,1,0:T(8,128)(2,1)S(1)}, bf16[10,80,256]{2,1,0:T(8,128)(2,1)S(1)}, u32[]{:S(2)}, u32[]{:S(2)}) collective-permute-start(bf16[10,80,256]{2,1,0:T(8,128)(2,1)S(1)} %get-tuple-element.29.refs_0_.refs_1_), channel_id=1, source_target_pairs={{0,4},{4,0},{8,12},{12,8},{16,20},{20,16},{24,28},{28,24},{1,5},{5... | collective-permute-start | bytes 1228808 | tf_op jit(solution)/shard_map/ppermute | solution.py:30
  7.0 10.4 %collective-permute-start.4 = (bf16[64,1280]{1,0:T(8,128)(2,1)S(1)}, bf16[64,1280]{1,0:T(8,128)(2,1)S(1)}, u32[]{:S(2)}, u32[]{:S(2)}) collective-permute-start(bf16[64,1280]{1,0:T(8,128)(2,1)S(1)} %get-tuple-element.28.refs_4_), channel_id=1, source_target_pairs={{0,8},{4,12},{8,0},{12,4},{16,24},{20,28},{24,16},{28,20},{1,9},{5... | collective-permute-start | bytes 491528 | tf_op jit(solution)/shard_map/ppermute | solution.py:30
  8.6 11.1 %collective-permute-start.7 = (bf16[64,1280]{1,0:T(8,128)(2,1)S(1)}, bf16[64,1280]{1,0:T(8,128)(2,1)S(1)}, u32[]{:S(2)}, u32[]{:S(2)}) collective-permute-start(bf16[64,1280]{1,0:T(8,128)(2,1)S(1)} %get-tuple-element.35), channel_id=1, source_target_pairs={{0,24},{4,28},{8,16},{12,20},{16,8},{20,12},{24,0},{28,4},{1,25},{... | collective-permute-start | bytes 491528 | tf_op jit(solution)/shard_map/ppermute | solution.py:30
  11.0 15.3 %collective-permute-start.11 = (bf16[64,1280]{1,0:T(8,128)(2,1)S(1)}, bf16[64,1280]{1,0:T(8,128)(2,1)S(1)}, u32[]{:S(2)}, u32[]{:S(2)}) collective-permute-start(bf16[64,1280]{1,0:T(8,128)(2,1)S(1)} %get-tuple-element.36), channel_id=1, source_target_pairs={{0,16},{4,20},{8,24},{12,28},{16,0},{20,4},{24,8},{28,12},{1,17},{... | collective-permute-start | bytes 491528 | tf_op jit(solution)/shard_map/ppermute | solution.py:30
  16.4 13.0 %collective-permute-start.2 = (bf16[10,80,256]{2,1,0:T(8,128)(2,1)S(1)}, bf16[10,80,256]{2,1,0:T(8,128)(2,1)S(1)}, u32[]{:S(2)}, u32[]{:S(2)}) collective-permute-start(bf16[10,80,256]{2,1,0:T(8,128)(2,1)S(1)} %collective-permute-done.refs_0_.refs_1_.refs_2_), channel_id=1, source_target_pairs={{0,4},{4,0},{8,12},{12,8},{16,20},{20,16},{24,28},{28,24},{1,5},{5... | collective-permute-start | bytes 1228808 | tf_op jit(solution)/shard_map/ppermute | solution.py:30
  16.5 12.0 %copy-start.5 = (bf16[128,512]{1,0:T(8,128)(2,1)S(1)}, bf16[128,512]{1,0:T(8,128)(2,1)}, u32[]{:S(2)}) copy-start(bf16[128,512]{1,0:T(8,128)(2,1)} %refs_1_.1) | copy-start | bytes 393220
  16.5 12.0 %copy-start.7 = (s32[16]{0:T(128)S(1)}, s32[16]{0:T(128)}, u32[]{:S(2)}) copy-start(s32[16]{0:T(128)} %refs_0_.4) | copy-start | bytes 196
  16.6 11.3 %collective-permute-start.3 = (bf16[4,80,256]{2,1,0:T(8,128)(2,1)S(1)}, bf16[4,80,256]{2,1,0:T(8,128)(2,1)S(1)}, u32[]{:S(2)}, u32[]{:S(2)}) collective-permute-start(bf16[4,80,256]{2,1,0:T(8,128)(2,1)S(1)} %get-tuple-element.31), channel_id=1, source_target_pairs={{4,8},{8,4},{12,16},{16,12},{20,24},{24,20},{5,9},{9,5},{13,17},{1... | collective-permute-start | bytes 491528 | tf_op jit(solution)/shard_map/ppermute | solution.py:37
  17.4 10.5 %collective-permute-start.5 = (bf16[64,1280]{1,0:T(8,128)(2,1)S(1)}, bf16[64,1280]{1,0:T(8,128)(2,1)S(1)}, u32[]{:S(2)}, u32[]{:S(2)}) collective-permute-start(bf16[64,1280]{1,0:T(8,128)(2,1)S(1)} %collective-permute-done.4.refs_0_.refs_1_), channel_id=1, source_target_pairs={{0,2},{2,0},{1,3},{3,1},{4,6},{6,4},{5,7},{7,5},{8,10},{10,8},{9,1... | collective-permute-start | bytes 491528 | tf_op jit(solution)/shard_map/ppermute | solution.py:30
  19.6 10.6 %collective-permute-start.8 = (bf16[64,1280]{1,0:T(8,128)(2,1)S(1)}, bf16[64,1280]{1,0:T(8,128)(2,1)S(1)}, u32[]{:S(2)}, u32[]{:S(2)}) collective-permute-start(bf16[64,1280]{1,0:T(8,128)(2,1)S(1)} %collective-permute-done.7.refs_0_.refs_5_), channel_id=1, source_target_pairs={{0,2},{2,0},{1,3},{3,1},{4,6},{6,4},{5,7},{7,5},{8,10},{10,8},{9,1... | collective-permute-start | bytes 491528 | tf_op jit(solution)/shard_map/ppermute | solution.py:30
  26.4 8.0 %collective-permute-start.12 = (bf16[64,1280]{1,0:T(8,128)(2,1)S(1)}, bf16[64,1280]{1,0:T(8,128)(2,1)S(1)}, u32[]{:S(2)}, u32[]{:S(2)}) collective-permute-start(bf16[64,1280]{1,0:T(8,128)(2,1)S(1)} %collective-permute-done.11.refs_0_.refs_3_), channel_id=1, source_target_pairs={{0,2},{2,0},{1,3},{3,1},{4,6},{6,4},{5,7},{7,5},{8,10},{10,8},{9,1... | collective-permute-start | bytes 491528 | tf_op jit(solution)/shard_map/ppermute | solution.py:30
  27.9 8.6 %collective-permute-start.14 = (bf16[4,80,256]{2,1,0:T(8,128)(2,1)S(1)}, bf16[4,80,256]{2,1,0:T(8,128)(2,1)S(1)}, u32[]{:S(2)}, u32[]{:S(2)}) collective-permute-start(bf16[4,80,256]{2,1,0:T(8,128)(2,1)S(1)} %get-tuple-element.38), channel_id=1, source_target_pairs={{0,4},{4,0},{8,12},{12,8},{16,20},{20,16},{24,28},{28,24},{1,5},{5... | collective-permute-start | bytes 491528 | tf_op jit(solution)/shard_map/ppermute | solution.py:30
  27.9 1.5 %copy-start.6 = (s32[4,9]{1,0:T(4,128)S(1)}, s32[4,9]{1,0:T(4,128)}, u32[]{:S(2)}) copy-start(s32[4,9]{1,0:T(4,128)} %refs_0_.5) | copy-start | bytes 436
  27.9 1.5 %collective-permute-start.6 = (bf16[2,80,256]{2,1,0:T(8,128)(2,1)S(1)}, bf16[2,80,256]{2,1,0:T(8,128)(2,1)S(1)}, u32[]{:S(2)}, u32[]{:S(2)}) collective-permute-start(bf16[2,80,256]{2,1,0:T(8,128)(2,1)S(1)} %slice.4.refs_5_), channel_id=1, source_target_pairs={{0,4},{4,0},{8,12},{12,8},{16,20},{20,16},{24,28},{28,24},{1,5},{5... | collective-permute-start | bytes 245768 | tf_op jit(solution)/shard_map/ppermute | solution.py:30
  30.5 15.0 %collective-permute-start.9 = (bf16[128,512]{1,0:T(8,128)(2,1)S(1)}, bf16[128,512]{1,0:T(8,128)(2,1)S(1)}, u32[]{:S(2)}, u32[]{:S(2)}) collective-permute-start(bf16[128,512]{1,0:T(8,128)(2,1)S(1)} %shard_map.118.refs_4_), channel_id=1, source_target_pairs={{0,24},{4,28},{8,16},{12,20},{16,8},{20,12},{24,0},{28,4},{1,25},{... | collective-permute-start | bytes 393224 | tf_op jit(solution)/shard_map/ppermute | solution.py:30
  34.3 11.3 %collective-permute-start.10 = (bf16[128,512]{1,0:T(8,128)(2,1)S(1)}, bf16[128,512]{1,0:T(8,128)(2,1)S(1)}, u32[]{:S(2)}, u32[]{:S(2)}) collective-permute-start(bf16[128,512]{1,0:T(8,128)(2,1)S(1)} %shard_map.119.refs_4_), channel_id=1, source_target_pairs={{0,8},{4,12},{8,0},{12,4},{16,24},{20,28},{24,16},{28,20},{1,9},{5... | collective-permute-start | bytes 393224 | tf_op jit(solution)/shard_map/ppermute | solution.py:30
  34.7 10.8 %collective-permute-start.13 = (bf16[128,512]{1,0:T(8,128)(2,1)S(1)}, bf16[128,512]{1,0:T(8,128)(2,1)S(1)}, u32[]{:S(2)}, u32[]{:S(2)}) collective-permute-start(bf16[128,512]{1,0:T(8,128)(2,1)S(1)} %shard_map.120.refs_7_), channel_id=1, source_target_pairs={{0,16},{4,20},{8,24},{12,28},{16,0},{20,4},{24,8},{28,12},{1,17},{... | collective-permute-start | bytes 393224 | tf_op jit(solution)/shard_map/ppermute | solution.py:30
  37.7 13.0 %collective-permute-start.15 = (bf16[3,4,80,256]{3,2,1,0:T(8,128)(2,1)S(1)}, bf16[3,4,80,256]{3,2,1,0:T(8,128)(2,1)S(1)}, u32[]{:S(2)}, u32[]{:S(2)}) collective-permute-start(bf16[3,4,80,256]{3,2,1,0:T(8,128)(2,1)S(1)} %get-tuple-element.40), channel_id=1, source_target_pairs={{0,1},{1,0},{2,3},{3,2},{4,5},{5,4},{6,7},{7,6},{8,9},{9,8},{10,11... | collective-permute-start | bytes 1474568 | tf_op jit(solution)/shard_map/ppermute | solution.py:30
  45.7 8.3 %collective-permute-start.18 = (bf16[128,512]{1,0:T(8,128)(2,1)S(1)}, bf16[128,512]{1,0:T(8,128)(2,1)S(1)}, u32[]{:S(2)}, u32[]{:S(2)}) collective-permute-start(bf16[128,512]{1,0:T(8,128)(2,1)S(1)} %get-tuple-element.41.refs_8_.refs_1_), channel_id=1, source_target_pairs={{0,24},{4,28},{8,16},{12,20},{16,8},{20,12},{24,0},{28,4},{1,25},{... | collective-permute-start | bytes 393224 | tf_op jit(solution)/shard_map/ppermute | solution.py:30
  48.3 10.1 %collective-permute-start.17 = (bf16[128,512]{1,0:T(8,128)(2,1)S(1)}, bf16[128,512]{1,0:T(8,128)(2,1)S(1)}, u32[]{:S(2)}, u32[]{:S(2)}) collective-permute-start(bf16[128,512]{1,0:T(8,128)(2,1)S(1)} %get-tuple-element.41.refs_8_.refs_1_), channel_id=1, source_target_pairs={{0,16},{4,20},{8,24},{12,28},{16,0},{20,4},{24,8},{28,12},{1,17},{... | collective-permute-start | bytes 393224 | tf_op jit(solution)/shard_map/ppermute | solution.py:30
  48.3 10.1 %collective-permute-start.16 = (bf16[128,512]{1,0:T(8,128)(2,1)S(1)}, bf16[128,512]{1,0:T(8,128)(2,1)S(1)}, u32[]{:S(2)}, u32[]{:S(2)}) collective-permute-start(bf16[128,512]{1,0:T(8,128)(2,1)S(1)} %get-tuple-element.41.refs_8_.refs_1_), channel_id=1, source_target_pairs={{0,8},{4,12},{8,0},{12,4},{16,24},{20,28},{24,16},{28,20},{1,9},{5... | collective-permute-start | bytes 393224 | tf_op jit(solution)/shard_map/ppermute | solution.py:30
  59.0 1.7 %collective-permute-start.20 = (bf16[320,512]{1,0:T(8,128)(2,1)S(1)}, bf16[320,512]{1,0:T(8,128)(2,1)S(1)}, u32[]{:S(2)}, u32[]{:S(2)}) collective-permute-start(bf16[320,512]{1,0:T(8,128)(2,1)S(1)} %get-tuple-element.43), channel_id=1, source_target_pairs={{0,4},{4,0},{8,12},{12,8},{16,20},{20,16},{24,28},{28,24},{1,5},{5... | collective-permute-start | bytes 983048 | tf_op jit(solution)/shard_map/ppermute | solution.py:30
  59.1 4.4 %collective-permute-start.19 = (bf16[320,512]{1,0:T(8,128)(2,1)S(1)}, bf16[320,512]{1,0:T(8,128)(2,1)S(1)}, u32[]{:S(2)}, u32[]{:S(2)}) collective-permute-start(bf16[320,512]{1,0:T(8,128)(2,1)S(1)} %get-tuple-element.42), channel_id=1, source_target_pairs={{0,4},{4,0},{8,12},{12,8},{16,20},{20,16},{24,28},{28,24},{1,5},{5... | collective-permute-start | bytes 983048 | tf_op jit(solution)/shard_map/ppermute | solution.py:30
  60.7 7.1 %collective-permute-start.22 = (bf16[160,512]{1,0:T(8,128)(2,1)S(1)}, bf16[160,512]{1,0:T(8,128)(2,1)S(1)}, u32[]{:S(2)}, u32[]{:S(2)}) collective-permute-start(bf16[160,512]{1,0:T(8,128)(2,1)S(1)} %get-tuple-element.45), channel_id=1, source_target_pairs={{0,1},{1,0},{2,3},{3,2},{4,5},{5,4},{6,7},{7,6},{8,9},{9,8},{10,11... | collective-permute-start | bytes 491528 | tf_op jit(solution)/shard_map/ppermute | solution.py:30
  62.6 8.0 %collective-permute-start.21 = (bf16[160,512]{1,0:T(8,128)(2,1)S(1)}, bf16[160,512]{1,0:T(8,128)(2,1)S(1)}, u32[]{:S(2)}, u32[]{:S(2)}) collective-permute-start(bf16[160,512]{1,0:T(8,128)(2,1)S(1)} %get-tuple-element.44), channel_id=1, source_target_pairs={{0,1},{1,0},{2,3},{3,2},{4,5},{5,4},{6,7},{7,6},{8,9},{9,8},{10,11... | collective-permute-start | bytes 491528 | tf_op jit(solution)/shard_map/ppermute | solution.py:30

commit v7 on v6

--- a/solution.py
+++ b/solution.py
@@ -19,7 +19,7 @@
 CORES = 2
 f32, bf16 = jnp.float32, jnp.bfloat16
 VMEM = 16 * 2**20
-CUTS = 2
+CUTS = 4
 LAST = 1
 DIRECT = 1
 LONG = 10**11
@@ -263,10 +263,6 @@
         out[there] = value[here]
 
 
-def place_kernel(value, out):
-    out[...] = value[...]
-
-
 def zero_kernel(out):
     out[...] = jnp.zeros(out.shape, out.dtype)
 
@@ -434,6 +430,7 @@
     ]
 
     mate_window = swap(window, "dp", 1)
+
     to_mate, to_next = call(
         border_kernel,
         [shape((4, rows, old_cols), bf16)] * 2,
@@ -488,15 +485,15 @@
         after=parts[-1:],
     )
     incoming = swap(leaving, "group", 1)
-    own_block = blocks[0][0]
-    total = part([own_block], weights, f32, LONG)
+
+    total = part(blocks[0], weights, f32, LONG)
     activated, delta = call(
         delta_kernel, [shape((slots, cols), bf16)] * 2, total, *back, turned
     )
 
-    deltas = [delta] + [swap(delta, "dp", step * CORES) for step in range(1, chips)]
-
-    flat = [p for step in range(chips) for p in blocks[step]]
+    deltas = [delta] + [swap(delta, "dp", step * CORES) for step in steps]
+
+    flat = [p for step in (0, *steps) for p in blocks[step]]
     gathered = call(
         gather_kernel,
         shape((chips * slots, depth), bf16),

time: 72.1 us -> 71.2 us (0.988)
  waiting for transfers between devices: 31.7 us -> 27 us
  starting transfers between devices: 27.2 us -> 29.2 us
  Pallas kernels: 9.73 us -> 11.1 us
    ppermute x22 -> x24, waiting for transfers between devices: 31.7 us -> 27 us  [swap(): return lax.ppermute(value, axis, pairs)]
    ppermute x22 -> x24, starting transfers between devices: 26.4 us -> 28.4 us  [swap(): return lax.ppermute(value, axis, pairs)]
    pallas_call x2 -> x4, Pallas kernels: 2.58 us -> 4.01 us  [second_adam(): pl.pallas_call(functools.partial(second_adam_kernel, cut), out_shape=[sha...]
  transfers between devices with their start and end apart: 23 -> 25, of which waited for: 11 -> 13; matrix products, arithmetic and copies ran while one was open for 0% -> 0% of each run, Pallas kernels for 10% -> 12%
where the time goes in v7:
time: 71.2 us; the launch traced here: 70.7 us
  starting transfers between devices  29.2 us (41%)
  waiting for transfers between devices  27 us (38%)
  Pallas kernels  11.1 us (16%)
  local copies, waits for them, and re-layouts  2.47 us (3%)
  between operations  0.92 us (1%)
    ppermute x24, starting transfers between devices, swap(): return lax.ppermute(value, axis, pairs)  28.4 us
    ppermute x24, waiting for transfers between devices, swap(): return lax.ppermute(value, axis, pairs)  27 us
    pallas_call x16, Pallas kernels, call(): pl.pallas_call(body, out_shape=shapes, in_specs=[small] * scalars + [whol...  6.89 us
    pallas_call x4, Pallas kernels, second_adam(): pl.pallas_call(functools.partial(second_adam_kernel, cut), out_shape=[sha...  4.01 us
    unnamed x16, local copies, waits for them, and re-layouts  2.46 us
  transfers between devices with their start and end apart: 25, of which 13 were waited for; matrix products, arithmetic and copies ran while one was open for 0% of the time, Pallas kernels for 12%

profile of v7, /device:TPU:0, one launch (start us, length us, event | category | flops | bytes accessed | tf_op | source)
XLA Modules:
  0.0 70.7 jit_solution(3155940595247142189)
XLA Ops:
  0.7 1.3 %copy-done = bf16[128,5120]{1,0:T(8,128)(2,1)S(1)} copy-done((bf16[128,5120]{1,0:T(8,128)(2,1)S(1)}, bf16[128,5120]{1,0:T(8,128)(2,1)}, u32[]{:S(2)}) %copy-start) | copy-done | bytes 1310744
  2.7 0.6 copy-done.1
  3.3 0.7 shard_map.113
  3.9 3.0 %collective-permute-start = (bf16[10,80,256]{2,1,0:T(8,128)(2,1)S(1)}, bf16[10,80,256]{2,1,0:T(8,128)(2,1)S(1)}, u32[]{:S(2)}, u32[]{:S(2)}) collective-permute-start(bf16[10,80,256]{2,1,0:T(8,128)(2,1)S(1)} %get-tuple-element.37.refs_0_.refs_1_), channel_id=1, source_target_pairs={{0,1},{1,0},{2,3},{3,2},{4,5},{5,4},{6,7},{7,6},{8,9},{9,8},{10,11... | collective-permute-start | bytes 1228808 | tf_op jit(solution)/shard_map/ppermute | solution.py:30
  7.0 1.6 %collective-permute-start.4 = (bf16[64,1280]{1,0:T(8,128)(2,1)S(1)}, bf16[64,1280]{1,0:T(8,128)(2,1)S(1)}, u32[]{:S(2)}, u32[]{:S(2)}) collective-permute-start(bf16[64,1280]{1,0:T(8,128)(2,1)S(1)} %get-tuple-element.36.refs_4_), channel_id=1, source_target_pairs={{0,8},{4,12},{8,0},{12,4},{16,24},{20,28},{24,16},{28,20},{1,9},{5... | collective-permute-start | bytes 491528 | tf_op jit(solution)/shard_map/ppermute | solution.py:30
  8.6 2.5 %collective-permute-start.7 = (bf16[64,1280]{1,0:T(8,128)(2,1)S(1)}, bf16[64,1280]{1,0:T(8,128)(2,1)S(1)}, u32[]{:S(2)}, u32[]{:S(2)}) collective-permute-start(bf16[64,1280]{1,0:T(8,128)(2,1)S(1)} %get-tuple-element.43), channel_id=1, source_target_pairs={{0,24},{4,28},{8,16},{12,20},{16,8},{20,12},{24,0},{28,4},{1,25},{... | collective-permute-start | bytes 491528 | tf_op jit(solution)/shard_map/ppermute | solution.py:30
  11.1 5.3 %collective-permute-done.refs_0_.refs_1_.refs_2_ = bf16[10,80,256]{2,1,0:T(8,128)(2,1)S(1)} collective-permute-done((bf16[10,80,256]{2,1,0:T(8,128)(2,1)S(1)}, bf16[10,80,256]{2,1,0:T(8,128)(2,1)S(1)}, u32[]{:S(2)}, u32[]{:S(2)}) %collective-permute-start) | collective-permute-done | bytes 409632 | tf_op jit(solution)/shard_map/ppermute | solution.py:30
  16.6 0.8 %collective-permute-start.3 = (bf16[4,80,256]{2,1,0:T(8,128)(2,1)S(1)}, bf16[4,80,256]{2,1,0:T(8,128)(2,1)S(1)}, u32[]{:S(2)}, u32[]{:S(2)}) collective-permute-start(bf16[4,80,256]{2,1,0:T(8,128)(2,1)S(1)} %get-tuple-element.39), channel_id=1, source_target_pairs={{4,8},{8,4},{12,16},{16,12},{20,24},{24,20},{5,9},{9,5},{13,17},{1... | collective-permute-start | bytes 491528 | tf_op jit(solution)/shard_map/ppermute | solution.py:37
  17.4 1.8 %collective-permute-start.5 = (bf16[64,1280]{1,0:T(8,128)(2,1)S(1)}, bf16[64,1280]{1,0:T(8,128)(2,1)S(1)}, u32[]{:S(2)}, u32[]{:S(2)}) collective-permute-start(bf16[64,1280]{1,0:T(8,128)(2,1)S(1)} %collective-permute-done.4.refs_0_.refs_3_), channel_id=1, source_target_pairs={{0,2},{2,0},{1,3},{3,1},{4,6},{6,4},{5,7},{7,5},{8,10},{10,8},{9,1... | collective-permute-start | bytes 491528 | tf_op jit(solution)/shard_map/ppermute | solution.py:30
  19.6 1.5 %collective-permute-start.8 = (bf16[64,1280]{1,0:T(8,128)(2,1)S(1)}, bf16[64,1280]{1,0:T(8,128)(2,1)S(1)}, u32[]{:S(2)}, u32[]{:S(2)}) collective-permute-start(bf16[64,1280]{1,0:T(8,128)(2,1)S(1)} %collective-permute-done.7.refs_0_.refs_1_), channel_id=1, source_target_pairs={{0,2},{2,0},{1,3},{3,1},{4,6},{6,4},{5,7},{7,5},{8,10},{10,8},{9,1... | collective-permute-start | bytes 491528 | tf_op jit(solution)/shard_map/ppermute | solution.py:30
  21.1 5.3 %collective-permute-done.11.refs_0_.refs_5_ = bf16[64,1280]{1,0:T(8,128)(2,1)S(1)} collective-permute-done((bf16[64,1280]{1,0:T(8,128)(2,1)S(1)}, bf16[64,1280]{1,0:T(8,128)(2,1)S(1)}, u32[]{:S(2)}, u32[]{:S(2)}) %collective-permute-start.11) | collective-permute-done | bytes 163872 | tf_op jit(solution)/shard_map/ppermute | solution.py:30
  26.4 1.5 %collective-permute-start.12 = (bf16[64,1280]{1,0:T(8,128)(2,1)S(1)}, bf16[64,1280]{1,0:T(8,128)(2,1)S(1)}, u32[]{:S(2)}, u32[]{:S(2)}) collective-permute-start(bf16[64,1280]{1,0:T(8,128)(2,1)S(1)} %collective-permute-done.11.refs_0_.refs_5_), channel_id=1, source_target_pairs={{0,2},{2,0},{1,3},{3,1},{4,6},{6,4},{5,7},{7,5},{8,10},{10,8},{9,1... | collective-permute-start | bytes 491528 | tf_op jit(solution)/shard_map/ppermute | solution.py:30
  29.4 0.8 %shard_map.116 = (bf16[8,80,512]{2,1,0:T(8,128)(2,1)S(1)}, bf16[8,80,512]{2,1,0:T(8,128)(2,1)S(1)}) custom-call(s32[4,9]{1,0:T(4,128)S(1)} %copy-done.6, bf16[10,80,256]{2,1,0:T(8,128)(2,1)S(1)} %get-tuple-element.37.refs_0_.refs_1_, bf16[10,80,256]{2,1,0:T(8,128)(2,1)S(1)} %collective-permute-done.refs_0_.refs_1_.refs_2_, ...), custom_call_target="tpu_custom_call" | custom-call | bytes 1802384 | tf_op jit(solution)/shard_map/pallas_call | solution.py:58
  30.5 3.3 %collective-permute-start.9 = (bf16[128,512]{1,0:T(8,128)(2,1)S(1)}, bf16[128,512]{1,0:T(8,128)(2,1)S(1)}, u32[]{:S(2)}, u32[]{:S(2)}) collective-permute-start(bf16[128,512]{1,0:T(8,128)(2,1)S(1)} %shard_map.118.refs_4_), channel_id=1, source_target_pairs={{0,24},{4,28},{8,16},{12,20},{16,8},{20,12},{24,0},{28,4},{1,25},{... | collective-permute-start | bytes 393224 | tf_op jit(solution)/shard_map/ppermute | solution.py:30
  34.7 1.7 %collective-permute-start.13 = (bf16[128,512]{1,0:T(8,128)(2,1)S(1)}, bf16[128,512]{1,0:T(8,128)(2,1)S(1)}, u32[]{:S(2)}, u32[]{:S(2)}) collective-permute-start(bf16[128,512]{1,0:T(8,128)(2,1)S(1)} %shard_map.120.refs_7_), channel_id=1, source_target_pairs={{0,16},{4,20},{8,24},{12,28},{16,0},{20,4},{24,8},{28,12},{1,17},{... | collective-permute-start | bytes 393224 | tf_op jit(solution)/shard_map/ppermute | solution.py:30
  36.4 1.3 %shard_map.124 = (bf16[3,4,80,256]{3,2,1,0:T(8,128)(2,1)S(1)}, f32[3,4,80,256]{3,2,1,0:T(8,128)S(1)}) custom-call(s32[4,9]{1,0:T(4,128)S(1)} %copy-done.6, f32[10,160,128]{2,1,0:T(8,128)S(1)} %bitcast.15, f32[10,160,128]{2,1,0:T(8,128)S(1)} %bitcast.17, f32[10,160,128]{2,1,0:T(8,128)S(1)} %bitcast.19, f32[10,160,128]{2,1,0:T(8,128)S(1)} %bitcast.21, ...), custom_call_target="tpu_custom_call" | custom-call | bytes 3604624 | tf_op jit(solution)/shard_map/pallas_call | solution.py:58
  37.7 1.6 %collective-permute-start.15 = (bf16[3,4,80,256]{3,2,1,0:T(8,128)(2,1)S(1)}, bf16[3,4,80,256]{3,2,1,0:T(8,128)(2,1)S(1)}, u32[]{:S(2)}, u32[]{:S(2)}) collective-permute-start(bf16[3,4,80,256]{3,2,1,0:T(8,128)(2,1)S(1)} %get-tuple-element.48), channel_id=1, source_target_pairs={{0,1},{1,0},{2,3},{3,2},{4,5},{5,4},{6,7},{7,6},{8,9},{9,8},{10,11... | collective-permute-start | bytes 1474568 | tf_op jit(solution)/shard_map/ppermute | solution.py:30
  39.7 5.8 %collective-permute-done.13.refs_3_ = bf16[128,512]{1,0:T(8,128)(2,1)S(1)} collective-permute-done((bf16[128,512]{1,0:T(8,128)(2,1)S(1)}, bf16[128,512]{1,0:T(8,128)(2,1)S(1)}, u32[]{:S(2)}, u32[]{:S(2)}) %collective-permute-start.13) | collective-permute-done | bytes 131104 | tf_op jit(solution)/shard_map/ppermute | solution.py:30
  45.7 0.9 %collective-permute-start.18 = (bf16[128,512]{1,0:T(8,128)(2,1)S(1)}, bf16[128,512]{1,0:T(8,128)(2,1)S(1)}, u32[]{:S(2)}, u32[]{:S(2)}) collective-permute-start(bf16[128,512]{1,0:T(8,128)(2,1)S(1)} %get-tuple-element.49.refs_8_.refs_1_), channel_id=1, source_target_pairs={{0,16},{4,20},{8,24},{12,28},{16,0},{20,4},{24,8},{28,12},{1,17},{... | collective-permute-start | bytes 393224 | tf_op jit(solution)/shard_map/ppermute | solution.py:30
  46.5 2.3 %collective-permute-start.17 = (bf16[128,512]{1,0:T(8,128)(2,1)S(1)}, bf16[128,512]{1,0:T(8,128)(2,1)S(1)}, u32[]{:S(2)}, u32[]{:S(2)}) collective-permute-start(bf16[128,512]{1,0:T(8,128)(2,1)S(1)} %get-tuple-element.49.refs_8_.refs_1_), channel_id=1, source_target_pairs={{0,8},{4,12},{8,0},{12,4},{16,24},{20,28},{24,16},{28,20},{1,9},{5... | collective-permute-start | bytes 393224 | tf_op jit(solution)/shard_map/ppermute | solution.py:30
  48.9 1.3 %collective-permute-start.16 = (bf16[128,512]{1,0:T(8,128)(2,1)S(1)}, bf16[128,512]{1,0:T(8,128)(2,1)S(1)}, u32[]{:S(2)}, u32[]{:S(2)}) collective-permute-start(bf16[128,512]{1,0:T(8,128)(2,1)S(1)} %get-tuple-element.49.refs_8_.refs_1_), channel_id=1, source_target_pairs={{0,24},{4,28},{8,16},{12,20},{16,8},{20,12},{24,0},{28,4},{1,25},{... | collective-permute-start | bytes 393224 | tf_op jit(solution)/shard_map/ppermute | solution.py:30
  50.1 0.6 collective-permute-done.15.refs_7_.incoming
  50.8 6.6 %collective-permute-done.18.refs_4_ = bf16[128,512]{1,0:T(8,128)(2,1)S(1)} collective-permute-done((bf16[128,512]{1,0:T(8,128)(2,1)S(1)}, bf16[128,512]{1,0:T(8,128)(2,1)S(1)}, u32[]{:S(2)}, u32[]{:S(2)}) %collective-permute-start.18) | collective-permute-done | bytes 131104 | tf_op jit(solution)/shard_map/ppermute | solution.py:30
  59.8 1.6 %collective-permute-start.24 = (bf16[80,512]{1,0:T(8,128)(2,1)S(1)}, bf16[80,512]{1,0:T(8,128)(2,1)S(1)}, u32[]{:S(2)}, u32[]{:S(2)}) collective-permute-start(bf16[80,512]{1,0:T(8,128)(2,1)S(1)} %get-tuple-element.55), channel_id=1, source_target_pairs={{0,1},{1,0},{2,3},{3,2},{4,5},{5,4},{6,7},{7,6},{8,9},{9,8},{10,11... | collective-permute-start | bytes 245768 | tf_op jit(solution)/shard_map/ppermute | solution.py:30
  61.9 1.5 %collective-permute-start.22 = (bf16[80,512]{1,0:T(8,128)(2,1)S(1)}, bf16[80,512]{1,0:T(8,128)(2,1)S(1)}, u32[]{:S(2)}, u32[]{:S(2)}) collective-permute-start(bf16[80,512]{1,0:T(8,128)(2,1)S(1)} %get-tuple-element.53), channel_id=1, source_target_pairs={{0,1},{1,0},{2,3},{3,2},{4,5},{5,4},{6,7},{7,6},{8,9},{9,8},{10,11... | collective-permute-start | bytes 245768 | tf_op jit(solution)/shard_map/ppermute | solution.py:30
  64.0 0.7 shard_map.123
  65.0 1.0 %shard_map.129 = (f32[320,512]{1,0:T(8,128)}, f32[320,512]{1,0:T(8,128)}, f32[320,512]{1,0:T(8,128)}) custom-call(f32[3,4,80,256]{3,2,1,0:T(8,128)S(1)} %get-tuple-element.47.staying, bf16[3,4,80,256]{3,2,1,0:T(8,128)(2,1)S(1)} %collective-permute-done.15.refs_7_.incoming, f32[2,320,512]{2,1,0:T(8,128)S(1)} %shard_map.126.refs_0_.mine, ...), custom_call_target="tpu_custom_call" | custom-call | bytes 1000000 | tf_op jit(solution)/shard_map/pallas_call | solution.py:350
  66.0 0.8 %collective-permute-done.23.back = bf16[80,512]{1,0:T(8,128)(2,1)S(1)} collective-permute-done((bf16[80,512]{1,0:T(8,128)(2,1)S(1)}, bf16[80,512]{1,0:T(8,128)(2,1)S(1)}, u32[]{:S(2)}, u32[]{:S(2)}) %collective-permute-start.23) | collective-permute-done | bytes 81952 | tf_op jit(solution)/shard_map/ppermute | solution.py:30
  66.8 1.0 %shard_map.130 = (f32[320,512]{1,0:T(8,128)}, f32[320,512]{1,0:T(8,128)}, f32[320,512]{1,0:T(8,128)}) custom-call(f32[3,4,80,256]{3,2,1,0:T(8,128)S(1)} %get-tuple-element.47.staying, bf16[3,4,80,256]{3,2,1,0:T(8,128)(2,1)S(1)} %collective-permute-done.15.refs_7_.incoming, ...), custom_call_target="tpu_custom_call", output_to_operand_aliasing={{0}: (5, {}), {1}: (6, {}), {2}: (7, {})} | custom-call | bytes 1000000 | tf_op jit(solution)/shard_map/pallas_call | solution.py:350
  67.8 0.7 %collective-permute-done.22.back = bf16[80,512]{1,0:T(8,128)(2,1)S(1)} collective-permute-done((bf16[80,512]{1,0:T(8,128)(2,1)S(1)}, bf16[80,512]{1,0:T(8,128)(2,1)S(1)}, u32[]{:S(2)}, u32[]{:S(2)}) %collective-permute-start.22) | collective-permute-done | bytes 81952 | tf_op jit(solution)/shard_map/ppermute | solution.py:30
  68.5 1.0 %shard_map.131 = (f32[320,512]{1,0:T(8,128)}, f32[320,512]{1,0:T(8,128)}, f32[320,512]{1,0:T(8,128)}) custom-call(f32[3,4,80,256]{3,2,1,0:T(8,128)S(1)} %get-tuple-element.47.staying, bf16[3,4,80,256]{3,2,1,0:T(8,128)(2,1)S(1)} %collective-permute-done.15.refs_7_.incoming, ...), custom_call_target="tpu_custom_call", output_to_operand_aliasing={{0}: (5, {}), {1}: (6, {}), {2}: (7, {})} | custom-call | bytes 1000000 | tf_op jit(solution)/shard_map/pallas_call | solution.py:350
  69.7 1.0 %shard_map.132 = (f32[320,512]{1,0:T(8,128)}, f32[320,512]{1,0:T(8,128)}, f32[320,512]{1,0:T(8,128)}) custom-call(f32[3,4,80,256]{3,2,1,0:T(8,128)S(1)} %get-tuple-element.47.staying, bf16[3,4,80,256]{3,2,1,0:T(8,128)(2,1)S(1)} %collective-permute-done.15.refs_7_.incoming, ...), custom_call_target="tpu_custom_call", output_to_operand_aliasing={{0}: (5, {}), {1}: (6, {}), {2}: (7, {})} | custom-call | bytes 1000000 | tf_op jit(solution)/shard_map/pallas_call | solution.py:350
  (57 shorter events, 8.6 us)
Async XLA Ops:
  0.6 1.5 %copy-start.2 = (f32[1,1,204800]{2,1,0:T(1,128)S(1)}, f32[1,1,204800]{2,1,0:T(1,128)}, u32[]{:S(2)}) copy-start(f32[1,1,204800]{2,1,0:T(1,128)} %param.13) | copy-start | bytes 2457604
  0.7 1.8 %copy-start.3 = (f32[1,1,204800]{2,1,0:T(1,128)S(1)}, f32[1,1,204800]{2,1,0:T(1,128)}, u32[]{:S(2)}) copy-start(f32[1,1,204800]{2,1,0:T(1,128)} %param.14) | copy-start | bytes 2457604
  0.7 2.0 %copy-start.4 = (f32[1,1,204800]{2,1,0:T(1,128)S(1)}, f32[1,1,204800]{2,1,0:T(1,128)}, u32[]{:S(2)}) copy-start(f32[1,1,204800]{2,1,0:T(1,128)} %param.15) | copy-start | bytes 2457604
  1.9 1.3 %copy-start.1 = (f32[1,1,204800]{2,1,0:T(1,128)S(1)}, f32[1,1,204800]{2,1,0:T(1,128)}, u32[]{:S(2)}) copy-start(f32[1,1,204800]{2,1,0:T(1,128)} %param.12) | copy-start | bytes 2457604
  3.9 12.5 %collective-permute-start = (bf16[10,80,256]{2,1,0:T(8,128)(2,1)S(1)}, bf16[10,80,256]{2,1,0:T(8,128)(2,1)S(1)}, u32[]{:S(2)}, u32[]{:S(2)}) collective-permute-start(bf16[10,80,256]{2,1,0:T(8,128)(2,1)S(1)} %get-tuple-element.37.refs_0_.refs_1_), channel_id=1, source_target_pairs={{0,1},{1,0},{2,3},{3,2},{4,5},{5,4},{6,7},{7,6},{8,9},{9,8},{10,11... | collective-permute-start | bytes 1228808 | tf_op jit(solution)/shard_map/ppermute | solution.py:30
  7.0 9.5 %collective-permute-start.1 = (bf16[10,80,256]{2,1,0:T(8,128)(2,1)S(1)}, bf16[10,80,256]{2,1,0:T(8,128)(2,1)S(1)}, u32[]{:S(2)}, u32[]{:S(2)}) collective-permute-start(bf16[10,80,256]{2,1,0:T(8,128)(2,1)S(1)} %get-tuple-element.37.refs_0_.refs_1_), channel_id=1, source_target_pairs={{0,4},{4,0},{8,12},{12,8},{16,20},{20,16},{24,28},{28,24},{1,5},{5... | collective-permute-start | bytes 1228808 | tf_op jit(solution)/shard_map/ppermute | solution.py:30
  7.0 10.4 %collective-permute-start.4 = (bf16[64,1280]{1,0:T(8,128)(2,1)S(1)}, bf16[64,1280]{1,0:T(8,128)(2,1)S(1)}, u32[]{:S(2)}, u32[]{:S(2)}) collective-permute-start(bf16[64,1280]{1,0:T(8,128)(2,1)S(1)} %get-tuple-element.36.refs_4_), channel_id=1, source_target_pairs={{0,8},{4,12},{8,0},{12,4},{16,24},{20,28},{24,16},{28,20},{1,9},{5... | collective-permute-start | bytes 491528 | tf_op jit(solution)/shard_map/ppermute | solution.py:30
  8.6 11.1 %collective-permute-start.7 = (bf16[64,1280]{1,0:T(8,128)(2,1)S(1)}, bf16[64,1280]{1,0:T(8,128)(2,1)S(1)}, u32[]{:S(2)}, u32[]{:S(2)}) collective-permute-start(bf16[64,1280]{1,0:T(8,128)(2,1)S(1)} %get-tuple-element.43), channel_id=1, source_target_pairs={{0,24},{4,28},{8,16},{12,20},{16,8},{20,12},{24,0},{28,4},{1,25},{... | collective-permute-start | bytes 491528 | tf_op jit(solution)/shard_map/ppermute | solution.py:30
  11.0 15.3 %collective-permute-start.11 = (bf16[64,1280]{1,0:T(8,128)(2,1)S(1)}, bf16[64,1280]{1,0:T(8,128)(2,1)S(1)}, u32[]{:S(2)}, u32[]{:S(2)}) collective-permute-start(bf16[64,1280]{1,0:T(8,128)(2,1)S(1)} %get-tuple-element.44), channel_id=1, source_target_pairs={{0,16},{4,20},{8,24},{12,28},{16,0},{20,4},{24,8},{28,12},{1,17},{... | collective-permute-start | bytes 491528 | tf_op jit(solution)/shard_map/ppermute | solution.py:30
  16.4 13.0 %collective-permute-start.2 = (bf16[10,80,256]{2,1,0:T(8,128)(2,1)S(1)}, bf16[10,80,256]{2,1,0:T(8,128)(2,1)S(1)}, u32[]{:S(2)}, u32[]{:S(2)}) collective-permute-start(bf16[10,80,256]{2,1,0:T(8,128)(2,1)S(1)} %collective-permute-done.refs_0_.refs_1_.refs_2_), channel_id=1, source_target_pairs={{0,4},{4,0},{8,12},{12,8},{16,20},{20,16},{24,28},{28,24},{1,5},{5... | collective-permute-start | bytes 1228808 | tf_op jit(solution)/shard_map/ppermute | solution.py:30
  16.5 12.0 %copy-start.5 = (bf16[128,512]{1,0:T(8,128)(2,1)S(1)}, bf16[128,512]{1,0:T(8,128)(2,1)}, u32[]{:S(2)}) copy-start(bf16[128,512]{1,0:T(8,128)(2,1)} %refs_1_.1) | copy-start | bytes 393220
  16.5 12.0 %copy-start.7 = (s32[16]{0:T(128)S(1)}, s32[16]{0:T(128)}, u32[]{:S(2)}) copy-start(s32[16]{0:T(128)} %refs_0_.4) | copy-start | bytes 196
  16.6 11.3 %collective-permute-start.3 = (bf16[4,80,256]{2,1,0:T(8,128)(2,1)S(1)}, bf16[4,80,256]{2,1,0:T(8,128)(2,1)S(1)}, u32[]{:S(2)}, u32[]{:S(2)}) collective-permute-start(bf16[4,80,256]{2,1,0:T(8,128)(2,1)S(1)} %get-tuple-element.39), channel_id=1, source_target_pairs={{4,8},{8,4},{12,16},{16,12},{20,24},{24,20},{5,9},{9,5},{13,17},{1... | collective-permute-start | bytes 491528 | tf_op jit(solution)/shard_map/ppermute | solution.py:37
  17.4 10.5 %collective-permute-start.5 = (bf16[64,1280]{1,0:T(8,128)(2,1)S(1)}, bf16[64,1280]{1,0:T(8,128)(2,1)S(1)}, u32[]{:S(2)}, u32[]{:S(2)}) collective-permute-start(bf16[64,1280]{1,0:T(8,128)(2,1)S(1)} %collective-permute-done.4.refs_0_.refs_3_), channel_id=1, source_target_pairs={{0,2},{2,0},{1,3},{3,1},{4,6},{6,4},{5,7},{7,5},{8,10},{10,8},{9,1... | collective-permute-start | bytes 491528 | tf_op jit(solution)/shard_map/ppermute | solution.py:30
  19.6 10.5 %collective-permute-start.8 = (bf16[64,1280]{1,0:T(8,128)(2,1)S(1)}, bf16[64,1280]{1,0:T(8,128)(2,1)S(1)}, u32[]{:S(2)}, u32[]{:S(2)}) collective-permute-start(bf16[64,1280]{1,0:T(8,128)(2,1)S(1)} %collective-permute-done.7.refs_0_.refs_1_), channel_id=1, source_target_pairs={{0,2},{2,0},{1,3},{3,1},{4,6},{6,4},{5,7},{7,5},{8,10},{10,8},{9,1... | collective-permute-start | bytes 491528 | tf_op jit(solution)/shard_map/ppermute | solution.py:30
  26.4 8.0 %collective-permute-start.12 = (bf16[64,1280]{1,0:T(8,128)(2,1)S(1)}, bf16[64,1280]{1,0:T(8,128)(2,1)S(1)}, u32[]{:S(2)}, u32[]{:S(2)}) collective-permute-start(bf16[64,1280]{1,0:T(8,128)(2,1)S(1)} %collective-permute-done.11.refs_0_.refs_5_), channel_id=1, source_target_pairs={{0,2},{2,0},{1,3},{3,1},{4,6},{6,4},{5,7},{7,5},{8,10},{10,8},{9,1... | collective-permute-start | bytes 491528 | tf_op jit(solution)/shard_map/ppermute | solution.py:30
  27.9 8.6 %collective-permute-start.14 = (bf16[4,80,256]{2,1,0:T(8,128)(2,1)S(1)}, bf16[4,80,256]{2,1,0:T(8,128)(2,1)S(1)}, u32[]{:S(2)}, u32[]{:S(2)}) collective-permute-start(bf16[4,80,256]{2,1,0:T(8,128)(2,1)S(1)} %get-tuple-element.46), channel_id=1, source_target_pairs={{0,4},{4,0},{8,12},{12,8},{16,20},{20,16},{24,28},{28,24},{1,5},{5... | collective-permute-start | bytes 491528 | tf_op jit(solution)/shard_map/ppermute | solution.py:30
  27.9 1.5 %copy-start.6 = (s32[4,9]{1,0:T(4,128)S(1)}, s32[4,9]{1,0:T(4,128)}, u32[]{:S(2)}) copy-start(s32[4,9]{1,0:T(4,128)} %refs_0_.5) | copy-start | bytes 436
  27.9 1.5 %collective-permute-start.6 = (bf16[2,80,256]{2,1,0:T(8,128)(2,1)S(1)}, bf16[2,80,256]{2,1,0:T(8,128)(2,1)S(1)}, u32[]{:S(2)}, u32[]{:S(2)}) collective-permute-start(bf16[2,80,256]{2,1,0:T(8,128)(2,1)S(1)} %slice.4.refs_5_), channel_id=1, source_target_pairs={{0,4},{4,0},{8,12},{12,8},{16,20},{20,16},{24,28},{28,24},{1,5},{5... | collective-permute-start | bytes 245768 | tf_op jit(solution)/shard_map/ppermute | solution.py:30
  30.5 15.0 %collective-permute-start.9 = (bf16[128,512]{1,0:T(8,128)(2,1)S(1)}, bf16[128,512]{1,0:T(8,128)(2,1)S(1)}, u32[]{:S(2)}, u32[]{:S(2)}) collective-permute-start(bf16[128,512]{1,0:T(8,128)(2,1)S(1)} %shard_map.118.refs_4_), channel_id=1, source_target_pairs={{0,24},{4,28},{8,16},{12,20},{16,8},{20,12},{24,0},{28,4},{1,25},{... | collective-permute-start | bytes 393224 | tf_op jit(solution)/shard_map/ppermute | solution.py:30
  34.3 11.3 %collective-permute-start.10 = (bf16[128,512]{1,0:T(8,128)(2,1)S(1)}, bf16[128,512]{1,0:T(8,128)(2,1)S(1)}, u32[]{:S(2)}, u32[]{:S(2)}) collective-permute-start(bf16[128,512]{1,0:T(8,128)(2,1)S(1)} %shard_map.119.refs_4_), channel_id=1, source_target_pairs={{0,8},{4,12},{8,0},{12,4},{16,24},{20,28},{24,16},{28,20},{1,9},{5... | collective-permute-start | bytes 393224 | tf_op jit(solution)/shard_map/ppermute | solution.py:30
  34.7 10.8 %collective-permute-start.13 = (bf16[128,512]{1,0:T(8,128)(2,1)S(1)}, bf16[128,512]{1,0:T(8,128)(2,1)S(1)}, u32[]{:S(2)}, u32[]{:S(2)}) collective-permute-start(bf16[128,512]{1,0:T(8,128)(2,1)S(1)} %shard_map.120.refs_7_), channel_id=1, source_target_pairs={{0,16},{4,20},{8,24},{12,28},{16,0},{20,4},{24,8},{28,12},{1,17},{... | collective-permute-start | bytes 393224 | tf_op jit(solution)/shard_map/ppermute | solution.py:30
  37.7 13.0 %collective-permute-start.15 = (bf16[3,4,80,256]{3,2,1,0:T(8,128)(2,1)S(1)}, bf16[3,4,80,256]{3,2,1,0:T(8,128)(2,1)S(1)}, u32[]{:S(2)}, u32[]{:S(2)}) collective-permute-start(bf16[3,4,80,256]{3,2,1,0:T(8,128)(2,1)S(1)} %get-tuple-element.48), channel_id=1, source_target_pairs={{0,1},{1,0},{2,3},{3,2},{4,5},{5,4},{6,7},{7,6},{8,9},{9,8},{10,11... | collective-permute-start | bytes 1474568 | tf_op jit(solution)/shard_map/ppermute | solution.py:30
  45.7 11.7 %collective-permute-start.18 = (bf16[128,512]{1,0:T(8,128)(2,1)S(1)}, bf16[128,512]{1,0:T(8,128)(2,1)S(1)}, u32[]{:S(2)}, u32[]{:S(2)}) collective-permute-start(bf16[128,512]{1,0:T(8,128)(2,1)S(1)} %get-tuple-element.49.refs_8_.refs_1_), channel_id=1, source_target_pairs={{0,16},{4,20},{8,24},{12,28},{16,0},{20,4},{24,8},{28,12},{1,17},{... | collective-permute-start | bytes 393224 | tf_op jit(solution)/shard_map/ppermute | solution.py:30
  46.5 11.0 %collective-permute-start.17 = (bf16[128,512]{1,0:T(8,128)(2,1)S(1)}, bf16[128,512]{1,0:T(8,128)(2,1)S(1)}, u32[]{:S(2)}, u32[]{:S(2)}) collective-permute-start(bf16[128,512]{1,0:T(8,128)(2,1)S(1)} %get-tuple-element.49.refs_8_.refs_1_), channel_id=1, source_target_pairs={{0,8},{4,12},{8,0},{12,4},{16,24},{20,28},{24,16},{28,20},{1,9},{5... | collective-permute-start | bytes 393224 | tf_op jit(solution)/shard_map/ppermute | solution.py:30
  48.9 8.6 %collective-permute-start.16 = (bf16[128,512]{1,0:T(8,128)(2,1)S(1)}, bf16[128,512]{1,0:T(8,128)(2,1)S(1)}, u32[]{:S(2)}, u32[]{:S(2)}) collective-permute-start(bf16[128,512]{1,0:T(8,128)(2,1)S(1)} %get-tuple-element.49.refs_8_.refs_1_), channel_id=1, source_target_pairs={{0,24},{4,28},{8,16},{12,20},{16,8},{20,12},{24,0},{28,4},{1,25},{... | collective-permute-start | bytes 393224 | tf_op jit(solution)/shard_map/ppermute | solution.py:30
  58.1 1.7 %collective-permute-start.20 = (bf16[320,512]{1,0:T(8,128)(2,1)S(1)}, bf16[320,512]{1,0:T(8,128)(2,1)S(1)}, u32[]{:S(2)}, u32[]{:S(2)}) collective-permute-start(bf16[320,512]{1,0:T(8,128)(2,1)S(1)} %get-tuple-element.51), channel_id=1, source_target_pairs={{0,4},{4,0},{8,12},{12,8},{16,20},{20,16},{24,28},{28,24},{1,5},{5... | collective-permute-start | bytes 983048 | tf_op jit(solution)/shard_map/ppermute | solution.py:30
  58.2 6.5 %collective-permute-start.19 = (bf16[320,512]{1,0:T(8,128)(2,1)S(1)}, bf16[320,512]{1,0:T(8,128)(2,1)S(1)}, u32[]{:S(2)}, u32[]{:S(2)}) collective-permute-start(bf16[320,512]{1,0:T(8,128)(2,1)S(1)} %get-tuple-element.50), channel_id=1, source_target_pairs={{0,4},{4,0},{8,12},{12,8},{16,20},{20,16},{24,28},{28,24},{1,5},{5... | collective-permute-start | bytes 983048 | tf_op jit(solution)/shard_map/ppermute | solution.py:30
  59.8 5.2 %collective-permute-start.24 = (bf16[80,512]{1,0:T(8,128)(2,1)S(1)}, bf16[80,512]{1,0:T(8,128)(2,1)S(1)}, u32[]{:S(2)}, u32[]{:S(2)}) collective-permute-start(bf16[80,512]{1,0:T(8,128)(2,1)S(1)} %get-tuple-element.55), channel_id=1, source_target_pairs={{0,1},{1,0},{2,3},{3,2},{4,5},{5,4},{6,7},{7,6},{8,9},{9,8},{10,11... | collective-permute-start | bytes 245768 | tf_op jit(solution)/shard_map/ppermute | solution.py:30
  61.4 5.3 %collective-permute-start.23 = (bf16[80,512]{1,0:T(8,128)(2,1)S(1)}, bf16[80,512]{1,0:T(8,128)(2,1)S(1)}, u32[]{:S(2)}, u32[]{:S(2)}) collective-permute-start(bf16[80,512]{1,0:T(8,128)(2,1)S(1)} %get-tuple-element.54), channel_id=1, source_target_pairs={{0,1},{1,0},{2,3},{3,2},{4,5},{5,4},{6,7},{7,6},{8,9},{9,8},{10,11... | collective-permute-start | bytes 245768 | tf_op jit(solution)/shard_map/ppermute | solution.py:30
  61.9 6.6 %collective-permute-start.22 = (bf16[80,512]{1,0:T(8,128)(2,1)S(1)}, bf16[80,512]{1,0:T(8,128)(2,1)S(1)}, u32[]{:S(2)}, u32[]{:S(2)}) collective-permute-start(bf16[80,512]{1,0:T(8,128)(2,1)S(1)} %get-tuple-element.53), channel_id=1, source_target_pairs={{0,1},{1,0},{2,3},{3,2},{4,5},{5,4},{6,7},{7,6},{8,9},{9,8},{10,11... | collective-permute-start | bytes 245768 | tf_op jit(solution)/shard_map/ppermute | solution.py:30
  63.5 6.2 %collective-permute-start.21 = (bf16[80,512]{1,0:T(8,128)(2,1)S(1)}, bf16[80,512]{1,0:T(8,128)(2,1)S(1)}, u32[]{:S(2)}, u32[]{:S(2)}) collective-permute-start(bf16[80,512]{1,0:T(8,128)(2,1)S(1)} %get-tuple-element.52), channel_id=1, source_target_pairs={{0,1},{1,0},{2,3},{3,2},{4,5},{5,4},{6,7},{7,6},{8,9},{9,8},{10,11... | collective-permute-start | bytes 245768 | tf_op jit(solution)/shard_map/ppermute | solution.py:30
  (1 other events, 1.3 us)

commit v8 on v7

--- a/solution.py
+++ b/solution.py
@@ -414,14 +414,14 @@
         ]
 
     ahead = call(zero_kernel, shape((8, LANES), f32), flops=LONG)
-    leaving_blocks = blocks_of(plan, sizes, [ahead])
     count, rows = windows[0].shape[0] - 2, windows[0].shape[1] * LANES // old_cols
     window, ends = call(
         first_weights_kernel,
         [shape((count + 2, rows, old_cols), bf16), shape((2, 2, rows, old_cols), bf16)],
         *windows,
-        after=leaving_blocks[:1],
-    )
+        after=[ahead],
+    )
+    leaving_blocks = blocks_of(plan, sizes, [window])
 
     other = swap(window, "group", 1)
     arrived = [

time: 71.2 us -> 70.3 us (0.987)
  transfers between devices with their start and end apart: 25 -> 25, of which waited for: 13 -> 13; matrix products, arithmetic and copies ran while one was open for 0% -> 0% of each run, Pallas kernels for 12% -> 13%
where the time goes in v8:
time: 70.3 us; the launch traced here: 69.8 us
  starting transfers between devices  29 us (41%)
  waiting for transfers between devices  26.8 us (38%)
  Pallas kernels  11.1 us (16%)
  local copies, waits for them, and re-layouts  1.88 us (3%)
  between operations  0.92 us (1%)
    ppermute x24, starting transfers between devices, swap(): return lax.ppermute(value, axis, pairs)  28.2 us
    ppermute x24, waiting for transfers between devices, swap(): return lax.ppermute(value, axis, pairs)  26.8 us
    pallas_call x16, Pallas kernels, call(): pl.pallas_call(body, out_shape=shapes, in_specs=[small] * scalars + [whol...  6.89 us
    pallas_call x4, Pallas kernels, second_adam(): pl.pallas_call(functools.partial(second_adam_kernel, cut), out_shape=[sha...  4.02 us
    unnamed x16, local copies, waits for them, and re-layouts  1.87 us
  transfers between devices with their start and end apart: 25, of which 13 were waited for; matrix products, arithmetic and copies ran while one was open for 0% of the time, Pallas kernels for 13%

profile of v8, /device:TPU:0, one launch (start us, length us, event | category | flops | bytes accessed | tf_op | source)
XLA Modules:
  0.0 69.8 jit_solution(6700157308414860909)
XLA Ops:
  0.7 1.1 %copy-done.4 = f32[1,1,204800]{2,1,0:T(1,128)S(1)} copy-done((f32[1,1,204800]{2,1,0:T(1,128)S(1)}, f32[1,1,204800]{2,1,0:T(1,128)}, u32[]{:S(2)}) %copy-start.4) | copy-done | bytes 819224
  3.2 3.0 %collective-permute-start = (bf16[10,80,256]{2,1,0:T(8,128)(2,1)S(1)}, bf16[10,80,256]{2,1,0:T(8,128)(2,1)S(1)}, u32[]{:S(2)}, u32[]{:S(2)}) collective-permute-start(bf16[10,80,256]{2,1,0:T(8,128)(2,1)S(1)} %get-tuple-element.36.refs_0_.refs_1_), channel_id=1, source_target_pairs={{0,1},{1,0},{2,3},{3,2},{4,5},{5,4},{6,7},{7,6},{8,9},{9,8},{10,11... | collective-permute-start | bytes 1228808 | tf_op jit(solution)/shard_map/ppermute | solution.py:30
  6.4 1.6 %collective-permute-start.4 = (bf16[64,1280]{1,0:T(8,128)(2,1)S(1)}, bf16[64,1280]{1,0:T(8,128)(2,1)S(1)}, u32[]{:S(2)}, u32[]{:S(2)}) collective-permute-start(bf16[64,1280]{1,0:T(8,128)(2,1)S(1)} %get-tuple-element.39), channel_id=1, source_target_pairs={{0,8},{4,12},{8,0},{12,4},{16,24},{20,28},{24,16},{28,20},{1,9},{5... | collective-permute-start | bytes 491528 | tf_op jit(solution)/shard_map/ppermute | solution.py:30
  8.0 2.5 %collective-permute-start.7 = (bf16[64,1280]{1,0:T(8,128)(2,1)S(1)}, bf16[64,1280]{1,0:T(8,128)(2,1)S(1)}, u32[]{:S(2)}, u32[]{:S(2)}) collective-permute-start(bf16[64,1280]{1,0:T(8,128)(2,1)S(1)} %get-tuple-element.43), channel_id=1, source_target_pairs={{0,24},{4,28},{8,16},{12,20},{16,8},{20,12},{24,0},{28,4},{1,25},{... | collective-permute-start | bytes 491528 | tf_op jit(solution)/shard_map/ppermute | solution.py:30
  10.6 5.1 %collective-permute-done.refs_0_.refs_1_.refs_2_ = bf16[10,80,256]{2,1,0:T(8,128)(2,1)S(1)} collective-permute-done((bf16[10,80,256]{2,1,0:T(8,128)(2,1)S(1)}, bf16[10,80,256]{2,1,0:T(8,128)(2,1)S(1)}, u32[]{:S(2)}, u32[]{:S(2)}) %collective-permute-start) | collective-permute-done | bytes 409632 | tf_op jit(solution)/shard_map/ppermute | solution.py:30
  15.8 0.8 %collective-permute-start.3 = (bf16[4,80,256]{2,1,0:T(8,128)(2,1)S(1)}, bf16[4,80,256]{2,1,0:T(8,128)(2,1)S(1)}, u32[]{:S(2)}, u32[]{:S(2)}) collective-permute-start(bf16[4,80,256]{2,1,0:T(8,128)(2,1)S(1)} %get-tuple-element.38), channel_id=1, source_target_pairs={{4,8},{8,4},{12,16},{16,12},{20,24},{24,20},{5,9},{9,5},{13,17},{1... | collective-permute-start | bytes 491528 | tf_op jit(solution)/shard_map/ppermute | solution.py:37
  16.6 1.8 %collective-permute-start.5 = (bf16[64,1280]{1,0:T(8,128)(2,1)S(1)}, bf16[64,1280]{1,0:T(8,128)(2,1)S(1)}, u32[]{:S(2)}, u32[]{:S(2)}) collective-permute-start(bf16[64,1280]{1,0:T(8,128)(2,1)S(1)} %collective-permute-done.4.refs_0_.refs_3_), channel_id=1, source_target_pairs={{0,2},{2,0},{1,3},{3,1},{4,6},{6,4},{5,7},{7,5},{8,10},{10,8},{9,1... | collective-permute-start | bytes 491528 | tf_op jit(solution)/shard_map/ppermute | solution.py:30
  18.4 0.7 collective-permute-done.7.refs_0_.refs_1_
  19.1 1.5 %collective-permute-start.8 = (bf16[64,1280]{1,0:T(8,128)(2,1)S(1)}, bf16[64,1280]{1,0:T(8,128)(2,1)S(1)}, u32[]{:S(2)}, u32[]{:S(2)}) collective-permute-start(bf16[64,1280]{1,0:T(8,128)(2,1)S(1)} %collective-permute-done.7.refs_0_.refs_1_), channel_id=1, source_target_pairs={{0,2},{2,0},{1,3},{3,1},{4,6},{6,4},{5,7},{7,5},{8,10},{10,8},{9,1... | collective-permute-start | bytes 491528 | tf_op jit(solution)/shard_map/ppermute | solution.py:30
  20.6 5.3 %collective-permute-done.11.refs_0_.refs_5_ = bf16[64,1280]{1,0:T(8,128)(2,1)S(1)} collective-permute-done((bf16[64,1280]{1,0:T(8,128)(2,1)S(1)}, bf16[64,1280]{1,0:T(8,128)(2,1)S(1)}, u32[]{:S(2)}, u32[]{:S(2)}) %collective-permute-start.11) | collective-permute-done | bytes 163872 | tf_op jit(solution)/shard_map/ppermute | solution.py:30
  25.8 1.5 %collective-permute-start.12 = (bf16[64,1280]{1,0:T(8,128)(2,1)S(1)}, bf16[64,1280]{1,0:T(8,128)(2,1)S(1)}, u32[]{:S(2)}, u32[]{:S(2)}) collective-permute-start(bf16[64,1280]{1,0:T(8,128)(2,1)S(1)} %collective-permute-done.11.refs_0_.refs_5_), channel_id=1, source_target_pairs={{0,2},{2,0},{1,3},{3,1},{4,6},{6,4},{5,7},{7,5},{8,10},{10,8},{9,1... | collective-permute-start | bytes 491528 | tf_op jit(solution)/shard_map/ppermute | solution.py:30
  28.9 0.8 %shard_map.116 = (bf16[8,80,512]{2,1,0:T(8,128)(2,1)S(1)}, bf16[8,80,512]{2,1,0:T(8,128)(2,1)S(1)}) custom-call(s32[4,9]{1,0:T(4,128)S(1)} %copy-done.6, bf16[10,80,256]{2,1,0:T(8,128)(2,1)S(1)} %get-tuple-element.36.refs_0_.refs_1_, bf16[10,80,256]{2,1,0:T(8,128)(2,1)S(1)} %collective-permute-done.refs_0_.refs_1_.refs_2_, ...), custom_call_target="tpu_custom_call" | custom-call | bytes 1802384 | tf_op jit(solution)/shard_map/pallas_call | solution.py:58
  30.0 3.3 %collective-permute-start.9 = (bf16[128,512]{1,0:T(8,128)(2,1)S(1)}, bf16[128,512]{1,0:T(8,128)(2,1)S(1)}, u32[]{:S(2)}, u32[]{:S(2)}) collective-permute-start(bf16[128,512]{1,0:T(8,128)(2,1)S(1)} %shard_map.118.refs_4_), channel_id=1, source_target_pairs={{0,24},{4,28},{8,16},{12,20},{16,8},{20,12},{24,0},{28,4},{1,25},{... | collective-permute-start | bytes 393224 | tf_op jit(solution)/shard_map/ppermute | solution.py:30
  34.2 1.6 %collective-permute-start.13 = (bf16[128,512]{1,0:T(8,128)(2,1)S(1)}, bf16[128,512]{1,0:T(8,128)(2,1)S(1)}, u32[]{:S(2)}, u32[]{:S(2)}) collective-permute-start(bf16[128,512]{1,0:T(8,128)(2,1)S(1)} %shard_map.120.refs_7_), channel_id=1, source_target_pairs={{0,16},{4,20},{8,24},{12,28},{16,0},{20,4},{24,8},{28,12},{1,17},{... | collective-permute-start | bytes 393224 | tf_op jit(solution)/shard_map/ppermute | solution.py:30
  35.8 1.3 %shard_map.124 = (bf16[3,4,80,256]{3,2,1,0:T(8,128)(2,1)S(1)}, f32[3,4,80,256]{3,2,1,0:T(8,128)S(1)}) custom-call(s32[4,9]{1,0:T(4,128)S(1)} %copy-done.6, f32[10,160,128]{2,1,0:T(8,128)S(1)} %bitcast.15, f32[10,160,128]{2,1,0:T(8,128)S(1)} %bitcast.17, f32[10,160,128]{2,1,0:T(8,128)S(1)} %bitcast.19, f32[10,160,128]{2,1,0:T(8,128)S(1)} %bitcast.21, ...), custom_call_target="tpu_custom_call" | custom-call | bytes 3604624 | tf_op jit(solution)/shard_map/pallas_call | solution.py:58
  37.1 1.5 %collective-permute-start.15 = (bf16[3,4,80,256]{3,2,1,0:T(8,128)(2,1)S(1)}, bf16[3,4,80,256]{3,2,1,0:T(8,128)(2,1)S(1)}, u32[]{:S(2)}, u32[]{:S(2)}) collective-permute-start(bf16[3,4,80,256]{3,2,1,0:T(8,128)(2,1)S(1)} %get-tuple-element.48), channel_id=1, source_target_pairs={{0,1},{1,0},{2,3},{3,2},{4,5},{5,4},{6,7},{7,6},{8,9},{9,8},{10,11... | collective-permute-start | bytes 1474568 | tf_op jit(solution)/shard_map/ppermute | solution.py:30
  38.9 3.1 %collective-permute-done.10.refs_2_ = bf16[128,512]{1,0:T(8,128)(2,1)S(1)} collective-permute-done((bf16[128,512]{1,0:T(8,128)(2,1)S(1)}, bf16[128,512]{1,0:T(8,128)(2,1)S(1)}, u32[]{:S(2)}, u32[]{:S(2)}) %collective-permute-start.10) | collective-permute-done | bytes 131104 | tf_op jit(solution)/shard_map/ppermute | solution.py:30
  42.0 2.8 %collective-permute-done.13.refs_3_ = bf16[128,512]{1,0:T(8,128)(2,1)S(1)} collective-permute-done((bf16[128,512]{1,0:T(8,128)(2,1)S(1)}, bf16[128,512]{1,0:T(8,128)(2,1)S(1)}, u32[]{:S(2)}, u32[]{:S(2)}) %collective-permute-start.13) | collective-permute-done | bytes 131104 | tf_op jit(solution)/shard_map/ppermute | solution.py:30
  44.9 1.1 %collective-permute-start.18 = (bf16[128,512]{1,0:T(8,128)(2,1)S(1)}, bf16[128,512]{1,0:T(8,128)(2,1)S(1)}, u32[]{:S(2)}, u32[]{:S(2)}) collective-permute-start(bf16[128,512]{1,0:T(8,128)(2,1)S(1)} %get-tuple-element.49.refs_8_.refs_1_), channel_id=1, source_target_pairs={{0,16},{4,20},{8,24},{12,28},{16,0},{20,4},{24,8},{28,12},{1,17},{... | collective-permute-start | bytes 393224 | tf_op jit(solution)/shard_map/ppermute | solution.py:30
  46.0 2.0 %collective-permute-start.17 = (bf16[128,512]{1,0:T(8,128)(2,1)S(1)}, bf16[128,512]{1,0:T(8,128)(2,1)S(1)}, u32[]{:S(2)}, u32[]{:S(2)}) collective-permute-start(bf16[128,512]{1,0:T(8,128)(2,1)S(1)} %get-tuple-element.49.refs_8_.refs_1_), channel_id=1, source_target_pairs={{0,8},{4,12},{8,0},{12,4},{16,24},{20,28},{24,16},{28,20},{1,9},{5... | collective-permute-start | bytes 393224 | tf_op jit(solution)/shard_map/ppermute | solution.py:30
  48.0 1.4 %collective-permute-start.16 = (bf16[128,512]{1,0:T(8,128)(2,1)S(1)}, bf16[128,512]{1,0:T(8,128)(2,1)S(1)}, u32[]{:S(2)}, u32[]{:S(2)}) collective-permute-start(bf16[128,512]{1,0:T(8,128)(2,1)S(1)} %get-tuple-element.49.refs_8_.refs_1_), channel_id=1, source_target_pairs={{0,24},{4,28},{8,16},{12,20},{16,8},{20,12},{24,0},{28,4},{1,25},{... | collective-permute-start | bytes 393224 | tf_op jit(solution)/shard_map/ppermute | solution.py:30
  49.4 0.7 %collective-permute-done.15.refs_7_.incoming = bf16[3,4,80,256]{3,2,1,0:T(8,128)(2,1)S(1)} collective-permute-done((bf16[3,4,80,256]{3,2,1,0:T(8,128)(2,1)S(1)}, bf16[3,4,80,256]{3,2,1,0:T(8,128)(2,1)S(1)}, u32[]{:S(2)}, u32[]{:S(2)}) %collective-permute-start.15) | collective-permute-done | bytes 491552 | tf_op jit(solution)/shard_map/ppermute | solution.py:30
  50.2 6.3 %collective-permute-done.18.refs_4_ = bf16[128,512]{1,0:T(8,128)(2,1)S(1)} collective-permute-done((bf16[128,512]{1,0:T(8,128)(2,1)S(1)}, bf16[128,512]{1,0:T(8,128)(2,1)S(1)}, u32[]{:S(2)}, u32[]{:S(2)}) %collective-permute-start.18) | collective-permute-done | bytes 131104 | tf_op jit(solution)/shard_map/ppermute | solution.py:30
  58.9 1.8 %collective-permute-start.24 = (bf16[80,512]{1,0:T(8,128)(2,1)S(1)}, bf16[80,512]{1,0:T(8,128)(2,1)S(1)}, u32[]{:S(2)}, u32[]{:S(2)}) collective-permute-start(bf16[80,512]{1,0:T(8,128)(2,1)S(1)} %get-tuple-element.55), channel_id=1, source_target_pairs={{0,1},{1,0},{2,3},{3,2},{4,5},{5,4},{6,7},{7,6},{8,9},{9,8},{10,11... | collective-permute-start | bytes 245768 | tf_op jit(solution)/shard_map/ppermute | solution.py:30
  61.0 1.7 %collective-permute-start.22 = (bf16[80,512]{1,0:T(8,128)(2,1)S(1)}, bf16[80,512]{1,0:T(8,128)(2,1)S(1)}, u32[]{:S(2)}, u32[]{:S(2)}) collective-permute-start(bf16[80,512]{1,0:T(8,128)(2,1)S(1)} %get-tuple-element.53), channel_id=1, source_target_pairs={{0,1},{1,0},{2,3},{3,2},{4,5},{5,4},{6,7},{7,6},{8,9},{9,8},{10,11... | collective-permute-start | bytes 245768 | tf_op jit(solution)/shard_map/ppermute | solution.py:30
  63.0 0.7 shard_map.123
  63.9 1.0 %shard_map.129 = (f32[320,512]{1,0:T(8,128)}, f32[320,512]{1,0:T(8,128)}, f32[320,512]{1,0:T(8,128)}) custom-call(f32[3,4,80,256]{3,2,1,0:T(8,128)S(1)} %get-tuple-element.47.staying, bf16[3,4,80,256]{3,2,1,0:T(8,128)(2,1)S(1)} %collective-permute-done.15.refs_7_.incoming, f32[2,320,512]{2,1,0:T(8,128)S(1)} %shard_map.126.refs_0_.mine, ...), custom_call_target="tpu_custom_call" | custom-call | bytes 1000000 | tf_op jit(solution)/shard_map/pallas_call | solution.py:350
  64.9 1.1 %collective-permute-done.23.back = bf16[80,512]{1,0:T(8,128)(2,1)S(1)} collective-permute-done((bf16[80,512]{1,0:T(8,128)(2,1)S(1)}, bf16[80,512]{1,0:T(8,128)(2,1)S(1)}, u32[]{:S(2)}, u32[]{:S(2)}) %collective-permute-start.23) | collective-permute-done | bytes 81952 | tf_op jit(solution)/shard_map/ppermute | solution.py:30
  66.0 1.0 %shard_map.130 = (f32[320,512]{1,0:T(8,128)}, f32[320,512]{1,0:T(8,128)}, f32[320,512]{1,0:T(8,128)}) custom-call(f32[3,4,80,256]{3,2,1,0:T(8,128)S(1)} %get-tuple-element.47.staying, bf16[3,4,80,256]{3,2,1,0:T(8,128)(2,1)S(1)} %collective-permute-done.15.refs_7_.incoming, ...), custom_call_target="tpu_custom_call", output_to_operand_aliasing={{0}: (5, {}), {1}: (6, {}), {2}: (7, {})} | custom-call | bytes 1000000 | tf_op jit(solution)/shard_map/pallas_call | solution.py:350
  67.0 0.7 %collective-permute-done.22.back = bf16[80,512]{1,0:T(8,128)(2,1)S(1)} collective-permute-done((bf16[80,512]{1,0:T(8,128)(2,1)S(1)}, bf16[80,512]{1,0:T(8,128)(2,1)S(1)}, u32[]{:S(2)}, u32[]{:S(2)}) %collective-permute-start.22) | collective-permute-done | bytes 81952 | tf_op jit(solution)/shard_map/ppermute | solution.py:30
  67.8 1.0 %shard_map.131 = (f32[320,512]{1,0:T(8,128)}, f32[320,512]{1,0:T(8,128)}, f32[320,512]{1,0:T(8,128)}) custom-call(f32[3,4,80,256]{3,2,1,0:T(8,128)S(1)} %get-tuple-element.47.staying, bf16[3,4,80,256]{3,2,1,0:T(8,128)(2,1)S(1)} %collective-permute-done.15.refs_7_.incoming, ...), custom_call_target="tpu_custom_call", output_to_operand_aliasing={{0}: (5, {}), {1}: (6, {}), {2}: (7, {})} | custom-call | bytes 1000000 | tf_op jit(solution)/shard_map/pallas_call | solution.py:350
  68.8 1.0 %shard_map.132 = (f32[320,512]{1,0:T(8,128)}, f32[320,512]{1,0:T(8,128)}, f32[320,512]{1,0:T(8,128)}) custom-call(f32[3,4,80,256]{3,2,1,0:T(8,128)S(1)} %get-tuple-element.47.staying, bf16[3,4,80,256]{3,2,1,0:T(8,128)(2,1)S(1)} %collective-permute-done.15.refs_7_.incoming, ...), custom_call_target="tpu_custom_call", output_to_operand_aliasing={{0}: (5, {}), {1}: (6, {}), {2}: (7, {})} | custom-call | bytes 1000000 | tf_op jit(solution)/shard_map/pallas_call | solution.py:350
  (57 shorter events, 8.3 us)
Async XLA Ops:
  0.6 1.4 %copy-start.3 = (f32[1,1,204800]{2,1,0:T(1,128)S(1)}, f32[1,1,204800]{2,1,0:T(1,128)}, u32[]{:S(2)}) copy-start(f32[1,1,204800]{2,1,0:T(1,128)} %param.14) | copy-start | bytes 2457604
  0.7 1.6 %copy-start.2 = (f32[1,1,204800]{2,1,0:T(1,128)S(1)}, f32[1,1,204800]{2,1,0:T(1,128)}, u32[]{:S(2)}) copy-start(f32[1,1,204800]{2,1,0:T(1,128)} %param.13) | copy-start | bytes 2457604
  0.7 1.9 %copy-start.1 = (f32[1,1,204800]{2,1,0:T(1,128)S(1)}, f32[1,1,204800]{2,1,0:T(1,128)}, u32[]{:S(2)}) copy-start(f32[1,1,204800]{2,1,0:T(1,128)} %param.12) | copy-start | bytes 2457604
  2.5 3.7 %copy-start = (bf16[128,5120]{1,0:T(8,128)(2,1)S(1)}, bf16[128,5120]{1,0:T(8,128)(2,1)}, u32[]{:S(2)}) copy-start(bf16[128,5120]{1,0:T(8,128)(2,1)} %tokens.3) | copy-start | bytes 3932164
  3.2 12.5 %collective-permute-start = (bf16[10,80,256]{2,1,0:T(8,128)(2,1)S(1)}, bf16[10,80,256]{2,1,0:T(8,128)(2,1)S(1)}, u32[]{:S(2)}, u32[]{:S(2)}) collective-permute-start(bf16[10,80,256]{2,1,0:T(8,128)(2,1)S(1)} %get-tuple-element.36.refs_0_.refs_1_), channel_id=1, source_target_pairs={{0,1},{1,0},{2,3},{3,2},{4,5},{5,4},{6,7},{7,6},{8,9},{9,8},{10,11... | collective-permute-start | bytes 1228808 | tf_op jit(solution)/shard_map/ppermute | solution.py:30
  6.2 9.5 %collective-permute-start.1 = (bf16[10,80,256]{2,1,0:T(8,128)(2,1)S(1)}, bf16[10,80,256]{2,1,0:T(8,128)(2,1)S(1)}, u32[]{:S(2)}, u32[]{:S(2)}) collective-permute-start(bf16[10,80,256]{2,1,0:T(8,128)(2,1)S(1)} %get-tuple-element.36.refs_0_.refs_1_), channel_id=1, source_target_pairs={{0,4},{4,0},{8,12},{12,8},{16,20},{20,16},{24,28},{28,24},{1,5},{5... | collective-permute-start | bytes 1228808 | tf_op jit(solution)/shard_map/ppermute | solution.py:30
  6.4 10.2 %collective-permute-start.4 = (bf16[64,1280]{1,0:T(8,128)(2,1)S(1)}, bf16[64,1280]{1,0:T(8,128)(2,1)S(1)}, u32[]{:S(2)}, u32[]{:S(2)}) collective-permute-start(bf16[64,1280]{1,0:T(8,128)(2,1)S(1)} %get-tuple-element.39), channel_id=1, source_target_pairs={{0,8},{4,12},{8,0},{12,4},{16,24},{20,28},{24,16},{28,20},{1,9},{5... | collective-permute-start | bytes 491528 | tf_op jit(solution)/shard_map/ppermute | solution.py:30
  8.0 11.1 %collective-permute-start.7 = (bf16[64,1280]{1,0:T(8,128)(2,1)S(1)}, bf16[64,1280]{1,0:T(8,128)(2,1)S(1)}, u32[]{:S(2)}, u32[]{:S(2)}) collective-permute-start(bf16[64,1280]{1,0:T(8,128)(2,1)S(1)} %get-tuple-element.43), channel_id=1, source_target_pairs={{0,24},{4,28},{8,16},{12,20},{16,8},{20,12},{24,0},{28,4},{1,25},{... | collective-permute-start | bytes 491528 | tf_op jit(solution)/shard_map/ppermute | solution.py:30
  10.5 15.3 %collective-permute-start.11 = (bf16[64,1280]{1,0:T(8,128)(2,1)S(1)}, bf16[64,1280]{1,0:T(8,128)(2,1)S(1)}, u32[]{:S(2)}, u32[]{:S(2)}) collective-permute-start(bf16[64,1280]{1,0:T(8,128)(2,1)S(1)} %get-tuple-element.44), channel_id=1, source_target_pairs={{0,16},{4,20},{8,24},{12,28},{16,0},{20,4},{24,8},{28,12},{1,17},{... | collective-permute-start | bytes 491528 | tf_op jit(solution)/shard_map/ppermute | solution.py:30
  15.7 13.2 %collective-permute-start.2 = (bf16[10,80,256]{2,1,0:T(8,128)(2,1)S(1)}, bf16[10,80,256]{2,1,0:T(8,128)(2,1)S(1)}, u32[]{:S(2)}, u32[]{:S(2)}) collective-permute-start(bf16[10,80,256]{2,1,0:T(8,128)(2,1)S(1)} %collective-permute-done.refs_0_.refs_1_.refs_2_), channel_id=1, source_target_pairs={{0,4},{4,0},{8,12},{12,8},{16,20},{20,16},{24,28},{28,24},{1,5},{5... | collective-permute-start | bytes 1228808 | tf_op jit(solution)/shard_map/ppermute | solution.py:30
  15.8 12.3 %copy-start.5 = (bf16[128,512]{1,0:T(8,128)(2,1)S(1)}, bf16[128,512]{1,0:T(8,128)(2,1)}, u32[]{:S(2)}) copy-start(bf16[128,512]{1,0:T(8,128)(2,1)} %refs_1_.1) | copy-start | bytes 393220
  15.8 12.3 %copy-start.7 = (s32[16]{0:T(128)S(1)}, s32[16]{0:T(128)}, u32[]{:S(2)}) copy-start(s32[16]{0:T(128)} %refs_0_.4) | copy-start | bytes 196
  15.8 11.5 %collective-permute-start.3 = (bf16[4,80,256]{2,1,0:T(8,128)(2,1)S(1)}, bf16[4,80,256]{2,1,0:T(8,128)(2,1)S(1)}, u32[]{:S(2)}, u32[]{:S(2)}) collective-permute-start(bf16[4,80,256]{2,1,0:T(8,128)(2,1)S(1)} %get-tuple-element.38), channel_id=1, source_target_pairs={{4,8},{8,4},{12,16},{16,12},{20,24},{24,20},{5,9},{9,5},{13,17},{1... | collective-permute-start | bytes 491528 | tf_op jit(solution)/shard_map/ppermute | solution.py:37
  16.6 10.7 %collective-permute-start.5 = (bf16[64,1280]{1,0:T(8,128)(2,1)S(1)}, bf16[64,1280]{1,0:T(8,128)(2,1)S(1)}, u32[]{:S(2)}, u32[]{:S(2)}) collective-permute-start(bf16[64,1280]{1,0:T(8,128)(2,1)S(1)} %collective-permute-done.4.refs_0_.refs_3_), channel_id=1, source_target_pairs={{0,2},{2,0},{1,3},{3,1},{4,6},{6,4},{5,7},{7,5},{8,10},{10,8},{9,1... | collective-permute-start | bytes 491528 | tf_op jit(solution)/shard_map/ppermute | solution.py:30
  19.1 10.5 %collective-permute-start.8 = (bf16[64,1280]{1,0:T(8,128)(2,1)S(1)}, bf16[64,1280]{1,0:T(8,128)(2,1)S(1)}, u32[]{:S(2)}, u32[]{:S(2)}) collective-permute-start(bf16[64,1280]{1,0:T(8,128)(2,1)S(1)} %collective-permute-done.7.refs_0_.refs_1_), channel_id=1, source_target_pairs={{0,2},{2,0},{1,3},{3,1},{4,6},{6,4},{5,7},{7,5},{8,10},{10,8},{9,1... | collective-permute-start | bytes 491528 | tf_op jit(solution)/shard_map/ppermute | solution.py:30
  25.8 8.0 %collective-permute-start.12 = (bf16[64,1280]{1,0:T(8,128)(2,1)S(1)}, bf16[64,1280]{1,0:T(8,128)(2,1)S(1)}, u32[]{:S(2)}, u32[]{:S(2)}) collective-permute-start(bf16[64,1280]{1,0:T(8,128)(2,1)S(1)} %collective-permute-done.11.refs_0_.refs_5_), channel_id=1, source_target_pairs={{0,2},{2,0},{1,3},{3,1},{4,6},{6,4},{5,7},{7,5},{8,10},{10,8},{9,1... | collective-permute-start | bytes 491528 | tf_op jit(solution)/shard_map/ppermute | solution.py:30
  27.3 8.4 %collective-permute-start.14 = (bf16[4,80,256]{2,1,0:T(8,128)(2,1)S(1)}, bf16[4,80,256]{2,1,0:T(8,128)(2,1)S(1)}, u32[]{:S(2)}, u32[]{:S(2)}) collective-permute-start(bf16[4,80,256]{2,1,0:T(8,128)(2,1)S(1)} %get-tuple-element.46), channel_id=1, source_target_pairs={{0,4},{4,0},{8,12},{12,8},{16,20},{20,16},{24,28},{28,24},{1,5},{5... | collective-permute-start | bytes 491528 | tf_op jit(solution)/shard_map/ppermute | solution.py:30
  27.4 1.5 %copy-start.6 = (s32[4,9]{1,0:T(4,128)S(1)}, s32[4,9]{1,0:T(4,128)}, u32[]{:S(2)}) copy-start(s32[4,9]{1,0:T(4,128)} %refs_0_.5) | copy-start | bytes 436
  27.4 1.5 %collective-permute-start.6 = (bf16[2,80,256]{2,1,0:T(8,128)(2,1)S(1)}, bf16[2,80,256]{2,1,0:T(8,128)(2,1)S(1)}, u32[]{:S(2)}, u32[]{:S(2)}) collective-permute-start(bf16[2,80,256]{2,1,0:T(8,128)(2,1)S(1)} %slice.4.refs_5_), channel_id=1, source_target_pairs={{0,4},{4,0},{8,12},{12,8},{16,20},{20,16},{24,28},{28,24},{1,5},{5... | collective-permute-start | bytes 245768 | tf_op jit(solution)/shard_map/ppermute | solution.py:30
  30.0 12.0 %collective-permute-start.9 = (bf16[128,512]{1,0:T(8,128)(2,1)S(1)}, bf16[128,512]{1,0:T(8,128)(2,1)S(1)}, u32[]{:S(2)}, u32[]{:S(2)}) collective-permute-start(bf16[128,512]{1,0:T(8,128)(2,1)S(1)} %shard_map.118.refs_4_), channel_id=1, source_target_pairs={{0,24},{4,28},{8,16},{12,20},{16,8},{20,12},{24,0},{28,4},{1,25},{... | collective-permute-start | bytes 393224 | tf_op jit(solution)/shard_map/ppermute | solution.py:30
  33.7 8.3 %collective-permute-start.10 = (bf16[128,512]{1,0:T(8,128)(2,1)S(1)}, bf16[128,512]{1,0:T(8,128)(2,1)S(1)}, u32[]{:S(2)}, u32[]{:S(2)}) collective-permute-start(bf16[128,512]{1,0:T(8,128)(2,1)S(1)} %shard_map.119.refs_4_), channel_id=1, source_target_pairs={{0,8},{4,12},{8,0},{12,4},{16,24},{20,28},{24,16},{28,20},{1,9},{5... | collective-permute-start | bytes 393224 | tf_op jit(solution)/shard_map/ppermute | solution.py:30
  34.2 10.6 %collective-permute-start.13 = (bf16[128,512]{1,0:T(8,128)(2,1)S(1)}, bf16[128,512]{1,0:T(8,128)(2,1)S(1)}, u32[]{:S(2)}, u32[]{:S(2)}) collective-permute-start(bf16[128,512]{1,0:T(8,128)(2,1)S(1)} %shard_map.120.refs_7_), channel_id=1, source_target_pairs={{0,16},{4,20},{8,24},{12,28},{16,0},{20,4},{24,8},{28,12},{1,17},{... | collective-permute-start | bytes 393224 | tf_op jit(solution)/shard_map/ppermute | solution.py:30
  37.1 13.0 %collective-permute-start.15 = (bf16[3,4,80,256]{3,2,1,0:T(8,128)(2,1)S(1)}, bf16[3,4,80,256]{3,2,1,0:T(8,128)(2,1)S(1)}, u32[]{:S(2)}, u32[]{:S(2)}) collective-permute-start(bf16[3,4,80,256]{3,2,1,0:T(8,128)(2,1)S(1)} %get-tuple-element.48), channel_id=1, source_target_pairs={{0,1},{1,0},{2,3},{3,2},{4,5},{5,4},{6,7},{7,6},{8,9},{9,8},{10,11... | collective-permute-start | bytes 1474568 | tf_op jit(solution)/shard_map/ppermute | solution.py:30
  44.9 11.5 %collective-permute-start.18 = (bf16[128,512]{1,0:T(8,128)(2,1)S(1)}, bf16[128,512]{1,0:T(8,128)(2,1)S(1)}, u32[]{:S(2)}, u32[]{:S(2)}) collective-permute-start(bf16[128,512]{1,0:T(8,128)(2,1)S(1)} %get-tuple-element.49.refs_8_.refs_1_), channel_id=1, source_target_pairs={{0,16},{4,20},{8,24},{12,28},{16,0},{20,4},{24,8},{28,12},{1,17},{... | collective-permute-start | bytes 393224 | tf_op jit(solution)/shard_map/ppermute | solution.py:30
  46.0 10.6 %collective-permute-start.17 = (bf16[128,512]{1,0:T(8,128)(2,1)S(1)}, bf16[128,512]{1,0:T(8,128)(2,1)S(1)}, u32[]{:S(2)}, u32[]{:S(2)}) collective-permute-start(bf16[128,512]{1,0:T(8,128)(2,1)S(1)} %get-tuple-element.49.refs_8_.refs_1_), channel_id=1, source_target_pairs={{0,8},{4,12},{8,0},{12,4},{16,24},{20,28},{24,16},{28,20},{1,9},{5... | collective-permute-start | bytes 393224 | tf_op jit(solution)/shard_map/ppermute | solution.py:30
  48.0 8.6 %collective-permute-start.16 = (bf16[128,512]{1,0:T(8,128)(2,1)S(1)}, bf16[128,512]{1,0:T(8,128)(2,1)S(1)}, u32[]{:S(2)}, u32[]{:S(2)}) collective-permute-start(bf16[128,512]{1,0:T(8,128)(2,1)S(1)} %get-tuple-element.49.refs_8_.refs_1_), channel_id=1, source_target_pairs={{0,24},{4,28},{8,16},{12,20},{16,8},{20,12},{24,0},{28,4},{1,25},{... | collective-permute-start | bytes 393224 | tf_op jit(solution)/shard_map/ppermute | solution.py:30
  57.2 1.7 %collective-permute-start.20 = (bf16[320,512]{1,0:T(8,128)(2,1)S(1)}, bf16[320,512]{1,0:T(8,128)(2,1)S(1)}, u32[]{:S(2)}, u32[]{:S(2)}) collective-permute-start(bf16[320,512]{1,0:T(8,128)(2,1)S(1)} %get-tuple-element.51), channel_id=1, source_target_pairs={{0,4},{4,0},{8,12},{12,8},{16,20},{20,16},{24,28},{28,24},{1,5},{5... | collective-permute-start | bytes 983048 | tf_op jit(solution)/shard_map/ppermute | solution.py:30
  57.2 6.5 %collective-permute-start.19 = (bf16[320,512]{1,0:T(8,128)(2,1)S(1)}, bf16[320,512]{1,0:T(8,128)(2,1)S(1)}, u32[]{:S(2)}, u32[]{:S(2)}) collective-permute-start(bf16[320,512]{1,0:T(8,128)(2,1)S(1)} %get-tuple-element.50), channel_id=1, source_target_pairs={{0,4},{4,0},{8,12},{12,8},{16,20},{20,16},{24,28},{28,24},{1,5},{5... | collective-permute-start | bytes 983048 | tf_op jit(solution)/shard_map/ppermute | solution.py:30
  58.9 5.0 %collective-permute-start.24 = (bf16[80,512]{1,0:T(8,128)(2,1)S(1)}, bf16[80,512]{1,0:T(8,128)(2,1)S(1)}, u32[]{:S(2)}, u32[]{:S(2)}) collective-permute-start(bf16[80,512]{1,0:T(8,128)(2,1)S(1)} %get-tuple-element.55), channel_id=1, source_target_pairs={{0,1},{1,0},{2,3},{3,2},{4,5},{5,4},{6,7},{7,6},{8,9},{9,8},{10,11... | collective-permute-start | bytes 245768 | tf_op jit(solution)/shard_map/ppermute | solution.py:30
  60.7 5.3 %collective-permute-start.23 = (bf16[80,512]{1,0:T(8,128)(2,1)S(1)}, bf16[80,512]{1,0:T(8,128)(2,1)S(1)}, u32[]{:S(2)}, u32[]{:S(2)}) collective-permute-start(bf16[80,512]{1,0:T(8,128)(2,1)S(1)} %get-tuple-element.54), channel_id=1, source_target_pairs={{0,1},{1,0},{2,3},{3,2},{4,5},{5,4},{6,7},{7,6},{8,9},{9,8},{10,11... | collective-permute-start | bytes 245768 | tf_op jit(solution)/shard_map/ppermute | solution.py:30
  61.0 6.7 %collective-permute-start.22 = (bf16[80,512]{1,0:T(8,128)(2,1)S(1)}, bf16[80,512]{1,0:T(8,128)(2,1)S(1)}, u32[]{:S(2)}, u32[]{:S(2)}) collective-permute-start(bf16[80,512]{1,0:T(8,128)(2,1)S(1)} %get-tuple-element.53), channel_id=1, source_target_pairs={{0,1},{1,0},{2,3},{3,2},{4,5},{5,4},{6,7},{7,6},{8,9},{9,8},{10,11... | collective-permute-start | bytes 245768 | tf_op jit(solution)/shard_map/ppermute | solution.py:30
  62.7 6.1 %collective-permute-start.21 = (bf16[80,512]{1,0:T(8,128)(2,1)S(1)}, bf16[80,512]{1,0:T(8,128)(2,1)S(1)}, u32[]{:S(2)}, u32[]{:S(2)}) collective-permute-start(bf16[80,512]{1,0:T(8,128)(2,1)S(1)} %get-tuple-element.52), channel_id=1, source_target_pairs={{0,1},{1,0},{2,3},{3,2},{4,5},{5,4},{6,7},{7,6},{8,9},{9,8},{10,11... | collective-permute-start | bytes 245768 | tf_op jit(solution)/shard_map/ppermute | solution.py:30
  (1 other events, 1.1 us)

commit v9 on v8

--- a/solution.py
+++ b/solution.py
@@ -442,9 +442,6 @@
     )
     inner, outer = swap(to_mate, "dp", 1), swap_border(to_next)
 
-    turned = call(
-        live_kernel, shape((slots, cols), bf16), counts, cotangent, scalars=1, after=[other]
-    )
     blocks = [blocks_of([(0, 0)], [slots], [other])]
     for step in range(1, chips):
         block = [b for at, b in arrived if at == step]
@@ -474,6 +471,10 @@
         parts.append(part(blocks[step], weights, bf16, after=parts[-1:]))
     back = [swap(p, "dp", step * CORES) for step, p in zip(steps, parts, strict=True)]
 
+    turned = call(
+        live_kernel, shape((slots, cols), bf16), counts, cotangent, scalars=1, after=parts[-1:]
+    )
+
     leaving, staying = call(
         states_kernel,
         [shape((3, count // groups, rows, old_cols), dtype) for dtype in (bf16, f32)],

time: 70.3 us -> 70.1 us (level)
  transfers between devices with their start and end apart: 25 -> 25, of which waited for: 13 -> 14; matrix products, arithmetic and copies ran while one was open for 0% -> 0% of each run, Pallas kernels for 13% -> 13%
where the time goes in v9:
time: 70.1 us; the launch traced here: 69.7 us
  starting transfers between devices  28.8 us (41%)
  waiting for transfers between devices  27 us (39%)
  Pallas kernels  11.2 us (16%)
  local copies, waits for them, and re-layouts  1.88 us (3%)
  between operations  0.91 us (1%)
    ppermute x24, starting transfers between devices, swap(): return lax.ppermute(value, axis, pairs)  28.1 us
    ppermute x24, waiting for transfers between devices, swap(): return lax.ppermute(value, axis, pairs)  27 us
    pallas_call x16, Pallas kernels, call(): pl.pallas_call(body, out_shape=shapes, in_specs=[small] * scalars + [whol...  6.9 us
    pallas_call x4, Pallas kernels, second_adam(): pl.pallas_call(functools.partial(second_adam_kernel, cut), out_shape=[sha...  4.01 us
    unnamed x16, local copies, waits for them, and re-layouts  1.87 us
  transfers between devices with their start and end apart: 25, of which 14 were waited for; matrix products, arithmetic and copies ran while one was open for 0% of the time, Pallas kernels for 13%

profile of v9, /device:TPU:0, one launch (start us, length us, event | category | flops | bytes accessed | tf_op | source)
XLA Modules:
  0.0 69.7 jit_solution(3743388216374333564)
XLA Ops:
  0.7 1.1 %copy-done.4 = f32[1,1,204800]{2,1,0:T(1,128)S(1)} copy-done((f32[1,1,204800]{2,1,0:T(1,128)S(1)}, f32[1,1,204800]{2,1,0:T(1,128)}, u32[]{:S(2)}) %copy-start.4) | copy-done | bytes 819224
  3.2 3.0 %collective-permute-start = (bf16[10,80,256]{2,1,0:T(8,128)(2,1)S(1)}, bf16[10,80,256]{2,1,0:T(8,128)(2,1)S(1)}, u32[]{:S(2)}, u32[]{:S(2)}) collective-permute-start(bf16[10,80,256]{2,1,0:T(8,128)(2,1)S(1)} %get-tuple-element.36.refs_0_.refs_1_), channel_id=1, source_target_pairs={{0,1},{1,0},{2,3},{3,2},{4,5},{5,4},{6,7},{7,6},{8,9},{9,8},{10,11... | collective-permute-start | bytes 1228808 | tf_op jit(solution)/shard_map/ppermute | solution.py:30
  6.4 1.6 %collective-permute-start.4 = (bf16[64,1280]{1,0:T(8,128)(2,1)S(1)}, bf16[64,1280]{1,0:T(8,128)(2,1)S(1)}, u32[]{:S(2)}, u32[]{:S(2)}) collective-permute-start(bf16[64,1280]{1,0:T(8,128)(2,1)S(1)} %get-tuple-element.39), channel_id=1, source_target_pairs={{0,8},{4,12},{8,0},{12,4},{16,24},{20,28},{24,16},{28,20},{1,9},{5... | collective-permute-start | bytes 491528 | tf_op jit(solution)/shard_map/ppermute | solution.py:30
  8.0 2.5 %collective-permute-start.7 = (bf16[64,1280]{1,0:T(8,128)(2,1)S(1)}, bf16[64,1280]{1,0:T(8,128)(2,1)S(1)}, u32[]{:S(2)}, u32[]{:S(2)}) collective-permute-start(bf16[64,1280]{1,0:T(8,128)(2,1)S(1)} %get-tuple-element.43), channel_id=1, source_target_pairs={{0,24},{4,28},{8,16},{12,20},{16,8},{20,12},{24,0},{28,4},{1,25},{... | collective-permute-start | bytes 491528 | tf_op jit(solution)/shard_map/ppermute | solution.py:30
  10.6 5.1 %collective-permute-done.refs_0_.refs_1_.refs_2_ = bf16[10,80,256]{2,1,0:T(8,128)(2,1)S(1)} collective-permute-done((bf16[10,80,256]{2,1,0:T(8,128)(2,1)S(1)}, bf16[10,80,256]{2,1,0:T(8,128)(2,1)S(1)}, u32[]{:S(2)}, u32[]{:S(2)}) %collective-permute-start) | collective-permute-done | bytes 409632 | tf_op jit(solution)/shard_map/ppermute | solution.py:30
  15.8 0.7 collective-permute-start.3
  16.5 1.8 %collective-permute-start.5 = (bf16[64,1280]{1,0:T(8,128)(2,1)S(1)}, bf16[64,1280]{1,0:T(8,128)(2,1)S(1)}, u32[]{:S(2)}, u32[]{:S(2)}) collective-permute-start(bf16[64,1280]{1,0:T(8,128)(2,1)S(1)} %collective-permute-done.4.refs_0_.refs_3_), channel_id=1, source_target_pairs={{0,2},{2,0},{1,3},{3,1},{4,6},{6,4},{5,7},{7,5},{8,10},{10,8},{9,1... | collective-permute-start | bytes 491528 | tf_op jit(solution)/shard_map/ppermute | solution.py:30
  18.3 0.8 %collective-permute-done.7.refs_0_.refs_1_ = bf16[64,1280]{1,0:T(8,128)(2,1)S(1)} collective-permute-done((bf16[64,1280]{1,0:T(8,128)(2,1)S(1)}, bf16[64,1280]{1,0:T(8,128)(2,1)S(1)}, u32[]{:S(2)}, u32[]{:S(2)}) %collective-permute-start.7) | collective-permute-done | bytes 163872 | tf_op jit(solution)/shard_map/ppermute | solution.py:30
  19.1 1.5 %collective-permute-start.8 = (bf16[64,1280]{1,0:T(8,128)(2,1)S(1)}, bf16[64,1280]{1,0:T(8,128)(2,1)S(1)}, u32[]{:S(2)}, u32[]{:S(2)}) collective-permute-start(bf16[64,1280]{1,0:T(8,128)(2,1)S(1)} %collective-permute-done.7.refs_0_.refs_1_), channel_id=1, source_target_pairs={{0,2},{2,0},{1,3},{3,1},{4,6},{6,4},{5,7},{7,5},{8,10},{10,8},{9,1... | collective-permute-start | bytes 491528 | tf_op jit(solution)/shard_map/ppermute | solution.py:30
  20.6 5.3 %collective-permute-done.11.refs_0_.refs_5_ = bf16[64,1280]{1,0:T(8,128)(2,1)S(1)} collective-permute-done((bf16[64,1280]{1,0:T(8,128)(2,1)S(1)}, bf16[64,1280]{1,0:T(8,128)(2,1)S(1)}, u32[]{:S(2)}, u32[]{:S(2)}) %collective-permute-start.11) | collective-permute-done | bytes 163872 | tf_op jit(solution)/shard_map/ppermute | solution.py:30
  25.8 1.5 %collective-permute-start.12 = (bf16[64,1280]{1,0:T(8,128)(2,1)S(1)}, bf16[64,1280]{1,0:T(8,128)(2,1)S(1)}, u32[]{:S(2)}, u32[]{:S(2)}) collective-permute-start(bf16[64,1280]{1,0:T(8,128)(2,1)S(1)} %collective-permute-done.11.refs_0_.refs_5_), channel_id=1, source_target_pairs={{0,2},{2,0},{1,3},{3,1},{4,6},{6,4},{5,7},{7,5},{8,10},{10,8},{9,1... | collective-permute-start | bytes 491528 | tf_op jit(solution)/shard_map/ppermute | solution.py:30
  28.0 0.8 %collective-permute-done.6.refs_6_ = bf16[2,80,256]{2,1,0:T(8,128)(2,1)S(1)} collective-permute-done((bf16[2,80,256]{2,1,0:T(8,128)(2,1)S(1)}, bf16[2,80,256]{2,1,0:T(8,128)(2,1)S(1)}, u32[]{:S(2)}, u32[]{:S(2)}) %collective-permute-start.6) | collective-permute-done | bytes 81952 | tf_op jit(solution)/shard_map/ppermute | solution.py:30
  28.9 0.8 %shard_map.116 = (bf16[8,80,512]{2,1,0:T(8,128)(2,1)S(1)}, bf16[8,80,512]{2,1,0:T(8,128)(2,1)S(1)}) custom-call(s32[4,9]{1,0:T(4,128)S(1)} %copy-done.6, bf16[10,80,256]{2,1,0:T(8,128)(2,1)S(1)} %get-tuple-element.36.refs_0_.refs_1_, bf16[10,80,256]{2,1,0:T(8,128)(2,1)S(1)} %collective-permute-done.refs_0_.refs_1_.refs_2_, ...), custom_call_target="tpu_custom_call" | custom-call | bytes 1802384 | tf_op jit(solution)/shard_map/pallas_call | solution.py:58
  30.0 3.3 %collective-permute-start.9 = (bf16[128,512]{1,0:T(8,128)(2,1)S(1)}, bf16[128,512]{1,0:T(8,128)(2,1)S(1)}, u32[]{:S(2)}, u32[]{:S(2)}) collective-permute-start(bf16[128,512]{1,0:T(8,128)(2,1)S(1)} %shard_map.118.refs_4_), channel_id=1, source_target_pairs={{0,24},{4,28},{8,16},{12,20},{16,8},{20,12},{24,0},{28,4},{1,25},{... | collective-permute-start | bytes 393224 | tf_op jit(solution)/shard_map/ppermute | solution.py:30
  34.2 1.5 %collective-permute-start.13 = (bf16[128,512]{1,0:T(8,128)(2,1)S(1)}, bf16[128,512]{1,0:T(8,128)(2,1)S(1)}, u32[]{:S(2)}, u32[]{:S(2)}) collective-permute-start(bf16[128,512]{1,0:T(8,128)(2,1)S(1)} %shard_map.120.refs_2_.refs_7_), channel_id=1, source_target_pairs={{0,16},{4,20},{8,24},{12,28},{16,0},{20,4},{24,8},{28,12},{1,17},{... | collective-permute-start | bytes 393224 | tf_op jit(solution)/shard_map/ppermute | solution.py:30
  35.7 1.3 %shard_map.124 = (bf16[3,4,80,256]{3,2,1,0:T(8,128)(2,1)S(1)}, f32[3,4,80,256]{3,2,1,0:T(8,128)S(1)}) custom-call(s32[4,9]{1,0:T(4,128)S(1)} %copy-done.6, f32[10,160,128]{2,1,0:T(8,128)S(1)} %bitcast.15, f32[10,160,128]{2,1,0:T(8,128)S(1)} %bitcast.17, f32[10,160,128]{2,1,0:T(8,128)S(1)} %bitcast.19, f32[10,160,128]{2,1,0:T(8,128)S(1)} %bitcast.21, ...), custom_call_target="tpu_custom_call" | custom-call | bytes 3604624 | tf_op jit(solution)/shard_map/pallas_call | solution.py:58
  37.0 1.4 %collective-permute-start.15 = (bf16[3,4,80,256]{3,2,1,0:T(8,128)(2,1)S(1)}, bf16[3,4,80,256]{3,2,1,0:T(8,128)(2,1)S(1)}, u32[]{:S(2)}, u32[]{:S(2)}) collective-permute-start(bf16[3,4,80,256]{3,2,1,0:T(8,128)(2,1)S(1)} %get-tuple-element.48), channel_id=1, source_target_pairs={{0,1},{1,0},{2,3},{3,2},{4,5},{5,4},{6,7},{7,6},{8,9},{9,8},{10,11... | collective-permute-start | bytes 1474568 | tf_op jit(solution)/shard_map/ppermute | solution.py:30
  39.4 2.8 %collective-permute-done.10.refs_2_ = bf16[128,512]{1,0:T(8,128)(2,1)S(1)} collective-permute-done((bf16[128,512]{1,0:T(8,128)(2,1)S(1)}, bf16[128,512]{1,0:T(8,128)(2,1)S(1)}, u32[]{:S(2)}, u32[]{:S(2)}) %collective-permute-start.10) | collective-permute-done | bytes 131104 | tf_op jit(solution)/shard_map/ppermute | solution.py:30
  42.2 2.3 %collective-permute-done.13.refs_3_ = bf16[128,512]{1,0:T(8,128)(2,1)S(1)} collective-permute-done((bf16[128,512]{1,0:T(8,128)(2,1)S(1)}, bf16[128,512]{1,0:T(8,128)(2,1)S(1)}, u32[]{:S(2)}, u32[]{:S(2)}) %collective-permute-start.13) | collective-permute-done | bytes 131104 | tf_op jit(solution)/shard_map/ppermute | solution.py:30
  44.7 1.3 %collective-permute-start.18 = (bf16[128,512]{1,0:T(8,128)(2,1)S(1)}, bf16[128,512]{1,0:T(8,128)(2,1)S(1)}, u32[]{:S(2)}, u32[]{:S(2)}) collective-permute-start(bf16[128,512]{1,0:T(8,128)(2,1)S(1)} %get-tuple-element.49.refs_8_.refs_1_), channel_id=1, source_target_pairs={{0,16},{4,20},{8,24},{12,28},{16,0},{20,4},{24,8},{28,12},{1,17},{... | collective-permute-start | bytes 393224 | tf_op jit(solution)/shard_map/ppermute | solution.py:30
  46.0 1.9 %collective-permute-start.17 = (bf16[128,512]{1,0:T(8,128)(2,1)S(1)}, bf16[128,512]{1,0:T(8,128)(2,1)S(1)}, u32[]{:S(2)}, u32[]{:S(2)}) collective-permute-start(bf16[128,512]{1,0:T(8,128)(2,1)S(1)} %get-tuple-element.49.refs_8_.refs_1_), channel_id=1, source_target_pairs={{0,8},{4,12},{8,0},{12,4},{16,24},{20,28},{24,16},{28,20},{1,9},{5... | collective-permute-start | bytes 393224 | tf_op jit(solution)/shard_map/ppermute | solution.py:30
  47.9 1.3 %collective-permute-start.16 = (bf16[128,512]{1,0:T(8,128)(2,1)S(1)}, bf16[128,512]{1,0:T(8,128)(2,1)S(1)}, u32[]{:S(2)}, u32[]{:S(2)}) collective-permute-start(bf16[128,512]{1,0:T(8,128)(2,1)S(1)} %get-tuple-element.49.refs_8_.refs_1_), channel_id=1, source_target_pairs={{0,24},{4,28},{8,16},{12,20},{16,8},{20,12},{24,0},{28,4},{1,25},{... | collective-permute-start | bytes 393224 | tf_op jit(solution)/shard_map/ppermute | solution.py:30
  49.2 0.8 %collective-permute-done.15.refs_7_.incoming = bf16[3,4,80,256]{3,2,1,0:T(8,128)(2,1)S(1)} collective-permute-done((bf16[3,4,80,256]{3,2,1,0:T(8,128)(2,1)S(1)}, bf16[3,4,80,256]{3,2,1,0:T(8,128)(2,1)S(1)}, u32[]{:S(2)}, u32[]{:S(2)}) %collective-permute-start.15) | collective-permute-done | bytes 491552 | tf_op jit(solution)/shard_map/ppermute | solution.py:30
  50.1 6.4 %collective-permute-done.18.refs_4_ = bf16[128,512]{1,0:T(8,128)(2,1)S(1)} collective-permute-done((bf16[128,512]{1,0:T(8,128)(2,1)S(1)}, bf16[128,512]{1,0:T(8,128)(2,1)S(1)}, u32[]{:S(2)}, u32[]{:S(2)}) %collective-permute-start.18) | collective-permute-done | bytes 131104 | tf_op jit(solution)/shard_map/ppermute | solution.py:30
  58.9 1.7 %collective-permute-start.24 = (bf16[80,512]{1,0:T(8,128)(2,1)S(1)}, bf16[80,512]{1,0:T(8,128)(2,1)S(1)}, u32[]{:S(2)}, u32[]{:S(2)}) collective-permute-start(bf16[80,512]{1,0:T(8,128)(2,1)S(1)} %get-tuple-element.55), channel_id=1, source_target_pairs={{0,1},{1,0},{2,3},{3,2},{4,5},{5,4},{6,7},{7,6},{8,9},{9,8},{10,11... | collective-permute-start | bytes 245768 | tf_op jit(solution)/shard_map/ppermute | solution.py:30
  61.0 1.6 %collective-permute-start.22 = (bf16[80,512]{1,0:T(8,128)(2,1)S(1)}, bf16[80,512]{1,0:T(8,128)(2,1)S(1)}, u32[]{:S(2)}, u32[]{:S(2)}) collective-permute-start(bf16[80,512]{1,0:T(8,128)(2,1)S(1)} %get-tuple-element.53), channel_id=1, source_target_pairs={{0,1},{1,0},{2,3},{3,2},{4,5},{5,4},{6,7},{7,6},{8,9},{9,8},{10,11... | collective-permute-start | bytes 245768 | tf_op jit(solution)/shard_map/ppermute | solution.py:30
  64.0 1.0 %shard_map.129 = (f32[320,512]{1,0:T(8,128)}, f32[320,512]{1,0:T(8,128)}, f32[320,512]{1,0:T(8,128)}) custom-call(f32[3,4,80,256]{3,2,1,0:T(8,128)S(1)} %get-tuple-element.47.staying, bf16[3,4,80,256]{3,2,1,0:T(8,128)(2,1)S(1)} %collective-permute-done.15.refs_7_.incoming, f32[2,320,512]{2,1,0:T(8,128)S(1)} %shard_map.126.refs_0_.mine, ...), custom_call_target="tpu_custom_call" | custom-call | bytes 1000000 | tf_op jit(solution)/shard_map/pallas_call | solution.py:350
  65.0 0.9 %collective-permute-done.23.back = bf16[80,512]{1,0:T(8,128)(2,1)S(1)} collective-permute-done((bf16[80,512]{1,0:T(8,128)(2,1)S(1)}, bf16[80,512]{1,0:T(8,128)(2,1)S(1)}, u32[]{:S(2)}, u32[]{:S(2)}) %collective-permute-start.23) | collective-permute-done | bytes 81952 | tf_op jit(solution)/shard_map/ppermute | solution.py:30
  65.9 1.0 %shard_map.130 = (f32[320,512]{1,0:T(8,128)}, f32[320,512]{1,0:T(8,128)}, f32[320,512]{1,0:T(8,128)}) custom-call(f32[3,4,80,256]{3,2,1,0:T(8,128)S(1)} %get-tuple-element.47.staying, bf16[3,4,80,256]{3,2,1,0:T(8,128)(2,1)S(1)} %collective-permute-done.15.refs_7_.incoming, ...), custom_call_target="tpu_custom_call", output_to_operand_aliasing={{0}: (5, {}), {1}: (6, {}), {2}: (7, {})} | custom-call | bytes 1000000 | tf_op jit(solution)/shard_map/pallas_call | solution.py:350
  66.9 0.7 %collective-permute-done.22.back = bf16[80,512]{1,0:T(8,128)(2,1)S(1)} collective-permute-done((bf16[80,512]{1,0:T(8,128)(2,1)S(1)}, bf16[80,512]{1,0:T(8,128)(2,1)S(1)}, u32[]{:S(2)}, u32[]{:S(2)}) %collective-permute-start.22) | collective-permute-done | bytes 81952 | tf_op jit(solution)/shard_map/ppermute | solution.py:30
  67.6 1.0 %shard_map.131 = (f32[320,512]{1,0:T(8,128)}, f32[320,512]{1,0:T(8,128)}, f32[320,512]{1,0:T(8,128)}) custom-call(f32[3,4,80,256]{3,2,1,0:T(8,128)S(1)} %get-tuple-element.47.staying, bf16[3,4,80,256]{3,2,1,0:T(8,128)(2,1)S(1)} %collective-permute-done.15.refs_7_.incoming, ...), custom_call_target="tpu_custom_call", output_to_operand_aliasing={{0}: (5, {}), {1}: (6, {}), {2}: (7, {})} | custom-call | bytes 1000000 | tf_op jit(solution)/shard_map/pallas_call | solution.py:350
  68.7 1.0 %shard_map.132 = (f32[320,512]{1,0:T(8,128)}, f32[320,512]{1,0:T(8,128)}, f32[320,512]{1,0:T(8,128)}) custom-call(f32[3,4,80,256]{3,2,1,0:T(8,128)S(1)} %get-tuple-element.47.staying, bf16[3,4,80,256]{3,2,1,0:T(8,128)(2,1)S(1)} %collective-permute-done.15.refs_7_.incoming, ...), custom_call_target="tpu_custom_call", output_to_operand_aliasing={{0}: (5, {}), {1}: (6, {}), {2}: (7, {})} | custom-call | bytes 1000000 | tf_op jit(solution)/shard_map/pallas_call | solution.py:350
  (57 shorter events, 9.2 us)
Async XLA Ops:
  0.6 1.4 %copy-start.3 = (f32[1,1,204800]{2,1,0:T(1,128)S(1)}, f32[1,1,204800]{2,1,0:T(1,128)}, u32[]{:S(2)}) copy-start(f32[1,1,204800]{2,1,0:T(1,128)} %param.14) | copy-start | bytes 2457604
  0.7 1.6 %copy-start.2 = (f32[1,1,204800]{2,1,0:T(1,128)S(1)}, f32[1,1,204800]{2,1,0:T(1,128)}, u32[]{:S(2)}) copy-start(f32[1,1,204800]{2,1,0:T(1,128)} %param.13) | copy-start | bytes 2457604
  0.7 1.9 %copy-start.1 = (f32[1,1,204800]{2,1,0:T(1,128)S(1)}, f32[1,1,204800]{2,1,0:T(1,128)}, u32[]{:S(2)}) copy-start(f32[1,1,204800]{2,1,0:T(1,128)} %param.12) | copy-start | bytes 2457604
  2.5 3.7 %copy-start = (bf16[128,5120]{1,0:T(8,128)(2,1)S(1)}, bf16[128,5120]{1,0:T(8,128)(2,1)}, u32[]{:S(2)}) copy-start(bf16[128,5120]{1,0:T(8,128)(2,1)} %tokens.3) | copy-start | bytes 3932164
  3.2 12.5 %collective-permute-start = (bf16[10,80,256]{2,1,0:T(8,128)(2,1)S(1)}, bf16[10,80,256]{2,1,0:T(8,128)(2,1)S(1)}, u32[]{:S(2)}, u32[]{:S(2)}) collective-permute-start(bf16[10,80,256]{2,1,0:T(8,128)(2,1)S(1)} %get-tuple-element.36.refs_0_.refs_1_), channel_id=1, source_target_pairs={{0,1},{1,0},{2,3},{3,2},{4,5},{5,4},{6,7},{7,6},{8,9},{9,8},{10,11... | collective-permute-start | bytes 1228808 | tf_op jit(solution)/shard_map/ppermute | solution.py:30
  6.2 9.5 %collective-permute-start.1 = (bf16[10,80,256]{2,1,0:T(8,128)(2,1)S(1)}, bf16[10,80,256]{2,1,0:T(8,128)(2,1)S(1)}, u32[]{:S(2)}, u32[]{:S(2)}) collective-permute-start(bf16[10,80,256]{2,1,0:T(8,128)(2,1)S(1)} %get-tuple-element.36.refs_0_.refs_1_), channel_id=1, source_target_pairs={{0,4},{4,0},{8,12},{12,8},{16,20},{20,16},{24,28},{28,24},{1,5},{5... | collective-permute-start | bytes 1228808 | tf_op jit(solution)/shard_map/ppermute | solution.py:30
  6.4 10.1 %collective-permute-start.4 = (bf16[64,1280]{1,0:T(8,128)(2,1)S(1)}, bf16[64,1280]{1,0:T(8,128)(2,1)S(1)}, u32[]{:S(2)}, u32[]{:S(2)}) collective-permute-start(bf16[64,1280]{1,0:T(8,128)(2,1)S(1)} %get-tuple-element.39), channel_id=1, source_target_pairs={{0,8},{4,12},{8,0},{12,4},{16,24},{20,28},{24,16},{28,20},{1,9},{5... | collective-permute-start | bytes 491528 | tf_op jit(solution)/shard_map/ppermute | solution.py:30
  8.0 11.1 %collective-permute-start.7 = (bf16[64,1280]{1,0:T(8,128)(2,1)S(1)}, bf16[64,1280]{1,0:T(8,128)(2,1)S(1)}, u32[]{:S(2)}, u32[]{:S(2)}) collective-permute-start(bf16[64,1280]{1,0:T(8,128)(2,1)S(1)} %get-tuple-element.43), channel_id=1, source_target_pairs={{0,24},{4,28},{8,16},{12,20},{16,8},{20,12},{24,0},{28,4},{1,25},{... | collective-permute-start | bytes 491528 | tf_op jit(solution)/shard_map/ppermute | solution.py:30
  10.5 15.3 %collective-permute-start.11 = (bf16[64,1280]{1,0:T(8,128)(2,1)S(1)}, bf16[64,1280]{1,0:T(8,128)(2,1)S(1)}, u32[]{:S(2)}, u32[]{:S(2)}) collective-permute-start(bf16[64,1280]{1,0:T(8,128)(2,1)S(1)} %get-tuple-element.44), channel_id=1, source_target_pairs={{0,16},{4,20},{8,24},{12,28},{16,0},{20,4},{24,8},{28,12},{1,17},{... | collective-permute-start | bytes 491528 | tf_op jit(solution)/shard_map/ppermute | solution.py:30
  15.7 13.2 %collective-permute-start.2 = (bf16[10,80,256]{2,1,0:T(8,128)(2,1)S(1)}, bf16[10,80,256]{2,1,0:T(8,128)(2,1)S(1)}, u32[]{:S(2)}, u32[]{:S(2)}) collective-permute-start(bf16[10,80,256]{2,1,0:T(8,128)(2,1)S(1)} %collective-permute-done.refs_0_.refs_1_.refs_2_), channel_id=1, source_target_pairs={{0,4},{4,0},{8,12},{12,8},{16,20},{20,16},{24,28},{28,24},{1,5},{5... | collective-permute-start | bytes 1228808 | tf_op jit(solution)/shard_map/ppermute | solution.py:30
  15.8 13.1 %copy-start.6 = (s32[4,9]{1,0:T(4,128)S(1)}, s32[4,9]{1,0:T(4,128)}, u32[]{:S(2)}) copy-start(s32[4,9]{1,0:T(4,128)} %refs_0_.5) | copy-start | bytes 436
  15.8 11.5 %collective-permute-start.3 = (bf16[4,80,256]{2,1,0:T(8,128)(2,1)S(1)}, bf16[4,80,256]{2,1,0:T(8,128)(2,1)S(1)}, u32[]{:S(2)}, u32[]{:S(2)}) collective-permute-start(bf16[4,80,256]{2,1,0:T(8,128)(2,1)S(1)} %get-tuple-element.38), channel_id=1, source_target_pairs={{4,8},{8,4},{12,16},{16,12},{20,24},{24,20},{5,9},{9,5},{13,17},{1... | collective-permute-start | bytes 491528 | tf_op jit(solution)/shard_map/ppermute | solution.py:37
  16.5 10.9 %collective-permute-start.5 = (bf16[64,1280]{1,0:T(8,128)(2,1)S(1)}, bf16[64,1280]{1,0:T(8,128)(2,1)S(1)}, u32[]{:S(2)}, u32[]{:S(2)}) collective-permute-start(bf16[64,1280]{1,0:T(8,128)(2,1)S(1)} %collective-permute-done.4.refs_0_.refs_3_), channel_id=1, source_target_pairs={{0,2},{2,0},{1,3},{3,1},{4,6},{6,4},{5,7},{7,5},{8,10},{10,8},{9,1... | collective-permute-start | bytes 491528 | tf_op jit(solution)/shard_map/ppermute | solution.py:30
  19.1 10.5 %collective-permute-start.8 = (bf16[64,1280]{1,0:T(8,128)(2,1)S(1)}, bf16[64,1280]{1,0:T(8,128)(2,1)S(1)}, u32[]{:S(2)}, u32[]{:S(2)}) collective-permute-start(bf16[64,1280]{1,0:T(8,128)(2,1)S(1)} %collective-permute-done.7.refs_0_.refs_1_), channel_id=1, source_target_pairs={{0,2},{2,0},{1,3},{3,1},{4,6},{6,4},{5,7},{7,5},{8,10},{10,8},{9,1... | collective-permute-start | bytes 491528 | tf_op jit(solution)/shard_map/ppermute | solution.py:30
  25.8 8.0 %collective-permute-start.12 = (bf16[64,1280]{1,0:T(8,128)(2,1)S(1)}, bf16[64,1280]{1,0:T(8,128)(2,1)S(1)}, u32[]{:S(2)}, u32[]{:S(2)}) collective-permute-start(bf16[64,1280]{1,0:T(8,128)(2,1)S(1)} %collective-permute-done.11.refs_0_.refs_5_), channel_id=1, source_target_pairs={{0,2},{2,0},{1,3},{3,1},{4,6},{6,4},{5,7},{7,5},{8,10},{10,8},{9,1... | collective-permute-start | bytes 491528 | tf_op jit(solution)/shard_map/ppermute | solution.py:30
  27.3 8.4 %collective-permute-start.14 = (bf16[4,80,256]{2,1,0:T(8,128)(2,1)S(1)}, bf16[4,80,256]{2,1,0:T(8,128)(2,1)S(1)}, u32[]{:S(2)}, u32[]{:S(2)}) collective-permute-start(bf16[4,80,256]{2,1,0:T(8,128)(2,1)S(1)} %get-tuple-element.46), channel_id=1, source_target_pairs={{0,4},{4,0},{8,12},{12,8},{16,20},{20,16},{24,28},{28,24},{1,5},{5... | collective-permute-start | bytes 491528 | tf_op jit(solution)/shard_map/ppermute | solution.py:30
  27.4 1.5 %collective-permute-start.6 = (bf16[2,80,256]{2,1,0:T(8,128)(2,1)S(1)}, bf16[2,80,256]{2,1,0:T(8,128)(2,1)S(1)}, u32[]{:S(2)}, u32[]{:S(2)}) collective-permute-start(bf16[2,80,256]{2,1,0:T(8,128)(2,1)S(1)} %slice.4.refs_5_), channel_id=1, source_target_pairs={{0,4},{4,0},{8,12},{12,8},{16,20},{20,16},{24,28},{28,24},{1,5},{5... | collective-permute-start | bytes 245768 | tf_op jit(solution)/shard_map/ppermute | solution.py:30
  30.0 12.2 %collective-permute-start.9 = (bf16[128,512]{1,0:T(8,128)(2,1)S(1)}, bf16[128,512]{1,0:T(8,128)(2,1)S(1)}, u32[]{:S(2)}, u32[]{:S(2)}) collective-permute-start(bf16[128,512]{1,0:T(8,128)(2,1)S(1)} %shard_map.118.refs_4_), channel_id=1, source_target_pairs={{0,24},{4,28},{8,16},{12,20},{16,8},{20,12},{24,0},{28,4},{1,25},{... | collective-permute-start | bytes 393224 | tf_op jit(solution)/shard_map/ppermute | solution.py:30
  33.7 8.5 %collective-permute-start.10 = (bf16[128,512]{1,0:T(8,128)(2,1)S(1)}, bf16[128,512]{1,0:T(8,128)(2,1)S(1)}, u32[]{:S(2)}, u32[]{:S(2)}) collective-permute-start(bf16[128,512]{1,0:T(8,128)(2,1)S(1)} %shard_map.119.refs_4_), channel_id=1, source_target_pairs={{0,8},{4,12},{8,0},{12,4},{16,24},{20,28},{24,16},{28,20},{1,9},{5... | collective-permute-start | bytes 393224 | tf_op jit(solution)/shard_map/ppermute | solution.py:30
  34.2 10.3 %collective-permute-start.13 = (bf16[128,512]{1,0:T(8,128)(2,1)S(1)}, bf16[128,512]{1,0:T(8,128)(2,1)S(1)}, u32[]{:S(2)}, u32[]{:S(2)}) collective-permute-start(bf16[128,512]{1,0:T(8,128)(2,1)S(1)} %shard_map.120.refs_2_.refs_7_), channel_id=1, source_target_pairs={{0,16},{4,20},{8,24},{12,28},{16,0},{20,4},{24,8},{28,12},{1,17},{... | collective-permute-start | bytes 393224 | tf_op jit(solution)/shard_map/ppermute | solution.py:30
  37.0 1.8 %copy-start.5 = (bf16[128,512]{1,0:T(8,128)(2,1)S(1)}, bf16[128,512]{1,0:T(8,128)(2,1)}, u32[]{:S(2)}) copy-start(bf16[128,512]{1,0:T(8,128)(2,1)} %refs_1_.1) | copy-start | bytes 393220
  37.0 1.8 %copy-start.7 = (s32[16]{0:T(128)S(1)}, s32[16]{0:T(128)}, u32[]{:S(2)}) copy-start(s32[16]{0:T(128)} %refs_0_.4) | copy-start | bytes 196
  37.0 12.9 %collective-permute-start.15 = (bf16[3,4,80,256]{3,2,1,0:T(8,128)(2,1)S(1)}, bf16[3,4,80,256]{3,2,1,0:T(8,128)(2,1)S(1)}, u32[]{:S(2)}, u32[]{:S(2)}) collective-permute-start(bf16[3,4,80,256]{3,2,1,0:T(8,128)(2,1)S(1)} %get-tuple-element.48), channel_id=1, source_target_pairs={{0,1},{1,0},{2,3},{3,2},{4,5},{5,4},{6,7},{7,6},{8,9},{9,8},{10,11... | collective-permute-start | bytes 1474568 | tf_op jit(solution)/shard_map/ppermute | solution.py:30
  44.7 11.8 %collective-permute-start.18 = (bf16[128,512]{1,0:T(8,128)(2,1)S(1)}, bf16[128,512]{1,0:T(8,128)(2,1)S(1)}, u32[]{:S(2)}, u32[]{:S(2)}) collective-permute-start(bf16[128,512]{1,0:T(8,128)(2,1)S(1)} %get-tuple-element.49.refs_8_.refs_1_), channel_id=1, source_target_pairs={{0,16},{4,20},{8,24},{12,28},{16,0},{20,4},{24,8},{28,12},{1,17},{... | collective-permute-start | bytes 393224 | tf_op jit(solution)/shard_map/ppermute | solution.py:30
  46.0 10.6 %collective-permute-start.17 = (bf16[128,512]{1,0:T(8,128)(2,1)S(1)}, bf16[128,512]{1,0:T(8,128)(2,1)S(1)}, u32[]{:S(2)}, u32[]{:S(2)}) collective-permute-start(bf16[128,512]{1,0:T(8,128)(2,1)S(1)} %get-tuple-element.49.refs_8_.refs_1_), channel_id=1, source_target_pairs={{0,8},{4,12},{8,0},{12,4},{16,24},{20,28},{24,16},{28,20},{1,9},{5... | collective-permute-start | bytes 393224 | tf_op jit(solution)/shard_map/ppermute | solution.py:30
  47.9 8.7 %collective-permute-start.16 = (bf16[128,512]{1,0:T(8,128)(2,1)S(1)}, bf16[128,512]{1,0:T(8,128)(2,1)S(1)}, u32[]{:S(2)}, u32[]{:S(2)}) collective-permute-start(bf16[128,512]{1,0:T(8,128)(2,1)S(1)} %get-tuple-element.49.refs_8_.refs_1_), channel_id=1, source_target_pairs={{0,24},{4,28},{8,16},{12,20},{16,8},{20,12},{24,0},{28,4},{1,25},{... | collective-permute-start | bytes 393224 | tf_op jit(solution)/shard_map/ppermute | solution.py:30
  57.1 1.7 %collective-permute-start.20 = (bf16[320,512]{1,0:T(8,128)(2,1)S(1)}, bf16[320,512]{1,0:T(8,128)(2,1)S(1)}, u32[]{:S(2)}, u32[]{:S(2)}) collective-permute-start(bf16[320,512]{1,0:T(8,128)(2,1)S(1)} %get-tuple-element.51), channel_id=1, source_target_pairs={{0,4},{4,0},{8,12},{12,8},{16,20},{20,16},{24,28},{28,24},{1,5},{5... | collective-permute-start | bytes 983048 | tf_op jit(solution)/shard_map/ppermute | solution.py:30
  57.2 6.5 %collective-permute-start.19 = (bf16[320,512]{1,0:T(8,128)(2,1)S(1)}, bf16[320,512]{1,0:T(8,128)(2,1)S(1)}, u32[]{:S(2)}, u32[]{:S(2)}) collective-permute-start(bf16[320,512]{1,0:T(8,128)(2,1)S(1)} %get-tuple-element.50), channel_id=1, source_target_pairs={{0,4},{4,0},{8,12},{12,8},{16,20},{20,16},{24,28},{28,24},{1,5},{5... | collective-permute-start | bytes 983048 | tf_op jit(solution)/shard_map/ppermute | solution.py:30
  58.9 5.1 %collective-permute-start.24 = (bf16[80,512]{1,0:T(8,128)(2,1)S(1)}, bf16[80,512]{1,0:T(8,128)(2,1)S(1)}, u32[]{:S(2)}, u32[]{:S(2)}) collective-permute-start(bf16[80,512]{1,0:T(8,128)(2,1)S(1)} %get-tuple-element.55), channel_id=1, source_target_pairs={{0,1},{1,0},{2,3},{3,2},{4,5},{5,4},{6,7},{7,6},{8,9},{9,8},{10,11... | collective-permute-start | bytes 245768 | tf_op jit(solution)/shard_map/ppermute | solution.py:30
  60.5 5.3 %collective-permute-start.23 = (bf16[80,512]{1,0:T(8,128)(2,1)S(1)}, bf16[80,512]{1,0:T(8,128)(2,1)S(1)}, u32[]{:S(2)}, u32[]{:S(2)}) collective-permute-start(bf16[80,512]{1,0:T(8,128)(2,1)S(1)} %get-tuple-element.54), channel_id=1, source_target_pairs={{0,1},{1,0},{2,3},{3,2},{4,5},{5,4},{6,7},{7,6},{8,9},{9,8},{10,11... | collective-permute-start | bytes 245768 | tf_op jit(solution)/shard_map/ppermute | solution.py:30
  61.0 6.6 %collective-permute-start.22 = (bf16[80,512]{1,0:T(8,128)(2,1)S(1)}, bf16[80,512]{1,0:T(8,128)(2,1)S(1)}, u32[]{:S(2)}, u32[]{:S(2)}) collective-permute-start(bf16[80,512]{1,0:T(8,128)(2,1)S(1)} %get-tuple-element.53), channel_id=1, source_target_pairs={{0,1},{1,0},{2,3},{3,2},{4,5},{5,4},{6,7},{7,6},{8,9},{9,8},{10,11... | collective-permute-start | bytes 245768 | tf_op jit(solution)/shard_map/ppermute | solution.py:30
  62.6 6.1 %collective-permute-start.21 = (bf16[80,512]{1,0:T(8,128)(2,1)S(1)}, bf16[80,512]{1,0:T(8,128)(2,1)S(1)}, u32[]{:S(2)}, u32[]{:S(2)}) collective-permute-start(bf16[80,512]{1,0:T(8,128)(2,1)S(1)} %get-tuple-element.52), channel_id=1, source_target_pairs={{0,1},{1,0},{2,3},{3,2},{4,5},{5,4},{6,7},{7,6},{8,9},{9,8},{10,11... | collective-permute-start | bytes 245768 | tf_op jit(solution)/shard_map/ppermute | solution.py:30
  (1 other events, 1.1 us)
